TPU v7x, 32 devices: a whole 2x2x4 slice. The times are simulated.
32 devices in a mesh: dp: 8 (over z, y), pipe: 4 (over x, core).
Axes of the slice: x: 2, y: 2, z: 4, core: 2. Of those that a mesh axis runs over, the one named last changes fastest.
Arguments:
- inputs: bfloat16 [4, 32, 196, 384], P(None, 'dp'), may hold values from -6 to 6
- patch_masks: int32 [4, 32, 2, 196], P(None, 'dp'), may hold values 0 or 1
- out_grad: bfloat16 [4, 32, 196, 384], P(None, 'dp'), may hold values from -6 to 6
- cross_aff_scale: float32 [2, 384], replicated, may hold values from 0.5 to 2
- cross_aff_shift: float32 [2, 384], replicated, may hold values from -3 to 3
- cross_weight: bfloat16 [2, 196, 196], replicated, may hold values from -0.4375 to 0.4375
- cross_bias: float32 [2, 196], replicated, may hold values from -3 to 3
- cross_scale: float32 [2, 384], replicated, may hold values from 0.3 to 1.5
- mixer_aff_scale: float32 [2, 384], replicated, may hold values from 0.5 to 2
- mixer_aff_shift: float32 [2, 384], replicated, may hold values from -3 to 3
- mixer_in: bfloat16 [2, 384, 1536], replicated, may hold values from -0.3125 to 0.3125
- mixer_in_bias: float32 [2, 1536], replicated, may hold values from -3 to 3
- mixer_out: bfloat16 [2, 1536, 384], replicated, may hold values from -0.21875 to 0.21875
- mixer_out_bias: float32 [2, 384], replicated, may hold values from -3 to 3
- mixer_scale: float32 [2, 384], replicated, may hold values from 0.3 to 1.5
Outputs:
- output: bfloat16 [4, 32, 196, 384], P('pipe', 'dp')
- input_grad: bfloat16 [4, 32, 196, 384], P('pipe', 'dp')
- cross_aff_scale_grad: float32 [2, 384], replicated
- cross_aff_shift_grad: float32 [2, 384], replicated
- cross_weight_grad: float32 [2, 196, 196], replicated
- cross_bias_grad: float32 [2, 196], replicated
- cross_scale_grad: float32 [2, 384], replicated
- mixer_aff_scale_grad: float32 [2, 384], replicated
- mixer_aff_shift_grad: float32 [2, 384], replicated
- mixer_in_grad: float32 [2, 384, 1536], replicated
- mixer_in_bias_grad: float32 [2, 1536], replicated
- mixer_out_grad: float32 [2, 1536, 384], replicated
- mixer_out_bias_grad: float32 [2, 384], replicated
- mixer_scale_grad: float32 [2, 384], replicated
- magnitudes: float32 [2, 2, 2], replicated
Inputs may be any that keep to these rules, and one draw needn't show every extreme that they name: `patch_masks`: 1 keeps a patch row, 0 zeroes it.
All inputs are finite; a program needn't handle non-finite values. No bound on the sum of `patch_masks` on one device may be relied on, other than what follows from the above.
Results may differ from a plain program's by a relative error of at most 0.018.
The roundings to bfloat16 on the way count: a program that leaves them out, or rounds other values in their place, can miss the bound.
Values may be sent and summed in bfloat16 or wider, within the bound.
No kernel may reach another device: no remote copies, remote signals or barrier semaphores. Data moves between devices by JAX's collectives and lax.ppermute only.
A program may use at most 320 MiB of HBM per device.

v0:
```python
import jax
import jax.numpy as jnp
from jax import lax
from jax.sharding import PartitionSpec as P

SQRT_HALF = 0.7071067811865476
INV_ROOT_TAU = 0.3989422804014327


def cross_parts(stream, keep_rows, aff_scale, aff_shift, weight, offset):
    normed = aff_scale * stream + aff_shift
    masked = (normed * keep_rows[:, :, None]).astype(jnp.bfloat16)
    mixing = jnp.einsum("qp,ipd->iqd", weight, masked, preferred_element_type=jnp.float32)
    return (normed, masked, mixing + offset[None, :, None])


def cross_forward(stream, keep_rows, aff_scale, aff_shift, weight, offset, layer_scale):
    normed, masked, shifted = cross_parts(stream, keep_rows, aff_scale, aff_shift, weight, offset)
    branch = layer_scale * shifted
    return (stream + branch, jnp.stack([jnp.sum(branch * branch), jnp.sum(normed * normed)]))


def cross_backward(
    stream, upper_grad, keep_rows, aff_scale, aff_shift, weight, offset, layer_scale
):
    normed, masked, shifted = cross_parts(stream, keep_rows, aff_scale, aff_shift, weight, offset)
    scale_grad = jnp.sum(upper_grad * shifted, axis=(0, 1))
    shifted_grad = upper_grad * layer_scale
    offset_grad = jnp.sum(shifted_grad, axis=(0, 2))
    mixing_low = shifted_grad.astype(jnp.bfloat16)
    weight_grad = jnp.einsum("iqd,ipd->qp", mixing_low, masked, preferred_element_type=jnp.float32)
    masked_grad = jnp.einsum("qp,iqd->ipd", weight, mixing_low, preferred_element_type=jnp.float32)
    normed_grad = masked_grad * keep_rows[:, :, None]
    aff_scale_grad = jnp.sum(normed_grad * stream, axis=(0, 1))
    aff_shift_grad = jnp.sum(normed_grad, axis=(0, 1))
    stream_grad = upper_grad + normed_grad * aff_scale
    return (stream_grad, (aff_scale_grad, aff_shift_grad, weight_grad, offset_grad, scale_grad))


def mixer_parts(stream, aff_scale, aff_shift, inner_weight, inner_bias, outer_weight, outer_bias):
    tokens = stream.reshape(-1, stream.shape[-1])
    normed = aff_scale * tokens + aff_shift
    normed_low = normed.astype(jnp.bfloat16)
    hidden = jnp.dot(normed_low, inner_weight, preferred_element_type=jnp.float32) + inner_bias
    gelu_low = jax.nn.gelu(hidden, approximate=False).astype(jnp.bfloat16)
    result = jnp.dot(gelu_low, outer_weight, preferred_element_type=jnp.float32) + outer_bias
    return (tokens, normed, normed_low, hidden, gelu_low, result)


def mixer_forward(
    stream, aff_scale, aff_shift, inner_weight, inner_bias, outer_weight, outer_bias, layer_scale
):
    tokens, normed, normed_low, hidden, gelu_low, result = mixer_parts(
        stream, aff_scale, aff_shift, inner_weight, inner_bias, outer_weight, outer_bias
    )
    branch = layer_scale * result
    leaving = (tokens + branch).reshape(stream.shape)
    return (leaving, jnp.stack([jnp.sum(branch * branch), jnp.sum(normed * normed)]))


def mixer_backward(
    stream,
    upper_grad,
    aff_scale,
    aff_shift,
    inner_weight,
    inner_bias,
    outer_weight,
    outer_bias,
    layer_scale,
):
    tokens, normed, normed_low, hidden, gelu_low, result = mixer_parts(
        stream, aff_scale, aff_shift, inner_weight, inner_bias, outer_weight, outer_bias
    )
    up_rows = upper_grad.reshape(tokens.shape)
    scale_grad = jnp.sum(up_rows * result, axis=0)
    result_grad = up_rows * layer_scale
    outer_bias_grad = jnp.sum(result_grad, axis=0)
    result_low = result_grad.astype(jnp.bfloat16)
    outer_grad = jnp.einsum("th,td->hd", gelu_low, result_low, preferred_element_type=jnp.float32)
    gelu_grad = jnp.einsum(
        "td,hd->th", result_low, outer_weight, preferred_element_type=jnp.float32
    )
    normal_cdf = 0.5 * (1.0 + lax.erf(hidden * SQRT_HALF))
    density = INV_ROOT_TAU * jnp.exp(-0.5 * hidden * hidden)
    hidden_grad = gelu_grad * (normal_cdf + hidden * density)
    inner_bias_grad = jnp.sum(hidden_grad, axis=0)
    hidden_low = hidden_grad.astype(jnp.bfloat16)
    inner_grad = jnp.einsum("td,th->dh", normed_low, hidden_low, preferred_element_type=jnp.float32)
    normed_grad = jnp.einsum(
        "th,dh->td", hidden_low, inner_weight, preferred_element_type=jnp.float32
    )
    aff_scale_grad = jnp.sum(normed_grad * tokens, axis=0)
    aff_shift_grad = jnp.sum(normed_grad, axis=0)
    stream_grad = (up_rows + normed_grad * aff_scale).reshape(stream.shape)
    return (
        stream_grad,
        (
            aff_scale_grad,
            aff_shift_grad,
            inner_grad,
            inner_bias_grad,
            outer_grad,
            outer_bias_grad,
            scale_grad,
        ),
    )


def on_device(
    inputs,
    patch_masks,
    out_grad,
    *weights,
):
    micros = inputs.shape[0]
    depth_count = weights[2].shape[0]
    own = lax.axis_index("pipe")
    per = micros // lax.axis_size("pipe")
    images = per * inputs.shape[1]

    def mine(array):
        part = lax.dynamic_slice_in_dim(array, own * per, per, 0)
        return part.reshape((images,) + part.shape[2:])

    stream = mine(inputs)
    upper = mine(out_grad)
    keep = mine(patch_masks).astype(jnp.float32)
    saved = []
    squares = []
    for layer in range(depth_count):
        saved.append(stream)
        leaving, sums = cross_forward(
            stream.astype(jnp.float32), keep[:, layer], *(w[layer] for w in weights[:5])
        )
        squares.append(sums)
        stream = leaving.astype(jnp.bfloat16)
        saved.append(stream)
        leaving, sums = mixer_forward(stream.astype(jnp.float32), *(w[layer] for w in weights[5:]))
        squares.append(sums)
        stream = leaving.astype(jnp.bfloat16)
    output = stream
    grads = [None] * depth_count
    for layer in reversed(range(depth_count)):
        upper, mixer_terms = mixer_backward(
            saved[2 * layer + 1].astype(jnp.float32),
            upper.astype(jnp.float32),
            *(w[layer] for w in weights[5:]),
        )
        upper = upper.astype(jnp.bfloat16)
        upper, cross_terms = cross_backward(
            saved[2 * layer].astype(jnp.float32),
            upper.astype(jnp.float32),
            keep[:, layer],
            *(w[layer] for w in weights[:5]),
        )
        upper = upper.astype(jnp.bfloat16)
        grads[layer] = cross_terms + mixer_terms
    gradient = tuple((jnp.stack(parts) for parts in zip(*grads)))
    totals = jnp.stack(squares).reshape(depth_count, 2, 2)
    gradient, totals = lax.psum((gradient, totals), ("dp", "pipe"))
    images_all = micros * inputs.shape[1] * lax.axis_size("dp")
    magnitudes = jnp.sqrt(totals / (images_all * inputs.shape[2] * inputs.shape[3]))
    local = (per,) + inputs.shape[1:]
    return (
        output.reshape(local),
        upper.reshape(local),
        *(part / images_all for part in gradient),
        magnitudes,
    )


def solution(mesh):
    in_specs = (
        P(None, "dp", None, None),
        P(None, "dp", None, None),
        P(None, "dp", None, None),
        P(),
        P(),
        P(),
        P(),
        P(),
        P(),
        P(),
        P(),
        P(),
        P(),
        P(),
        P(),
    )
    out_specs = (
        P("pipe", "dp", None, None),
        P("pipe", "dp", None, None),
        P(),
        P(),
        P(),
        P(),
        P(),
        P(),
        P(),
        P(),
        P(),
        P(),
        P(),
        P(),
        P(),
    )
    return jax.shard_map(
        on_device, mesh=mesh, in_specs=in_specs, out_specs=out_specs, check_vma=False
    )
```

profile of v0, /device:TPU:0, one launch (start us, length us, event | category | flops | bytes accessed | tf_op | source)
XLA Modules:
  0.0 331.3 jit_solution(4432573290865257821)
XLA Ops:
  7.2 0.8 fusion.115
  8.0 0.8 slice_reduce_fusion.8
  8.8 0.7 convert_bitcast_fusion.1
  9.5 1.4 fusion.113
  10.9 0.8 slice_reduce_fusion.6
  11.7 0.8 slice_reduce_fusion.3
  12.5 2.6 dynamic-slice_convert_fusion
  15.2 2.2 multiply_reduce_fusion.2
  18.3 14.1 %fusion.2 = (bf16[784,1536]{1,0:T(8,128)(2,1)S(1)}, f32[784,1536]{1,0:T(8,128)}) fusion(f32[1536]{0:T(1024)S(1)} %get-tuple-element.75, bf16[784,384]{1,0:T(8,128)(2,1)S(1)} %convert_element_type.204, bf16[2,384,1536]{2,1,0:T(8,128)(2,1)} %param.25), kind=kOutput, calls=%fused_computation.6 | convolution fusion | flops 1004322816 | bytes 9013248 | tf_op jit(solution)/shard_map/dot_general | solution.py:44
  32.3 3.2 multiply_reduce_fusion.7
  35.6 1.0 multiply_convert_fusion.5
  36.7 1.2 convert_element_type.211
  37.8 2.1 multiply_reduce_fusion
  40.1 1.2 reshape.165
  41.2 1.5 multiply_reduce_fusion.16
  42.9 0.9 convert_element_type.223
  43.8 1.4 copy.56
  45.1 1.1 reshape.171
  46.4 12.8 %fusion.5 = (bf16[784,1536]{1,0:T(8,128)(2,1)S(1)}, f32[784,1536]{1,0:T(8,128)S(1)}) fusion(f32[1536]{0:T(1024)S(1)} %get-tuple-element.74, bf16[784,384]{1,0:T(8,128)(2,1)S(1)} %convert_element_type.215, bf16[2,384,1536]{2,1,0:T(8,128)(2,1)} %param.25), kind=kOutput, calls=%fused_computation.9 | convolution fusion | flops 1004322816 | bytes 9013248 | tf_op jit(solution)/shard_map/dot_general | solution.py:44
  59.3 3.8 %fusion.117 = (f32[1536]{0:T(1024)S(1)}, bf16[784,1536]{1,0:T(8,128)(2,1)S(1)}) fusion(f32[784,1536]{1,0:T(8,128)S(1)} %get-tuple-element.145, f32[1536]{0:T(1024)S(1)} %get-tuple-element.74, bf16[784,384]{1,0:T(8,128)(2,1)S(1)} %copy-done.18, bf16[2,1536,384]{2,1,0:T(8,128)(2,1)S(1)} %copy-done.30), kind=kOutput, calls=%fused_computation.237 | convolution fusion | flops 939293184 | bytes 9021440 | tf_op jit(solution)/shard_map/td,hd->th/dot_general | solution.py:81
  63.1 1.4 fusion.54
  64.5 2.9 convolution_bitcast_fusion.2
  67.4 3.2 convolution_bitcast_fusion
  70.5 3.3 %multiply_reduce_fusion.6 = (f32[]{:T(128)}, f32[384]{0:T(512)}, bf16[784,384]{1,0:T(8,128)(2,1)}, f32[384]{0:T(512)}, f32[384]{0:T(512)}, /*index=5*/f32[784]{0:T(1024)S(1)}, f32[784,384]{1,0:T(8,128)S(1)}) fusion(f32[384]{0:T(512)S(1)} %get-tuple-element.162, f32[784,384]{1,0:T(8,128)S(1)} %copy-done.14, f32[784,384]{1,0:T(8,128)S(1)} %copy-done.7, ...), kind=kOutput, calls=%fused_computation.101 | convolution fusion | flops 929960064 | bytes 9023044 | tf_op jit(solution)/shard_map/dot_general | solution.py:46
  73.9 1.0 copy-done.9
  74.9 0.9 multiply_convert_fusion.8
  75.8 1.4 reshape.172
  77.2 1.2 convert_element_type.230
  78.9 0.8 copy-done.4
  79.7 2.4 multiply_reduce_fusion.1
  82.1 1.0 copy-done
  83.2 1.4 reshape.166
  84.6 5.3 %convolution_bitcast_fusion.1 = f32[1,1536,384]{2,1,0:T(8,128)} fusion(bf16[784,1536]{1,0:T(8,128)(2,1)} %copy-done.33, f32[784,384]{1,0:T(8,128)S(1)} %reshape.166, f32[384]{0:T(512)S(1)} %get-tuple-element.161), kind=kOutput, calls=%fused_computation.53 | convolution fusion | flops 925446144 | bytes 5973504 | tf_op jit(solution)/shard_map/th,td->hd/dot_general | solution.py:80
  90.1 5.5 %fusion.118 = (f32[1536]{0:T(1024)S(1)}, bf16[784,1536]{1,0:T(8,128)(2,1)S(1)}) fusion(f32[784,1536]{1,0:T(8,128)} %get-tuple-element.141, f32[1536]{0:T(1024)S(1)} %get-tuple-element.75, bf16[784,384]{1,0:T(8,128)(2,1)S(1)} %convert_element_type.234, bf16[2,1536,384]{2,1,0:T(8,128)(2,1)} %param.27), kind=kOutput, calls=%fused_computation.238 | convolution fusion | flops 939293184 | bytes 9019392 | tf_op jit(solution)/shard_map/td,hd->th/dot_general | solution.py:81
  95.7 1.4 convolution_bitcast_fusion.3
  98.0 3.4 %multiply_reduce_fusion.8 = (f32[]{:T(128)}, f32[384]{0:T(512)}, f32[784]{0:T(1024)S(1)}, f32[784,384]{1,0:T(8,128)}, f32[384]{0:T(512)}, /*index=5*/f32[384]{0:T(512)S(1)}) fusion(f32[784,384]{1,0:T(8,128)S(1)} %copy-done.34, f32[384]{0:T(512)S(1)} %get-tuple-element.161, f32[784,384]{1,0:T(8,128)S(1)} %copy-done.16, f32[384]{0:T(512)S(1)} %get-tuple-element.85, ...), kind=kOutput, calls=%fused_computation.103 | convolution fusion | flops 929056896 | bytes 8418884 | tf_op jit(solution)/shard_map/th,dh->td/dot_general | solution.py:90
  101.4 2.5 reshape.173
  103.9 1.9 convolution_bitcast_fusion.5
  106.0 4.3 %pad_maximum_fusion.1 = f32[2,1536,384]{2,1,0:T(8,128)} fusion(f32[1,1536,384]{2,1,0:T(8,128)S(1)} %copy-done.12, f32[1,1536,384]{2,1,0:T(8,128)} %convolution_bitcast_fusion.1), kind=kLoop, calls=%fused_computation.51 | loop fusion | flops 1179648 | bytes 9437184 | tf_op jit(solution)/shard_map/stack | solution.py:159
  110.3 0.8 pad_maximum_fusion.2
  111.0 2.5 pad_maximum_fusion
  113.6 1.2 copy-done.8
  114.8 0.9 multiply_convert_fusion.7
  116.6 1.2 convert_element_type.241
  118.3 0.8 copy-done.13
  119.1 1.2 fusion.41
  120.4 1.4 maximum_bitcast_fusion.3
  121.7 1.4 maximum_bitcast_fusion.2
  123.1 1.3 maximum_bitcast_fusion.1
  124.4 1.4 maximum_bitcast_fusion
  126.0 44.4 %all-reduce = (f32[2,384]{1,0:T(2,128)S(1)}, f32[2,384]{1,0:T(2,128)S(1)}, f32[2,196]{1,0:T(2,128)S(1)}, f32[2,384]{1,0:T(2,128)S(1)}, f32[2,384]{1,0:T(2,128)S(...) all-reduce(f32[2,384]{1,0:T(2,128)S(1)} %pad_maximum_fusion.4, ...), channel_id=1, replica_groups=mesh['dp'=8,'pipe'=4] {'dp','pipe'}, use_global_device_ids=true, to_apply=%region_2.0 | all-reduce | flops 8848 | bytes 70784 | tf_op jit(solution)/shard_map/psum | solution.py:161
  170.5 0.7 copy.64
  171.1 1.1 copy.62
  172.3 1.1 copy.61
  173.9 0.6 broadcast_multiply_fusion.10
  174.5 0.6 broadcast_multiply_fusion.9
  175.1 0.6 broadcast_multiply_fusion.8
  175.7 0.6 broadcast_multiply_fusion.7
  178.0 0.6 broadcast_multiply_fusion.3
  178.6 136.2 %all-reduce.4.cloned.1.call-done = (f32[2,196,196]{2,1,0:T(8,128)}, f32[2,384,1536]{2,1,0:T(8,128)}, f32[2,1536,384]{2,1,0:T(8,128)}) async-done(((f32[2,196,196]{2,1,0:T(8,128)}, f32[2,384,1536]{2,1,0:T(8,128)}, f32[2,1536,384]{2,1,0:T(8,128)}), (f32[2,196,196]{2,1,0:T(8,128)}, f32[2,384,1536]{2,1,0:T(8,128)}, f32[2,1536,384]{2,1,0:T(8,128)})) %all-reduce.4.cloned.1.call-update) | async-done | bytes 9744528 | tf_op jit(solution)/shard_map/psum | solution.py:161
  314.8 1.0 broadcast_multiply_fusion.2
  315.8 1.0 copy.63
  316.8 5.1 %broadcast_multiply_fusion.1 = f32[2,384,1536]{2,1,0:T(8,128)} fusion(f32[2,384,1536]{2,1,0:T(8,128)} %get-tuple-element.101), kind=kLoop, calls=%fused_computation.57 | loop fusion | flops 1179648 | bytes 9437184 | tf_op jit(solution)/shard_map/div | solution.py:168
  321.9 2.5 broadcast_multiply_fusion
  (126 shorter events, 7.1 us)
Async XLA Ops:
  7.2 307.6 %all-reduce.4.cloned.1.call-start = ((), (), s32[]{:S(2)}) async-start(), calls=%async_computation | async-start | bytes 19693568 | tf_op jit(solution)/shard_map/psum | solution.py:161
  10.9 6.5 %copy-start.19 = (bf16[1,196,196]{2,0,1:T(2,128)(2,1)}, bf16[1,196,196]{2,0,1:T(2,128)(2,1)S(1)}, u32[]{:S(2)}) copy-start(bf16[1,196,196]{2,0,1:T(2,128)(2,1)S(1)} %get-tuple-element.133) | copy-start | bytes 230500
  15.2 2.2 copy-start.10
  17.4 0.7 copy-start.21
  17.4 0.9 copy-start.22
  17.4 0.9 copy-start.23
  17.6 14.7 %copy-start.5 = (f32[784,384]{1,0:T(8,128)}, f32[784,384]{1,0:T(8,128)S(1)}, u32[]{:S(2)}) copy-start(f32[784,384]{1,0:T(8,128)S(1)} %reshape.164) | copy-start | bytes 3612676
  18.3 14.1 %copy-start.29 = (bf16[2,1536,384]{2,1,0:T(8,128)(2,1)S(1)}, bf16[2,1536,384]{2,1,0:T(8,128)(2,1)}, u32[]{:S(2)}) copy-start(bf16[2,1536,384]{2,1,0:T(8,128)(2,1)} %param.27) | copy-start | bytes 7077892
  32.3 3.2 copy-start.33
  46.4 12.8 %copy-start.18 = (bf16[784,384]{1,0:T(8,128)(2,1)S(1)}, bf16[784,384]{1,0:T(8,128)(2,1)}, u32[]{:S(2)}) copy-start(bf16[784,384]{1,0:T(8,128)(2,1)} %convert_element_type.223) | copy-start | bytes 1806340
  46.4 12.8 %copy-start.30 = (bf16[2,1536,384]{2,1,0:T(8,128)(2,1)S(1)}, bf16[2,1536,384]{2,1,0:T(8,128)(2,1)}, u32[]{:S(2)}) copy-start(bf16[2,1536,384]{2,1,0:T(8,128)(2,1)} %param.27) | copy-start | bytes 7077892
  59.2 3.8 %copy-start.31 = (bf16[2,384,1536]{2,1,0:T(8,128)(2,1)S(1)}, bf16[2,384,1536]{2,1,0:T(8,128)(2,1)}, u32[]{:S(2)}) copy-start(bf16[2,384,1536]{2,1,0:T(8,128)(2,1)} %param.25) | copy-start | bytes 7077892
  63.0 1.4 copy-start.7
  64.5 2.9 copy-start.14
  73.9 1.0 copy-start.9
  78.4 1.3 copy-start.4
  82.1 1.0 copy-start
  84.6 5.3 %copy-start.15 = (f32[784,384]{1,0:T(8,128)}, f32[784,384]{1,0:T(8,128)S(1)}, u32[]{:S(2)}) copy-start(f32[784,384]{1,0:T(8,128)S(1)} %reshape.166) | copy-start | bytes 3612676
  90.1 5.6 %copy-start.6 = (f32[784,384]{1,0:T(8,128)S(1)}, f32[784,384]{1,0:T(8,128)}, u32[]{:S(2)}) copy-start(f32[784,384]{1,0:T(8,128)} %copy-done.5) | copy-start | bytes 3612676
  95.6 1.5 copy-start.16
  95.6 2.0 copy-start.32
  95.7 2.3 copy-start.34
  101.4 2.5 copy-start.11
  103.9 2.0 copy-start.12
  105.9 5.1 %copy-start.1 = (f32[1,384,1536]{2,1,0:T(8,128)S(1)}, f32[1,384,1536]{2,1,0:T(8,128)}, u32[]{:S(2)}) copy-start(f32[1,384,1536]{2,1,0:T(8,128)} %convolution_bitcast_fusion.2) | copy-start | bytes 7077892
  113.5 1.3 copy-start.8
  113.5 2.2 copy-start.26
  113.5 2.2 copy-start.25
  113.5 2.2 copy-start.24
  114.8 1.5 copy-start.2
  114.8 1.7 copy-start.28
  114.8 1.7 copy-start.27
  114.8 3.0 copy-start.20
  115.7 2.6 copy-start.3
  117.8 1.3 copy-start.13
  119.1 53.1 %copy-start.17 = (bf16[784,384]{1,0:T(8,128)(2,1)S(1)}, bf16[784,384]{1,0:T(8,128)(2,1)}, u32[]{:S(2)}) copy-start(bf16[784,384]{1,0:T(8,128)(2,1)} %get-tuple-element.123) | copy-start | bytes 1806340
  316.8 5.1 %slice-start = ((s8[4718592]{0:T(1024)(128)(4,1)}), s8[4194304]{0:T(1024)(128)(4,1)S(1)}, s32[]{:S(2)}) async-start(s8[4718592]{0:T(1024)(128)(4,1)} %bitcast.170), calls=%async_computation.1 | async-start | bytes 8388608
  316.8 5.1 %slice-start.1 = ((s8[4718592]{0:T(1024)(128)(4,1)}), s8[524288]{0:T(1024)(128)(4,1)S(1)}, s32[]{:S(2)}) async-start(s8[4718592]{0:T(1024)(128)(4,1)} %bitcast.170), calls=%async_computation.2 | async-start | bytes 1048576
Sparse Core Ops, SparseCore 0:
  113.7 201.0 all-reduce.3
where the time goes:
time: 332 us; the launch traced here: 331 us
  waiting for transfers between devices  136 us (41%)
  matrix products  69.7 us (21%)
  blocking collectives  44.4 us (13%)
  other arithmetic  36.5 us (11%)
  local copies, waits for them, and re-layouts  29.8 us (9%)
  between operations  14.6 us (4%)
    psum x1, waiting for transfers between devices, on_device(): gradient, totals = lax.psum((gradient, totals), ('dp', 'pipe'))  136 us
    psum x1, blocking collectives, on_device(): gradient, totals = lax.psum((gradient, totals), ('dp', 'pipe'))  44.4 us
    dot_general x2, matrix products, mixer_parts(): jnp.dot(normed_low, inner_weight, preferred_element_type=jnp.float32)  26.8 us
    div x12, other arithmetic, on_device(): part / images_all  13.9 us
    unnamed x79, local copies, waits for them, and re-layouts  10.6 us
    dot_general x2, matrix products, mixer_backward(): jnp.einsum('td,hd->th', result_low, outer_weight, preferred_element_type=...  9.31 us
    dot_general x2, matrix products, mixer_backward(): jnp.einsum('th,td->hd', gelu_low, result_low, preferred_element_type=jnp....  8.49 us
    another operation x12, other arithmetic, on_device(): gradient = tuple((jnp.stack(parts) for parts in zip(*grads)))  7.66 us
  transfers between devices with their start and end apart: 1, of which 1 were waited for; matrix products, arithmetic and copies ran while one was open for 5% of the time, Pallas kernels for 0%

commit v1 on v0

v1 whole, which is shorter than its diff:
```python
import functools

import jax
import jax.numpy as jnp
from jax import lax
from jax.experimental import pallas as pl
from jax.experimental.pallas import tpu as pltpu
from jax.sharding import PartitionSpec as P

SQRT_HALF = 0.7071067811865476
INV_ROOT_TAU = 0.3989422804014327
AXES = ("dp", "pipe")
BLOCKS = 32
HALF = BLOCKS // 2
SCATTERED = 5
LANES = 384
VECTOR_ROWS = 16
BF = jnp.bfloat16
F32 = jnp.float32
VMEM = pl.BlockSpec(memory_space=pltpu.VMEM)
ANY = pl.BlockSpec(memory_space=pl.ANY)
PARAMS = pltpu.CompilerParams(vmem_limit_bytes=56 * 2**20)

CROSS_AFF_SCALE, CROSS_AFF_SHIFT, CROSS_SCALE, CROSS_BIAS = 0, 1, 2, 3
MIXER_AFF_SCALE, MIXER_AFF_SHIFT, MIXER_OUT_BIAS, MIXER_SCALE = 4, 5, 6, 7
MIXER_IN_BIAS = 8
SQUARES = 12


def dot(a, b, a_dim=1, b_dim=0):
    return lax.dot_general(
        a, b, (((a_dim,), (b_dim,)), ((), ())), preferred_element_type=F32
    )


def row_sum(values):
    return jnp.sum(values, axis=0, keepdims=True)


def phase_bits(mesh_shape):
    pipe_bits = [1 << b for b in range(mesh_shape["pipe"].bit_length() - 1)]
    dp_bits = [mesh_shape["pipe"] << b for b in range(mesh_shape["dp"].bit_length() - 1)]
    even = [pipe_bits[0], *pipe_bits[1:], *dp_bits]
    odd = list(even)
    odd[1], odd[2] = even[2], even[1]
    return even, odd


def exchange(values, mesh_shape, phase):
    even, odd = phase_bits(mesh_shape)
    places = range(mesh_shape["dp"] * mesh_shape["pipe"])
    return lax.ppermute(
        values, AXES, [(i, i ^ (odd if i & 1 else even)[phase]) for i in places]
    )


def block_code(mesh_shape, place):
    even, odd = phase_bits(mesh_shape)
    odd_place = place & 1
    code = jnp.int32(0)
    for even_bit, odd_bit in zip(even[:SCATTERED], odd[:SCATTERED]):
        bit = jnp.where(odd_place == 1, (place & odd_bit) != 0, (place & even_bit) != 0)
        code = 2 * code + bit.astype(jnp.int32)
    return code


def own_codes(mesh_shape):
    place = lax.axis_index("dp") * mesh_shape["pipe"] + lax.axis_index("pipe")
    return block_code(mesh_shape, place), block_code(mesh_shape, place ^ 1)


def kept_block(codes, slot):
    return codes[0] ^ slot


def sent_block(codes, slot):
    return codes[1] ^ slot


def inner_spot(block, rows, columns):
    across = columns // LANES
    row_at = pl.multiple_of((block // across) * rows, rows)
    return row_at, pl.multiple_of((block % across) * LANES, LANES)


def pack_blocks(codes, inner_ref, outer_ref, kept_ref, sent_ref, small_ref=None):
    depth = inner_ref.shape[0] * inner_ref.shape[1] // (BLOCKS * LANES)

    def pack(block, slot, out_ref):
        row_at, column_at = inner_spot(block, depth, inner_ref.shape[1])
        out_ref[slot, 0:depth, :] = inner_ref[pl.ds(row_at, depth), pl.ds(column_at, LANES)]
        outer_at = pl.multiple_of(block * depth, depth)
        out_ref[slot, depth : 2 * depth, :] = outer_ref[pl.ds(outer_at, depth), :]
        if small_ref is not None:
            out_ref[slot, 2 * depth :, :] = small_ref[block]

    @pl.loop(0, HALF)
    def _(slot):
        pack(sent_block(codes, slot), slot, sent_ref)
        pack(kept_block(codes, slot), slot, kept_ref)


def pad_masks(mask_ref, keep_ref, layers):
    keep_ref[...] = jnp.zeros_like(keep_ref)
    patches = mask_ref.shape[-1]
    for image in range(mask_ref.shape[0]):
        keep_ref[image, 0:layers, 0:patches] = mask_ref[image].astype(F32)


def pad_rows(source_ref, padded_ref, patches, padded):
    for image in range(source_ref.shape[0]):
        base = image * padded
        padded_ref[base + padded - 16 : base + padded, :] = jnp.zeros((16, LANES), BF)
        padded_ref[base : base + patches, :] = source_ref[image]


def kept_weight(weight_ref, keep_ref, image, layer):
    keep_row = keep_ref[image, layer : layer + 1, :]
    return (weight_ref[layer].astype(F32) * keep_row).astype(BF)


def cross_forward(
    layer, source_ref, target_ref, vectors_ref, keep_ref, weight_ref, bias_ref,
    aff_scale_ref, aff_shift_ref, scale_ref, patches, padded,
):
    aff_scale = aff_scale_ref[layer : layer + 1, :]
    aff_shift = aff_shift_ref[layer : layer + 1, :]
    scale = scale_ref[layer : layer + 1, :]
    branch_squares = jnp.zeros((1, LANES), F32)
    normed_squares = jnp.zeros((1, LANES), F32)
    for image in range(keep_ref.shape[0]):
        rows = slice(image * padded, (image + 1) * padded)
        stream = source_ref[rows, :].astype(F32)
        normed = aff_scale * stream + aff_shift
        mixing = dot(kept_weight(weight_ref, keep_ref, image, layer), normed.astype(BF))
        branch = scale * (mixing + bias_ref[:, layer : layer + 1])
        target_ref[rows, :] = (stream + branch).astype(BF)
        branch_squares += row_sum(branch[0:patches] * branch[0:patches])
        normed_squares += row_sum(normed[0:patches] * normed[0:patches])
    vectors_ref[layer, SQUARES : SQUARES + 1, :] = branch_squares
    vectors_ref[layer, SQUARES + 1 : SQUARES + 2, :] = normed_squares


def mixer_hidden(
    layer, stream_ref, low_ref, fired_ref, slope_ref, vectors_ref,
    aff_scale_ref, aff_shift_ref, inner_ref, inner_bias_ref, images, patches, padded,
):
    aff_scale = aff_scale_ref[layer : layer + 1, :]
    aff_shift = aff_shift_ref[layer : layer + 1, :]
    squares = jnp.zeros((1, LANES), F32)
    for image in range(images):
        rows = slice(image * padded, (image + 1) * padded)
        normed = aff_scale * stream_ref[rows, :].astype(F32) + aff_shift
        low_ref[rows, :] = normed.astype(BF)
        squares += row_sum(normed[0:patches] * normed[0:patches])
    vectors_ref[layer, SQUARES + 3 : SQUARES + 4, :] = squares
    columns = inner_ref.shape[1]
    step = columns // 2

    @pl.loop(0, 2)
    def _(part):
        at = pl.ds(pl.multiple_of(part * step, step), step)
        for image in range(images):
            rows = slice(image * padded, (image + 1) * padded)
            hidden = dot(low_ref[rows, :], inner_ref[:, at]) + inner_bias_ref[layer : layer + 1, at]
            normal_cdf = 0.5 * (1.0 + lax.erf(hidden * SQRT_HALF))
            density = INV_ROOT_TAU * jnp.exp(-0.5 * hidden * hidden)
            fired_ref[rows, at] = (hidden * normal_cdf).astype(BF)
            slope_ref[rows, at] = (normal_cdf + hidden * density).astype(BF)


def mixer_result(layer, fired_ref, outer_ref, outer_bias_ref, rows):
    return dot(fired_ref[rows, :], outer_ref[...]) + outer_bias_ref[layer : layer + 1, :]


def mixer_backward(
    layer, upper_ref, low_ref, fired_ref, slope_ref, scaled_ref, inner_ref, outer_ref,
    inner_grad_ref, outer_grad_ref, vectors_ref, scale_ref, images, padded,
):
    scale = scale_ref[layer : layer + 1, :]
    bias = jnp.zeros((1, LANES), F32)
    for image in range(images):
        rows = slice(image * padded, (image + 1) * padded)
        result_grad = upper_ref[rows, :].astype(F32) * scale
        bias += row_sum(result_grad)
        scaled_ref[rows, :] = result_grad.astype(BF)
    vectors_ref[layer, MIXER_OUT_BIAS : MIXER_OUT_BIAS + 1, :] = bias
    columns = inner_ref.shape[1]
    step = 2 * LANES
    for part in range(columns // step):
        at = slice(part * step, (part + 1) * step)
        outer_grad_ref[at, :] = dot(fired_ref[:, at], scaled_ref[...], 0, 0).astype(BF)
        inner_bias = jnp.zeros((1, step), F32)
        for image in range(images):
            rows = slice(image * padded, (image + 1) * padded)
            hidden_grad = dot(scaled_ref[rows, :], outer_ref[at, :], 1, 1) * slope_ref[
                rows, at
            ].astype(F32)
            inner_bias += row_sum(hidden_grad)
            slope_ref[rows, at] = hidden_grad.astype(BF)
        for piece in range(step // LANES):
            row = MIXER_IN_BIAS + part * (step // LANES) + piece
            vectors_ref[layer, row : row + 1, :] = inner_bias[:, piece * LANES : (piece + 1) * LANES]
        inner_grad_ref[:, at] = dot(low_ref[...], slope_ref[:, at], 0, 0).astype(BF)


def mixer_input_grad(
    layer, upper_ref, stream_ref, hidden_grad_ref, target_ref, inner_ref, vectors_ref,
    aff_scale_ref, images, padded,
):
    aff_scale = aff_scale_ref[layer : layer + 1, :]
    scale_grad = jnp.zeros((1, LANES), F32)
    shift_grad = jnp.zeros((1, LANES), F32)
    for image in range(images):
        rows = slice(image * padded, (image + 1) * padded)
        normed_grad = dot(hidden_grad_ref[rows, :], inner_ref[...], 1, 1)
        scale_grad += row_sum(normed_grad * stream_ref[rows, :].astype(F32))
        shift_grad += row_sum(normed_grad)
        target_ref[rows, :] = (
            upper_ref[rows, :].astype(F32) + normed_grad * aff_scale
        ).astype(BF)
    vectors_ref[layer, MIXER_AFF_SCALE : MIXER_AFF_SCALE + 1, :] = scale_grad
    vectors_ref[layer, MIXER_AFF_SHIFT : MIXER_AFF_SHIFT + 1, :] = shift_grad


def cross_backward(
    layer, stream_ref, upper_ref, target_ref, weight_grad_ref, vectors_ref, keep_ref, weight_ref,
    bias_ref, aff_scale_ref, aff_shift_ref, scale_ref, padded,
):
    aff_scale = aff_scale_ref[layer : layer + 1, :]
    aff_shift = aff_shift_ref[layer : layer + 1, :]
    scale = scale_ref[layer : layer + 1, :]
    aff_scale_grad = jnp.zeros((1, LANES), F32)
    aff_shift_grad = jnp.zeros((1, LANES), F32)
    scale_grad = jnp.zeros((1, LANES), F32)
    bias_grad = jnp.zeros((8, padded), F32)
    weight_grad = jnp.zeros((padded, padded), F32)
    ones = jnp.ones((8, LANES), BF)
    for image in range(keep_ref.shape[0]):
        rows = slice(image * padded, (image + 1) * padded)
        stream = stream_ref[rows, :].astype(F32)
        upper = upper_ref[rows, :].astype(F32)
        normed_low = (aff_scale * stream + aff_shift).astype(BF)
        kept = kept_weight(weight_ref, keep_ref, image, layer)
        shifted = dot(kept, normed_low) + bias_ref[:, layer : layer + 1]
        scale_grad += row_sum(upper * shifted)
        mixing_low = (upper * scale).astype(BF)
        bias_grad += dot(ones, mixing_low, 1, 1)
        weight_grad += dot(mixing_low, normed_low, 1, 1) * keep_ref[image, layer : layer + 1, :]
        normed_grad = dot(kept, mixing_low, 0, 0)
        aff_scale_grad += row_sum(normed_grad * stream)
        aff_shift_grad += row_sum(normed_grad)
        target_ref[rows, :] = (upper + normed_grad * aff_scale).astype(BF)
    weight_grad_ref[layer] = weight_grad
    vectors_ref[layer, CROSS_AFF_SCALE : CROSS_AFF_SCALE + 1, :] = aff_scale_grad
    vectors_ref[layer, CROSS_AFF_SHIFT : CROSS_AFF_SHIFT + 1, :] = aff_shift_grad
    vectors_ref[layer, CROSS_SCALE : CROSS_SCALE + 1, :] = scale_grad
    vectors_ref[layer, CROSS_BIAS : CROSS_BIAS + 1, 0:padded] = bias_grad[0:1]


def cross_setup(mask_ref, weight_ref, keep_ref, padded_weight_ref):
    layers, patches = weight_ref.shape[0], weight_ref.shape[1]
    pad_masks(mask_ref, keep_ref, layers)
    padded_weight_ref[...] = jnp.zeros_like(padded_weight_ref)
    for layer in range(layers):
        padded_weight_ref[layer, 0:patches, 0:patches] = weight_ref[layer]


def first_kernel(
    mesh_shape, patches, padded,
    x_hbm, mask_hbm, g_hbm, cross_weight, inner_hbm, outer_hbm,
    cross_aff_scale, cross_aff_shift, bias_columns, cross_scale,
    mixer_aff_scale, mixer_aff_shift, inner_bias, outer_bias, mixer_scale,
    output, kept, sent, vectors, s1, s2, fired0, slope0, result0, g1,
    x_in, mask_in, g_in, inner0, outer0, inner1, outer1, keep, weight, x_rows, g_rows,
    s3, low, fired1, slope1, scaled, inner_grad, outer_grad, sems,
):
    images = mask_in.shape[0]
    per = x_hbm.shape[0] // mesh_shape["pipe"]
    each = x_hbm.shape[1]
    own = lax.axis_index("pipe") * per
    copies = []
    for number, (source, target) in enumerate(
        ((x_hbm, x_in), (mask_hbm, mask_in), (g_hbm, g_in))
    ):
        for part in range(per):
            copies.append(
                pltpu.make_async_copy(
                    source.at[own + part],
                    target.at[part * each : (part + 1) * each],
                    sems.at[number * per + part],
                )
            )
    base = 3 * per
    for number, (source, target) in enumerate(
        (
            (inner_hbm.at[0], inner0),
            (outer_hbm.at[0], outer0),
            (inner_hbm.at[1], inner1),
            (outer_hbm.at[1], outer1),
        )
    ):
        copies.append(pltpu.make_async_copy(source, target, sems.at[base + number]))
    for copy in copies:
        copy.start()
    for copy in copies[: 2 * per]:
        copy.wait()
    vectors[...] = jnp.zeros_like(vectors)
    cross_setup(mask_in, cross_weight, keep, weight)
    pad_rows(x_in, x_rows, patches, padded)
    cross = (keep, weight, bias_columns, cross_aff_scale, cross_aff_shift, cross_scale)
    cross_forward(0, x_rows, s1, vectors, *cross, patches, padded)
    copies[base].wait()
    mixer = (mixer_aff_scale, mixer_aff_shift)
    mixer_hidden(
        0, s1, low, fired0, slope0, vectors, *mixer, inner0, inner_bias, images, patches, padded
    )
    copies[base + 1].wait()
    squares = jnp.zeros((1, LANES), F32)
    for image in range(images):
        rows = slice(image * padded, (image + 1) * padded)
        result = mixer_result(0, fired0, outer0, outer_bias, rows)
        result0[rows, :] = result.astype(BF)
        branch = mixer_scale[0:1, :] * result
        s2[rows, :] = (s1[rows, :].astype(F32) + branch).astype(BF)
        squares += row_sum(branch[0:patches] * branch[0:patches])
    vectors[0, SQUARES + 2 : SQUARES + 3, :] = squares
    cross_forward(1, s2, s3, vectors, *cross, patches, padded)
    copies[base + 2].wait()
    mixer_hidden(
        1, s3, low, fired1, slope1, vectors, *mixer, inner1, inner_bias, images, patches, padded
    )
    copies[base + 3].wait()
    for copy in copies[2 * per : 3 * per]:
        copy.wait()
    pad_rows(g_in, g_rows, patches, padded)
    mixer_backward(
        1, g_rows, low, fired1, slope1, scaled, inner1, outer1, inner_grad, outer_grad,
        vectors, mixer_scale, images, padded,
    )
    codes = own_codes(mesh_shape)
    pack_blocks(codes, inner_grad, outer_grad, kept, sent)
    squares = jnp.zeros((1, LANES), F32)
    scale_grad = jnp.zeros((1, LANES), F32)
    for image in range(images):
        rows = slice(image * padded, (image + 1) * padded)
        result = mixer_result(1, fired1, outer1, outer_bias, rows)
        scale_grad += row_sum(g_rows[rows, :].astype(F32) * result)
        branch = mixer_scale[1:2, :] * result
        leaving = (s3[rows, :].astype(F32) + branch).astype(BF)
        output[image // each, image % each] = leaving[0:patches]
        squares += row_sum(branch[0:patches] * branch[0:patches])
    vectors[1, SQUARES + 2 : SQUARES + 3, :] = squares
    vectors[1, MIXER_SCALE : MIXER_SCALE + 1, :] = scale_grad
    mixer_input_grad(
        1, g_rows, s3, slope1, g1, inner1, vectors, mixer_aff_scale, images, padded
    )


def second_kernel(
    mesh_shape, patches, padded,
    x_hbm, mask_hbm, cross_weight, inner_hbm, outer_hbm,
    s1, s2, fired0_hbm, slope0_hbm, result0, g1, vectors_in,
    cross_aff_scale, cross_aff_shift, bias_columns, cross_scale,
    mixer_aff_scale, mixer_aff_shift, mixer_scale,
    input_grad, kept, sent,
    x_in, mask_in, inner0, outer0, fired0, slope0, keep, weight, x_rows, g2, low, scaled, g0,
    inner_grad, outer_grad, weight_grad, vectors, small, sems,
):
    images = mask_in.shape[0]
    per = x_hbm.shape[0] // mesh_shape["pipe"]
    each = x_hbm.shape[1]
    own = lax.axis_index("pipe") * per
    copies = []
    for number, (source, target) in enumerate(((mask_hbm, mask_in), (x_hbm, x_in))):
        for part in range(per):
            copies.append(
                pltpu.make_async_copy(
                    source.at[own + part],
                    target.at[part * each : (part + 1) * each],
                    sems.at[number * per + part],
                )
            )
    base = 2 * per
    for number, (source, target) in enumerate(
        (
            (fired0_hbm, fired0),
            (outer_hbm.at[0], outer0),
            (slope0_hbm, slope0),
            (inner_hbm.at[0], inner0),
        )
    ):
        copies.append(pltpu.make_async_copy(source, target, sems.at[base + number]))
    for copy in copies:
        copy.start()
    for copy in copies[:per]:
        copy.wait()
    vectors[...] = vectors_in[...]
    cross_setup(mask_in, cross_weight, keep, weight)
    cross = (keep, weight, bias_columns, cross_aff_scale, cross_aff_shift, cross_scale)
    cross_backward(1, s2, g1, g2, weight_grad, vectors, *cross, padded)
    for image in range(images):
        rows = slice(image * padded, (image + 1) * padded)
        normed = mixer_aff_scale[0:1, :] * s1[rows, :].astype(F32) + mixer_aff_shift[0:1, :]
        low[rows, :] = normed.astype(BF)
    for copy in copies[base:]:
        copy.wait()
    mixer_backward(
        0, g2, low, fired0, slope0, scaled, inner0, outer0, inner_grad, outer_grad,
        vectors, mixer_scale, images, padded,
    )
    vectors[0, MIXER_SCALE : MIXER_SCALE + 1, :] = row_sum(
        g2[...].astype(F32) * result0[...].astype(F32)
    )
    mixer_input_grad(
        0, g2, s1, slope0, scaled, inner0, vectors, mixer_aff_scale, images, padded
    )
    for copy in copies[per:base]:
        copy.wait()
    pad_rows(x_in, x_rows, patches, padded)
    cross_backward(0, x_rows, scaled, g0, weight_grad, vectors, *cross, padded)
    for image in range(images):
        input_grad[image // each, image % each] = g0[image * padded : image * padded + patches, :]
    small[...] = jnp.zeros_like(small)
    groups = padded // VECTOR_ROWS
    layers = cross_weight.shape[0]
    for layer in range(layers):
        for group in range(groups):
            rows = slice(group * VECTOR_ROWS, (group + 1) * VECTOR_ROWS)
            small[layer * groups + group, :, 0:padded] = weight_grad[layer, rows, :].astype(BF)
        small[layers * groups + layer] = vectors[layer].astype(BF)
    pack_blocks(own_codes(mesh_shape), inner_grad, outer_grad, kept, sent, small)


def reduce_blocks(kept, sent, mesh_shape):
    terms = [kept]
    width = HALF
    terms.append(exchange(sent, mesh_shape, 0))
    for phase in range(1, SCATTERED):
        half = width // 2
        leaving = sum(t[half:width].astype(F32) for t in terms).astype(BF)
        terms.append(exchange(leaving, mesh_shape, phase))
        width = half
    total = sum(t[0:1].astype(F32) for t in terms)
    for phase in range(SCATTERED, len(phase_bits(mesh_shape)[0])):
        total = total.astype(BF)
        total = total.astype(F32) + exchange(total, mesh_shape, phase).astype(F32)
    return total.astype(BF)


def gather_blocks(own, mesh_shape):
    held = own
    for phase in reversed(range(1, SCATTERED)):
        held = jnp.concatenate([held, exchange(held, mesh_shape, phase)], axis=0)
    return held, exchange(held, mesh_shape, 0)


def last_kernel(
    mesh_shape, images_all, layers,
    kept1, other1, kept0, other0,
    inner_out, outer_out, weight_out, vectors_out,
):
    codes = own_codes(mesh_shape)
    depth = kept1.shape[1] // 2
    columns = inner_out.shape[2]
    groups = weight_out.shape[1] // VECTOR_ROWS

    def unpack(block, slot, values, layer):
        row_at, column_at = inner_spot(block, depth, columns)
        inner_out[layer, pl.ds(row_at, depth), pl.ds(column_at, LANES)] = (
            values[slot, 0:depth, :].astype(F32) / images_all
        )
        outer_at = pl.multiple_of(block * depth, depth)
        outer_out[layer, pl.ds(outer_at, depth), :] = (
            values[slot, depth : 2 * depth, :].astype(F32) / images_all
        )
        if layer == 0:
            small = values[slot, 2 * depth :, :].astype(F32) / images_all

            @pl.when(block < layers * groups)
            def _():
                at = pl.multiple_of((block % groups) * VECTOR_ROWS, VECTOR_ROWS)
                weight_out[block // groups, pl.ds(at, VECTOR_ROWS), :] = small

            @pl.when((block >= layers * groups) & (block < layers * (groups + 1)))
            def _():
                vectors_out[block - layers * groups] = small

    @pl.loop(0, HALF)
    def _(slot):
        unpack(kept_block(codes, slot), slot, kept1, 1)
        unpack(sent_block(codes, slot), slot, other1, 1)
        unpack(kept_block(codes, slot), slot, kept0, 0)
        unpack(sent_block(codes, slot), slot, other0, 0)


def on_device(
    mesh_shape,
    inputs,
    patch_masks,
    out_grad,
    cross_aff_scale,
    cross_aff_shift,
    cross_weight,
    cross_bias,
    cross_scale,
    mixer_aff_scale,
    mixer_aff_shift,
    mixer_in,
    mixer_in_bias,
    mixer_out,
    mixer_out_bias,
    mixer_scale,
):
    micros, each, patches, width = inputs.shape
    layers, _, columns = mixer_in.shape
    per = micros // mesh_shape["pipe"]
    images = per * each
    padded = -(-patches // 16) * 16
    rows = images * padded
    depth = width * columns // (BLOCKS * LANES)
    bias_columns = jnp.pad(cross_bias.T, ((0, padded - patches), (0, 0)))

    def struct(*shape, dtype=BF):
        return jax.ShapeDtypeStruct(shape, dtype)

    def scratch(*shape, dtype=BF):
        return pltpu.VMEM(shape, dtype)

    local = (per, each, patches, width)
    taken = [
        scratch(images, patches, width),
        scratch(images, layers, patches, dtype=jnp.int32),
    ]
    first_outs = (
        struct(*local),
        struct(HALF, 2 * depth, LANES),
        struct(HALF, 2 * depth, LANES),
        struct(layers, VECTOR_ROWS, LANES, dtype=F32),
        struct(rows, width),
        struct(rows, width),
        struct(rows, columns),
        struct(rows, columns),
        struct(rows, width),
        struct(rows, width),
    )
    output, kept1, sent1, vectors, s1, s2, fired0, slope0, result0, g1 = pl.pallas_call(
        functools.partial(first_kernel, mesh_shape, patches, padded),
        out_shape=first_outs,
        in_specs=[ANY] * 3 + [VMEM] + [ANY] * 2 + [VMEM] * 9,
        out_specs=[VMEM] * len(first_outs),
        scratch_shapes=[
            *taken,
            scratch(images, patches, width),
            scratch(width, columns),
            scratch(columns, width),
            scratch(width, columns),
            scratch(columns, width),
            scratch(images, 8, padded, dtype=F32),
            scratch(layers, padded, padded),
            scratch(rows, width),
            scratch(rows, width),
            scratch(rows, width),
            scratch(rows, width),
            scratch(rows, columns),
            scratch(rows, columns),
            scratch(rows, width),
            scratch(width, columns),
            scratch(columns, width),
            pltpu.SemaphoreType.DMA((3 * per + 4,)),
        ],
        compiler_params=PARAMS,
        name="forward_and_top",
    )(
        inputs, patch_masks, out_grad, cross_weight, mixer_in, mixer_out,
        cross_aff_scale, cross_aff_shift, bias_columns, cross_scale,
        mixer_aff_scale, mixer_aff_shift, mixer_in_bias, mixer_out_bias, mixer_scale,
    )
    second_outs = (
        struct(*local),
        struct(HALF, 2 * depth + VECTOR_ROWS, LANES),
        struct(HALF, 2 * depth + VECTOR_ROWS, LANES),
    )
    input_grad, kept0, sent0 = pl.pallas_call(
        functools.partial(second_kernel, mesh_shape, patches, padded),
        out_shape=second_outs,
        in_specs=[ANY] * 2 + [VMEM] + [ANY] * 2 + [VMEM] * 2 + [ANY] * 2 + [VMEM] * 10,
        out_specs=[VMEM] * len(second_outs),
        scratch_shapes=[
            *taken,
            scratch(width, columns),
            scratch(columns, width),
            scratch(rows, columns),
            scratch(rows, columns),
            scratch(images, 8, padded, dtype=F32),
            scratch(layers, padded, padded),
            scratch(rows, width),
            scratch(rows, width),
            scratch(rows, width),
            scratch(rows, width),
            scratch(rows, width),
            scratch(width, columns),
            scratch(columns, width),
            scratch(layers, padded, padded, dtype=F32),
            scratch(layers, VECTOR_ROWS, LANES, dtype=F32),
            scratch(BLOCKS, VECTOR_ROWS, LANES),
            pltpu.SemaphoreType.DMA((2 * per + 4,)),
        ],
        compiler_params=PARAMS,
        name="rest_of_backward",
    )(
        inputs, patch_masks, cross_weight, mixer_in, mixer_out,
        s1, s2, fired0, slope0, result0, g1, vectors,
        cross_aff_scale, cross_aff_shift, bias_columns, cross_scale,
        mixer_aff_scale, mixer_aff_shift, mixer_scale,
    )
    gathered1 = gather_blocks(reduce_blocks(kept1, sent1, mesh_shape), mesh_shape)
    gathered0 = gather_blocks(reduce_blocks(kept0, sent0, mesh_shape), mesh_shape)
    images_all = micros * each * mesh_shape["dp"]
    last_outs = (
        struct(layers, width, columns, dtype=F32),
        struct(layers, columns, width, dtype=F32),
        struct(layers, padded, LANES, dtype=F32),
        struct(layers, VECTOR_ROWS, LANES, dtype=F32),
    )
    inner_grad, outer_grad, weight_grad, sums = pl.pallas_call(
        functools.partial(last_kernel, mesh_shape, images_all, layers),
        out_shape=last_outs,
        in_specs=[VMEM] * 4,
        out_specs=[VMEM] * len(last_outs),
        compiler_params=PARAMS,
        name="unpack",
    )(*gathered1, *gathered0)
    squares = jnp.sum(sums[:, SQUARES:], axis=2).reshape(layers, 2, 2)
    return (
        output,
        input_grad,
        sums[:, CROSS_AFF_SCALE],
        sums[:, CROSS_AFF_SHIFT],
        weight_grad[:, :patches, :patches],
        sums[:, CROSS_BIAS, :patches],
        sums[:, CROSS_SCALE],
        sums[:, MIXER_AFF_SCALE],
        sums[:, MIXER_AFF_SHIFT],
        inner_grad,
        sums[:, MIXER_IN_BIAS:SQUARES].reshape(layers, columns),
        outer_grad,
        sums[:, MIXER_OUT_BIAS],
        sums[:, MIXER_SCALE],
        jnp.sqrt(squares / (patches * width)),
    )


def solution(mesh):
    split = P(None, "dp", None, None)
    owned = P("pipe", "dp", None, None)
    return jax.shard_map(
        functools.partial(on_device, dict(mesh.shape)),
        mesh=mesh,
        in_specs=(split,) * 3 + (P(),) * 12,
        out_specs=(owned,) * 2 + (P(),) * 13,
        check_vma=False,
    )
```

time: 332 us -> 151 us (0.45)
  waiting for transfers between devices: 136 us -> 45.8 us
  matrix products: 69.7 us -> 0 us
  blocking collectives: 44.4 us -> 0 us
  Pallas kernels: 0 us -> 43.4 us
  starting transfers between devices: 0.04 us -> 34.6 us
  other arithmetic: 36.5 us -> 3.4 us
  between operations: 14.6 us -> 0.88 us
  local copies, waits for them, and re-layouts: 29.8 us -> 21.2 us
    psum x1 -> x0, waiting for transfers between devices: 136 us -> none  [on_device(): gradient, totals = lax.psum((gradient, totals), ('dp', 'pipe'))]
    dot_general x18 -> x0, matrix products: 69.7 us -> none  [the longest x2 26.8 us: mixer_parts(): jnp.dot(normed_low, inner_weight, preferred_element_type=jnp.float32)]
    ppermute x0 -> x20, waiting for transfers between devices: none -> 45.8 us  [exchange(): lax.ppermute(values, AXES, [(i, i ^ (odd if i & 1 else even)[phase]) for...]
    psum x1 -> x0, blocking collectives: 44.4 us -> none  [on_device(): gradient, totals = lax.psum((gradient, totals), ('dp', 'pipe'))]
    pallas_call x0 -> x3, Pallas kernels: none -> 43.4 us  [the longest x1 20.9 us: on_device(): pl.pallas_call(functools.partial(first_kernel, mesh_shape, patches, padde...]
    ppermute x0 -> x20, starting transfers between devices: none -> 34.6 us  [exchange(): lax.ppermute(values, AXES, [(i, i ^ (odd if i & 1 else even)[phase]) for...]
    div x12 -> x0, other arithmetic: 13.9 us -> none  [on_device(): part / images_all]
    another operation x17 -> x0, other arithmetic: 13.1 us -> none  [the longest x12 7.66 us: on_device(): gradient = tuple((jnp.stack(parts) for parts in zip(*grads)))]
  transfers between devices with their start and end apart: 1 -> 20, of which waited for: 1 -> 15; matrix products, arithmetic and copies ran while one was open for 5% -> 3% of each run, Pallas kernels for 0% -> 0%
where the time goes in v1:
time: 151 us; the launch traced here: 149 us
  waiting for transfers between devices  45.8 us (30%)
  Pallas kernels  43.4 us (29%)
  starting transfers between devices  34.6 us (23%)
  local copies, waits for them, and re-layouts  21.2 us (14%)
  other arithmetic  3.4 us (2%)
    ppermute x20, waiting for transfers between devices, exchange(): lax.ppermute(values, AXES, [(i, i ^ (odd if i & 1 else even)[phase]) for...  45.8 us
    ppermute x20, starting transfers between devices, exchange(): lax.ppermute(values, AXES, [(i, i ^ (odd if i & 1 else even)[phase]) for...  34.6 us
    pallas_call x1, Pallas kernels, on_device(): pl.pallas_call(functools.partial(first_kernel, mesh_shape, patches, padde...  20.9 us
    unnamed x39, local copies, waits for them, and re-layouts  16.8 us
    pallas_call x1, Pallas kernels, on_device(): pl.pallas_call(functools.partial(second_kernel, mesh_shape, patches, padd...  14.8 us
    pallas_call x1, Pallas kernels, on_device(): pl.pallas_call(functools.partial(last_kernel, mesh_shape, images_all, lay...  7.66 us
  transfers between devices with their start and end apart: 20, of which 15 were waited for; matrix products, arithmetic and copies ran while one was open for 3% of the time, Pallas kernels for 0%

profile of v1, /device:TPU:0, one launch (start us, length us, event | category | flops | bytes accessed | tf_op | source)
XLA Modules:
  0.0 149.3 jit_solution(1254442586861396743)
XLA Ops:
  0.6 0.8 copy.30
  1.4 1.6 %copy.33.cross_weight = bf16[2,196,196]{2,1,0:T(8,128)(2,1)} copy(bf16[2,196,196]{2,0,1:T(2,128)(2,1)} %param.20) | data formatting | bytes 307328 | tf_op args[5]
  3.1 3.6 %copy.31.x_hbm = bf16[4,4,196,384]{3,2,1,0:T(8,128)(2,1)} copy(bf16[4,4,196,384]{3,1,2,0:T(4,128)(2,1)} %param.15) | data formatting | bytes 4816896 | tf_op args[0]
  6.7 1.8 %copy.32.g_hbm = bf16[4,4,196,384]{3,2,1,0:T(8,128)(2,1)} copy(bf16[4,4,196,384]{3,1,2,0:T(4,128)(2,1)S(1)} %copy-done) | data formatting | bytes 4816896 | tf_op args[2]
  8.5 0.7 pad.4.bias_columns
  9.1 20.9 %forward_and_top.1 = (bf16[1,4,196,384]{3,2,1,0:T(8,128)(2,1)}, bf16[16,96,384]{2,1,0:T(8,128)(2,1)}, bf16[16,96,384]{2,1,0:T(8,128)(2,1)}, f32[2,16,384]{2,1,0:...) custom-call(bf16[4,4,196,384]{3,2,1,0:T(8,128)(2,1)} %copy.31.x_hbm,, ...), custom_call_target="tpu_custom_call" | custom-call | tf_op jit(solution)/shard_map/forward_and_top/pallas_call | solution.py:547
  30.0 14.8 %rest_of_backward.1 = (bf16[1,4,196,384]{3,2,1,0:T(8,128)(2,1)}, bf16[16,112,384]{2,1,0:T(8,128)(2,1)}, bf16[16,112,384]{2,1,0:T(8,128)(2,1)}) custom-call(bf16[4,4,196,384]{3,2,1,0:T(8,128)(2,1)} %copy.31.x_hbm, s32[4,4,2,196]{3,2,1,0:T(2,128)} %mask_hbm.3, bf16[2,196,196]{2,1,0:T(8,128)(2,1)} %copy.33.cross_weight, bf16[2,384,1536]{2,1,0:T(8,128)(2,1)} %inner_hbm.3, ...), custom_call_target="tpu_custom_call" | custom-call | tf_op jit(solution)/shard_map/rest_of_backward/pallas_call | solution.py:584
  44.9 0.5 collective-permute-start.10
  45.5 4.0 %collective-permute-done.10 = bf16[16,112,384]{2,1,0:T(8,128)(2,1)S(1)} collective-permute-done((bf16[16,112,384]{2,1,0:T(8,128)(2,1)}, bf16[16,112,384]{2,1,0:T(8,128)(2,1)S(1)}, u32[]{:S(2)}, u32[]{:S(2)}) %collective-permute-start.10) | collective-permute-done | bytes 1376288 | tf_op jit(solution)/shard_map/ppermute | solution.py:52
  49.5 1.4 add_convert_fusion
  50.8 3.0 %collective-permute-start.11 = (bf16[8,112,384]{2,1,0:T(8,128)(2,1)S(1)}, bf16[8,112,384]{2,1,0:T(8,128)(2,1)S(1)}, u32[]{:S(2)}, u32[]{:S(2)}) collective-permute-start(bf16[8,112,384]{2,1,0:T(8,128)(2,1)S(1)} %add_convert_fusion), channel_id=1, source_target_pairs={{0,2},{1,5},{2,0},{3,7},{4,6},{5,1},{6,4},{7,3},{8,10},{9,13},{10,... | collective-permute-start | bytes 2064392 | tf_op jit(solution)/shard_map/ppermute | solution.py:52
  53.8 8.9 %collective-permute-done.11 = bf16[8,112,384]{2,1,0:T(8,128)(2,1)S(1)} collective-permute-done((bf16[8,112,384]{2,1,0:T(8,128)(2,1)S(1)}, bf16[8,112,384]{2,1,0:T(8,128)(2,1)S(1)}, u32[]{:S(2)}, u32[]{:S(2)}) %collective-permute-start.11) | collective-permute-done | bytes 688160 | tf_op jit(solution)/shard_map/ppermute | solution.py:52
  62.7 0.1 add_convert_fusion.2
  62.9 2.1 %collective-permute-start.12 = (bf16[4,112,384]{2,1,0:T(8,128)(2,1)S(1)}, bf16[4,112,384]{2,1,0:T(8,128)(2,1)S(1)}, u32[]{:S(2)}, u32[]{:S(2)}) collective-permute-start(bf16[4,112,384]{2,1,0:T(8,128)(2,1)S(1)} %add_convert_fusion.2), channel_id=1, source_target_pairs={{0,4},{1,3},{2,6},{3,1},{4,0},{5,7},{6,2},{7,5},{8,12},{9,11},{10,... | collective-permute-start | bytes 1032200 | tf_op jit(solution)/shard_map/ppermute | solution.py:52
  64.9 0.2 add_convert_fusion.1
  65.1 1.5 %collective-permute-start.1 = (bf16[8,96,384]{2,1,0:T(8,128)(2,1)S(1)}, bf16[8,96,384]{2,1,0:T(8,128)(2,1)S(1)}, u32[]{:S(2)}, u32[]{:S(2)}) collective-permute-start(bf16[8,96,384]{2,1,0:T(8,128)(2,1)S(1)} %add_convert_fusion.1), channel_id=1, source_target_pairs={{0,2},{1,5},{2,0},{3,7},{4,6},{5,1},{6,4},{7,3},{8,10},{9,13},{10,... | collective-permute-start | bytes 1769480 | tf_op jit(solution)/shard_map/ppermute | solution.py:52
  66.7 6.9 %collective-permute-done.12 = bf16[4,112,384]{2,1,0:T(8,128)(2,1)S(1)} collective-permute-done((bf16[4,112,384]{2,1,0:T(8,128)(2,1)S(1)}, bf16[4,112,384]{2,1,0:T(8,128)(2,1)S(1)}, u32[]{:S(2)}, u32[]{:S(2)}) %collective-permute-start.12) | collective-permute-done | bytes 344096 | tf_op jit(solution)/shard_map/ppermute | solution.py:52
  73.6 0.1 add_convert_fusion.4
  73.7 2.4 %collective-permute-start.13 = (bf16[2,112,384]{2,1,0:T(8,128)(2,1)S(1)}, bf16[2,112,384]{2,1,0:T(8,128)(2,1)S(1)}, u32[]{:S(2)}, u32[]{:S(2)}) collective-permute-start(bf16[2,112,384]{2,1,0:T(8,128)(2,1)S(1)} %add_convert_fusion.4), channel_id=1, source_target_pairs={{0,8},{1,9},{2,10},{3,11},{4,12},{5,13},{6,14},{7,15},{8,0},{9,1},... | collective-permute-start | bytes 516104 | tf_op jit(solution)/shard_map/ppermute | solution.py:52
  76.1 0.1 add_convert_fusion.3
  76.2 1.6 %collective-permute-start.2 = (bf16[4,96,384]{2,1,0:T(8,128)(2,1)S(1)}, bf16[4,96,384]{2,1,0:T(8,128)(2,1)S(1)}, u32[]{:S(2)}, u32[]{:S(2)}) collective-permute-start(bf16[4,96,384]{2,1,0:T(8,128)(2,1)S(1)} %add_convert_fusion.3), channel_id=1, source_target_pairs={{0,4},{1,3},{2,6},{3,1},{4,0},{5,7},{6,2},{7,5},{8,12},{9,11},{10,... | collective-permute-start | bytes 884744 | tf_op jit(solution)/shard_map/ppermute | solution.py:52
  77.8 1.7 %collective-permute-done.13 = bf16[2,112,384]{2,1,0:T(8,128)(2,1)S(1)} collective-permute-done((bf16[2,112,384]{2,1,0:T(8,128)(2,1)S(1)}, bf16[2,112,384]{2,1,0:T(8,128)(2,1)S(1)}, u32[]{:S(2)}, u32[]{:S(2)}) %collective-permute-start.13) | collective-permute-done | bytes 172064 | tf_op jit(solution)/shard_map/ppermute | solution.py:52
  79.5 3.3 %collective-permute-start.14 = (bf16[1,112,384]{2,1,0:T(8,128)(2,1)S(1)}, bf16[1,112,384]{2,1,0:T(8,128)(2,1)S(1)}, u32[]{:S(2)}, u32[]{:S(2)}) collective-permute-start(bf16[1,112,384]{2,1,0:T(8,128)(2,1)S(1)} %add_convert_fusion.7), channel_id=1, source_target_pairs={{0,16},{1,17},{2,18},{3,19},{4,20},{5,21},{6,22},{7,23},{8,24},{9,... | collective-permute-start | bytes 258056 | tf_op jit(solution)/shard_map/ppermute | solution.py:52
  82.9 0.1 collective-permute-done.2
  83.1 1.3 collective-permute-start.3
  84.4 1.2 collective-permute-done.14
  85.7 3.5 %collective-permute-start.15 = (bf16[1,112,384]{2,1,0:T(8,128)(2,1)S(1)}, bf16[1,112,384]{2,1,0:T(8,128)(2,1)S(1)}, u32[]{:S(2)}, u32[]{:S(2)}) collective-permute-start(bf16[1,112,384]{2,1,0:T(8,128)(2,1)S(1)} %get-tuple-element.65), channel_id=1, source_target_pairs={{0,16},{1,17},{2,18},{3,19},{4,20},{5,21},{6,22},{7,23},{8,24},{9,... | collective-permute-start | bytes 258056 | tf_op jit(solution)/shard_map/ppermute | solution.py:52
  89.1 0.3 collective-permute-done.3
  89.5 2.7 %collective-permute-start.4 = (bf16[1,96,384]{2,1,0:T(8,128)(2,1)S(1)}, bf16[1,96,384]{2,1,0:T(8,128)(2,1)S(1)}, u32[]{:S(2)}, u32[]{:S(2)}) collective-permute-start(bf16[1,96,384]{2,1,0:T(8,128)(2,1)S(1)} %add_convert_fusion.9), channel_id=1, source_target_pairs={{0,16},{1,17},{2,18},{3,19},{4,20},{5,21},{6,22},{7,23},{8,24},{9,... | collective-permute-start | bytes 221192 | tf_op jit(solution)/shard_map/ppermute | solution.py:52
  92.2 2.5 %collective-permute-start.16 = (bf16[2,112,384]{2,1,0:T(8,128)(2,1)S(1)}, bf16[2,112,384]{2,1,0:T(8,128)(2,1)S(1)}, u32[]{:S(2)}, u32[]{:S(2)}) collective-permute-start(bf16[2,112,384]{2,1,0:T(8,128)(2,1)S(1)} %pad_maximum_fusion.4), channel_id=1, source_target_pairs={{0,8},{1,9},{2,10},{3,11},{4,12},{5,13},{6,14},{7,15},{8,0},{9,1},... | collective-permute-start | bytes 516104 | tf_op jit(solution)/shard_map/ppermute | solution.py:52
  94.7 1.2 collective-permute-done.4
  96.0 2.3 %collective-permute-start.5 = (bf16[1,96,384]{2,1,0:T(8,128)(2,1)S(1)}, bf16[1,96,384]{2,1,0:T(8,128)(2,1)S(1)}, u32[]{:S(2)}, u32[]{:S(2)}) collective-permute-start(bf16[1,96,384]{2,1,0:T(8,128)(2,1)S(1)} %get-tuple-element.67), channel_id=1, source_target_pairs={{0,16},{1,17},{2,18},{3,19},{4,20},{5,21},{6,22},{7,23},{8,24},{9,... | collective-permute-start | bytes 221192 | tf_op jit(solution)/shard_map/ppermute | solution.py:52
  98.3 1.3 collective-permute-done.16
  99.6 1.7 %collective-permute-start.17 = (bf16[4,112,384]{2,1,0:T(8,128)(2,1)S(1)}, bf16[4,112,384]{2,1,0:T(8,128)(2,1)S(1)}, u32[]{:S(2)}, u32[]{:S(2)}) collective-permute-start(bf16[4,112,384]{2,1,0:T(8,128)(2,1)S(1)} %pad_maximum_fusion.2), channel_id=1, source_target_pairs={{0,4},{1,3},{2,6},{3,1},{4,0},{5,7},{6,2},{7,5},{8,12},{9,11},{10,... | collective-permute-start | bytes 1032200 | tf_op jit(solution)/shard_map/ppermute | solution.py:52
  101.3 0.6 collective-permute-done.5
  101.9 1.4 collective-permute-start.6
  103.3 3.8 %collective-permute-done.6 = bf16[2,96,384]{2,1,0:T(8,128)(2,1)S(1)} collective-permute-done((bf16[2,96,384]{2,1,0:T(8,128)(2,1)S(1)}, bf16[2,96,384]{2,1,0:T(8,128)(2,1)S(1)}, u32[]{:S(2)}, u32[]{:S(2)}) %collective-permute-start.6) | collective-permute-done | bytes 147488 | tf_op jit(solution)/shard_map/ppermute | solution.py:52
  107.1 2.4 %collective-permute-start.7 = (bf16[4,96,384]{2,1,0:T(8,128)(2,1)S(1)}, bf16[4,96,384]{2,1,0:T(8,128)(2,1)S(1)}, u32[]{:S(2)}, u32[]{:S(2)}) collective-permute-start(bf16[4,96,384]{2,1,0:T(8,128)(2,1)S(1)} %pad_maximum_fusion.3), channel_id=1, source_target_pairs={{0,4},{1,3},{2,6},{3,1},{4,0},{5,7},{6,2},{7,5},{8,12},{9,11},{10,... | collective-permute-start | bytes 884744 | tf_op jit(solution)/shard_map/ppermute | solution.py:52
  109.6 0.1 pad_maximum_fusion
  109.7 0.8 collective-permute-start.18
  110.6 7.0 %collective-permute-done.7 = bf16[4,96,384]{2,1,0:T(8,128)(2,1)S(1)} collective-permute-done((bf16[4,96,384]{2,1,0:T(8,128)(2,1)S(1)}, bf16[4,96,384]{2,1,0:T(8,128)(2,1)S(1)}, u32[]{:S(2)}, u32[]{:S(2)}) %collective-permute-start.7) | collective-permute-done | bytes 294944 | tf_op jit(solution)/shard_map/ppermute | solution.py:52
  117.6 1.3 collective-permute-start.8
  119.1 1.6 %collective-permute-done.18 = bf16[8,112,384]{2,1,0:T(8,128)(2,1)S(1)} collective-permute-done((bf16[8,112,384]{2,1,0:T(8,128)(2,1)S(1)}, bf16[8,112,384]{2,1,0:T(8,128)(2,1)S(1)}, u32[]{:S(2)}, u32[]{:S(2)}) %collective-permute-start.18) | collective-permute-done | bytes 688160 | tf_op jit(solution)/shard_map/ppermute | solution.py:52
  120.7 0.1 constant_dynamic-update-slice_fusion.5.kept0
  121.0 6.6 %collective-permute-done.8 = bf16[8,96,384]{2,1,0:T(8,128)(2,1)S(1)} collective-permute-done((bf16[8,96,384]{2,1,0:T(8,128)(2,1)S(1)}, bf16[8,96,384]{2,1,0:T(8,128)(2,1)S(1)}, u32[]{:S(2)}, u32[]{:S(2)}) %collective-permute-start.8) | collective-permute-done | bytes 589856 | tf_op jit(solution)/shard_map/ppermute | solution.py:52
  127.6 0.1 constant_dynamic-update-slice_fusion.kept1
  127.8 1.1 copy.36
  128.9 1.1 copy.37
  129.9 0.7 collective-permute-done.9.other1
  130.6 1.0 copy-done.5
  131.6 1.1 copy-done.2
  132.7 7.7 %unpack.1 = (f32[2,384,1536]{2,1,0:T(8,128)}, f32[2,1536,384]{2,1,0:T(8,128)}, f32[2,208,384]{2,1,0:T(8,128)}, f32[2,16,384]{2,1,0:T(8,128)}) custom-call(bf16[16,96,384]{2,1,0:T(8,128)(2,1)} %copy-done.4, bf16[16,96,384]{2,1,0:T(8,128)(2,1)} %copy-done.5, bf16[16,112,384]{2,1,0:T(8,128)(2,1)} %copy-done.1, bf16[16,112,384]{2,1,0:T(8,128)(2,1)} %copy-done.2), custom_call_target="tpu_custom_call" | custom-call | tf_op jit(solution)/shard_map/unpack/pallas_call | solution.py:626
  140.4 0.7 slice.188
  141.1 0.9 slice_reduce_fusion
  142.0 1.1 fusion
  143.1 1.0 slice.187
  144.1 1.0 copy.38
  145.1 0.6 copy.57
  145.7 0.7 sqrt.7
  146.3 0.6 copy.56
  146.9 0.6 copy.47
  147.5 0.6 copy_bitcast_fusion
  148.1 0.6 copy_bitcast_fusion.2
  148.7 0.6 copy_bitcast_fusion.4
  (43 shorter events, 1.0 us)
Async XLA Ops:
  3.1 3.6 %copy-start = (bf16[4,4,196,384]{3,1,2,0:T(4,128)(2,1)S(1)}, bf16[4,4,196,384]{3,1,2,0:T(4,128)(2,1)}, u32[]{:S(2)}) copy-start(bf16[4,4,196,384]{3,1,2,0:T(4,128)(2,1)} %param.17) | copy-start | bytes 7225348
  30.0 15.4 %copy-start.9 = (bf16[16,96,384]{2,1,0:T(8,128)(2,1)S(1)}, bf16[16,96,384]{2,1,0:T(8,128)(2,1)}, u32[]{:S(2)}) copy-start(bf16[16,96,384]{2,1,0:T(8,128)(2,1)} %get-tuple-element.42) | copy-start | bytes 3538948
  44.9 17.8 %copy-start.3 = (bf16[16,112,384]{2,1,0:T(8,128)(2,1)S(1)}, bf16[16,112,384]{2,1,0:T(8,128)(2,1)}, u32[]{:S(2)}) copy-start(bf16[16,112,384]{2,1,0:T(8,128)(2,1)} %get-tuple-element.43) | copy-start | bytes 4128772
  44.9 4.6 %collective-permute-start.10 = (bf16[16,112,384]{2,1,0:T(8,128)(2,1)}, bf16[16,112,384]{2,1,0:T(8,128)(2,1)S(1)}, u32[]{:S(2)}, u32[]{:S(2)}) collective-permute-start(bf16[16,112,384]{2,1,0:T(8,128)(2,1)} %get-tuple-element.44), channel_id=1, source_target_pairs={{0,1},{1,0},{2,3},{3,2},{4,5},{5,4},{6,7},{7,6},{8,9},{9,8},{10,11... | collective-permute-start | bytes 4128776 | tf_op jit(solution)/shard_map/ppermute | solution.py:52
  45.4 19.5 %collective-permute-start = (bf16[16,96,384]{2,1,0:T(8,128)(2,1)S(1)}, bf16[16,96,384]{2,1,0:T(8,128)(2,1)S(1)}, u32[]{:S(2)}, u32[]{:S(2)}) collective-permute-start(bf16[16,96,384]{2,1,0:T(8,128)(2,1)S(1)} %copy-done.9), channel_id=1, source_target_pairs={{0,1},{1,0},{2,3},{3,2},{4,5},{5,4},{6,7},{7,6},{8,9},{9,8},{10,11... | collective-permute-start | bytes 3538952 | tf_op jit(solution)/shard_map/ppermute | solution.py:52
  49.5 15.5 %copy-start.6 = (bf16[16,96,384]{2,1,0:T(8,128)(2,1)S(1)}, bf16[16,96,384]{2,1,0:T(8,128)(2,1)}, u32[]{:S(2)}) copy-start(bf16[16,96,384]{2,1,0:T(8,128)(2,1)} %get-tuple-element.41) | copy-start | bytes 3538948
  50.8 11.9 %collective-permute-start.11 = (bf16[8,112,384]{2,1,0:T(8,128)(2,1)S(1)}, bf16[8,112,384]{2,1,0:T(8,128)(2,1)S(1)}, u32[]{:S(2)}, u32[]{:S(2)}) collective-permute-start(bf16[8,112,384]{2,1,0:T(8,128)(2,1)S(1)} %add_convert_fusion), channel_id=1, source_target_pairs={{0,2},{1,5},{2,0},{3,7},{4,6},{5,1},{6,4},{7,3},{8,10},{9,13},{10,... | collective-permute-start | bytes 2064392 | tf_op jit(solution)/shard_map/ppermute | solution.py:52
  62.9 10.7 %collective-permute-start.12 = (bf16[4,112,384]{2,1,0:T(8,128)(2,1)S(1)}, bf16[4,112,384]{2,1,0:T(8,128)(2,1)S(1)}, u32[]{:S(2)}, u32[]{:S(2)}) collective-permute-start(bf16[4,112,384]{2,1,0:T(8,128)(2,1)S(1)} %add_convert_fusion.2), channel_id=1, source_target_pairs={{0,4},{1,3},{2,6},{3,1},{4,0},{5,7},{6,2},{7,5},{8,12},{9,11},{10,... | collective-permute-start | bytes 1032200 | tf_op jit(solution)/shard_map/ppermute | solution.py:52
  65.1 11.0 %collective-permute-start.1 = (bf16[8,96,384]{2,1,0:T(8,128)(2,1)S(1)}, bf16[8,96,384]{2,1,0:T(8,128)(2,1)S(1)}, u32[]{:S(2)}, u32[]{:S(2)}) collective-permute-start(bf16[8,96,384]{2,1,0:T(8,128)(2,1)S(1)} %add_convert_fusion.1), channel_id=1, source_target_pairs={{0,2},{1,5},{2,0},{3,7},{4,6},{5,1},{6,4},{7,3},{8,10},{9,13},{10,... | collective-permute-start | bytes 1769480 | tf_op jit(solution)/shard_map/ppermute | solution.py:52
  73.7 5.8 %collective-permute-start.13 = (bf16[2,112,384]{2,1,0:T(8,128)(2,1)S(1)}, bf16[2,112,384]{2,1,0:T(8,128)(2,1)S(1)}, u32[]{:S(2)}, u32[]{:S(2)}) collective-permute-start(bf16[2,112,384]{2,1,0:T(8,128)(2,1)S(1)} %add_convert_fusion.4), channel_id=1, source_target_pairs={{0,8},{1,9},{2,10},{3,11},{4,12},{5,13},{6,14},{7,15},{8,0},{9,1},... | collective-permute-start | bytes 516104 | tf_op jit(solution)/shard_map/ppermute | solution.py:52
  76.2 6.8 %collective-permute-start.2 = (bf16[4,96,384]{2,1,0:T(8,128)(2,1)S(1)}, bf16[4,96,384]{2,1,0:T(8,128)(2,1)S(1)}, u32[]{:S(2)}, u32[]{:S(2)}) collective-permute-start(bf16[4,96,384]{2,1,0:T(8,128)(2,1)S(1)} %add_convert_fusion.3), channel_id=1, source_target_pairs={{0,4},{1,3},{2,6},{3,1},{4,0},{5,7},{6,2},{7,5},{8,12},{9,11},{10,... | collective-permute-start | bytes 884744 | tf_op jit(solution)/shard_map/ppermute | solution.py:52
  79.5 6.0 %collective-permute-start.14 = (bf16[1,112,384]{2,1,0:T(8,128)(2,1)S(1)}, bf16[1,112,384]{2,1,0:T(8,128)(2,1)S(1)}, u32[]{:S(2)}, u32[]{:S(2)}) collective-permute-start(bf16[1,112,384]{2,1,0:T(8,128)(2,1)S(1)} %add_convert_fusion.7), channel_id=1, source_target_pairs={{0,16},{1,17},{2,18},{3,19},{4,20},{5,21},{6,22},{7,23},{8,24},{9,... | collective-permute-start | bytes 258056 | tf_op jit(solution)/shard_map/ppermute | solution.py:52
  83.1 6.3 %collective-permute-start.3 = (bf16[2,96,384]{2,1,0:T(8,128)(2,1)S(1)}, bf16[2,96,384]{2,1,0:T(8,128)(2,1)S(1)}, u32[]{:S(2)}, u32[]{:S(2)}) collective-permute-start(bf16[2,96,384]{2,1,0:T(8,128)(2,1)S(1)} %add_convert_fusion.5), channel_id=1, source_target_pairs={{0,8},{1,9},{2,10},{3,11},{4,12},{5,13},{6,14},{7,15},{8,0},{9,1},... | collective-permute-start | bytes 442376 | tf_op jit(solution)/shard_map/ppermute | solution.py:52
  85.7 6.5 %collective-permute-start.15 = (bf16[1,112,384]{2,1,0:T(8,128)(2,1)S(1)}, bf16[1,112,384]{2,1,0:T(8,128)(2,1)S(1)}, u32[]{:S(2)}, u32[]{:S(2)}) collective-permute-start(bf16[1,112,384]{2,1,0:T(8,128)(2,1)S(1)} %get-tuple-element.65), channel_id=1, source_target_pairs={{0,16},{1,17},{2,18},{3,19},{4,20},{5,21},{6,22},{7,23},{8,24},{9,... | collective-permute-start | bytes 258056 | tf_op jit(solution)/shard_map/ppermute | solution.py:52
  89.5 6.4 %collective-permute-start.4 = (bf16[1,96,384]{2,1,0:T(8,128)(2,1)S(1)}, bf16[1,96,384]{2,1,0:T(8,128)(2,1)S(1)}, u32[]{:S(2)}, u32[]{:S(2)}) collective-permute-start(bf16[1,96,384]{2,1,0:T(8,128)(2,1)S(1)} %add_convert_fusion.9), channel_id=1, source_target_pairs={{0,16},{1,17},{2,18},{3,19},{4,20},{5,21},{6,22},{7,23},{8,24},{9,... | collective-permute-start | bytes 221192 | tf_op jit(solution)/shard_map/ppermute | solution.py:52
  92.2 7.4 %collective-permute-start.16 = (bf16[2,112,384]{2,1,0:T(8,128)(2,1)S(1)}, bf16[2,112,384]{2,1,0:T(8,128)(2,1)S(1)}, u32[]{:S(2)}, u32[]{:S(2)}) collective-permute-start(bf16[2,112,384]{2,1,0:T(8,128)(2,1)S(1)} %pad_maximum_fusion.4), channel_id=1, source_target_pairs={{0,8},{1,9},{2,10},{3,11},{4,12},{5,13},{6,14},{7,15},{8,0},{9,1},... | collective-permute-start | bytes 516104 | tf_op jit(solution)/shard_map/ppermute | solution.py:52
  96.0 5.9 %collective-permute-start.5 = (bf16[1,96,384]{2,1,0:T(8,128)(2,1)S(1)}, bf16[1,96,384]{2,1,0:T(8,128)(2,1)S(1)}, u32[]{:S(2)}, u32[]{:S(2)}) collective-permute-start(bf16[1,96,384]{2,1,0:T(8,128)(2,1)S(1)} %get-tuple-element.67), channel_id=1, source_target_pairs={{0,16},{1,17},{2,18},{3,19},{4,20},{5,21},{6,22},{7,23},{8,24},{9,... | collective-permute-start | bytes 221192 | tf_op jit(solution)/shard_map/ppermute | solution.py:52
  99.6 10.0 %collective-permute-start.17 = (bf16[4,112,384]{2,1,0:T(8,128)(2,1)S(1)}, bf16[4,112,384]{2,1,0:T(8,128)(2,1)S(1)}, u32[]{:S(2)}, u32[]{:S(2)}) collective-permute-start(bf16[4,112,384]{2,1,0:T(8,128)(2,1)S(1)} %pad_maximum_fusion.2), channel_id=1, source_target_pairs={{0,4},{1,3},{2,6},{3,1},{4,0},{5,7},{6,2},{7,5},{8,12},{9,11},{10,... | collective-permute-start | bytes 1032200 | tf_op jit(solution)/shard_map/ppermute | solution.py:52
  101.9 5.2 %collective-permute-start.6 = (bf16[2,96,384]{2,1,0:T(8,128)(2,1)S(1)}, bf16[2,96,384]{2,1,0:T(8,128)(2,1)S(1)}, u32[]{:S(2)}, u32[]{:S(2)}) collective-permute-start(bf16[2,96,384]{2,1,0:T(8,128)(2,1)S(1)} %pad_maximum_fusion.5), channel_id=1, source_target_pairs={{0,8},{1,9},{2,10},{3,11},{4,12},{5,13},{6,14},{7,15},{8,0},{9,1},... | collective-permute-start | bytes 442376 | tf_op jit(solution)/shard_map/ppermute | solution.py:52
  107.1 10.4 %collective-permute-start.7 = (bf16[4,96,384]{2,1,0:T(8,128)(2,1)S(1)}, bf16[4,96,384]{2,1,0:T(8,128)(2,1)S(1)}, u32[]{:S(2)}, u32[]{:S(2)}) collective-permute-start(bf16[4,96,384]{2,1,0:T(8,128)(2,1)S(1)} %pad_maximum_fusion.3), channel_id=1, source_target_pairs={{0,4},{1,3},{2,6},{3,1},{4,0},{5,7},{6,2},{7,5},{8,12},{9,11},{10,... | collective-permute-start | bytes 884744 | tf_op jit(solution)/shard_map/ppermute | solution.py:52
  109.7 11.0 %collective-permute-start.18 = (bf16[8,112,384]{2,1,0:T(8,128)(2,1)S(1)}, bf16[8,112,384]{2,1,0:T(8,128)(2,1)S(1)}, u32[]{:S(2)}, u32[]{:S(2)}) collective-permute-start(bf16[8,112,384]{2,1,0:T(8,128)(2,1)S(1)} %pad_maximum_fusion), channel_id=1, source_target_pairs={{0,2},{1,5},{2,0},{3,7},{4,6},{5,1},{6,4},{7,3},{8,10},{9,13},{10,... | collective-permute-start | bytes 2064392 | tf_op jit(solution)/shard_map/ppermute | solution.py:52
  117.6 9.9 %collective-permute-start.8 = (bf16[8,96,384]{2,1,0:T(8,128)(2,1)S(1)}, bf16[8,96,384]{2,1,0:T(8,128)(2,1)S(1)}, u32[]{:S(2)}, u32[]{:S(2)}) collective-permute-start(bf16[8,96,384]{2,1,0:T(8,128)(2,1)S(1)} %pad_maximum_fusion.1), channel_id=1, source_target_pairs={{0,2},{1,5},{2,0},{3,7},{4,6},{5,1},{6,4},{7,3},{8,10},{9,13},{10,... | collective-permute-start | bytes 1769480 | tf_op jit(solution)/shard_map/ppermute | solution.py:52
  119.1 8.7 %copy-start.7 = (bf16[1,4,196,384]{3,2,1,0:T(8,128)(2,1)S(1)}, bf16[1,4,196,384]{3,2,1,0:T(8,128)(2,1)}, u32[]{:S(2)}) copy-start(bf16[1,4,196,384]{3,2,1,0:T(8,128)(2,1)} %get-tuple-element.49) | copy-start | bytes 1806340
  120.8 8.0 %copy-start.1 = (bf16[16,112,384]{2,1,0:T(8,128)(2,1)}, bf16[16,112,384]{2,1,0:T(8,128)(2,1)S(1)}, u32[]{:S(2)}) copy-start(bf16[16,112,384]{2,1,0:T(8,128)(2,1)S(1)} %constant_dynamic-update-slice_fusion.5.kept0) | copy-start | bytes 4128772
  120.8 8.0 %copy-start.8 = (bf16[1,4,196,384]{3,2,1,0:T(8,128)(2,1)S(1)}, bf16[1,4,196,384]{3,2,1,0:T(8,128)(2,1)}, u32[]{:S(2)}) copy-start(bf16[1,4,196,384]{3,2,1,0:T(8,128)(2,1)} %get-tuple-element.50) | copy-start | bytes 1806340
  120.8 9.7 %collective-permute-start.19 = (bf16[16,112,384]{2,1,0:T(8,128)(2,1)S(1)}, bf16[16,112,384]{2,1,0:T(8,128)(2,1)S(1)}, u32[]{:S(2)}, u32[]{:S(2)}) collective-permute-start(bf16[16,112,384]{2,1,0:T(8,128)(2,1)S(1)} %constant_dynamic-update-slice_fusion.5.kept0), channel_id=1, source_target_pairs={{0,1},{1,0},{2,3},{3,2},{4,5},{5,4},{6,7},{7,6},{8,9},{9,8},{10,11... | collective-permute-start | bytes 4128776 | tf_op jit(solution)/shard_map/ppermute | solution.py:52
  127.7 2.9 %copy-start.4 = (bf16[16,96,384]{2,1,0:T(8,128)(2,1)}, bf16[16,96,384]{2,1,0:T(8,128)(2,1)S(1)}, u32[]{:S(2)}) copy-start(bf16[16,96,384]{2,1,0:T(8,128)(2,1)S(1)} %constant_dynamic-update-slice_fusion.kept1) | copy-start | bytes 3538948
  127.7 2.9 %collective-permute-start.9 = (bf16[16,96,384]{2,1,0:T(8,128)(2,1)S(1)}, bf16[16,96,384]{2,1,0:T(8,128)(2,1)S(1)}, u32[]{:S(2)}, u32[]{:S(2)}) collective-permute-start(bf16[16,96,384]{2,1,0:T(8,128)(2,1)S(1)} %constant_dynamic-update-slice_fusion.kept1), channel_id=1, source_target_pairs={{0,1},{1,0},{2,3},{3,2},{4,5},{5,4},{6,7},{7,6},{8,9},{9,8},{10,11... | collective-permute-start | bytes 3538952 | tf_op jit(solution)/shard_map/ppermute | solution.py:52
  130.6 1.0 copy-start.5
  131.6 1.1 copy-start.2

commit v2 on v0

v2 whole, which is shorter than its diff:
```python
import functools

import jax
import jax.numpy as jnp
from jax import lax
from jax.experimental import pallas as pl
from jax.experimental.pallas import tpu as pltpu
from jax.sharding import PartitionSpec as P

SQRT_HALF = 0.7071067811865476
INV_ROOT_TAU = 0.3989422804014327
AXES = ("dp", "pipe")
BLOCKS = 32
HALF = BLOCKS // 2
SCATTERED = 5
LANES = 384
VECTOR_ROWS = 16
BF = jnp.bfloat16
F32 = jnp.float32
VMEM = pl.BlockSpec(memory_space=pltpu.VMEM)
HBM = pl.BlockSpec(memory_space=pltpu.HBM)
VMEM_LIMIT = 28 * 2**20

CROSS_AFF_SCALE, CROSS_AFF_SHIFT, CROSS_SCALE, CROSS_BIAS = 0, 1, 2, 3
MIXER_AFF_SCALE, MIXER_AFF_SHIFT, MIXER_OUT_BIAS, MIXER_SCALE = 4, 5, 6, 7
MIXER_IN_BIAS = 8
SQUARES = 12


def dot(a, b, a_dim=1, b_dim=0):
    return lax.dot_general(
        a, b, (((a_dim,), (b_dim,)), ((), ())), preferred_element_type=F32
    )


def row_sum(values):
    return jnp.sum(values, axis=0, keepdims=True)


def phase_bits(mesh_shape):
    pipe_bits = [1 << b for b in range(mesh_shape["pipe"].bit_length() - 1)]
    dp_bits = [mesh_shape["pipe"] << b for b in range(mesh_shape["dp"].bit_length() - 1)]
    even = [pipe_bits[0], *pipe_bits[1:], *dp_bits]
    odd = list(even)
    odd[1], odd[2] = even[2], even[1]
    return even, odd


def block_code(mesh_shape, place):
    even, odd = phase_bits(mesh_shape)
    odd_place = place & 1
    code = jnp.int32(0)
    for even_bit, odd_bit in zip(even[:SCATTERED], odd[:SCATTERED]):
        bit = jnp.where(odd_place == 1, (place & odd_bit) != 0, (place & even_bit) != 0)
        code = 2 * code + bit.astype(jnp.int32)
    return code


def own_codes(mesh_shape):
    place = lax.axis_index("dp") * mesh_shape["pipe"] + lax.axis_index("pipe")
    return block_code(mesh_shape, place), block_code(mesh_shape, place ^ 1)


def kept_block(codes, slot):
    return codes[0] ^ slot


def sent_block(codes, slot):
    return codes[1] ^ slot


def inner_spot(block, rows, columns):
    across = columns // LANES
    row_at = pl.multiple_of((block // across) * rows, rows)
    return row_at, pl.multiple_of((block % across) * LANES, LANES)


def pack_halves(codes, block_at, kept_ref, sent_ref):
    @pl.loop(0, HALF)
    def _(slot):
        for block, out_ref in ((sent_block(codes, slot), sent_ref), (kept_block(codes, slot), kept_ref)):
            at = 0
            for piece in block_at(block):
                out_ref[slot, at : at + piece.shape[0], :] = piece
                at += piece.shape[0]


def pack_products(codes, inner_ref, outer_ref, kept_ref, sent_ref):
    depth = outer_ref.shape[0] // BLOCKS

    def block_at(block):
        row_at, column_at = inner_spot(block, depth, inner_ref.shape[1])
        outer_at = pl.multiple_of(block * depth, depth)
        return (
            inner_ref[pl.ds(row_at, depth), pl.ds(column_at, LANES)],
            outer_ref[pl.ds(outer_at, depth), :],
        )

    pack_halves(codes, block_at, kept_ref, sent_ref)


def read(ref, rows):
    return jnp.concatenate([ref[plane, rows, :] for plane in range(ref.shape[0])], axis=1)


def write(ref, rows, values):
    for plane in range(ref.shape[0]):
        ref[plane, rows, :] = values[:, plane * 128 : (plane + 1) * 128]


def rounded(values):
    return values.astype(BF).astype(F32)


def spread_rows(source_ref, target_ref):
    parts, patches, each, _ = source_ref.shape
    for part in range(parts):
        for patch in range(patches):
            base = (part * patches + patch) * each
            write(target_ref, slice(base, base + each), source_ref[part, patch].astype(F32))


def gather_rows(source_ref, target_ref):
    parts, patches, each, _ = target_ref.shape
    for part in range(parts):
        for patch in range(patches):
            base = (part * patches + patch) * each
            target_ref[part, patch] = read(source_ref, slice(base, base + each)).astype(BF)


def image_rows(image, patches, each):
    return pl.ds((image // each) * patches * each + image % each, patches, stride=each)


def row_tiles(rows):
    tile = max(t for t in range(16, 209, 16) if rows % t == 0)
    return [slice(at, at + tile) for at in range(0, rows, tile)]


def cross_setup(mask_ref, weight_ref, bias_ref, kept_ref, keep_ref, bias_columns_ref, rows_ref):
    patches, layers, _ = weight_ref.shape
    padded = kept_ref.shape[2]
    for patch in range(patches):
        base = patch * layers
        weight = weight_ref[patch].astype(F32)
        rows_ref[0, base : base + layers, :] = weight[:, 0:128]
        rows_ref[1, base : base + layers, 0 : patches - 128] = weight[:, 128:]
    keep_ref[...] = jnp.zeros_like(keep_ref)
    kept_ref[...] = jnp.zeros_like(kept_ref)
    for layer in range(layers):
        weight = read(rows_ref, pl.ds(layer, patches, stride=layers))[:, 0:patches]
        for image in range(mask_ref.shape[0]):
            keep_row = mask_ref[image, layer : layer + 1, :].astype(F32)
            keep_ref[image, layer : layer + 1, 0:patches] = keep_row
            kept_ref[layer, image, 0:patches, 0:patches] = (weight * keep_row).astype(BF)
    bias_rows = jnp.concatenate([bias_ref[...], jnp.zeros((8 - layers, patches), F32)], axis=0)
    bias_rows = jnp.concatenate([bias_rows, jnp.zeros((8, 256 - patches), F32)], axis=1)
    bias_columns_ref[...] = jnp.transpose(bias_rows)[0:padded]


def cross_forward(
    layer, source_ref, target_ref, vectors_ref, kept_ref, bias_ref,
    aff_scale_ref, aff_shift_ref, scale_ref, low_ref, patches, each,
):
    aff_scale = aff_scale_ref[layer : layer + 1, :]
    aff_shift = aff_shift_ref[layer : layer + 1, :]
    scale = scale_ref[layer : layer + 1, :]
    branch_squares = jnp.zeros((1, LANES), F32)
    normed_squares = jnp.zeros((1, LANES), F32)
    for image in range(kept_ref.shape[1]):
        rows = image_rows(image, patches, each)
        stream = read(source_ref, rows)
        normed = aff_scale * stream + aff_shift
        low_ref[image, 0:patches, :] = normed.astype(BF)
        mixing = dot(kept_ref[layer, image], low_ref[image])
        branch = scale * (mixing + bias_ref[:, layer : layer + 1])[0:patches]
        write(target_ref, rows, rounded(stream + branch))
        branch_squares += row_sum(branch * branch)
        normed_squares += row_sum(normed * normed)
    vectors_ref[layer, SQUARES : SQUARES + 1, :] = branch_squares
    vectors_ref[layer, SQUARES + 1 : SQUARES + 2, :] = normed_squares


def mixer_hidden(
    layer, stream_ref, low_ref, fired_ref, slope_ref, vectors_ref,
    aff_scale_ref, aff_shift_ref, inner_ref, inner_bias_ref,
):
    aff_scale = aff_scale_ref[layer : layer + 1, :]
    aff_shift = aff_shift_ref[layer : layer + 1, :]
    tiles = row_tiles(stream_ref.shape[1])
    squares = jnp.zeros((1, LANES), F32)
    for rows in tiles:
        normed = aff_scale * read(stream_ref, rows) + aff_shift
        low_ref[rows, :] = normed.astype(BF)
        squares += row_sum(normed * normed)
    vectors_ref[layer, SQUARES + 3 : SQUARES + 4, :] = squares
    step = inner_ref.shape[1] // 2

    @pl.loop(0, 2)
    def _(part):
        at = pl.ds(pl.multiple_of(part * step, step), step)
        for rows in tiles:
            hidden = dot(low_ref[rows, :], inner_ref[:, at]) + inner_bias_ref[layer : layer + 1, at]
            normal_cdf = 0.5 * (1.0 + lax.erf(hidden * SQRT_HALF))
            density = INV_ROOT_TAU * jnp.exp(-0.5 * hidden * hidden)
            fired_ref[rows, at] = (hidden * normal_cdf).astype(BF)
            slope_ref[rows, at] = (normal_cdf + hidden * density).astype(BF)


def mixer_backward(
    layer, upper_ref, low_ref, fired_ref, slope_ref, scaled_ref, inner_ref, outer_ref,
    inner_grad_ref, outer_grad_ref, vectors_ref, scale_ref,
):
    scale = scale_ref[layer : layer + 1, :]
    tiles = row_tiles(upper_ref.shape[1])
    bias = jnp.zeros((1, LANES), F32)
    for rows in tiles:
        result_grad = read(upper_ref, rows) * scale
        bias += row_sum(result_grad)
        scaled_ref[rows, :] = result_grad.astype(BF)
    vectors_ref[layer, MIXER_OUT_BIAS : MIXER_OUT_BIAS + 1, :] = bias
    columns = inner_ref.shape[1]
    step = 2 * LANES
    for part in range(columns // step):
        at = slice(part * step, (part + 1) * step)
        outer_grad_ref[at, :] = dot(fired_ref[:, at], scaled_ref[...], 0, 0).astype(BF)
        inner_bias = jnp.zeros((1, step), F32)
        for rows in tiles:
            hidden_grad = dot(scaled_ref[rows, :], outer_ref[at, :], 1, 1) * slope_ref[
                rows, at
            ].astype(F32)
            inner_bias += row_sum(hidden_grad)
            slope_ref[rows, at] = hidden_grad.astype(BF)
        for piece in range(step // LANES):
            row = MIXER_IN_BIAS + part * (step // LANES) + piece
            vectors_ref[layer, row : row + 1, :] = inner_bias[:, piece * LANES : (piece + 1) * LANES]
        inner_grad_ref[:, at] = dot(low_ref[...], slope_ref[:, at], 0, 0).astype(BF)


def mixer_input_grad(
    layer, upper_ref, stream_ref, hidden_grad_ref, target_ref, inner_ref, vectors_ref,
    aff_scale_ref,
):
    aff_scale = aff_scale_ref[layer : layer + 1, :]
    scale_grad = jnp.zeros((1, LANES), F32)
    shift_grad = jnp.zeros((1, LANES), F32)
    for rows in row_tiles(upper_ref.shape[1]):
        normed_grad = dot(hidden_grad_ref[rows, :], inner_ref[...], 1, 1)
        scale_grad += row_sum(normed_grad * read(stream_ref, rows))
        shift_grad += row_sum(normed_grad)
        write(target_ref, rows, rounded(read(upper_ref, rows) + normed_grad * aff_scale))
    vectors_ref[layer, MIXER_AFF_SCALE : MIXER_AFF_SCALE + 1, :] = scale_grad
    vectors_ref[layer, MIXER_AFF_SHIFT : MIXER_AFF_SHIFT + 1, :] = shift_grad


def cross_backward(
    layer, stream_ref, upper_ref, target_ref, weight_grad_ref, vectors_ref, kept_ref, keep_ref,
    bias_ref, aff_scale_ref, aff_shift_ref, scale_ref, low_ref, mixing_low_ref, patches, each,
):
    padded = kept_ref.shape[2]
    aff_scale = aff_scale_ref[layer : layer + 1, :]
    aff_shift = aff_shift_ref[layer : layer + 1, :]
    scale = scale_ref[layer : layer + 1, :]
    aff_scale_grad = jnp.zeros((1, LANES), F32)
    aff_shift_grad = jnp.zeros((1, LANES), F32)
    scale_grad = jnp.zeros((1, LANES), F32)
    bias_grad = jnp.zeros((8, padded), F32)
    weight_grad = jnp.zeros((padded, padded), F32)
    ones = jnp.ones((8, LANES), BF)
    for image in range(kept_ref.shape[1]):
        rows = image_rows(image, patches, each)
        stream = read(stream_ref, rows)
        upper = read(upper_ref, rows)
        low_ref[image, 0:patches, :] = (aff_scale * stream + aff_shift).astype(BF)
        mixing_low_ref[image, 0:patches, :] = (upper * scale).astype(BF)
        kept = kept_ref[layer, image]
        shifted = dot(kept, low_ref[image]) + bias_ref[:, layer : layer + 1]
        scale_grad += row_sum(upper * shifted[0:patches])
        mixing_low = mixing_low_ref[image]
        bias_grad += dot(ones, mixing_low, 1, 1)
        weight_grad += (
            dot(mixing_low, low_ref[image], 1, 1) * keep_ref[image, layer : layer + 1, :]
        )
        normed_grad = dot(kept, mixing_low, 0, 0)[0:patches]
        aff_scale_grad += row_sum(normed_grad * stream)
        aff_shift_grad += row_sum(normed_grad)
        write(target_ref, rows, rounded(upper + normed_grad * aff_scale))
    weight_grad_ref[...] = weight_grad
    vectors_ref[layer, CROSS_AFF_SCALE : CROSS_AFF_SCALE + 1, :] = aff_scale_grad
    vectors_ref[layer, CROSS_AFF_SHIFT : CROSS_AFF_SHIFT + 1, :] = aff_shift_grad
    vectors_ref[layer, CROSS_SCALE : CROSS_SCALE + 1, :] = scale_grad
    vectors_ref[layer, CROSS_BIAS : CROSS_BIAS + 1, 0:padded] = bias_grad[0:1]


def clear_padding(*padded_refs, patches):
    for ref in padded_refs:
        images, padded, width = ref.shape
        for image in range(images):
            ref[image, padded - 16 :, :] = jnp.zeros((16, width), BF)


def first_kernel(
    mesh_shape,
    x_hbm, mask_hbm, g_hbm, inner_hbm, outer_hbm, cross_weight_hbm, cross_bias_hbm,
    inner_bias_hbm, mixer_aff_shift_hbm, *parameters_hbm_and_rest,
):
    parameters_hbm, rest = parameters_hbm_and_rest[:6], parameters_hbm_and_rest[6:]
    parameters, rest = rest[:6], rest[6:]
    cross_aff_scale, cross_aff_shift, cross_scale, mixer_aff_scale, outer_bias, mixer_scale = parameters
    (
    kept, sent, vectors, s0, s1, s2, s3, g_rows, low0, fired0, slope0, result0, fired1, slope1,
    inner0, outer0, inner1, outer1, kept_weight, keep, bias_columns,
    x_in, mask_in, g_in, cross_weight, cross_bias, inner_bias, mixer_aff_shift, weight_rows, padded_low,
    low1, scaled, inner_grad, outer_grad, sems,
    ) = rest
    _, patches, each, _ = x_in.shape
    per = x_in.shape[0]
    own = lax.axis_index("pipe") * per
    sources = (
        (cross_weight_hbm, cross_weight),
        (cross_bias_hbm, cross_bias),
        (inner_bias_hbm, inner_bias),
        (mixer_aff_shift_hbm, mixer_aff_shift),
        *zip(parameters_hbm, parameters),
        (mask_hbm.at[pl.ds(own, per)], mask_in),
        (x_hbm.at[pl.ds(own, per)], x_in),
        (inner_hbm.at[0], inner0),
        (outer_hbm.at[0], outer0),
        (inner_hbm.at[1], inner1),
        (g_hbm.at[pl.ds(own, per)], g_in),
        (outer_hbm.at[1], outer1),
    )
    copies = [
        pltpu.make_async_copy(source, target, sems.at[number])
        for number, (source, target) in enumerate(sources)
    ]
    for copy in copies:
        copy.start()
    vectors[...] = jnp.zeros_like(vectors)
    clear_padding(padded_low, patches=patches)
    for copy in copies[:-6]:
        copy.wait()
    copies = copies[-7:]
    masks = mask_in[...].reshape((per * each,) + mask_in.shape[2:])
    cross_setup(masks, cross_weight, cross_bias, kept_weight, keep, bias_columns, weight_rows)
    copies[1].wait()
    spread_rows(x_in, s0)
    cross = (kept_weight, bias_columns, cross_aff_scale, cross_aff_shift, cross_scale, padded_low)
    cross_forward(0, s0, s1, vectors, *cross, patches, each)
    copies[2].wait()
    mixer = (mixer_aff_scale, mixer_aff_shift)
    mixer_hidden(0, s1, low0, fired0, slope0, vectors, *mixer, inner0, inner_bias)
    copies[3].wait()
    squares = jnp.zeros((1, LANES), F32)
    for rows in row_tiles(s1.shape[1]):
        result = dot(fired0[rows, :], outer0[...]) + outer_bias[0:1, :]
        result0[rows, :] = result.astype(BF)
        branch = mixer_scale[0:1, :] * result
        write(s2, rows, rounded(read(s1, rows) + branch))
        squares += row_sum(branch * branch)
    vectors[0, SQUARES + 2 : SQUARES + 3, :] = squares
    cross_forward(1, s2, s3, vectors, *cross, patches, each)
    copies[4].wait()
    mixer_hidden(1, s3, low1, fired1, slope1, vectors, *mixer, inner1, inner_bias)
    copies[5].wait()
    spread_rows(g_in, g_rows)
    copies[6].wait()
    mixer_backward(
        1, g_rows, low1, fired1, slope1, scaled, inner1, outer1, inner_grad, outer_grad,
        vectors, mixer_scale,
    )
    pack_products(own_codes(mesh_shape), inner_grad, outer_grad, kept, sent)


def second_kernel(
    s2, s3, g_rows, fired1, hidden_grad, inner1, outer1, kept_weight, keep, bias_columns,
    vectors_in, cross_aff_scale, cross_aff_shift, cross_scale, mixer_aff_scale, outer_bias,
    mixer_scale,
    output, g2, weight_grad, vectors,
    leaving, g1, padded_low, padded_mixing,
):
    _, patches, each, _ = output.shape
    vectors[...] = vectors_in[...]
    clear_padding(padded_low, padded_mixing, patches=patches)
    squares = jnp.zeros((1, LANES), F32)
    scale_grad = jnp.zeros((1, LANES), F32)
    for rows in row_tiles(s3.shape[1]):
        result = dot(fired1[rows, :], outer1[...]) + outer_bias[1:2, :]
        scale_grad += row_sum(read(g_rows, rows) * result)
        branch = mixer_scale[1:2, :] * result
        write(leaving, rows, read(s3, rows) + branch)
        squares += row_sum(branch * branch)
    vectors[1, SQUARES + 2 : SQUARES + 3, :] = squares
    vectors[1, MIXER_SCALE : MIXER_SCALE + 1, :] = scale_grad
    mixer_input_grad(1, g_rows, s3, hidden_grad, g1, inner1, vectors, mixer_aff_scale)
    gather_rows(leaving, output)
    cross_backward(
        1, s2, g1, g2, weight_grad, vectors, kept_weight, keep, bias_columns,
        cross_aff_scale, cross_aff_shift, cross_scale, padded_low, padded_mixing, patches, each,
    )


def third_kernel(
    mesh_shape,
    g2, low0, fired0, slope0, result0, inner0, outer0, vectors_in, mixer_scale,
    kept, sent, hidden_grad, vectors,
    scaled, inner_grad, outer_grad,
):
    vectors[...] = vectors_in[...]
    hidden_grad[...] = slope0[...]
    mixer_backward(
        0, g2, low0, fired0, hidden_grad, scaled, inner0, outer0, inner_grad, outer_grad,
        vectors, mixer_scale,
    )
    pack_products(own_codes(mesh_shape), inner_grad, outer_grad, kept, sent)
    scale_grad = jnp.zeros((1, LANES), F32)
    for rows in row_tiles(g2.shape[1]):
        scale_grad += row_sum(read(g2, rows) * result0[rows, :].astype(F32))
    vectors[0, MIXER_SCALE : MIXER_SCALE + 1, :] = scale_grad


def fourth_kernel(
    mesh_shape,
    s0, s1, g2, hidden_grad, inner0, kept_weight, keep, bias_columns, weight_grad1, vectors_in,
    cross_aff_scale, cross_aff_shift, cross_scale, mixer_aff_scale,
    input_grad, kept, sent,
    g1, g0, weight_grad0, vectors, small, padded_low, padded_mixing,
):
    _, patches, each, _ = input_grad.shape
    vectors[...] = vectors_in[...]
    clear_padding(padded_low, padded_mixing, patches=patches)
    mixer_input_grad(0, g2, s1, hidden_grad, g1, inner0, vectors, mixer_aff_scale)
    cross_backward(
        0, s0, g1, g0, weight_grad0, vectors, kept_weight, keep, bias_columns,
        cross_aff_scale, cross_aff_shift, cross_scale, padded_low, padded_mixing, patches, each,
    )
    layers, padded = kept_weight.shape[0], kept_weight.shape[2]
    groups = padded // VECTOR_ROWS
    small[...] = jnp.zeros_like(small)
    for layer, weight_grad in enumerate((weight_grad0, weight_grad1)):
        for group in range(groups):
            rows = slice(group * VECTOR_ROWS, (group + 1) * VECTOR_ROWS)
            small[layer * groups + group, :, 0:padded] = weight_grad[rows, :].astype(BF)
        small[layers * groups + layer] = vectors[layer].astype(BF)
    pack_halves(own_codes(mesh_shape), lambda block: (small[block],), kept, sent)
    gather_rows(g0, input_grad)


def exchange_bits(values, mesh_shape, phases):
    even, odd = phase_bits(mesh_shape)
    places = range(mesh_shape["dp"] * mesh_shape["pipe"])

    def partner(place):
        for phase in phases:
            place ^= (odd if place & 1 else even)[phase]
        return place

    return lax.ppermute(values, AXES, [(i, partner(i)) for i in places])


def across(slot):
    return [phase for phase, bit in ((SCATTERED - 2, 2), (SCATTERED - 1, 1)) if slot & bit]


def part_sum(terms, start, stop):
    return sum(t[start:stop].astype(F32) for t in terms)


def halve(terms, width, mesh_shape, phase):
    half = width // 2
    leaving = part_sum(terms, half, width).astype(BF)
    return leaving, terms + [exchange_bits(leaving, mesh_shape, [phase])]


def scatter_last(terms, mesh_shape):
    arrived = [
        exchange_bits(part_sum(terms, slot, slot + 1).astype(BF), mesh_shape, across(slot))
        for slot in (1, 3, 2)
    ]
    total = part_sum(terms, 0, 1) + sum(a.astype(F32) for a in arrived)
    for phase in range(SCATTERED, len(phase_bits(mesh_shape)[0])):
        total = total.astype(BF)
        total = total.astype(F32) + exchange_bits(total, mesh_shape, [phase]).astype(F32)
    return total.astype(BF)


def gather_last(own, mesh_shape):
    arrived = {slot: exchange_bits(own, mesh_shape, across(slot)) for slot in (1, 3, 2)}
    return jnp.concatenate([own, arrived[1], arrived[2], arrived[3]], axis=0)


def double(held, mesh_shape, phase):
    return jnp.concatenate([held, exchange_bits(held, mesh_shape, [phase])], axis=0)


def after(values, *others):
    return lax.optimization_barrier((values, *others))[0]


def unpack_block(block, values, images_all, layer, inner_rows, outer_rows, inner_out, outer_out, sems):
    depth = outer_rows.shape[0] // BLOCKS
    row_at, column_at = inner_spot(block, depth, inner_rows.shape[1])
    inner_at = (pl.ds(row_at, depth), pl.ds(column_at, LANES))
    outer_at = pl.ds(pl.multiple_of(block * depth, depth), depth)
    copies = (
        pltpu.make_async_copy(inner_rows.at[inner_at], inner_out.at[(layer,) + inner_at], sems.at[0, block]),
        pltpu.make_async_copy(outer_rows.at[outer_at], outer_out.at[layer, outer_at], sems.at[1, block]),
    )
    if values is not None:
        inner_rows[inner_at] = values[0:depth, :].astype(F32) / images_all
        outer_rows[outer_at, :] = values[depth : 2 * depth, :].astype(F32) / images_all
    return copies


def unpack_layer(mesh_shape, images_all, layer, quarters, rows, outs, sems, extra=None):
    codes = own_codes(mesh_shape)
    quarter = HALF // 2
    places = []
    for number, values in enumerate(quarters):
        block_of = kept_block if number < 2 else sent_block
        places.append((values, block_of, (number % 2) * quarter))

    @pl.loop(0, quarter)
    def _(slot):
        for values, block_of, base in places:
            block = block_of(codes, slot + base)
            for copy in unpack_block(block, values.at[slot], images_all, layer, *rows, *outs, sems):
                copy.start()
            if extra is not None:
                extra(block, values.at[slot])

    @pl.loop(0, BLOCKS)
    def _(block):
        for copy in unpack_block(block, None, images_all, layer, *rows, *outs, sems):
            copy.wait()


def unpack_last_layer(
    mesh_shape, images_all, held, late, other_held, other_late,
    inner_out, outer_out, inner_rows, outer_rows, sems,
):
    unpack_layer(
        mesh_shape, images_all, 1, (held, late, other_held, other_late),
        (inner_rows, outer_rows), (inner_out, outer_out), sems,
    )


def unpack_first_layer(
    mesh_shape, images_all, held, late, other_held, other_late, inner_in, outer_in,
    inner_out, outer_out, weight_out, aff_scale_out, aff_shift_out, cross_bias_out,
    cross_scale_out, mixer_aff_scale_out, mixer_aff_shift_out, inner_bias_out, outer_bias_out,
    mixer_scale_out, magnitudes_out,
    inner_rows, outer_rows, weight_rows, vectors, sems,
):
    patches, layers, _ = weight_out.shape
    depth = outer_rows.shape[0] // BLOCKS
    groups = weight_rows.shape[1] // VECTOR_ROWS

    def extra(block, values):
        small = values[2 * depth :, :].astype(F32) / images_all

        @pl.when(block < layers * groups)
        def _():
            at = pl.multiple_of((block % groups) * VECTOR_ROWS, VECTOR_ROWS)
            weight_rows[block // groups, pl.ds(at, VECTOR_ROWS), :] = small

        @pl.when((block >= layers * groups) & (block < layers * (groups + 1)))
        def _():
            vectors[block - layers * groups] = small

    unpack_layer(
        mesh_shape, images_all, 0, (held, late, other_held, other_late),
        (inner_rows, outer_rows), (inner_out, outer_out), sems, extra,
    )
    for layer in range(layers):
        row = slice(layer, layer + 1)
        weight_out[:, layer, :] = weight_rows[layer, 0:patches, 0:patches]
        aff_scale_out[row, :] = vectors[layer, CROSS_AFF_SCALE : CROSS_AFF_SCALE + 1, :]
        aff_shift_out[row, :] = vectors[layer, CROSS_AFF_SHIFT : CROSS_AFF_SHIFT + 1, :]
        cross_bias_out[row, :] = vectors[layer, CROSS_BIAS : CROSS_BIAS + 1, 0:patches]
        cross_scale_out[row, :] = vectors[layer, CROSS_SCALE : CROSS_SCALE + 1, :]
        mixer_aff_scale_out[row, :] = vectors[layer, MIXER_AFF_SCALE : MIXER_AFF_SCALE + 1, :]
        mixer_aff_shift_out[row, :] = vectors[layer, MIXER_AFF_SHIFT : MIXER_AFF_SHIFT + 1, :]
        outer_bias_out[row, :] = vectors[layer, MIXER_OUT_BIAS : MIXER_OUT_BIAS + 1, :]
        mixer_scale_out[row, :] = vectors[layer, MIXER_SCALE : MIXER_SCALE + 1, :]
        for piece in range(SQUARES - MIXER_IN_BIAS):
            at = slice(piece * LANES, (piece + 1) * LANES)
            inner_bias_out[row, at] = vectors[layer, MIXER_IN_BIAS + piece : MIXER_IN_BIAS + piece + 1, :]
        squares = vectors[layer, SQUARES : SQUARES + 4, :] / (patches * LANES)
        means = jnp.sqrt(jnp.sum(squares, axis=1, keepdims=True))
        for kind in range(2):
            for which in range(2):
                at = 2 * kind + which
                magnitudes_out[layer, kind : kind + 1, which : which + 1] = means[at : at + 1]


def call(kernel, name, args, outs, scratch, in_specs=None, out_specs=None, aliases=None, us=1):
    return pl.pallas_call(
        kernel,
        out_shape=outs,
        in_specs=[VMEM] * len(args) if in_specs is None else in_specs,
        out_specs=[VMEM] * len(outs) if out_specs is None else out_specs,
        scratch_shapes=scratch,
        input_output_aliases=aliases or {},
        compiler_params=pltpu.CompilerParams(vmem_limit_bytes=VMEM_LIMIT),
        cost_estimate=pl.CostEstimate(
            flops=int(us * 1e9), bytes_accessed=int(us * 3e6), transcendentals=0
        ),
        name=name,
    )(*args)


def in_vmem(arrays):
    return [pltpu.with_memory_space_constraint(a, pltpu.VMEM) for a in arrays]


def in_hbm(arrays):
    return [pltpu.with_memory_space_constraint(a, pltpu.HBM) for a in arrays]


def on_device(
    mesh_shape,
    inputs,
    patch_masks,
    out_grad,
    cross_aff_scale,
    cross_aff_shift,
    cross_weight,
    cross_bias,
    cross_scale,
    mixer_aff_scale,
    mixer_aff_shift,
    mixer_in,
    mixer_in_bias,
    mixer_out,
    mixer_out_bias,
    mixer_scale,
):
    micros, each, patches, width = inputs.shape
    layers, _, columns = mixer_in.shape
    per = micros // mesh_shape["pipe"]
    images = per * each
    padded = -(-patches // 16) * 16
    rows = images * patches
    depth = width * columns // (BLOCKS * LANES)
    images_all = micros * each * mesh_shape["dp"]
    x_rows = jnp.transpose(inputs, (0, 2, 1, 3))
    g_rows = jnp.transpose(out_grad, (0, 2, 1, 3))
    weight_rows = jnp.transpose(cross_weight, (1, 0, 2))

    def vmem(*shape, dtype=BF):
        return pltpu.VMEM(shape, dtype)

    def hbm(*shape, dtype=F32):
        return jax.ShapeDtypeStruct(shape, dtype)

    stream = vmem(width // 128, rows, 128, dtype=F32)
    hidden = vmem(rows, columns)
    inner, outer = vmem(width, columns), vmem(columns, width)
    vectors = vmem(layers, VECTOR_ROWS, LANES, dtype=F32)
    padded_images = vmem(images, padded, width)
    local = (per, patches, each, width)
    first = call(
        functools.partial(first_kernel, mesh_shape),
        "forward",
        in_hbm((
            x_rows, patch_masks, g_rows, mixer_in, mixer_out, weight_rows, cross_bias,
            mixer_in_bias, mixer_aff_shift, cross_aff_scale, cross_aff_shift, cross_scale,
            mixer_aff_scale, mixer_out_bias, mixer_scale,
        )),
        (
            *[vmem(layers, width, dtype=F32)] * 6,
            vmem(HALF, 2 * depth, LANES),
            vmem(HALF, 2 * depth, LANES),
            vectors,
            *[stream] * 5,
            vmem(rows, width),
            hidden,
            hidden,
            vmem(rows, width),
            hidden,
            hidden,
            inner,
            outer,
            inner,
            outer,
            vmem(layers, images, padded, padded),
            vmem(images, 8, padded, dtype=F32),
            vmem(padded, 8, dtype=F32),
        ),
        [
            vmem(*local),
            vmem(per, each, layers, patches, dtype=jnp.int32),
            vmem(*local),
            vmem(patches, layers, patches),
            vmem(layers, patches, dtype=F32),
            vmem(layers, columns, dtype=F32),
            vmem(layers, width, dtype=F32),
            vmem(2, layers * patches, 128, dtype=F32),
            padded_images,
            vmem(rows, width),
            vmem(rows, width),
            inner,
            outer,
            pltpu.SemaphoreType.DMA((17,)),
        ],
        in_specs=[HBM] * 15,
        us=18,
    )
    aff_scale, aff_shift, scale, mixer_aff, result_bias, result_scale = in_vmem(first[:6])
    (
        kept1, sent1, sums, s0, s1, s2, s3, upper, low0, fired0, slope0, result0, fired1,
        hidden_grad1, inner0, outer0, inner1, outer1, kept_weight, keep, bias_columns,
    ) = first[6:]
    output, g2, weight_grad1, sums = call(
        second_kernel,
        "middle",
        (
            *in_vmem((
                s2, s3, upper, fired1, hidden_grad1, inner1, outer1, kept_weight, keep,
                bias_columns, sums,
            )),
            aff_scale, aff_shift, scale, mixer_aff, result_bias, result_scale,
        ),
        (hbm(*local, dtype=BF), stream, vmem(padded, padded, dtype=F32), vectors),
        [stream, stream, padded_images, padded_images],
        us=5,
    )
    terms1 = [kept1, exchange_bits(sent1, mesh_shape, [0])]
    leaving1, terms1 = halve(terms1, HALF, mesh_shape, 1)
    g2, _ = lax.optimization_barrier((g2, leaving1))
    halves = vmem(HALF, 2 * depth, LANES)
    kept0, sent0, hidden_grad0, sums = call(
        functools.partial(third_kernel, mesh_shape),
        "first_layer_weights",
        (*in_vmem((g2, low0, fired0, slope0, result0, inner0, outer0, sums)), result_scale),
        (halves, halves, hidden, vectors),
        [vmem(rows, width), inner, outer],
        us=7,
    )
    sent0, sums, _ = lax.optimization_barrier((sent0, sums, terms1[-1]))
    arrived0 = exchange_bits(sent0, mesh_shape, [0])
    halves = vmem(HALF, VECTOR_ROWS, LANES)
    input_grad, kept_small, sent_small = call(
        functools.partial(fourth_kernel, mesh_shape),
        "first_layer_input",
        (
            *in_vmem((
                s0, s1, g2, hidden_grad0, inner0, kept_weight, keep, bias_columns, weight_grad1,
                sums,
            )),
            aff_scale, aff_shift, scale, mixer_aff,
        ),
        (hbm(*local, dtype=BF), halves, halves),
        [
            stream,
            stream,
            vmem(padded, padded, dtype=F32),
            vectors,
            vmem(BLOCKS, VECTOR_ROWS, LANES),
            padded_images,
            padded_images,
        ],
        us=5,
    )
    _, terms1 = halve(terms1, HALF // 2, mesh_shape, 2)
    sent_small = after(sent_small, terms1[-1])
    arrived_small = exchange_bits(sent_small, mesh_shape, [0])
    terms0 = [
        jnp.concatenate([kept0, kept_small], axis=1),
        jnp.concatenate([arrived0, arrived_small], axis=1),
    ]
    _, terms0 = halve(terms0, HALF, mesh_shape, 1)
    own1 = scatter_last(terms1, mesh_shape)
    terms0[-1], own1 = lax.optimization_barrier((terms0[-1], own1))
    _, terms0 = halve(terms0, HALF // 2, mesh_shape, 2)
    four1 = gather_last(own1, mesh_shape)
    terms0[-1], four1 = lax.optimization_barrier((terms0[-1], four1))
    own0 = scatter_last(terms0, mesh_shape)
    held1 = double(four1, mesh_shape, 2)
    own0, held1 = lax.optimization_barrier((own0, held1))
    four0 = gather_last(own0, mesh_shape)
    late1 = exchange_bits(held1, mesh_shape, [1])
    other_held1 = exchange_bits(held1, mesh_shape, [0])
    four0, late1 = lax.optimization_barrier((four0, late1))
    held0 = double(four0, mesh_shape, 2)
    other_late1 = exchange_bits(late1, mesh_shape, [0])
    held0, other_late1 = lax.optimization_barrier((held0, other_late1))
    late0 = exchange_bits(held0, mesh_shape, [1])
    other_held0 = exchange_bits(held0, mesh_shape, [0])
    quarters1 = (held1, late1, other_held1, other_late1)
    inner_out, outer_out = hbm(layers, width, columns), hbm(layers, columns, width)
    unpacked = [
        vmem(width, columns, dtype=F32),
        vmem(columns, width, dtype=F32),
    ]
    sems = pltpu.SemaphoreType.DMA((2, BLOCKS))
    grads = call(
        functools.partial(unpack_last_layer, mesh_shape, images_all),
        "unpack_last_layer",
        in_vmem(quarters1),
        (inner_out, outer_out),
        unpacked + [sems],
        out_specs=[HBM] * 2,
        us=3,
    )
    late0, grads = lax.optimization_barrier((late0, grads))
    quarters0 = (held0, late0, other_held0, exchange_bits(late0, mesh_shape, [0]))
    row = hbm(layers, width)
    (
        inner_grad, outer_grad, weight_grad, aff_scale_grad, aff_shift_grad, bias_grad,
        scale_grad, mixer_aff_scale_grad, mixer_aff_shift_grad, inner_bias_grad,
        outer_bias_grad, mixer_scale_grad, magnitudes,
    ) = call(
        functools.partial(unpack_first_layer, mesh_shape, images_all),
        "unpack_first_layer",
        (*in_vmem(quarters0), *grads),
        (
            inner_out, outer_out, hbm(patches, layers, patches), row, row,
            hbm(layers, patches), row, row, row, hbm(layers, columns), row, row,
            hbm(layers, 2, 2),
        ),
        unpacked + [vmem(layers, padded, LANES, dtype=F32), vectors, sems],
        in_specs=[VMEM] * 4 + [HBM] * 2,
        out_specs=[HBM] * 2 + [VMEM] * 11,
        aliases={4: 0, 5: 1},
        us=3,
    )
    return (
        jnp.transpose(output, (0, 2, 1, 3)),
        jnp.transpose(input_grad, (0, 2, 1, 3)),
        aff_scale_grad,
        aff_shift_grad,
        jnp.transpose(weight_grad, (1, 0, 2)),
        bias_grad,
        scale_grad,
        mixer_aff_scale_grad,
        mixer_aff_shift_grad,
        inner_grad,
        inner_bias_grad,
        outer_grad,
        outer_bias_grad,
        mixer_scale_grad,
        magnitudes,
    )


def solution(mesh):
    split = P(None, "dp", None, None)
    owned = P("pipe", "dp", None, None)
    return jax.shard_map(
        functools.partial(on_device, dict(mesh.shape)),
        mesh=mesh,
        in_specs=(split,) * 3 + (P(),) * 12,
        out_specs=(owned,) * 2 + (P(),) * 13,
        check_vma=False,
    )
```

time: 332 us -> 112 us (0.34)
  waiting for transfers between devices: 136 us -> 36.7 us
  matrix products: 69.7 us -> 0 us
  blocking collectives: 44.4 us -> 0 us
  Pallas kernels: 0 us -> 39.7 us
  other arithmetic: 36.5 us -> 1.25 us
  starting transfers between devices: 0.04 us -> 32.7 us
  local copies, waits for them, and re-layouts: 29.8 us -> 0.3 us
  between operations: 14.6 us -> 0.99 us
    psum x1 -> x0, waiting for transfers between devices: 136 us -> none  [on_device(): gradient, totals = lax.psum((gradient, totals), ('dp', 'pipe'))]
    dot_general x18 -> x0, matrix products: 69.7 us -> none  [the longest x2 26.8 us: mixer_parts(): jnp.dot(normed_low, inner_weight, preferred_element_type=jnp.float32)]
    psum x1 -> x0, blocking collectives: 44.4 us -> none  [on_device(): gradient, totals = lax.psum((gradient, totals), ('dp', 'pipe'))]
    pallas_call x0 -> x6, Pallas kernels: none -> 39.7 us  [call(): pl.pallas_call(kernel, out_shape=outs, in_specs=[VMEM] * len(args) if in_...]
    ppermute x0 -> x27, waiting for transfers between devices: none -> 36.7 us  [exchange_bits(): return lax.ppermute(values, AXES, [(i, partner(i)) for i in places])]
    ppermute x0 -> x27, starting transfers between devices: none -> 32.7 us  [exchange_bits(): return lax.ppermute(values, AXES, [(i, partner(i)) for i in places])]
    div x12 -> x0, other arithmetic: 13.9 us -> none  [on_device(): part / images_all]
    another operation x17 -> x0, other arithmetic: 13.1 us -> none  [the longest x12 7.66 us: on_device(): gradient = tuple((jnp.stack(parts) for parts in zip(*grads)))]
  transfers between devices with their start and end apart: 1 -> 27, of which waited for: 1 -> 17; matrix products, arithmetic and copies ran while one was open for 5% -> 1% of each run, Pallas kernels for 0% -> 17%
where the time goes in v2:
time: 112 us
  Pallas kernels  39.7 us (35%)
  waiting for transfers between devices  36.7 us (33%)
  starting transfers between devices  32.7 us (29%)
  other arithmetic  1.25 us (1%)
    pallas_call x6, Pallas kernels, call(): pl.pallas_call(kernel, out_shape=outs, in_specs=[VMEM] * len(args) if in_...  39.7 us
    ppermute x27, waiting for transfers between devices, exchange_bits(): return lax.ppermute(values, AXES, [(i, partner(i)) for i in places])  36.7 us
    ppermute x27, starting transfers between devices, exchange_bits(): return lax.ppermute(values, AXES, [(i, partner(i)) for i in places])  32.7 us
  transfers between devices with their start and end apart: 27, of which 17 were waited for; matrix products, arithmetic and copies ran while one was open for 1% of the time, Pallas kernels for 17%

profile of v2, /device:TPU:0, one launch (start us, length us, event | category | flops | bytes accessed | tf_op | source)
XLA Modules:
  0.0 111.6 jit_solution(17409068161808930769)
XLA Ops:
  0.7 16.5 %forward.1 = (f32[2,384]{1,0:T(2,128)S(1)}, f32[2,384]{1,0:T(2,128)S(1)}, f32[2,384]{1,0:T(2,128)S(1)}, f32[2,384]{1,0:T(2,128)S(1)}, f32[2,384]{1,0:T(2,128)S(1...) custom-call(bf16[4,196,4,384]{3,2,1,0:T(4,128)(2,1)} %bitcast.6, ...), custom_call_target="tpu_custom_call" | custom-call | flops 17999998976 | bytes 54000000 | tf_op jit(solution)/shard_map/forward/pallas_call | solution.py:598
  17.2 0.5 collective-permute-start
  17.7 5.3 %middle.1 = (bf16[1,196,4,384]{3,2,1,0:T(4,128)(2,1)}, f32[3,784,128]{2,1,0:T(8,128)S(1)}, f32[208,208]{1,0:T(8,128)S(1)}, f32[2,16,384]{2,1,0:T(8,128)S(1)}) custom-call(f32[3,784,128]{2,1,0:T(8,128)S(1)} %get-tuple-element.85.s2, f32[3,784,128]{2,1,0:T(8,128)S(1)} %get-tuple-element.86.s3, f32[3,784,128]{2,1,0:T(8,128)S(1)} %get-tuple-element.87.g_rows, ...), custom_call_target="tpu_custom_call" | custom-call | flops 5000000000 | bytes 15000000 | tf_op jit(solution)/shard_map/middle/pallas_call | solution.py:598
  23.0 0.1 add_convert_fusion.1
  23.1 2.6 %collective-permute-start.1 = (bf16[8,96,384]{2,1,0:T(8,128)(2,1)S(1)}, bf16[8,96,384]{2,1,0:T(8,128)(2,1)S(1)}, u32[]{:S(2)}, u32[]{:S(2)}) collective-permute-start(bf16[8,96,384]{2,1,0:T(8,128)(2,1)S(1)} %add_convert_fusion.1), channel_id=1, source_target_pairs={{0,2},{1,5},{2,0},{3,7},{4,6},{5,1},{6,4},{7,3},{8,10},{9,13},{10,... | collective-permute-start | bytes 1769480 | tf_op jit(solution)/shard_map/ppermute | solution.py:458
  25.7 6.5 %first_layer_weights.1 = (bf16[16,96,384]{2,1,0:T(8,128)(2,1)S(1)}, bf16[16,96,384]{2,1,0:T(8,128)(2,1)S(1)}, bf16[784,1536]{1,0:T(8,128)(2,1)S(1)}, f32[2,16,384]{2,1,0:T(8,128)S(1)}) custom-call(f32[3,784,128]{2,1,0:T(8,128)S(1)} %get-tuple-element.108.g2, bf16[784,384]{1,0:T(8,128)(2,1)S(1)} %get-tuple-element.109.low0, ...), custom_call_target="tpu_custom_call" | custom-call | flops 7000000000 | bytes 21000000 | tf_op jit(solution)/shard_map/first_layer_weights/pallas_call | solution.py:598
  32.3 1.3 %collective-permute-done.1 = bf16[8,96,384]{2,1,0:T(8,128)(2,1)S(1)} collective-permute-done((bf16[8,96,384]{2,1,0:T(8,128)(2,1)S(1)}, bf16[8,96,384]{2,1,0:T(8,128)(2,1)S(1)}, u32[]{:S(2)}, u32[]{:S(2)}) %collective-permute-start.1) | collective-permute-done | bytes 589856 | tf_op jit(solution)/shard_map/ppermute | solution.py:458
  33.6 0.0 collective-permute-start.2
  33.6 0.1 constant_dynamic-update-slice_fusion.1
  33.7 0.1 add_convert_fusion.3
  33.8 2.1 %collective-permute-start.3 = (bf16[4,96,384]{2,1,0:T(8,128)(2,1)S(1)}, bf16[4,96,384]{2,1,0:T(8,128)(2,1)S(1)}, u32[]{:S(2)}, u32[]{:S(2)}) collective-permute-start(bf16[4,96,384]{2,1,0:T(8,128)(2,1)S(1)} %add_convert_fusion.3), channel_id=1, source_target_pairs={{0,4},{1,3},{2,6},{3,1},{4,0},{5,7},{6,2},{7,5},{8,12},{9,11},{10,... | collective-permute-start | bytes 884744 | tf_op jit(solution)/shard_map/ppermute | solution.py:458
  35.9 4.9 %first_layer_input.1 = (bf16[1,196,4,384]{3,2,1,0:T(4,128)(2,1)}, bf16[16,16,384]{2,1,0:T(8,128)(2,1)S(1)}, bf16[16,16,384]{2,1,0:T(8,128)(2,1)S(1)}) custom-call(f32[3,784,128]{2,1,0:T(8,128)S(1)} %get-tuple-element.103.s0, f32[3,784,128]{2,1,0:T(8,128)S(1)} %get-tuple-element.104.s1, f32[3,784,128]{2,1,0:T(8,128)S(1)} %get-tuple-element.108.g2, ...), custom_call_target="tpu_custom_call" | custom-call | flops 5000000000 | bytes 15000000 | tf_op jit(solution)/shard_map/first_layer_input/pallas_call | solution.py:598
  40.8 0.0 collective-permute-done.3
  40.8 0.2 collective-permute-start.4
  41.1 0.0 collective-permute-done.2
  41.1 0.1 constant_dynamic-update-slice_fusion.3
  41.2 1.1 collective-permute-done.4
  42.3 0.2 add_convert_fusion
  42.5 1.8 %collective-permute-start.5 = (bf16[8,112,384]{2,1,0:T(8,128)(2,1)S(1)}, bf16[8,112,384]{2,1,0:T(8,128)(2,1)S(1)}, u32[]{:S(2)}, u32[]{:S(2)}) collective-permute-start(bf16[8,112,384]{2,1,0:T(8,128)(2,1)S(1)} %add_convert_fusion), channel_id=1, source_target_pairs={{0,2},{1,5},{2,0},{3,7},{4,6},{5,1},{6,4},{7,3},{8,10},{9,13},{10,... | collective-permute-start | bytes 2064392 | tf_op jit(solution)/shard_map/ppermute | solution.py:458
  44.4 0.1 add_convert_fusion.11
  44.5 2.6 %collective-permute-start.6 = (bf16[1,96,384]{2,1,0:T(8,128)(2,1)S(1)}, bf16[1,96,384]{2,1,0:T(8,128)(2,1)S(1)}, u32[]{:S(2)}, u32[]{:S(2)}) collective-permute-start(bf16[1,96,384]{2,1,0:T(8,128)(2,1)S(1)} %get-tuple-element.158), channel_id=1, source_target_pairs={{0,16},{1,17},{2,18},{3,19},{4,20},{5,21},{6,22},{7,23},{8,24},{9,... | collective-permute-start | bytes 221192 | tf_op jit(solution)/shard_map/ppermute | solution.py:458
  47.1 1.4 %collective-permute-start.7 = (bf16[1,96,384]{2,1,0:T(8,128)(2,1)S(1)}, bf16[1,96,384]{2,1,0:T(8,128)(2,1)S(1)}, u32[]{:S(2)}, u32[]{:S(2)}) collective-permute-start(bf16[1,96,384]{2,1,0:T(8,128)(2,1)S(1)} %get-tuple-element.160), channel_id=1, source_target_pairs={{0,24},{1,25},{2,26},{3,27},{4,28},{5,29},{6,30},{7,31},{8,16},{9,... | collective-permute-start | bytes 221192 | tf_op jit(solution)/shard_map/ppermute | solution.py:458
  48.5 0.2 collective-permute-start.8
  48.7 3.9 %collective-permute-done.6 = bf16[1,96,384]{2,1,0:T(8,128)(2,1)S(1)} collective-permute-done((bf16[1,96,384]{2,1,0:T(8,128)(2,1)S(1)}, bf16[1,96,384]{2,1,0:T(8,128)(2,1)S(1)}, u32[]{:S(2)}, u32[]{:S(2)}) %collective-permute-start.6) | collective-permute-done | bytes 73760 | tf_op jit(solution)/shard_map/ppermute | solution.py:458
  52.6 1.0 collective-permute-done.7
  53.6 0.4 collective-permute-done.8
  54.1 0.1 add_convert_fusion.8
  54.1 0.0 collective-permute-done.5
  54.2 0.1 add_convert_fusion.2
  54.3 1.2 %collective-permute-start.9 = (bf16[4,112,384]{2,1,0:T(8,128)(2,1)S(1)}, bf16[4,112,384]{2,1,0:T(8,128)(2,1)S(1)}, u32[]{:S(2)}, u32[]{:S(2)}) collective-permute-start(bf16[4,112,384]{2,1,0:T(8,128)(2,1)S(1)} %add_convert_fusion.2), channel_id=1, source_target_pairs={{0,4},{1,3},{2,6},{3,1},{4,0},{5,7},{6,2},{7,5},{8,12},{9,11},{10,... | collective-permute-start | bytes 1032200 | tf_op jit(solution)/shard_map/ppermute | solution.py:458
  55.5 2.6 %collective-permute-start.10 = (bf16[1,96,384]{2,1,0:T(8,128)(2,1)S(1)}, bf16[1,96,384]{2,1,0:T(8,128)(2,1)S(1)}, u32[]{:S(2)}, u32[]{:S(2)}) collective-permute-start(bf16[1,96,384]{2,1,0:T(8,128)(2,1)S(1)} %add_convert_fusion.8), channel_id=1, source_target_pairs={{0,16},{1,17},{2,18},{3,19},{4,20},{5,21},{6,22},{7,23},{8,24},{9,... | collective-permute-start | bytes 221192 | tf_op jit(solution)/shard_map/ppermute | solution.py:458
  58.1 1.6 %collective-permute-start.11 = (bf16[1,96,384]{2,1,0:T(8,128)(2,1)S(1)}, bf16[1,96,384]{2,1,0:T(8,128)(2,1)S(1)}, u32[]{:S(2)}, u32[]{:S(2)}) collective-permute-start(bf16[1,96,384]{2,1,0:T(8,128)(2,1)S(1)} %add_convert_fusion.8), channel_id=1, source_target_pairs={{0,8},{1,9},{2,10},{3,11},{4,12},{5,13},{6,14},{7,15},{8,0},{9,1},... | collective-permute-start | bytes 221192 | tf_op jit(solution)/shard_map/ppermute | solution.py:458
  59.7 0.2 collective-permute-start.12
  59.9 3.0 %collective-permute-done.10 = bf16[1,96,384]{2,1,0:T(8,128)(2,1)S(1)} collective-permute-done((bf16[1,96,384]{2,1,0:T(8,128)(2,1)S(1)}, bf16[1,96,384]{2,1,0:T(8,128)(2,1)S(1)}, u32[]{:S(2)}, u32[]{:S(2)}) %collective-permute-start.10) | collective-permute-done | bytes 73760 | tf_op jit(solution)/shard_map/ppermute | solution.py:458
  62.9 0.4 collective-permute-done.11
  63.3 2.5 %collective-permute-done.12 = bf16[1,96,384]{2,1,0:T(8,128)(2,1)S(1)} collective-permute-done((bf16[1,96,384]{2,1,0:T(8,128)(2,1)S(1)}, bf16[1,96,384]{2,1,0:T(8,128)(2,1)S(1)}, u32[]{:S(2)}, u32[]{:S(2)}) %collective-permute-start.12) | collective-permute-done | bytes 73760 | tf_op jit(solution)/shard_map/ppermute | solution.py:458
  65.9 0.1 add_convert_fusion.7
  66.0 2.0 %collective-permute-start.13 = (bf16[1,112,384]{2,1,0:T(8,128)(2,1)S(1)}, bf16[1,112,384]{2,1,0:T(8,128)(2,1)S(1)}, u32[]{:S(2)}, u32[]{:S(2)}) collective-permute-start(bf16[1,112,384]{2,1,0:T(8,128)(2,1)S(1)} %get-tuple-element.155), channel_id=1, source_target_pairs={{0,16},{1,17},{2,18},{3,19},{4,20},{5,21},{6,22},{7,23},{8,24},{9,... | collective-permute-start | bytes 258056 | tf_op jit(solution)/shard_map/ppermute | solution.py:458
  68.0 0.4 collective-permute-start.14
  68.5 1.1 %collective-permute-start.15 = (bf16[1,112,384]{2,1,0:T(8,128)(2,1)S(1)}, bf16[1,112,384]{2,1,0:T(8,128)(2,1)S(1)}, u32[]{:S(2)}, u32[]{:S(2)}) collective-permute-start(bf16[1,112,384]{2,1,0:T(8,128)(2,1)S(1)} %get-tuple-element.156), channel_id=1, source_target_pairs={{0,8},{1,9},{2,10},{3,11},{4,12},{5,13},{6,14},{7,15},{8,0},{9,1},... | collective-permute-start | bytes 258056 | tf_op jit(solution)/shard_map/ppermute | solution.py:458
  69.6 0.5 collective-permute-start.16
  70.1 4.6 %collective-permute-done.13 = bf16[1,112,384]{2,1,0:T(8,128)(2,1)S(1)} collective-permute-done((bf16[1,112,384]{2,1,0:T(8,128)(2,1)S(1)}, bf16[1,112,384]{2,1,0:T(8,128)(2,1)S(1)}, u32[]{:S(2)}, u32[]{:S(2)}) %collective-permute-start.13) | collective-permute-done | bytes 86048 | tf_op jit(solution)/shard_map/ppermute | solution.py:458
  74.7 0.3 collective-permute-done.15
  75.0 0.1 add_convert_fusion.4
  75.1 1.2 %collective-permute-done.16 = bf16[4,96,384]{2,1,0:T(8,128)(2,1)S(1)} collective-permute-done((bf16[4,96,384]{2,1,0:T(8,128)(2,1)S(1)}, bf16[4,96,384]{2,1,0:T(8,128)(2,1)S(1)}, u32[]{:S(2)}, u32[]{:S(2)}) %collective-permute-start.16) | collective-permute-done | bytes 294944 | tf_op jit(solution)/shard_map/ppermute | solution.py:458
  76.3 0.1 pad_maximum_fusion.1.held
  76.4 2.9 %collective-permute-start.20 = (bf16[8,96,384]{2,1,0:T(8,128)(2,1)S(1)}, bf16[8,96,384]{2,1,0:T(8,128)(2,1)S(1)}, u32[]{:S(2)}, u32[]{:S(2)}) collective-permute-start(bf16[8,96,384]{2,1,0:T(8,128)(2,1)S(1)} %pad_maximum_fusion.1.held), channel_id=1, source_target_pairs={{0,2},{1,5},{2,0},{3,7},{4,6},{5,1},{6,4},{7,3},{8,10},{9,13},{10,... | collective-permute-start | bytes 1769480 | tf_op jit(solution)/shard_map/ppermute | solution.py:458
  79.3 0.3 collective-permute-start.17
  79.6 4.1 %collective-permute-start.19 = (bf16[1,112,384]{2,1,0:T(8,128)(2,1)S(1)}, bf16[1,112,384]{2,1,0:T(8,128)(2,1)S(1)}, u32[]{:S(2)}, u32[]{:S(2)}) collective-permute-start(bf16[1,112,384]{2,1,0:T(8,128)(2,1)S(1)} %add_convert_fusion.4), channel_id=1, source_target_pairs={{0,24},{1,25},{2,26},{3,27},{4,28},{5,29},{6,30},{7,31},{8,16},{9,... | collective-permute-start | bytes 258056 | tf_op jit(solution)/shard_map/ppermute | solution.py:458
  83.7 1.5 %collective-permute-done.17 = bf16[1,112,384]{2,1,0:T(8,128)(2,1)S(1)} collective-permute-done((bf16[1,112,384]{2,1,0:T(8,128)(2,1)S(1)}, bf16[1,112,384]{2,1,0:T(8,128)(2,1)S(1)}, u32[]{:S(2)}, u32[]{:S(2)}) %collective-permute-start.17) | collective-permute-done | bytes 86048 | tf_op jit(solution)/shard_map/ppermute | solution.py:458
  85.2 0.4 collective-permute-done.18
  85.6 1.5 %collective-permute-done.19 = bf16[1,112,384]{2,1,0:T(8,128)(2,1)S(1)} collective-permute-done((bf16[1,112,384]{2,1,0:T(8,128)(2,1)S(1)}, bf16[1,112,384]{2,1,0:T(8,128)(2,1)S(1)}, u32[]{:S(2)}, u32[]{:S(2)}) %collective-permute-start.19) | collective-permute-done | bytes 86048 | tf_op jit(solution)/shard_map/ppermute | solution.py:458
  87.1 0.1 pad_maximum_fusion.2
  87.1 0.0 collective-permute-done.20.late
  87.2 0.0 collective-permute-start.22
  87.2 0.4 collective-permute-start.21
  87.6 1.8 %collective-permute-start.24 = (bf16[8,96,384]{2,1,0:T(8,128)(2,1)S(1)}, bf16[8,96,384]{2,1,0:T(8,128)(2,1)S(1)}, u32[]{:S(2)}, u32[]{:S(2)}) collective-permute-start(bf16[8,96,384]{2,1,0:T(8,128)(2,1)S(1)} %pad_maximum_fusion.1.held), channel_id=1, source_target_pairs={{0,1},{1,0},{2,3},{3,2},{4,5},{5,4},{6,7},{7,6},{8,9},{9,8},{10,11... | collective-permute-start | bytes 1769480 | tf_op jit(solution)/shard_map/ppermute | solution.py:458
  89.4 5.1 %collective-permute-done.21 = bf16[4,112,384]{2,1,0:T(8,128)(2,1)S(1)} collective-permute-done((bf16[4,112,384]{2,1,0:T(8,128)(2,1)S(1)}, bf16[4,112,384]{2,1,0:T(8,128)(2,1)S(1)}, u32[]{:S(2)}, u32[]{:S(2)}) %collective-permute-start.21) | collective-permute-done | bytes 344096 | tf_op jit(solution)/shard_map/ppermute | solution.py:458
  94.5 0.1 pad_maximum_fusion.held
  94.6 2.0 %collective-permute-start.23 = (bf16[8,112,384]{2,1,0:T(8,128)(2,1)S(1)}, bf16[8,112,384]{2,1,0:T(8,128)(2,1)S(1)}, u32[]{:S(2)}, u32[]{:S(2)}) collective-permute-start(bf16[8,112,384]{2,1,0:T(8,128)(2,1)S(1)} %pad_maximum_fusion.held), channel_id=1, source_target_pairs={{0,2},{1,5},{2,0},{3,7},{4,6},{5,1},{6,4},{7,3},{8,10},{9,13},{10,... | collective-permute-start | bytes 2064392 | tf_op jit(solution)/shard_map/ppermute | solution.py:458
  96.6 2.8 %unpack_last_layer.1 = (f32[2,384,1536]{2,1,0:T(8,128)}, f32[2,1536,384]{2,1,0:T(8,128)}) custom-call(bf16[8,96,384]{2,1,0:T(8,128)(2,1)S(1)} %pad_maximum_fusion.1.held, bf16[8,96,384]{2,1,0:T(8,128)(2,1)S(1)} %collective-permute-done.20.late, bf16[8,96,384]{2,1,0:T(8,128)(2,1)S(1)} %collective-permute-done.24.other_held, ...), custom_call_target="tpu_custom_call" | custom-call | flops 3000000000 | bytes 9000000 | tf_op jit(solution)/shard_map/unpack_last_layer/pallas_call | solution.py:598
  99.4 6.3 %collective-permute-done.23.late = bf16[8,112,384]{2,1,0:T(8,128)(2,1)S(1)} collective-permute-done((bf16[8,112,384]{2,1,0:T(8,128)(2,1)S(1)}, bf16[8,112,384]{2,1,0:T(8,128)(2,1)S(1)}, u32[]{:S(2)}, u32[]{:S(2)}) %collective-permute-start.23) | collective-permute-done | bytes 688160 | tf_op jit(solution)/shard_map/ppermute | solution.py:458
  105.6 2.1 %collective-permute-done.26.other_late = bf16[8,112,384]{2,1,0:T(8,128)(2,1)S(1)} collective-permute-done((bf16[8,112,384]{2,1,0:T(8,128)(2,1)S(1)}, bf16[8,112,384]{2,1,0:T(8,128)(2,1)S(1)}, u32[]{:S(2)}, u32[]{:S(2)}) %collective-permute-start.26) | collective-permute-done | bytes 688160 | tf_op jit(solution)/shard_map/ppermute | solution.py:458
  107.8 3.6 %unpack_first_layer.1 = (f32[2,384,1536]{2,1,0:T(8,128)}, f32[2,1536,384]{2,1,0:T(8,128)}, f32[196,2,196]{2,1,0:T(2,128)}, f32[2,384]{1,0:T(2,128)}, f32[2,384]{...) custom-call(bf16[8,112,384]{2,1,0:T(8,128)(2,1)S(1)} %pad_maximum_fu, ...), custom_call_target="tpu_custom_call", output_to_operand_aliasing={{0}: (4, {}), {1}: (5, {})} | custom-call | flops 3000000000 | bytes 9000000 | tf_op jit(solution)/shard_map/unpack_first_layer/pallas_call | solution.py:598
  (12 shorter events, 0.1 us)
Async XLA Ops:
  17.2 5.8 %collective-permute-start = (bf16[16,96,384]{2,1,0:T(8,128)(2,1)S(1)}, bf16[16,96,384]{2,1,0:T(8,128)(2,1)S(1)}, u32[]{:S(2)}, u32[]{:S(2)}) collective-permute-start(bf16[16,96,384]{2,1,0:T(8,128)(2,1)S(1)} %get-tuple-element.107), channel_id=1, source_target_pairs={{0,1},{1,0},{2,3},{3,2},{4,5},{5,4},{6,7},{7,6},{8,9},{9,8},{10,11... | collective-permute-start | bytes 3538952 | tf_op jit(solution)/shard_map/ppermute | solution.py:458
  23.1 10.4 %collective-permute-start.1 = (bf16[8,96,384]{2,1,0:T(8,128)(2,1)S(1)}, bf16[8,96,384]{2,1,0:T(8,128)(2,1)S(1)}, u32[]{:S(2)}, u32[]{:S(2)}) collective-permute-start(bf16[8,96,384]{2,1,0:T(8,128)(2,1)S(1)} %add_convert_fusion.1), channel_id=1, source_target_pairs={{0,2},{1,5},{2,0},{3,7},{4,6},{5,1},{6,4},{7,3},{8,10},{9,13},{10,... | collective-permute-start | bytes 1769480 | tf_op jit(solution)/shard_map/ppermute | solution.py:458
  33.6 7.5 %collective-permute-start.2 = (bf16[16,96,384]{2,1,0:T(8,128)(2,1)S(1)}, bf16[16,96,384]{2,1,0:T(8,128)(2,1)S(1)}, u32[]{:S(2)}, u32[]{:S(2)}) collective-permute-start(bf16[16,96,384]{2,1,0:T(8,128)(2,1)S(1)} %get-tuple-element.124), channel_id=1, source_target_pairs={{0,1},{1,0},{2,3},{3,2},{4,5},{5,4},{6,7},{7,6},{8,9},{9,8},{10,11... | collective-permute-start | bytes 3538952 | tf_op jit(solution)/shard_map/ppermute | solution.py:458
  33.8 7.0 %collective-permute-start.3 = (bf16[4,96,384]{2,1,0:T(8,128)(2,1)S(1)}, bf16[4,96,384]{2,1,0:T(8,128)(2,1)S(1)}, u32[]{:S(2)}, u32[]{:S(2)}) collective-permute-start(bf16[4,96,384]{2,1,0:T(8,128)(2,1)S(1)} %add_convert_fusion.3), channel_id=1, source_target_pairs={{0,4},{1,3},{2,6},{3,1},{4,0},{5,7},{6,2},{7,5},{8,12},{9,11},{10,... | collective-permute-start | bytes 884744 | tf_op jit(solution)/shard_map/ppermute | solution.py:458
  40.8 1.4 %collective-permute-start.4 = (bf16[16,16,384]{2,1,0:T(8,128)(2,1)S(1)}, bf16[16,16,384]{2,1,0:T(8,128)(2,1)S(1)}, u32[]{:S(2)}, u32[]{:S(2)}) collective-permute-start(bf16[16,16,384]{2,1,0:T(8,128)(2,1)S(1)} %get-tuple-element.126), channel_id=1, source_target_pairs={{0,1},{1,0},{2,3},{3,2},{4,5},{5,4},{6,7},{7,6},{8,9},{9,8},{10,11... | collective-permute-start | bytes 589832 | tf_op jit(solution)/shard_map/ppermute | solution.py:458
  42.5 11.6 %collective-permute-start.5 = (bf16[8,112,384]{2,1,0:T(8,128)(2,1)S(1)}, bf16[8,112,384]{2,1,0:T(8,128)(2,1)S(1)}, u32[]{:S(2)}, u32[]{:S(2)}) collective-permute-start(bf16[8,112,384]{2,1,0:T(8,128)(2,1)S(1)} %add_convert_fusion), channel_id=1, source_target_pairs={{0,2},{1,5},{2,0},{3,7},{4,6},{5,1},{6,4},{7,3},{8,10},{9,13},{10,... | collective-permute-start | bytes 2064392 | tf_op jit(solution)/shard_map/ppermute | solution.py:458
  44.5 8.1 %collective-permute-start.6 = (bf16[1,96,384]{2,1,0:T(8,128)(2,1)S(1)}, bf16[1,96,384]{2,1,0:T(8,128)(2,1)S(1)}, u32[]{:S(2)}, u32[]{:S(2)}) collective-permute-start(bf16[1,96,384]{2,1,0:T(8,128)(2,1)S(1)} %get-tuple-element.158), channel_id=1, source_target_pairs={{0,16},{1,17},{2,18},{3,19},{4,20},{5,21},{6,22},{7,23},{8,24},{9,... | collective-permute-start | bytes 221192 | tf_op jit(solution)/shard_map/ppermute | solution.py:458
  47.1 6.5 %collective-permute-start.7 = (bf16[1,96,384]{2,1,0:T(8,128)(2,1)S(1)}, bf16[1,96,384]{2,1,0:T(8,128)(2,1)S(1)}, u32[]{:S(2)}, u32[]{:S(2)}) collective-permute-start(bf16[1,96,384]{2,1,0:T(8,128)(2,1)S(1)} %get-tuple-element.160), channel_id=1, source_target_pairs={{0,24},{1,25},{2,26},{3,27},{4,28},{5,29},{6,30},{7,31},{8,16},{9,... | collective-permute-start | bytes 221192 | tf_op jit(solution)/shard_map/ppermute | solution.py:458
  48.5 5.6 %collective-permute-start.8 = (bf16[1,96,384]{2,1,0:T(8,128)(2,1)S(1)}, bf16[1,96,384]{2,1,0:T(8,128)(2,1)S(1)}, u32[]{:S(2)}, u32[]{:S(2)}) collective-permute-start(bf16[1,96,384]{2,1,0:T(8,128)(2,1)S(1)} %get-tuple-element.159), channel_id=1, source_target_pairs={{0,8},{1,9},{2,10},{3,11},{4,12},{5,13},{6,14},{7,15},{8,0},{9,1},... | collective-permute-start | bytes 221192 | tf_op jit(solution)/shard_map/ppermute | solution.py:458
  54.3 11.6 %collective-permute-start.9 = (bf16[4,112,384]{2,1,0:T(8,128)(2,1)S(1)}, bf16[4,112,384]{2,1,0:T(8,128)(2,1)S(1)}, u32[]{:S(2)}, u32[]{:S(2)}) collective-permute-start(bf16[4,112,384]{2,1,0:T(8,128)(2,1)S(1)} %add_convert_fusion.2), channel_id=1, source_target_pairs={{0,4},{1,3},{2,6},{3,1},{4,0},{5,7},{6,2},{7,5},{8,12},{9,11},{10,... | collective-permute-start | bytes 1032200 | tf_op jit(solution)/shard_map/ppermute | solution.py:458
  55.5 7.4 %collective-permute-start.10 = (bf16[1,96,384]{2,1,0:T(8,128)(2,1)S(1)}, bf16[1,96,384]{2,1,0:T(8,128)(2,1)S(1)}, u32[]{:S(2)}, u32[]{:S(2)}) collective-permute-start(bf16[1,96,384]{2,1,0:T(8,128)(2,1)S(1)} %add_convert_fusion.8), channel_id=1, source_target_pairs={{0,16},{1,17},{2,18},{3,19},{4,20},{5,21},{6,22},{7,23},{8,24},{9,... | collective-permute-start | bytes 221192 | tf_op jit(solution)/shard_map/ppermute | solution.py:458
  58.1 5.2 %collective-permute-start.11 = (bf16[1,96,384]{2,1,0:T(8,128)(2,1)S(1)}, bf16[1,96,384]{2,1,0:T(8,128)(2,1)S(1)}, u32[]{:S(2)}, u32[]{:S(2)}) collective-permute-start(bf16[1,96,384]{2,1,0:T(8,128)(2,1)S(1)} %add_convert_fusion.8), channel_id=1, source_target_pairs={{0,8},{1,9},{2,10},{3,11},{4,12},{5,13},{6,14},{7,15},{8,0},{9,1},... | collective-permute-start | bytes 221192 | tf_op jit(solution)/shard_map/ppermute | solution.py:458
  59.7 6.2 %collective-permute-start.12 = (bf16[1,96,384]{2,1,0:T(8,128)(2,1)S(1)}, bf16[1,96,384]{2,1,0:T(8,128)(2,1)S(1)}, u32[]{:S(2)}, u32[]{:S(2)}) collective-permute-start(bf16[1,96,384]{2,1,0:T(8,128)(2,1)S(1)} %add_convert_fusion.8), channel_id=1, source_target_pairs={{0,24},{1,25},{2,26},{3,27},{4,28},{5,29},{6,30},{7,31},{8,16},{9,... | collective-permute-start | bytes 221192 | tf_op jit(solution)/shard_map/ppermute | solution.py:458
  66.0 8.7 %collective-permute-start.13 = (bf16[1,112,384]{2,1,0:T(8,128)(2,1)S(1)}, bf16[1,112,384]{2,1,0:T(8,128)(2,1)S(1)}, u32[]{:S(2)}, u32[]{:S(2)}) collective-permute-start(bf16[1,112,384]{2,1,0:T(8,128)(2,1)S(1)} %get-tuple-element.155), channel_id=1, source_target_pairs={{0,16},{1,17},{2,18},{3,19},{4,20},{5,21},{6,22},{7,23},{8,24},{9,... | collective-permute-start | bytes 258056 | tf_op jit(solution)/shard_map/ppermute | solution.py:458
  68.0 6.7 %collective-permute-start.14 = (bf16[1,112,384]{2,1,0:T(8,128)(2,1)S(1)}, bf16[1,112,384]{2,1,0:T(8,128)(2,1)S(1)}, u32[]{:S(2)}, u32[]{:S(2)}) collective-permute-start(bf16[1,112,384]{2,1,0:T(8,128)(2,1)S(1)} %get-tuple-element.157), channel_id=1, source_target_pairs={{0,24},{1,25},{2,26},{3,27},{4,28},{5,29},{6,30},{7,31},{8,16},{9,... | collective-permute-start | bytes 258056 | tf_op jit(solution)/shard_map/ppermute | solution.py:458
  68.5 6.6 %collective-permute-start.15 = (bf16[1,112,384]{2,1,0:T(8,128)(2,1)S(1)}, bf16[1,112,384]{2,1,0:T(8,128)(2,1)S(1)}, u32[]{:S(2)}, u32[]{:S(2)}) collective-permute-start(bf16[1,112,384]{2,1,0:T(8,128)(2,1)S(1)} %get-tuple-element.156), channel_id=1, source_target_pairs={{0,8},{1,9},{2,10},{3,11},{4,12},{5,13},{6,14},{7,15},{8,0},{9,1},... | collective-permute-start | bytes 258056 | tf_op jit(solution)/shard_map/ppermute | solution.py:458
  69.6 6.7 %collective-permute-start.16 = (bf16[4,96,384]{2,1,0:T(8,128)(2,1)S(1)}, bf16[4,96,384]{2,1,0:T(8,128)(2,1)S(1)}, u32[]{:S(2)}, u32[]{:S(2)}) collective-permute-start(bf16[4,96,384]{2,1,0:T(8,128)(2,1)S(1)} %pad_maximum_fusion.3), channel_id=1, source_target_pairs={{0,4},{1,3},{2,6},{3,1},{4,0},{5,7},{6,2},{7,5},{8,12},{9,11},{10,... | collective-permute-start | bytes 884744 | tf_op jit(solution)/shard_map/ppermute | solution.py:458
  76.4 10.8 %collective-permute-start.20 = (bf16[8,96,384]{2,1,0:T(8,128)(2,1)S(1)}, bf16[8,96,384]{2,1,0:T(8,128)(2,1)S(1)}, u32[]{:S(2)}, u32[]{:S(2)}) collective-permute-start(bf16[8,96,384]{2,1,0:T(8,128)(2,1)S(1)} %pad_maximum_fusion.1.held), channel_id=1, source_target_pairs={{0,2},{1,5},{2,0},{3,7},{4,6},{5,1},{6,4},{7,3},{8,10},{9,13},{10,... | collective-permute-start | bytes 1769480 | tf_op jit(solution)/shard_map/ppermute | solution.py:458
  79.3 5.9 %collective-permute-start.17 = (bf16[1,112,384]{2,1,0:T(8,128)(2,1)S(1)}, bf16[1,112,384]{2,1,0:T(8,128)(2,1)S(1)}, u32[]{:S(2)}, u32[]{:S(2)}) collective-permute-start(bf16[1,112,384]{2,1,0:T(8,128)(2,1)S(1)} %add_convert_fusion.4), channel_id=1, source_target_pairs={{0,16},{1,17},{2,18},{3,19},{4,20},{5,21},{6,22},{7,23},{8,24},{9,... | collective-permute-start | bytes 258056 | tf_op jit(solution)/shard_map/ppermute | solution.py:458
  79.6 5.9 %collective-permute-start.18 = (bf16[1,112,384]{2,1,0:T(8,128)(2,1)S(1)}, bf16[1,112,384]{2,1,0:T(8,128)(2,1)S(1)}, u32[]{:S(2)}, u32[]{:S(2)}) collective-permute-start(bf16[1,112,384]{2,1,0:T(8,128)(2,1)S(1)} %add_convert_fusion.4), channel_id=1, source_target_pairs={{0,8},{1,9},{2,10},{3,11},{4,12},{5,13},{6,14},{7,15},{8,0},{9,1},... | collective-permute-start | bytes 258056 | tf_op jit(solution)/shard_map/ppermute | solution.py:458
  79.6 7.4 %collective-permute-start.19 = (bf16[1,112,384]{2,1,0:T(8,128)(2,1)S(1)}, bf16[1,112,384]{2,1,0:T(8,128)(2,1)S(1)}, u32[]{:S(2)}, u32[]{:S(2)}) collective-permute-start(bf16[1,112,384]{2,1,0:T(8,128)(2,1)S(1)} %add_convert_fusion.4), channel_id=1, source_target_pairs={{0,24},{1,25},{2,26},{3,27},{4,28},{5,29},{6,30},{7,31},{8,16},{9,... | collective-permute-start | bytes 258056 | tf_op jit(solution)/shard_map/ppermute | solution.py:458
  87.2 7.5 %collective-permute-start.22 = (bf16[8,96,384]{2,1,0:T(8,128)(2,1)S(1)}, bf16[8,96,384]{2,1,0:T(8,128)(2,1)S(1)}, u32[]{:S(2)}, u32[]{:S(2)}) collective-permute-start(bf16[8,96,384]{2,1,0:T(8,128)(2,1)S(1)} %collective-permute-done.20.late), channel_id=1, source_target_pairs={{0,1},{1,0},{2,3},{3,2},{4,5},{5,4},{6,7},{7,6},{8,9},{9,8},{10,11... | collective-permute-start | bytes 1769480 | tf_op jit(solution)/shard_map/ppermute | solution.py:458
  87.2 7.3 %collective-permute-start.21 = (bf16[4,112,384]{2,1,0:T(8,128)(2,1)S(1)}, bf16[4,112,384]{2,1,0:T(8,128)(2,1)S(1)}, u32[]{:S(2)}, u32[]{:S(2)}) collective-permute-start(bf16[4,112,384]{2,1,0:T(8,128)(2,1)S(1)} %pad_maximum_fusion.2), channel_id=1, source_target_pairs={{0,4},{1,3},{2,6},{3,1},{4,0},{5,7},{6,2},{7,5},{8,12},{9,11},{10,... | collective-permute-start | bytes 1032200 | tf_op jit(solution)/shard_map/ppermute | solution.py:458
  87.6 9.0 %collective-permute-start.24 = (bf16[8,96,384]{2,1,0:T(8,128)(2,1)S(1)}, bf16[8,96,384]{2,1,0:T(8,128)(2,1)S(1)}, u32[]{:S(2)}, u32[]{:S(2)}) collective-permute-start(bf16[8,96,384]{2,1,0:T(8,128)(2,1)S(1)} %pad_maximum_fusion.1.held), channel_id=1, source_target_pairs={{0,1},{1,0},{2,3},{3,2},{4,5},{5,4},{6,7},{7,6},{8,9},{9,8},{10,11... | collective-permute-start | bytes 1769480 | tf_op jit(solution)/shard_map/ppermute | solution.py:458
  94.6 11.0 %collective-permute-start.23 = (bf16[8,112,384]{2,1,0:T(8,128)(2,1)S(1)}, bf16[8,112,384]{2,1,0:T(8,128)(2,1)S(1)}, u32[]{:S(2)}, u32[]{:S(2)}) collective-permute-start(bf16[8,112,384]{2,1,0:T(8,128)(2,1)S(1)} %pad_maximum_fusion.held), channel_id=1, source_target_pairs={{0,2},{1,5},{2,0},{3,7},{4,6},{5,1},{6,4},{7,3},{8,10},{9,13},{10,... | collective-permute-start | bytes 2064392 | tf_op jit(solution)/shard_map/ppermute | solution.py:458
  96.6 9.0 %collective-permute-start.25 = (bf16[8,112,384]{2,1,0:T(8,128)(2,1)S(1)}, bf16[8,112,384]{2,1,0:T(8,128)(2,1)S(1)}, u32[]{:S(2)}, u32[]{:S(2)}) collective-permute-start(bf16[8,112,384]{2,1,0:T(8,128)(2,1)S(1)} %pad_maximum_fusion.held), channel_id=1, source_target_pairs={{0,1},{1,0},{2,3},{3,2},{4,5},{5,4},{6,7},{7,6},{8,9},{9,8},{10,11... | collective-permute-start | bytes 2064392 | tf_op jit(solution)/shard_map/ppermute | solution.py:458
  105.6 2.1 %collective-permute-start.26 = (bf16[8,112,384]{2,1,0:T(8,128)(2,1)S(1)}, bf16[8,112,384]{2,1,0:T(8,128)(2,1)S(1)}, u32[]{:S(2)}, u32[]{:S(2)}) collective-permute-start(bf16[8,112,384]{2,1,0:T(8,128)(2,1)S(1)} %collective-permute-done.23.late), channel_id=1, source_target_pairs={{0,1},{1,0},{2,3},{3,2},{4,5},{5,4},{6,7},{7,6},{8,9},{9,8},{10,11... | collective-permute-start | bytes 2064392 | tf_op jit(solution)/shard_map/ppermute | solution.py:458

commit v3 on v2

--- a/solution.py
+++ b/solution.py
@@ -135,6 +135,11 @@
 def row_tiles(rows):
     tile = max(t for t in range(16, 209, 16) if rows % t == 0)
     return [slice(at, at + tile) for at in range(0, rows, tile)]
+
+
+def row_halves(rows):
+    middle = -(-rows // 32) * 16
+    return [slice(0, middle), slice(middle, rows)]
 
 
 def cross_setup(mask_ref, weight_ref, bias_ref, kept_ref, keep_ref, bias_columns_ref, rows_ref):
@@ -194,11 +199,9 @@
         low_ref[rows, :] = normed.astype(BF)
         squares += row_sum(normed * normed)
     vectors_ref[layer, SQUARES + 3 : SQUARES + 4, :] = squares
-    step = inner_ref.shape[1] // 2
-
-    @pl.loop(0, 2)
-    def _(part):
-        at = pl.ds(pl.multiple_of(part * step, step), step)
+    step = inner_ref.shape[1] // 3
+    for part in range(3):
+        at = slice(part * step, (part + 1) * step)
         for rows in tiles:
             hidden = dot(low_ref[rows, :], inner_ref[:, at]) + inner_bias_ref[layer : layer + 1, at]
             normal_cdf = 0.5 * (1.0 + lax.erf(hidden * SQRT_HALF))
@@ -221,6 +224,7 @@
     vectors_ref[layer, MIXER_OUT_BIAS : MIXER_OUT_BIAS + 1, :] = bias
     columns = inner_ref.shape[1]
     step = 2 * LANES
+    tiles = row_halves(upper_ref.shape[1])
     for part in range(columns // step):
         at = slice(part * step, (part + 1) * step)
         outer_grad_ref[at, :] = dot(fired_ref[:, at], scaled_ref[...], 0, 0).astype(BF)
@@ -244,7 +248,7 @@
     aff_scale = aff_scale_ref[layer : layer + 1, :]
     scale_grad = jnp.zeros((1, LANES), F32)
     shift_grad = jnp.zeros((1, LANES), F32)
-    for rows in row_tiles(upper_ref.shape[1]):
+    for rows in row_halves(upper_ref.shape[1]):
         normed_grad = dot(hidden_grad_ref[rows, :], inner_ref[...], 1, 1)
         scale_grad += row_sum(normed_grad * read(stream_ref, rows))
         shift_grad += row_sum(normed_grad)
@@ -352,7 +356,7 @@
     mixer_hidden(0, s1, low0, fired0, slope0, vectors, *mixer, inner0, inner_bias)
     copies[3].wait()
     squares = jnp.zeros((1, LANES), F32)
-    for rows in row_tiles(s1.shape[1]):
+    for rows in row_halves(s1.shape[1]):
         result = dot(fired0[rows, :], outer0[...]) + outer_bias[0:1, :]
         result0[rows, :] = result.astype(BF)
         branch = mixer_scale[0:1, :] * result
@@ -373,18 +377,59 @@
 
 
 def second_kernel(
-    s2, s3, g_rows, fired1, hidden_grad, inner1, outer1, kept_weight, keep, bias_columns,
-    vectors_in, cross_aff_scale, cross_aff_shift, cross_scale, mixer_aff_scale, outer_bias,
-    mixer_scale,
-    output, g2, weight_grad, vectors,
-    leaving, g1, padded_low, padded_mixing,
-):
-    _, patches, each, _ = output.shape
+    s2, s3, g_rows, hidden_grad, inner1, kept_weight, keep, bias_columns, vectors_in,
+    cross_aff_scale, cross_aff_shift, cross_scale, mixer_aff_scale,
+    g2, weight_grad, vectors,
+    g1, padded_low, padded_mixing, *, each,
+):
+    patches = s2.shape[1] // padded_low.shape[0]
     vectors[...] = vectors_in[...]
     clear_padding(padded_low, padded_mixing, patches=patches)
+    mixer_input_grad(1, g_rows, s3, hidden_grad, g1, inner1, vectors, mixer_aff_scale)
+    cross_backward(
+        1, s2, g1, g2, weight_grad, vectors, kept_weight, keep, bias_columns,
+        cross_aff_scale, cross_aff_shift, cross_scale, padded_low, padded_mixing, patches, each,
+    )
+
+
+def third_kernel(
+    mesh_shape,
+    s1, g2, low0, fired0, slope0, result0, inner0, outer0, vectors_in, mixer_aff_scale, mixer_scale,
+    kept, sent, g1, vectors,
+    hidden_grad, scaled, inner_grad, outer_grad,
+):
+    vectors[...] = vectors_in[...]
+    hidden_grad[...] = slope0[...]
+    mixer_backward(
+        0, g2, low0, fired0, hidden_grad, scaled, inner0, outer0, inner_grad, outer_grad,
+        vectors, mixer_scale,
+    )
+    pack_products(own_codes(mesh_shape), inner_grad, outer_grad, kept, sent)
+    scale_grad = jnp.zeros((1, LANES), F32)
+    for rows in row_tiles(g2.shape[1]):
+        scale_grad += row_sum(read(g2, rows) * result0[rows, :].astype(F32))
+    vectors[0, MIXER_SCALE : MIXER_SCALE + 1, :] = scale_grad
+    mixer_input_grad(0, g2, s1, hidden_grad, g1, inner0, vectors, mixer_aff_scale)
+
+
+def fourth_kernel(
+    mesh_shape,
+    s0, g1, kept_weight, keep, bias_columns, weight_grad1, vectors_in,
+    s3, g_rows, fired1, outer1,
+    cross_aff_scale, cross_aff_shift, cross_scale, outer_bias, mixer_scale,
+    input_grad, output, kept, sent,
+    g0, leaving, weight_grad0, vectors, small, padded_low, padded_mixing,
+):
+    _, patches, each, _ = input_grad.shape
+    vectors[...] = vectors_in[...]
+    clear_padding(padded_low, padded_mixing, patches=patches)
+    cross_backward(
+        0, s0, g1, g0, weight_grad0, vectors, kept_weight, keep, bias_columns,
+        cross_aff_scale, cross_aff_shift, cross_scale, padded_low, padded_mixing, patches, each,
+    )
     squares = jnp.zeros((1, LANES), F32)
     scale_grad = jnp.zeros((1, LANES), F32)
-    for rows in row_tiles(s3.shape[1]):
+    for rows in row_halves(s3.shape[1]):
         result = dot(fired1[rows, :], outer1[...]) + outer_bias[1:2, :]
         scale_grad += row_sum(read(g_rows, rows) * result)
         branch = mixer_scale[1:2, :] * result
@@ -392,48 +437,6 @@
         squares += row_sum(branch * branch)
     vectors[1, SQUARES + 2 : SQUARES + 3, :] = squares
     vectors[1, MIXER_SCALE : MIXER_SCALE + 1, :] = scale_grad
-    mixer_input_grad(1, g_rows, s3, hidden_grad, g1, inner1, vectors, mixer_aff_scale)
-    gather_rows(leaving, output)
-    cross_backward(
-        1, s2, g1, g2, weight_grad, vectors, kept_weight, keep, bias_columns,
-        cross_aff_scale, cross_aff_shift, cross_scale, padded_low, padded_mixing, patches, each,
-    )
-
-
-def third_kernel(
-    mesh_shape,
-    g2, low0, fired0, slope0, result0, inner0, outer0, vectors_in, mixer_scale,
-    kept, sent, hidden_grad, vectors,
-    scaled, inner_grad, outer_grad,
-):
-    vectors[...] = vectors_in[...]
-    hidden_grad[...] = slope0[...]
-    mixer_backward(
-        0, g2, low0, fired0, hidden_grad, scaled, inner0, outer0, inner_grad, outer_grad,
-        vectors, mixer_scale,
-    )
-    pack_products(own_codes(mesh_shape), inner_grad, outer_grad, kept, sent)
-    scale_grad = jnp.zeros((1, LANES), F32)
-    for rows in row_tiles(g2.shape[1]):
-        scale_grad += row_sum(read(g2, rows) * result0[rows, :].astype(F32))
-    vectors[0, MIXER_SCALE : MIXER_SCALE + 1, :] = scale_grad
-
-
-def fourth_kernel(
-    mesh_shape,
-    s0, s1, g2, hidden_grad, inner0, kept_weight, keep, bias_columns, weight_grad1, vectors_in,
-    cross_aff_scale, cross_aff_shift, cross_scale, mixer_aff_scale,
-    input_grad, kept, sent,
-    g1, g0, weight_grad0, vectors, small, padded_low, padded_mixing,
-):
-    _, patches, each, _ = input_grad.shape
-    vectors[...] = vectors_in[...]
-    clear_padding(padded_low, padded_mixing, patches=patches)
-    mixer_input_grad(0, g2, s1, hidden_grad, g1, inner0, vectors, mixer_aff_scale)
-    cross_backward(
-        0, s0, g1, g0, weight_grad0, vectors, kept_weight, keep, bias_columns,
-        cross_aff_scale, cross_aff_shift, cross_scale, padded_low, padded_mixing, patches, each,
-    )
     layers, padded = kept_weight.shape[0], kept_weight.shape[2]
     groups = padded // VECTOR_ROWS
     small[...] = jnp.zeros_like(small)
@@ -444,6 +447,7 @@
         small[layers * groups + layer] = vectors[layer].astype(BF)
     pack_halves(own_codes(mesh_shape), lambda block: (small[block],), kept, sent)
     gather_rows(g0, input_grad)
+    gather_rows(leaving, output)
 
 
 def exchange_bits(values, mesh_shape, phases):
@@ -466,18 +470,36 @@
     return sum(t[start:stop].astype(F32) for t in terms)
 
 
+def joint_sum(families, start, stop):
+    sums = [part_sum(terms, start, stop).astype(BF) for terms in families]
+    return sums[0] if len(sums) == 1 else jnp.concatenate(sums, axis=1)
+
+
 def halve(terms, width, mesh_shape, phase):
     half = width // 2
     leaving = part_sum(terms, half, width).astype(BF)
     return leaving, terms + [exchange_bits(leaving, mesh_shape, [phase])]
 
 
-def scatter_last(terms, mesh_shape):
+def halve_all(families, width, mesh_shape, phase):
+    half = width // 2
+    arrived = exchange_bits(joint_sum(families, half, width), mesh_shape, [phase])
+    grown, at = [], 0
+    for terms in families:
+        rows = terms[0].shape[1]
+        grown.append(terms + [arrived[:, at : at + rows]])
+        at += rows
+    return arrived, grown
+
+
+def scatter_last(families, mesh_shape):
     arrived = [
-        exchange_bits(part_sum(terms, slot, slot + 1).astype(BF), mesh_shape, across(slot))
-        for slot in (1, 3, 2)
+        exchange_bits(joint_sum(families, slot, slot + 1), mesh_shape, across(slot))
+        for slot in (2, 3, 1)
     ]
-    total = part_sum(terms, 0, 1) + sum(a.astype(F32) for a in arrived)
+    sums = [part_sum(terms, 0, 1) for terms in families]
+    total = sums[0] if len(sums) == 1 else jnp.concatenate(sums, axis=1)
+    total = total + sum(a.astype(F32) for a in arrived)
     for phase in range(SCATTERED, len(phase_bits(mesh_shape)[0])):
         total = total.astype(BF)
         total = total.astype(F32) + exchange_bits(total, mesh_shape, [phase]).astype(F32)
@@ -485,7 +507,7 @@
 
 
 def gather_last(own, mesh_shape):
-    arrived = {slot: exchange_bits(own, mesh_shape, across(slot)) for slot in (1, 3, 2)}
+    arrived = {slot: exchange_bits(own, mesh_shape, across(slot)) for slot in (2, 3, 1)}
     return jnp.concatenate([own, arrived[1], arrived[2], arrived[3]], axis=0)
 
 
@@ -497,81 +519,84 @@
     return lax.optimization_barrier((values, *others))[0]
 
 
-def unpack_block(block, values, images_all, layer, inner_rows, outer_rows, inner_out, outer_out, sems):
-    depth = outer_rows.shape[0] // BLOCKS
-    row_at, column_at = inner_spot(block, depth, inner_rows.shape[1])
-    inner_at = (pl.ds(row_at, depth), pl.ds(column_at, LANES))
-    outer_at = pl.ds(pl.multiple_of(block * depth, depth), depth)
-    copies = (
-        pltpu.make_async_copy(inner_rows.at[inner_at], inner_out.at[(layer,) + inner_at], sems.at[0, block]),
-        pltpu.make_async_copy(outer_rows.at[outer_at], outer_out.at[layer, outer_at], sems.at[1, block]),
-    )
-    if values is not None:
-        inner_rows[inner_at] = values[0:depth, :].astype(F32) / images_all
-        outer_rows[outer_at, :] = values[depth : 2 * depth, :].astype(F32) / images_all
-    return copies
-
-
-def unpack_layer(mesh_shape, images_all, layer, quarters, rows, outs, sems, extra=None):
+def unpack_quarters(mesh_shape, images_all, layer, plan, quarters, inner_out, outer_out, stage, sems):
     codes = own_codes(mesh_shape)
-    quarter = HALF // 2
-    places = []
+    quarter, depth = HALF // 2, stage.shape[2]
+    columns = inner_out.shape[2]
+
+    def copies(number, slot):
+        block_of, base = plan[number]
+        block = block_of(codes, slot + base)
+        row_at, column_at = inner_spot(block, depth, columns)
+        outer_at = pl.multiple_of(block * depth, depth)
+        index = number * quarter + slot
+        return (
+            pltpu.make_async_copy(
+                stage.at[0, index],
+                inner_out.at[layer, pl.ds(row_at, depth), pl.ds(column_at, LANES)],
+                sems.at[0, index],
+            ),
+            pltpu.make_async_copy(
+                stage.at[1, index], outer_out.at[layer, pl.ds(outer_at, depth), :], sems.at[1, index]
+            ),
+        )
+
     for number, values in enumerate(quarters):
-        block_of = kept_block if number < 2 else sent_block
-        places.append((values, block_of, (number % 2) * quarter))
-
-    @pl.loop(0, quarter)
-    def _(slot):
-        for values, block_of, base in places:
-            block = block_of(codes, slot + base)
-            for copy in unpack_block(block, values.at[slot], images_all, layer, *rows, *outs, sems):
+
+        @pl.loop(0, quarter)
+        def _(slot):
+            for kind, copy in enumerate(copies(number, slot)):
+                block = values[slot, kind * depth : (kind + 1) * depth, :]
+                stage[kind, number * quarter + slot] = block.astype(F32) / images_all
                 copy.start()
-            if extra is not None:
-                extra(block, values.at[slot])
-
-    @pl.loop(0, BLOCKS)
-    def _(block):
-        for copy in unpack_block(block, None, images_all, layer, *rows, *outs, sems):
-            copy.wait()
-
-
-def unpack_last_layer(
-    mesh_shape, images_all, held, late, other_held, other_late,
-    inner_out, outer_out, inner_rows, outer_rows, sems,
-):
-    unpack_layer(
-        mesh_shape, images_all, 1, (held, late, other_held, other_late),
-        (inner_rows, outer_rows), (inner_out, outer_out), sems,
-    )
-
-
-def unpack_first_layer(
+
+    for number in range(len(quarters)):
+
+        @pl.loop(0, quarter)
+        def _(slot):
+            for copy in copies(number, slot):
+                copy.wait()
+
+
+QUARTERS = ((kept_block, 0), (kept_block, HALF // 2), (sent_block, 0), (sent_block, HALF // 2))
+
+
+def unpack_first(mesh_shape, images_all, layer, numbers, *refs):
+    quarters, outs = refs[: len(numbers)], refs[len(numbers) :]
+    unpack_quarters(mesh_shape, images_all, layer, [QUARTERS[n] for n in numbers], quarters, *outs)
+
+
+def unpack_more(mesh_shape, images_all, layer, numbers, *refs):
+    quarters, outs = refs[: len(numbers)], refs[len(numbers) + 2 :]
+    unpack_quarters(mesh_shape, images_all, layer, [QUARTERS[n] for n in numbers], quarters, *outs)
+
+
+def unpack_rest(
     mesh_shape, images_all, held, late, other_held, other_late, inner_in, outer_in,
     inner_out, outer_out, weight_out, aff_scale_out, aff_shift_out, cross_bias_out,
     cross_scale_out, mixer_aff_scale_out, mixer_aff_shift_out, inner_bias_out, outer_bias_out,
     mixer_scale_out, magnitudes_out,
-    inner_rows, outer_rows, weight_rows, vectors, sems,
+    stage, weight_rows, vectors, sems,
 ):
     patches, layers, _ = weight_out.shape
-    depth = outer_rows.shape[0] // BLOCKS
     groups = weight_rows.shape[1] // VECTOR_ROWS
-
-    def extra(block, values):
-        small = values[2 * depth :, :].astype(F32) / images_all
-
-        @pl.when(block < layers * groups)
-        def _():
-            at = pl.multiple_of((block % groups) * VECTOR_ROWS, VECTOR_ROWS)
-            weight_rows[block // groups, pl.ds(at, VECTOR_ROWS), :] = small
-
-        @pl.when((block >= layers * groups) & (block < layers * (groups + 1)))
-        def _():
-            vectors[block - layers * groups] = small
-
-    unpack_layer(
-        mesh_shape, images_all, 0, (held, late, other_held, other_late),
-        (inner_rows, outer_rows), (inner_out, outer_out), sems, extra,
-    )
+    codes = own_codes(mesh_shape)
+    for values, (block_of, base) in zip((held, late, other_held, other_late), QUARTERS):
+
+        @pl.loop(0, HALF // 2)
+        def _(slot):
+            block = block_of(codes, slot + base)
+            small = values[slot, 2 * stage.shape[2] :, :].astype(F32) / images_all
+
+            @pl.when(block < layers * groups)
+            def _():
+                at = pl.multiple_of((block % groups) * VECTOR_ROWS, VECTOR_ROWS)
+                weight_rows[block // groups, pl.ds(at, VECTOR_ROWS), :] = small
+
+            @pl.when((block >= layers * groups) & (block < layers * (groups + 1)))
+            def _():
+                vectors[block - layers * groups] = small
+
     for layer in range(layers):
         row = slice(layer, layer + 1)
         weight_out[:, layer, :] = weight_rows[layer, 0:patches, 0:patches]
@@ -592,6 +617,9 @@
             for which in range(2):
                 at = 2 * kind + which
                 magnitudes_out[layer, kind : kind + 1, which : which + 1] = means[at : at + 1]
+    unpack_quarters(
+        mesh_shape, images_all, 0, [QUARTERS[3]], (other_late,), inner_out, outer_out, stage, sems
+    )
 
 
 def call(kernel, name, args, outs, scratch, in_specs=None, out_specs=None, aliases=None, us=1):
@@ -712,46 +740,50 @@
         kept1, sent1, sums, s0, s1, s2, s3, upper, low0, fired0, slope0, result0, fired1,
         hidden_grad1, inner0, outer0, inner1, outer1, kept_weight, keep, bias_columns,
     ) = first[6:]
-    output, g2, weight_grad1, sums = call(
-        second_kernel,
-        "middle",
+    g2, weight_grad1, sums = call(
+        functools.partial(second_kernel, each=each),
+        "last_layer",
         (
             *in_vmem((
-                s2, s3, upper, fired1, hidden_grad1, inner1, outer1, kept_weight, keep,
-                bias_columns, sums,
-            )),
-            aff_scale, aff_shift, scale, mixer_aff, result_bias, result_scale,
-        ),
-        (hbm(*local, dtype=BF), stream, vmem(padded, padded, dtype=F32), vectors),
-        [stream, stream, padded_images, padded_images],
-        us=5,
-    )
-    terms1 = [kept1, exchange_bits(sent1, mesh_shape, [0])]
-    leaving1, terms1 = halve(terms1, HALF, mesh_shape, 1)
-    g2, _ = lax.optimization_barrier((g2, leaving1))
-    halves = vmem(HALF, 2 * depth, LANES)
-    kept0, sent0, hidden_grad0, sums = call(
-        functools.partial(third_kernel, mesh_shape),
-        "first_layer_weights",
-        (*in_vmem((g2, low0, fired0, slope0, result0, inner0, outer0, sums)), result_scale),
-        (halves, halves, hidden, vectors),
-        [vmem(rows, width), inner, outer],
-        us=7,
-    )
-    sent0, sums, _ = lax.optimization_barrier((sent0, sums, terms1[-1]))
-    arrived0 = exchange_bits(sent0, mesh_shape, [0])
-    halves = vmem(HALF, VECTOR_ROWS, LANES)
-    input_grad, kept_small, sent_small = call(
-        functools.partial(fourth_kernel, mesh_shape),
-        "first_layer_input",
-        (
-            *in_vmem((
-                s0, s1, g2, hidden_grad0, inner0, kept_weight, keep, bias_columns, weight_grad1,
-                sums,
+                s2, s3, upper, hidden_grad1, inner1, kept_weight, keep, bias_columns, sums,
             )),
             aff_scale, aff_shift, scale, mixer_aff,
         ),
-        (hbm(*local, dtype=BF), halves, halves),
+        (stream, vmem(padded, padded, dtype=F32), vectors),
+        [stream, padded_images, padded_images],
+        us=4,
+    )
+    main1 = [kept1, exchange_bits(sent1, mesh_shape, [0])]
+    leaving1, main1 = halve(main1, HALF, mesh_shape, 1)
+    g2 = after(g2, leaving1)
+    halves = vmem(HALF, 2 * depth, LANES)
+    kept0, sent0, g1, sums = call(
+        functools.partial(third_kernel, mesh_shape),
+        "first_feed_forward",
+        (
+            *in_vmem((s1, g2, low0, fired0, slope0, result0, inner0, outer0, sums)),
+            mixer_aff, result_scale,
+        ),
+        (halves, halves, stream, vectors),
+        [hidden, vmem(rows, width), inner, outer],
+        us=9,
+    )
+    sent0, sums = lax.optimization_barrier((sent0, sums, main1[-1]))[:2]
+    main0 = [kept0, exchange_bits(sent0, mesh_shape, [0])]
+    leaving1, main1 = halve(main1, HALF // 2, mesh_shape, 2)
+    sums = after(sums, leaving1)
+    halves = vmem(HALF, VECTOR_ROWS, LANES)
+    input_grad, output, kept_small, sent_small = call(
+        functools.partial(fourth_kernel, mesh_shape),
+        "first_cross",
+        (
+            *in_vmem((
+                s0, g1, kept_weight, keep, bias_columns, weight_grad1, sums, s3, upper, fired1,
+                outer1,
+            )),
+            aff_scale, aff_shift, scale, result_bias, result_scale,
+        ),
+        (hbm(*local, dtype=BF), hbm(*local, dtype=BF), halves, halves),
         [
             stream,
             stream,
@@ -763,19 +795,17 @@
         ],
         us=5,
     )
-    _, terms1 = halve(terms1, HALF // 2, mesh_shape, 2)
-    sent_small = after(sent_small, terms1[-1])
-    arrived_small = exchange_bits(sent_small, mesh_shape, [0])
-    terms0 = [
-        jnp.concatenate([kept0, kept_small], axis=1),
-        jnp.concatenate([arrived0, arrived_small], axis=1),
-    ]
-    _, terms0 = halve(terms0, HALF, mesh_shape, 1)
-    own1 = scatter_last(terms1, mesh_shape)
-    terms0[-1], own1 = lax.optimization_barrier((terms0[-1], own1))
-    _, terms0 = halve(terms0, HALF // 2, mesh_shape, 2)
+    sent_small = after(sent_small, main1[-1])
+    small = [kept_small, exchange_bits(sent_small, mesh_shape, [0])]
+    _, main0 = halve(main0, HALF, mesh_shape, 1)
+    _, small = halve(small, HALF, mesh_shape, 1)
+    own1 = scatter_last([main1], mesh_shape)
+    main0[-1], small[-1], own1 = lax.optimization_barrier((main0[-1], small[-1], own1))
+    width0 = HALF // 2
+    terms0 = [[t[:width0] for t in main0], [t[:width0] for t in small]]
+    _, terms0 = halve_all(terms0, width0, mesh_shape, 2)
     four1 = gather_last(own1, mesh_shape)
-    terms0[-1], four1 = lax.optimization_barrier((terms0[-1], four1))
+    terms0, four1 = lax.optimization_barrier((terms0, four1))
     own0 = scatter_last(terms0, mesh_shape)
     held1 = double(four1, mesh_shape, 2)
     own0, held1 = lax.optimization_barrier((own0, held1))
@@ -790,41 +820,67 @@
     other_held0 = exchange_bits(held0, mesh_shape, [0])
     quarters1 = (held1, late1, other_held1, other_late1)
     inner_out, outer_out = hbm(layers, width, columns), hbm(layers, columns, width)
-    unpacked = [
-        vmem(width, columns, dtype=F32),
-        vmem(columns, width, dtype=F32),
-    ]
-    sems = pltpu.SemaphoreType.DMA((2, BLOCKS))
+    quarter = HALF // 2
+
+    def staging(quarters):
+        return [
+            vmem(2, quarters * quarter, depth, LANES, dtype=F32),
+            pltpu.SemaphoreType.DMA((2, quarters * quarter)),
+        ]
+
     grads = call(
-        functools.partial(unpack_last_layer, mesh_shape, images_all),
+        functools.partial(unpack_first, mesh_shape, images_all, 1, (0, 1, 2, 3)),
         "unpack_last_layer",
         in_vmem(quarters1),
         (inner_out, outer_out),
-        unpacked + [sems],
+        staging(4),
         out_specs=[HBM] * 2,
         us=3,
     )
+    grads = call(
+        functools.partial(unpack_more, mesh_shape, images_all, 0, (0, 2)),
+        "unpack_held",
+        (*in_vmem((held0, other_held0)), *grads),
+        (inner_out, outer_out),
+        staging(2),
+        in_specs=[VMEM] * 2 + [HBM] * 2,
+        out_specs=[HBM] * 2,
+        aliases={2: 0, 3: 1},
+        us=2,
+    )
     late0, grads = lax.optimization_barrier((late0, grads))
-    quarters0 = (held0, late0, other_held0, exchange_bits(late0, mesh_shape, [0]))
+    other_late0 = exchange_bits(late0, mesh_shape, [0])
+    grads = call(
+        functools.partial(unpack_more, mesh_shape, images_all, 0, (1,)),
+        "unpack_late",
+        (*in_vmem((late0,)), *grads),
+        (inner_out, outer_out),
+        staging(1),
+        in_specs=[VMEM] + [HBM] * 2,
+        out_specs=[HBM] * 2,
+        aliases={1: 0, 2: 1},
+        us=1,
+    )
     row = hbm(layers, width)
+    stage, sems = staging(1)
     (
         inner_grad, outer_grad, weight_grad, aff_scale_grad, aff_shift_grad, bias_grad,
         scale_grad, mixer_aff_scale_grad, mixer_aff_shift_grad, inner_bias_grad,
         outer_bias_grad, mixer_scale_grad, magnitudes,
     ) = call(
-        functools.partial(unpack_first_layer, mesh_shape, images_all),
-        "unpack_first_layer",
-        (*in_vmem(quarters0), *grads),
+        functools.partial(unpack_rest, mesh_shape, images_all),
+        "unpack_rest",
+        (*in_vmem((held0, late0, other_held0, other_late0)), *grads),
         (
             inner_out, outer_out, hbm(patches, layers, patches), row, row,
             hbm(layers, patches), row, row, row, hbm(layers, columns), row, row,
             hbm(layers, 2, 2),
         ),
-        unpacked + [vmem(layers, padded, LANES, dtype=F32), vectors, sems],
+        [stage, vmem(layers, padded, LANES, dtype=F32), vectors, sems],
         in_specs=[VMEM] * 4 + [HBM] * 2,
         out_specs=[HBM] * 2 + [VMEM] * 11,
         aliases={4: 0, 5: 1},
-        us=3,
+        us=2,
     )
     return (
         jnp.transpose(output, (0, 2, 1, 3)),

time: 112 us -> 105 us (0.938)
  Pallas kernels: 39.7 us -> 37.2 us
  waiting for transfers between devices: 36.7 us -> 34.4 us
  starting transfers between devices: 32.7 us -> 31 us
    pallas_call x6 -> x8, Pallas kernels: 39.7 us -> 37.2 us  [call(): pl.pallas_call(kernel, out_shape=outs, in_specs=[VMEM] * len(args) if in_...]
    ppermute x27 -> x28, waiting for transfers between devices: 36.7 us -> 34.4 us  [exchange_bits(): return lax.ppermute(values, AXES, [(i, partner(i)) for i in places])]
    ppermute x27 -> x28, starting transfers between devices: 32.7 us -> 31 us  [exchange_bits(): return lax.ppermute(values, AXES, [(i, partner(i)) for i in places])]
  transfers between devices with their start and end apart: 27 -> 28, of which waited for: 17 -> 18; matrix products, arithmetic and copies ran while one was open for 1% -> 1% of each run, Pallas kernels for 17% -> 18%
where the time goes in v3:
time: 105 us
  Pallas kernels  37.2 us (35%)
  waiting for transfers between devices  34.4 us (33%)
  starting transfers between devices  31 us (30%)
  other arithmetic  1.32 us (1%)
  between operations  1.14 us (1%)
    pallas_call x8, Pallas kernels, call(): pl.pallas_call(kernel, out_shape=outs, in_specs=[VMEM] * len(args) if in_...  37.2 us
    ppermute x28, waiting for transfers between devices, exchange_bits(): return lax.ppermute(values, AXES, [(i, partner(i)) for i in places])  34.4 us
    ppermute x28, starting transfers between devices, exchange_bits(): return lax.ppermute(values, AXES, [(i, partner(i)) for i in places])  31 us
  transfers between devices with their start and end apart: 28, of which 18 were waited for; matrix products, arithmetic and copies ran while one was open for 1% of the time, Pallas kernels for 18%

profile of v3, /device:TPU:0, one launch (start us, length us, event | category | flops | bytes accessed | tf_op | source)
XLA Modules:
  0.0 105.3 jit_solution(1148150955950913596)
XLA Ops:
  0.7 15.4 %forward.1 = (f32[2,384]{1,0:T(2,128)S(1)}, f32[2,384]{1,0:T(2,128)S(1)}, f32[2,384]{1,0:T(2,128)S(1)}, f32[2,384]{1,0:T(2,128)S(1)}, f32[2,384]{1,0:T(2,128)S(1...) custom-call(bf16[4,196,4,384]{3,2,1,0:T(4,128)(2,1)} %bitcast.6, ...), custom_call_target="tpu_custom_call" | custom-call | flops 17999998976 | bytes 54000000 | tf_op jit(solution)/shard_map/forward/pallas_call | solution.py:626
  16.1 0.5 collective-permute-start
  16.6 2.6 %last_layer.1 = (f32[3,784,128]{2,1,0:T(8,128)S(1)}, f32[208,208]{1,0:T(8,128)S(1)}, f32[2,16,384]{2,1,0:T(8,128)S(1)}) custom-call(f32[3,784,128]{2,1,0:T(8,128)S(1)} %get-tuple-element.100.s2, f32[3,784,128]{2,1,0:T(8,128)S(1)} %get-tuple-element.101.s3, f32[3,784,128]{2,1,0:T(8,128)S(1)} %get-tuple-element.102.g_rows, ...), custom_call_target="tpu_custom_call" | custom-call | flops 4000000000 | bytes 12000000 | tf_op jit(solution)/shard_map/last_layer/pallas_call | solution.py:626
  19.2 0.1 add_convert_fusion.1
  19.4 2.8 %collective-permute-start.1 = (bf16[8,96,384]{2,1,0:T(8,128)(2,1)S(1)}, bf16[8,96,384]{2,1,0:T(8,128)(2,1)S(1)}, u32[]{:S(2)}, u32[]{:S(2)}) collective-permute-start(bf16[8,96,384]{2,1,0:T(8,128)(2,1)S(1)} %add_convert_fusion.1), channel_id=1, source_target_pairs={{0,2},{1,5},{2,0},{3,7},{4,6},{5,1},{6,4},{7,3},{8,10},{9,13},{10,... | collective-permute-start | bytes 1769480 | tf_op jit(solution)/shard_map/ppermute | solution.py:462
  22.1 6.5 %first_feed_forward.1 = (bf16[16,96,384]{2,1,0:T(8,128)(2,1)S(1)}, bf16[16,96,384]{2,1,0:T(8,128)(2,1)S(1)}, f32[3,784,128]{2,1,0:T(8,128)S(1)}, f32[2,16,384]{2,1,0:T(8,128)S(1)}) custom-call(f32[3,784,128]{2,1,0:T(8,128)S(1)} %get-tuple-element.99.s1, f32[3,784,128]{2,1,0:T(8,128)S(1)} %get-tuple-element.116.g2, ...), custom_call_target="tpu_custom_call" | custom-call | flops 8999999488 | bytes 27000000 | tf_op jit(solution)/shard_map/first_feed_forward/pallas_call | solution.py:626
  28.7 1.3 %collective-permute-done.1 = bf16[8,96,384]{2,1,0:T(8,128)(2,1)S(1)} collective-permute-done((bf16[8,96,384]{2,1,0:T(8,128)(2,1)S(1)}, bf16[8,96,384]{2,1,0:T(8,128)(2,1)S(1)}, u32[]{:S(2)}, u32[]{:S(2)}) %collective-permute-start.1) | collective-permute-done | bytes 589856 | tf_op jit(solution)/shard_map/ppermute | solution.py:462
  30.0 0.0 collective-permute-start.2
  30.0 0.1 add_convert_fusion.3
  30.1 2.1 %collective-permute-start.4 = (bf16[4,96,384]{2,1,0:T(8,128)(2,1)S(1)}, bf16[4,96,384]{2,1,0:T(8,128)(2,1)S(1)}, u32[]{:S(2)}, u32[]{:S(2)}) collective-permute-start(bf16[4,96,384]{2,1,0:T(8,128)(2,1)S(1)} %add_convert_fusion.3), channel_id=1, source_target_pairs={{0,4},{1,3},{2,6},{3,1},{4,0},{5,7},{6,2},{7,5},{8,12},{9,11},{10,... | collective-permute-start | bytes 884744 | tf_op jit(solution)/shard_map/ppermute | solution.py:462
  32.2 4.2 %first_cross.1 = (bf16[1,196,4,384]{3,2,1,0:T(4,128)(2,1)}, bf16[1,196,4,384]{3,2,1,0:T(4,128)(2,1)}, bf16[16,16,384]{2,1,0:T(8,128)(2,1)S(1)}, bf16[16,16,384]{2,1,0:T(8,128)(2,1)S(1)}) custom-call(f32[3,784,128]{2,1,0:T(8,128)S(1)} %get-tuple-element.98.s0, f32[3,784,128]{2,1,0:T(8,128)S(1)} %get-tuple-element.125.g1, ...), custom_call_target="tpu_custom_call" | custom-call | flops 5000000000 | bytes 15000000 | tf_op jit(solution)/shard_map/first_cross/pallas_call | solution.py:626
  36.5 0.5 collective-permute-done.4
  37.0 0.0 collective-permute-start.5
  37.0 0.0 collective-permute-done.2
  37.0 0.1 add_convert_fusion
  37.1 2.1 %collective-permute-start.3 = (bf16[8,96,384]{2,1,0:T(8,128)(2,1)S(1)}, bf16[8,96,384]{2,1,0:T(8,128)(2,1)S(1)}, u32[]{:S(2)}, u32[]{:S(2)}) collective-permute-start(bf16[8,96,384]{2,1,0:T(8,128)(2,1)S(1)} %add_convert_fusion), channel_id=1, source_target_pairs={{0,2},{1,5},{2,0},{3,7},{4,6},{5,1},{6,4},{7,3},{8,10},{9,13},{10,... | collective-permute-start | bytes 1769480 | tf_op jit(solution)/shard_map/ppermute | solution.py:462
  39.2 0.1 add_convert_fusion.11
  39.3 2.7 %collective-permute-start.9 = (bf16[1,96,384]{2,1,0:T(8,128)(2,1)S(1)}, bf16[1,96,384]{2,1,0:T(8,128)(2,1)S(1)}, u32[]{:S(2)}, u32[]{:S(2)}) collective-permute-start(bf16[1,96,384]{2,1,0:T(8,128)(2,1)S(1)} %get-tuple-element.182), channel_id=1, source_target_pairs={{0,16},{1,17},{2,18},{3,19},{4,20},{5,21},{6,22},{7,23},{8,24},{9,... | collective-permute-start | bytes 221192 | tf_op jit(solution)/shard_map/ppermute | solution.py:462
  41.9 1.3 %collective-permute-start.8 = (bf16[1,96,384]{2,1,0:T(8,128)(2,1)S(1)}, bf16[1,96,384]{2,1,0:T(8,128)(2,1)S(1)}, u32[]{:S(2)}, u32[]{:S(2)}) collective-permute-start(bf16[1,96,384]{2,1,0:T(8,128)(2,1)S(1)} %get-tuple-element.183), channel_id=1, source_target_pairs={{0,24},{1,25},{2,26},{3,27},{4,28},{5,29},{6,30},{7,31},{8,16},{9,... | collective-permute-start | bytes 221192 | tf_op jit(solution)/shard_map/ppermute | solution.py:462
  43.3 0.2 collective-permute-start.7
  43.5 0.0 collective-permute-done.5
  43.6 0.6 collective-permute-start.6
  44.2 3.6 %collective-permute-done.9 = bf16[1,96,384]{2,1,0:T(8,128)(2,1)S(1)} collective-permute-done((bf16[1,96,384]{2,1,0:T(8,128)(2,1)S(1)}, bf16[1,96,384]{2,1,0:T(8,128)(2,1)S(1)}, u32[]{:S(2)}, u32[]{:S(2)}) %collective-permute-start.9) | collective-permute-done | bytes 73760 | tf_op jit(solution)/shard_map/ppermute | solution.py:462
  47.7 1.0 collective-permute-done.8
  48.7 0.5 collective-permute-done.7
  49.2 0.1 add_convert_fusion.8
  49.3 0.1 add_convert_fusion.2
  49.5 0.9 collective-permute-start.10
  50.4 3.6 %collective-permute-start.13 = (bf16[1,96,384]{2,1,0:T(8,128)(2,1)S(1)}, bf16[1,96,384]{2,1,0:T(8,128)(2,1)S(1)}, u32[]{:S(2)}, u32[]{:S(2)}) collective-permute-start(bf16[1,96,384]{2,1,0:T(8,128)(2,1)S(1)} %add_convert_fusion.8), channel_id=1, source_target_pairs={{0,24},{1,25},{2,26},{3,27},{4,28},{5,29},{6,30},{7,31},{8,16},{9,... | collective-permute-start | bytes 221192 | tf_op jit(solution)/shard_map/ppermute | solution.py:462
  54.0 0.8 collective-permute-start.11
  54.8 0.1 slice.216
  54.9 0.0 slice-start.1
  54.9 0.0 slice-start
  54.9 2.5 %collective-permute-done.13 = bf16[1,96,384]{2,1,0:T(8,128)(2,1)S(1)} collective-permute-done((bf16[1,96,384]{2,1,0:T(8,128)(2,1)S(1)}, bf16[1,96,384]{2,1,0:T(8,128)(2,1)S(1)}, u32[]{:S(2)}, u32[]{:S(2)}) %collective-permute-start.13) | collective-permute-done | bytes 73760 | tf_op jit(solution)/shard_map/ppermute | solution.py:462
  57.4 1.9 %collective-permute-done.12 = bf16[1,96,384]{2,1,0:T(8,128)(2,1)S(1)} collective-permute-done((bf16[1,96,384]{2,1,0:T(8,128)(2,1)S(1)}, bf16[1,96,384]{2,1,0:T(8,128)(2,1)S(1)}, u32[]{:S(2)}, u32[]{:S(2)}) %collective-permute-start.12) | collective-permute-done | bytes 73760 | tf_op jit(solution)/shard_map/ppermute | solution.py:462
  59.3 1.5 %collective-permute-done.11 = bf16[1,96,384]{2,1,0:T(8,128)(2,1)S(1)} collective-permute-done((bf16[1,96,384]{2,1,0:T(8,128)(2,1)S(1)}, bf16[1,96,384]{2,1,0:T(8,128)(2,1)S(1)}, u32[]{:S(2)}, u32[]{:S(2)}) %collective-permute-start.11) | collective-permute-done | bytes 73760 | tf_op jit(solution)/shard_map/ppermute | solution.py:462
  61.0 0.1 add_convert_fusion.7
  61.2 1.5 %collective-permute-start.16 = (bf16[1,112,384]{2,1,0:T(8,128)(2,1)S(1)}, bf16[1,112,384]{2,1,0:T(8,128)(2,1)S(1)}, u32[]{:S(2)}, u32[]{:S(2)}) collective-permute-start(bf16[1,112,384]{2,1,0:T(8,128)(2,1)S(1)} %pad_maximum_fusion.7), channel_id=1, source_target_pairs={{0,16},{1,17},{2,18},{3,19},{4,20},{5,21},{6,22},{7,23},{8,24},{9,... | collective-permute-start | bytes 258056 | tf_op jit(solution)/shard_map/ppermute | solution.py:462
  62.7 1.5 %collective-permute-start.15 = (bf16[1,112,384]{2,1,0:T(8,128)(2,1)S(1)}, bf16[1,112,384]{2,1,0:T(8,128)(2,1)S(1)}, u32[]{:S(2)}, u32[]{:S(2)}) collective-permute-start(bf16[1,112,384]{2,1,0:T(8,128)(2,1)S(1)} %pad_maximum_fusion.6), channel_id=1, source_target_pairs={{0,24},{1,25},{2,26},{3,27},{4,28},{5,29},{6,30},{7,31},{8,16},{9,... | collective-permute-start | bytes 258056 | tf_op jit(solution)/shard_map/ppermute | solution.py:462
  64.2 0.6 collective-permute-start.14
  64.9 0.7 collective-permute-start.17
  65.6 4.1 %collective-permute-done.16 = bf16[1,112,384]{2,1,0:T(8,128)(2,1)S(1)} collective-permute-done((bf16[1,112,384]{2,1,0:T(8,128)(2,1)S(1)}, bf16[1,112,384]{2,1,0:T(8,128)(2,1)S(1)}, u32[]{:S(2)}, u32[]{:S(2)}) %collective-permute-start.16) | collective-permute-done | bytes 86048 | tf_op jit(solution)/shard_map/ppermute | solution.py:462
  69.7 0.8 collective-permute-done.14
  70.5 1.1 %collective-permute-done.17 = bf16[4,96,384]{2,1,0:T(8,128)(2,1)S(1)} collective-permute-done((bf16[4,96,384]{2,1,0:T(8,128)(2,1)S(1)}, bf16[4,96,384]{2,1,0:T(8,128)(2,1)S(1)}, u32[]{:S(2)}, u32[]{:S(2)}) %collective-permute-start.17) | collective-permute-done | bytes 294944 | tf_op jit(solution)/shard_map/ppermute | solution.py:462
  71.6 0.1 pad_maximum_fusion.1.refs_0_
  71.7 1.3 %collective-permute-start.21 = (bf16[8,96,384]{2,1,0:T(8,128)(2,1)S(1)}, bf16[8,96,384]{2,1,0:T(8,128)(2,1)S(1)}, u32[]{:S(2)}, u32[]{:S(2)}) collective-permute-start(bf16[8,96,384]{2,1,0:T(8,128)(2,1)S(1)} %pad_maximum_fusion.1.refs_0_), channel_id=1, source_target_pairs={{0,2},{1,5},{2,0},{3,7},{4,6},{5,1},{6,4},{7,3},{8,10},{9,13},{10,... | collective-permute-start | bytes 1769480 | tf_op jit(solution)/shard_map/ppermute | solution.py:462
  73.0 2.6 %collective-permute-start.20 = (bf16[1,112,384]{2,1,0:T(8,128)(2,1)S(1)}, bf16[1,112,384]{2,1,0:T(8,128)(2,1)S(1)}, u32[]{:S(2)}, u32[]{:S(2)}) collective-permute-start(bf16[1,112,384]{2,1,0:T(8,128)(2,1)S(1)} %fusion), channel_id=1, source_target_pairs={{0,24},{1,25},{2,26},{3,27},{4,28},{5,29},{6,30},{7,31},{8,16},{9,... | collective-permute-start | bytes 258056 | tf_op jit(solution)/shard_map/ppermute | solution.py:462
  75.6 1.8 %collective-permute-start.18 = (bf16[1,112,384]{2,1,0:T(8,128)(2,1)S(1)}, bf16[1,112,384]{2,1,0:T(8,128)(2,1)S(1)}, u32[]{:S(2)}, u32[]{:S(2)}) collective-permute-start(bf16[1,112,384]{2,1,0:T(8,128)(2,1)S(1)} %fusion), channel_id=1, source_target_pairs={{0,16},{1,17},{2,18},{3,19},{4,20},{5,21},{6,22},{7,23},{8,24},{9,... | collective-permute-start | bytes 258056 | tf_op jit(solution)/shard_map/ppermute | solution.py:462
  77.4 2.1 %collective-permute-done.20 = bf16[1,112,384]{2,1,0:T(8,128)(2,1)S(1)} collective-permute-done((bf16[1,112,384]{2,1,0:T(8,128)(2,1)S(1)}, bf16[1,112,384]{2,1,0:T(8,128)(2,1)S(1)}, u32[]{:S(2)}, u32[]{:S(2)}) %collective-permute-start.20) | collective-permute-done | bytes 86048 | tf_op jit(solution)/shard_map/ppermute | solution.py:462
  79.5 0.9 collective-permute-done.19
  80.4 0.9 collective-permute-done.18
  81.3 0.1 pad_maximum_fusion.3
  81.3 0.3 collective-permute-done.21.refs_1_
  81.6 2.0 %collective-permute-start.22 = (bf16[4,112,384]{2,1,0:T(8,128)(2,1)S(1)}, bf16[4,112,384]{2,1,0:T(8,128)(2,1)S(1)}, u32[]{:S(2)}, u32[]{:S(2)}) collective-permute-start(bf16[4,112,384]{2,1,0:T(8,128)(2,1)S(1)} %pad_maximum_fusion.3), channel_id=1, source_target_pairs={{0,4},{1,3},{2,6},{3,1},{4,0},{5,7},{6,2},{7,5},{8,12},{9,11},{10,... | collective-permute-start | bytes 1032200 | tf_op jit(solution)/shard_map/ppermute | solution.py:462
  83.6 5.3 %collective-permute-done.22 = bf16[4,112,384]{2,1,0:T(8,128)(2,1)S(1)} collective-permute-done((bf16[4,112,384]{2,1,0:T(8,128)(2,1)S(1)}, bf16[4,112,384]{2,1,0:T(8,128)(2,1)S(1)}, u32[]{:S(2)}, u32[]{:S(2)}) %collective-permute-start.22) | collective-permute-done | bytes 344096 | tf_op jit(solution)/shard_map/ppermute | solution.py:462
  88.9 0.1 pad_maximum_fusion.refs_0_.held
  89.0 0.1 collective-permute-start.25
  89.1 1.3 %collective-permute-start.24 = (bf16[8,112,384]{2,1,0:T(8,128)(2,1)S(1)}, bf16[8,112,384]{2,1,0:T(8,128)(2,1)S(1)}, u32[]{:S(2)}, u32[]{:S(2)}) collective-permute-start(bf16[8,112,384]{2,1,0:T(8,128)(2,1)S(1)} %pad_maximum_fusion.refs_0_.held), channel_id=1, source_target_pairs={{0,2},{1,5},{2,0},{3,7},{4,6},{5,1},{6,4},{7,3},{8,10},{9,13},{10,... | collective-permute-start | bytes 2064392 | tf_op jit(solution)/shard_map/ppermute | solution.py:462
  90.4 2.7 %unpack_last_layer.1 = (f32[2,384,1536]{2,1,0:T(8,128)}, f32[2,1536,384]{2,1,0:T(8,128)}) custom-call(bf16[8,96,384]{2,1,0:T(8,128)(2,1)S(1)} %pad_maximum_fusion.1.refs_0_, bf16[8,96,384]{2,1,0:T(8,128)(2,1)S(1)} %collective-permute-done.21.refs_1_, bf16[8,96,384]{2,1,0:T(8,128)(2,1)S(1)} %collective-permute-done.26.refs_2_, ...), custom_call_target="tpu_custom_call" | custom-call | flops 3000000000 | bytes 9000000 | tf_op jit(solution)/shard_map/unpack_last_layer/pallas_call | solution.py:626
  93.1 1.7 %unpack_held.1 = (f32[2,384,1536]{2,1,0:T(8,128)}, f32[2,1536,384]{2,1,0:T(8,128)}) custom-call(bf16[8,112,384]{2,1,0:T(8,128)(2,1)S(1)} %pad_maximum_fusion.refs_0_.held, bf16[8,112,384]{2,1,0:T(8,128)(2,1)S(1)} %collective-permute-done.25.refs_1_.other_held, ...), custom_call_target="tpu_custom_call", output_to_operand_aliasing={{0}: (2, {}), {1}: (3, {})} | custom-call | flops 2000000000 | bytes 6000000 | tf_op jit(solution)/shard_map/unpack_held/pallas_call | solution.py:626
  94.9 5.2 %collective-permute-done.24.refs_0_.late = bf16[8,112,384]{2,1,0:T(8,128)(2,1)S(1)} collective-permute-done((bf16[8,112,384]{2,1,0:T(8,128)(2,1)S(1)}, bf16[8,112,384]{2,1,0:T(8,128)(2,1)S(1)}, u32[]{:S(2)}, u32[]{:S(2)}) %collective-permute-start.24) | collective-permute-done | bytes 688160 | tf_op jit(solution)/shard_map/ppermute | solution.py:462
  100.1 1.1 %unpack_late.1 = (f32[2,384,1536]{2,1,0:T(8,128)}, f32[2,1536,384]{2,1,0:T(8,128)}) custom-call(bf16[8,112,384]{2,1,0:T(8,128)(2,1)S(1)} %collective-permute-done.24.refs_0_.late, f32[2,384,1536]{2,1,0:T(8,128)} %get-tuple-element.164.refs_1_, f32[2,1536,384]{2,1,0:T(8,128)} %get-tuple-element.165.refs_2_), custom_call_target="tpu_custom_call", output_to_operand_aliasing={{0}: (1, {}), {1}: (2, {})} | custom-call | flops 1000000000 | bytes 3000000 | tf_op jit(solution)/shard_map/unpack_late/pallas_call | solution.py:626
  101.2 1.0 collective-permute-done.27.other_late
  102.2 2.9 %unpack_rest.1 = (f32[2,384,1536]{2,1,0:T(8,128)}, f32[2,1536,384]{2,1,0:T(8,128)}, f32[196,2,196]{2,1,0:T(2,128)}, f32[2,384]{1,0:T(2,128)}, f32[2,384]{1,0:T(2...) custom-call(bf16[8,112,384]{2,1,0:T(8,128)(2,1)S(1)} %pad_maximum_fu, ...), custom_call_target="tpu_custom_call", output_to_operand_aliasing={{0}: (4, {}), {1}: (5, {})} | custom-call | flops 2000000000 | bytes 6000000 | tf_op jit(solution)/shard_map/unpack_rest/pallas_call | solution.py:626
  (31 shorter events, 0.3 us)
Async XLA Ops:
  16.1 3.1 %collective-permute-start = (bf16[16,96,384]{2,1,0:T(8,128)(2,1)S(1)}, bf16[16,96,384]{2,1,0:T(8,128)(2,1)S(1)}, u32[]{:S(2)}, u32[]{:S(2)}) collective-permute-start(bf16[16,96,384]{2,1,0:T(8,128)(2,1)S(1)} %get-tuple-element.115), channel_id=1, source_target_pairs={{0,1},{1,0},{2,3},{3,2},{4,5},{5,4},{6,7},{7,6},{8,9},{9,8},{10,11... | collective-permute-start | bytes 3538952 | tf_op jit(solution)/shard_map/ppermute | solution.py:462
  19.4 10.6 %collective-permute-start.1 = (bf16[8,96,384]{2,1,0:T(8,128)(2,1)S(1)}, bf16[8,96,384]{2,1,0:T(8,128)(2,1)S(1)}, u32[]{:S(2)}, u32[]{:S(2)}) collective-permute-start(bf16[8,96,384]{2,1,0:T(8,128)(2,1)S(1)} %add_convert_fusion.1), channel_id=1, source_target_pairs={{0,2},{1,5},{2,0},{3,7},{4,6},{5,1},{6,4},{7,3},{8,10},{9,13},{10,... | collective-permute-start | bytes 1769480 | tf_op jit(solution)/shard_map/ppermute | solution.py:462
  30.0 6.9 %collective-permute-start.2 = (bf16[16,96,384]{2,1,0:T(8,128)(2,1)S(1)}, bf16[16,96,384]{2,1,0:T(8,128)(2,1)S(1)}, u32[]{:S(2)}, u32[]{:S(2)}) collective-permute-start(bf16[16,96,384]{2,1,0:T(8,128)(2,1)S(1)} %get-tuple-element.137), channel_id=1, source_target_pairs={{0,1},{1,0},{2,3},{3,2},{4,5},{5,4},{6,7},{7,6},{8,9},{9,8},{10,11... | collective-permute-start | bytes 3538952 | tf_op jit(solution)/shard_map/ppermute | solution.py:462
  30.1 6.8 %collective-permute-start.4 = (bf16[4,96,384]{2,1,0:T(8,128)(2,1)S(1)}, bf16[4,96,384]{2,1,0:T(8,128)(2,1)S(1)}, u32[]{:S(2)}, u32[]{:S(2)}) collective-permute-start(bf16[4,96,384]{2,1,0:T(8,128)(2,1)S(1)} %add_convert_fusion.3), channel_id=1, source_target_pairs={{0,4},{1,3},{2,6},{3,1},{4,0},{5,7},{6,2},{7,5},{8,12},{9,11},{10,... | collective-permute-start | bytes 884744 | tf_op jit(solution)/shard_map/ppermute | solution.py:462
  37.0 6.6 %collective-permute-start.5 = (bf16[16,16,384]{2,1,0:T(8,128)(2,1)S(1)}, bf16[16,16,384]{2,1,0:T(8,128)(2,1)S(1)}, u32[]{:S(2)}, u32[]{:S(2)}) collective-permute-start(bf16[16,16,384]{2,1,0:T(8,128)(2,1)S(1)} %get-tuple-element.140), channel_id=1, source_target_pairs={{0,1},{1,0},{2,3},{3,2},{4,5},{5,4},{6,7},{7,6},{8,9},{9,8},{10,11... | collective-permute-start | bytes 589832 | tf_op jit(solution)/shard_map/ppermute | solution.py:462
  37.0 17.9 %copy-start = (bf16[16,96,384]{2,1,0:T(8,128)(2,1)}, bf16[16,96,384]{2,1,0:T(8,128)(2,1)S(1)}, u32[]{:S(2)}) copy-start(bf16[16,96,384]{2,1,0:T(8,128)(2,1)S(1)} %collective-permute-done.2) | copy-start | bytes 3538948
  37.1 12.2 %collective-permute-start.3 = (bf16[8,96,384]{2,1,0:T(8,128)(2,1)S(1)}, bf16[8,96,384]{2,1,0:T(8,128)(2,1)S(1)}, u32[]{:S(2)}, u32[]{:S(2)}) collective-permute-start(bf16[8,96,384]{2,1,0:T(8,128)(2,1)S(1)} %add_convert_fusion), channel_id=1, source_target_pairs={{0,2},{1,5},{2,0},{3,7},{4,6},{5,1},{6,4},{7,3},{8,10},{9,13},{10,... | collective-permute-start | bytes 1769480 | tf_op jit(solution)/shard_map/ppermute | solution.py:462
  39.3 8.4 %collective-permute-start.9 = (bf16[1,96,384]{2,1,0:T(8,128)(2,1)S(1)}, bf16[1,96,384]{2,1,0:T(8,128)(2,1)S(1)}, u32[]{:S(2)}, u32[]{:S(2)}) collective-permute-start(bf16[1,96,384]{2,1,0:T(8,128)(2,1)S(1)} %get-tuple-element.182), channel_id=1, source_target_pairs={{0,16},{1,17},{2,18},{3,19},{4,20},{5,21},{6,22},{7,23},{8,24},{9,... | collective-permute-start | bytes 221192 | tf_op jit(solution)/shard_map/ppermute | solution.py:462
  41.9 6.7 %collective-permute-start.8 = (bf16[1,96,384]{2,1,0:T(8,128)(2,1)S(1)}, bf16[1,96,384]{2,1,0:T(8,128)(2,1)S(1)}, u32[]{:S(2)}, u32[]{:S(2)}) collective-permute-start(bf16[1,96,384]{2,1,0:T(8,128)(2,1)S(1)} %get-tuple-element.183), channel_id=1, source_target_pairs={{0,24},{1,25},{2,26},{3,27},{4,28},{5,29},{6,30},{7,31},{8,16},{9,... | collective-permute-start | bytes 221192 | tf_op jit(solution)/shard_map/ppermute | solution.py:462
  43.3 5.9 %collective-permute-start.7 = (bf16[1,96,384]{2,1,0:T(8,128)(2,1)S(1)}, bf16[1,96,384]{2,1,0:T(8,128)(2,1)S(1)}, u32[]{:S(2)}, u32[]{:S(2)}) collective-permute-start(bf16[1,96,384]{2,1,0:T(8,128)(2,1)S(1)} %get-tuple-element.181), channel_id=1, source_target_pairs={{0,8},{1,9},{2,10},{3,11},{4,12},{5,13},{6,14},{7,15},{8,0},{9,1},... | collective-permute-start | bytes 221192 | tf_op jit(solution)/shard_map/ppermute | solution.py:462
  43.5 11.4 %copy-start.1 = (bf16[16,16,384]{2,1,0:T(8,128)(2,1)}, bf16[16,16,384]{2,1,0:T(8,128)(2,1)S(1)}, u32[]{:S(2)}) copy-start(bf16[16,16,384]{2,1,0:T(8,128)(2,1)S(1)} %collective-permute-done.5) | copy-start | bytes 589828
  43.6 5.7 %collective-permute-start.6 = (bf16[8,16,384]{2,1,0:T(8,128)(2,1)S(1)}, bf16[8,16,384]{2,1,0:T(8,128)(2,1)S(1)}, u32[]{:S(2)}, u32[]{:S(2)}) collective-permute-start(bf16[8,16,384]{2,1,0:T(8,128)(2,1)S(1)} %add_convert_fusion.4), channel_id=1, source_target_pairs={{0,2},{1,5},{2,0},{3,7},{4,6},{5,1},{6,4},{7,3},{8,10},{9,13},{10,... | collective-permute-start | bytes 294920 | tf_op jit(solution)/shard_map/ppermute | solution.py:462
  49.5 11.4 %collective-permute-start.10 = (bf16[4,112,384]{2,1,0:T(8,128)(2,1)S(1)}, bf16[4,112,384]{2,1,0:T(8,128)(2,1)S(1)}, u32[]{:S(2)}, u32[]{:S(2)}) collective-permute-start(bf16[4,112,384]{2,1,0:T(8,128)(2,1)S(1)} %pad_maximum_fusion.2), channel_id=1, source_target_pairs={{0,4},{1,3},{2,6},{3,1},{4,0},{5,7},{6,2},{7,5},{8,12},{9,11},{10,... | collective-permute-start | bytes 1032200 | tf_op jit(solution)/shard_map/ppermute | solution.py:462
  50.4 7.0 %collective-permute-start.13 = (bf16[1,96,384]{2,1,0:T(8,128)(2,1)S(1)}, bf16[1,96,384]{2,1,0:T(8,128)(2,1)S(1)}, u32[]{:S(2)}, u32[]{:S(2)}) collective-permute-start(bf16[1,96,384]{2,1,0:T(8,128)(2,1)S(1)} %add_convert_fusion.8), channel_id=1, source_target_pairs={{0,24},{1,25},{2,26},{3,27},{4,28},{5,29},{6,30},{7,31},{8,16},{9,... | collective-permute-start | bytes 221192 | tf_op jit(solution)/shard_map/ppermute | solution.py:462
  54.0 5.3 %collective-permute-start.12 = (bf16[1,96,384]{2,1,0:T(8,128)(2,1)S(1)}, bf16[1,96,384]{2,1,0:T(8,128)(2,1)S(1)}, u32[]{:S(2)}, u32[]{:S(2)}) collective-permute-start(bf16[1,96,384]{2,1,0:T(8,128)(2,1)S(1)} %add_convert_fusion.8), channel_id=1, source_target_pairs={{0,8},{1,9},{2,10},{3,11},{4,12},{5,13},{6,14},{7,15},{8,0},{9,1},... | collective-permute-start | bytes 221192 | tf_op jit(solution)/shard_map/ppermute | solution.py:462
  54.0 6.8 %collective-permute-start.11 = (bf16[1,96,384]{2,1,0:T(8,128)(2,1)S(1)}, bf16[1,96,384]{2,1,0:T(8,128)(2,1)S(1)}, u32[]{:S(2)}, u32[]{:S(2)}) collective-permute-start(bf16[1,96,384]{2,1,0:T(8,128)(2,1)S(1)} %add_convert_fusion.8), channel_id=1, source_target_pairs={{0,16},{1,17},{2,18},{3,19},{4,20},{5,21},{6,22},{7,23},{8,24},{9,... | collective-permute-start | bytes 221192 | tf_op jit(solution)/shard_map/ppermute | solution.py:462
  54.9 6.1 %slice-start.1 = ((bf16[16,16,384]{2,1,0:T(8,128)(2,1)}), bf16[8,16,384]{2,1,0:T(8,128)(2,1)S(1)}, s32[]{:S(2)}) async-start(bf16[16,16,384]{2,1,0:T(8,128)(2,1)} %copy-done.1), calls=%async_computation.1 | async-start | bytes 196608 | tf_op jit(solution)/shard_map/slice | solution.py:805
  54.9 6.1 %slice-start = ((bf16[16,96,384]{2,1,0:T(8,128)(2,1)}), bf16[8,96,384]{2,1,0:T(8,128)(2,1)S(1)}, s32[]{:S(2)}) async-start(bf16[16,96,384]{2,1,0:T(8,128)(2,1)} %copy-done), calls=%async_computation | async-start | bytes 1179648 | tf_op jit(solution)/shard_map/slice | solution.py:805
  61.2 8.5 %collective-permute-start.16 = (bf16[1,112,384]{2,1,0:T(8,128)(2,1)S(1)}, bf16[1,112,384]{2,1,0:T(8,128)(2,1)S(1)}, u32[]{:S(2)}, u32[]{:S(2)}) collective-permute-start(bf16[1,112,384]{2,1,0:T(8,128)(2,1)S(1)} %pad_maximum_fusion.7), channel_id=1, source_target_pairs={{0,16},{1,17},{2,18},{3,19},{4,20},{5,21},{6,22},{7,23},{8,24},{9,... | collective-permute-start | bytes 258056 | tf_op jit(solution)/shard_map/ppermute | solution.py:462
  62.7 6.9 %collective-permute-start.15 = (bf16[1,112,384]{2,1,0:T(8,128)(2,1)S(1)}, bf16[1,112,384]{2,1,0:T(8,128)(2,1)S(1)}, u32[]{:S(2)}, u32[]{:S(2)}) collective-permute-start(bf16[1,112,384]{2,1,0:T(8,128)(2,1)S(1)} %pad_maximum_fusion.6), channel_id=1, source_target_pairs={{0,24},{1,25},{2,26},{3,27},{4,28},{5,29},{6,30},{7,31},{8,16},{9,... | collective-permute-start | bytes 258056 | tf_op jit(solution)/shard_map/ppermute | solution.py:462
  64.2 6.2 %collective-permute-start.14 = (bf16[1,112,384]{2,1,0:T(8,128)(2,1)S(1)}, bf16[1,112,384]{2,1,0:T(8,128)(2,1)S(1)}, u32[]{:S(2)}, u32[]{:S(2)}) collective-permute-start(bf16[1,112,384]{2,1,0:T(8,128)(2,1)S(1)} %pad_maximum_fusion.5), channel_id=1, source_target_pairs={{0,8},{1,9},{2,10},{3,11},{4,12},{5,13},{6,14},{7,15},{8,0},{9,1},... | collective-permute-start | bytes 258056 | tf_op jit(solution)/shard_map/ppermute | solution.py:462
  64.9 6.7 %collective-permute-start.17 = (bf16[4,96,384]{2,1,0:T(8,128)(2,1)S(1)}, bf16[4,96,384]{2,1,0:T(8,128)(2,1)S(1)}, u32[]{:S(2)}, u32[]{:S(2)}) collective-permute-start(bf16[4,96,384]{2,1,0:T(8,128)(2,1)S(1)} %pad_maximum_fusion.4), channel_id=1, source_target_pairs={{0,4},{1,3},{2,6},{3,1},{4,0},{5,7},{6,2},{7,5},{8,12},{9,11},{10,... | collective-permute-start | bytes 884744 | tf_op jit(solution)/shard_map/ppermute | solution.py:462
  71.7 9.9 %collective-permute-start.21 = (bf16[8,96,384]{2,1,0:T(8,128)(2,1)S(1)}, bf16[8,96,384]{2,1,0:T(8,128)(2,1)S(1)}, u32[]{:S(2)}, u32[]{:S(2)}) collective-permute-start(bf16[8,96,384]{2,1,0:T(8,128)(2,1)S(1)} %pad_maximum_fusion.1.refs_0_), channel_id=1, source_target_pairs={{0,2},{1,5},{2,0},{3,7},{4,6},{5,1},{6,4},{7,3},{8,10},{9,13},{10,... | collective-permute-start | bytes 1769480 | tf_op jit(solution)/shard_map/ppermute | solution.py:462
  73.0 6.5 %collective-permute-start.20 = (bf16[1,112,384]{2,1,0:T(8,128)(2,1)S(1)}, bf16[1,112,384]{2,1,0:T(8,128)(2,1)S(1)}, u32[]{:S(2)}, u32[]{:S(2)}) collective-permute-start(bf16[1,112,384]{2,1,0:T(8,128)(2,1)S(1)} %fusion), channel_id=1, source_target_pairs={{0,24},{1,25},{2,26},{3,27},{4,28},{5,29},{6,30},{7,31},{8,16},{9,... | collective-permute-start | bytes 258056 | tf_op jit(solution)/shard_map/ppermute | solution.py:462
  75.6 4.8 %collective-permute-start.19 = (bf16[1,112,384]{2,1,0:T(8,128)(2,1)S(1)}, bf16[1,112,384]{2,1,0:T(8,128)(2,1)S(1)}, u32[]{:S(2)}, u32[]{:S(2)}) collective-permute-start(bf16[1,112,384]{2,1,0:T(8,128)(2,1)S(1)} %fusion), channel_id=1, source_target_pairs={{0,8},{1,9},{2,10},{3,11},{4,12},{5,13},{6,14},{7,15},{8,0},{9,1},... | collective-permute-start | bytes 258056 | tf_op jit(solution)/shard_map/ppermute | solution.py:462
  75.6 5.7 %collective-permute-start.18 = (bf16[1,112,384]{2,1,0:T(8,128)(2,1)S(1)}, bf16[1,112,384]{2,1,0:T(8,128)(2,1)S(1)}, u32[]{:S(2)}, u32[]{:S(2)}) collective-permute-start(bf16[1,112,384]{2,1,0:T(8,128)(2,1)S(1)} %fusion), channel_id=1, source_target_pairs={{0,16},{1,17},{2,18},{3,19},{4,20},{5,21},{6,22},{7,23},{8,24},{9,... | collective-permute-start | bytes 258056 | tf_op jit(solution)/shard_map/ppermute | solution.py:462
  81.6 7.3 %collective-permute-start.23 = (bf16[8,96,384]{2,1,0:T(8,128)(2,1)S(1)}, bf16[8,96,384]{2,1,0:T(8,128)(2,1)S(1)}, u32[]{:S(2)}, u32[]{:S(2)}) collective-permute-start(bf16[8,96,384]{2,1,0:T(8,128)(2,1)S(1)} %collective-permute-done.21.refs_1_), channel_id=1, source_target_pairs={{0,1},{1,0},{2,3},{3,2},{4,5},{5,4},{6,7},{7,6},{8,9},{9,8},{10,11... | collective-permute-start | bytes 1769480 | tf_op jit(solution)/shard_map/ppermute | solution.py:462
  81.6 7.3 %collective-permute-start.22 = (bf16[4,112,384]{2,1,0:T(8,128)(2,1)S(1)}, bf16[4,112,384]{2,1,0:T(8,128)(2,1)S(1)}, u32[]{:S(2)}, u32[]{:S(2)}) collective-permute-start(bf16[4,112,384]{2,1,0:T(8,128)(2,1)S(1)} %pad_maximum_fusion.3), channel_id=1, source_target_pairs={{0,4},{1,3},{2,6},{3,1},{4,0},{5,7},{6,2},{7,5},{8,12},{9,11},{10,... | collective-permute-start | bytes 1032200 | tf_op jit(solution)/shard_map/ppermute | solution.py:462
  83.6 6.8 %collective-permute-start.26 = (bf16[8,96,384]{2,1,0:T(8,128)(2,1)S(1)}, bf16[8,96,384]{2,1,0:T(8,128)(2,1)S(1)}, u32[]{:S(2)}, u32[]{:S(2)}) collective-permute-start(bf16[8,96,384]{2,1,0:T(8,128)(2,1)S(1)} %pad_maximum_fusion.1.refs_0_), channel_id=1, source_target_pairs={{0,1},{1,0},{2,3},{3,2},{4,5},{5,4},{6,7},{7,6},{8,9},{9,8},{10,11... | collective-permute-start | bytes 1769480 | tf_op jit(solution)/shard_map/ppermute | solution.py:462
  89.0 4.1 %collective-permute-start.25 = (bf16[8,112,384]{2,1,0:T(8,128)(2,1)S(1)}, bf16[8,112,384]{2,1,0:T(8,128)(2,1)S(1)}, u32[]{:S(2)}, u32[]{:S(2)}) collective-permute-start(bf16[8,112,384]{2,1,0:T(8,128)(2,1)S(1)} %pad_maximum_fusion.refs_0_.held), channel_id=1, source_target_pairs={{0,1},{1,0},{2,3},{3,2},{4,5},{5,4},{6,7},{7,6},{8,9},{9,8},{10,11... | collective-permute-start | bytes 2064392 | tf_op jit(solution)/shard_map/ppermute | solution.py:462
  89.1 11.0 %collective-permute-start.24 = (bf16[8,112,384]{2,1,0:T(8,128)(2,1)S(1)}, bf16[8,112,384]{2,1,0:T(8,128)(2,1)S(1)}, u32[]{:S(2)}, u32[]{:S(2)}) collective-permute-start(bf16[8,112,384]{2,1,0:T(8,128)(2,1)S(1)} %pad_maximum_fusion.refs_0_.held), channel_id=1, source_target_pairs={{0,2},{1,5},{2,0},{3,7},{4,6},{5,1},{6,4},{7,3},{8,10},{9,13},{10,... | collective-permute-start | bytes 2064392 | tf_op jit(solution)/shard_map/ppermute | solution.py:462
  100.1 2.1 %collective-permute-start.27 = (bf16[8,112,384]{2,1,0:T(8,128)(2,1)S(1)}, bf16[8,112,384]{2,1,0:T(8,128)(2,1)S(1)}, u32[]{:S(2)}, u32[]{:S(2)}) collective-permute-start(bf16[8,112,384]{2,1,0:T(8,128)(2,1)S(1)} %collective-permute-done.24.refs_0_.late), channel_id=1, source_target_pairs={{0,1},{1,0},{2,3},{3,2},{4,5},{5,4},{6,7},{7,6},{8,9},{9,8},{10,11... | collective-permute-start | bytes 2064392 | tf_op jit(solution)/shard_map/ppermute | solution.py:462

commit v4 on v3

--- a/solution.py
+++ b/solution.py
@@ -394,9 +394,10 @@
 
 def third_kernel(
     mesh_shape,
-    s1, g2, low0, fired0, slope0, result0, inner0, outer0, vectors_in, mixer_aff_scale, mixer_scale,
-    kept, sent, g1, vectors,
-    hidden_grad, scaled, inner_grad, outer_grad,
+    s1, g2, low0, fired0, slope0, result0, inner0, outer0, s3, g_rows, fired1, outer1, vectors_in,
+    mixer_aff_scale, outer_bias, mixer_scale,
+    kept, sent, g1, vectors, output,
+    hidden_grad, scaled, inner_grad, outer_grad, leaving,
 ):
     vectors[...] = vectors_in[...]
     hidden_grad[...] = slope0[...]
@@ -410,23 +411,6 @@
         scale_grad += row_sum(read(g2, rows) * result0[rows, :].astype(F32))
     vectors[0, MIXER_SCALE : MIXER_SCALE + 1, :] = scale_grad
     mixer_input_grad(0, g2, s1, hidden_grad, g1, inner0, vectors, mixer_aff_scale)
-
-
-def fourth_kernel(
-    mesh_shape,
-    s0, g1, kept_weight, keep, bias_columns, weight_grad1, vectors_in,
-    s3, g_rows, fired1, outer1,
-    cross_aff_scale, cross_aff_shift, cross_scale, outer_bias, mixer_scale,
-    input_grad, output, kept, sent,
-    g0, leaving, weight_grad0, vectors, small, padded_low, padded_mixing,
-):
-    _, patches, each, _ = input_grad.shape
-    vectors[...] = vectors_in[...]
-    clear_padding(padded_low, padded_mixing, patches=patches)
-    cross_backward(
-        0, s0, g1, g0, weight_grad0, vectors, kept_weight, keep, bias_columns,
-        cross_aff_scale, cross_aff_shift, cross_scale, padded_low, padded_mixing, patches, each,
-    )
     squares = jnp.zeros((1, LANES), F32)
     scale_grad = jnp.zeros((1, LANES), F32)
     for rows in row_halves(s3.shape[1]):
@@ -437,6 +421,23 @@
         squares += row_sum(branch * branch)
     vectors[1, SQUARES + 2 : SQUARES + 3, :] = squares
     vectors[1, MIXER_SCALE : MIXER_SCALE + 1, :] = scale_grad
+    gather_rows(leaving, output)
+
+
+def fourth_kernel(
+    mesh_shape,
+    s0, g1, kept_weight, keep, bias_columns, weight_grad1, vectors_in,
+    cross_aff_scale, cross_aff_shift, cross_scale,
+    input_grad, kept, sent,
+    g0, weight_grad0, vectors, small, padded_low, padded_mixing,
+):
+    _, patches, each, _ = input_grad.shape
+    vectors[...] = vectors_in[...]
+    clear_padding(padded_low, padded_mixing, patches=patches)
+    cross_backward(
+        0, s0, g1, g0, weight_grad0, vectors, kept_weight, keep, bias_columns,
+        cross_aff_scale, cross_aff_shift, cross_scale, padded_low, padded_mixing, patches, each,
+    )
     layers, padded = kept_weight.shape[0], kept_weight.shape[2]
     groups = padded // VECTOR_ROWS
     small[...] = jnp.zeros_like(small)
@@ -447,7 +448,6 @@
         small[layers * groups + layer] = vectors[layer].astype(BF)
     pack_halves(own_codes(mesh_shape), lambda block: (small[block],), kept, sent)
     gather_rows(g0, input_grad)
-    gather_rows(leaving, output)
 
 
 def exchange_bits(values, mesh_shape, phases):
@@ -492,11 +492,17 @@
     return arrived, grown
 
 
-def scatter_last(families, mesh_shape):
-    arrived = [
-        exchange_bits(joint_sum(families, slot, slot + 1), mesh_shape, across(slot))
-        for slot in (2, 3, 1)
+LAST_SLOTS = (2, 3, 1)
+
+
+def send_last(families, mesh_shape):
+    leaving = [joint_sum(families, slot, slot + 1) for slot in LAST_SLOTS]
+    return leaving, [
+        exchange_bits(block, mesh_shape, across(slot)) for slot, block in zip(LAST_SLOTS, leaving)
     ]
+
+
+def sum_last(families, arrived, mesh_shape):
     sums = [part_sum(terms, 0, 1) for terms in families]
     total = sums[0] if len(sums) == 1 else jnp.concatenate(sums, axis=1)
     total = total + sum(a.astype(F32) for a in arrived)
@@ -507,7 +513,10 @@
 
 
 def gather_last(own, mesh_shape):
-    arrived = {slot: exchange_bits(own, mesh_shape, across(slot)) for slot in (2, 3, 1)}
+    return {slot: exchange_bits(own, mesh_shape, across(slot)) for slot in LAST_SLOTS}
+
+
+def join(own, arrived):
     return jnp.concatenate([own, arrived[1], arrived[2], arrived[3]], axis=0)
 
 
@@ -757,15 +766,18 @@
     leaving1, main1 = halve(main1, HALF, mesh_shape, 1)
     g2 = after(g2, leaving1)
     halves = vmem(HALF, 2 * depth, LANES)
-    kept0, sent0, g1, sums = call(
+    kept0, sent0, g1, sums, output = call(
         functools.partial(third_kernel, mesh_shape),
         "first_feed_forward",
         (
-            *in_vmem((s1, g2, low0, fired0, slope0, result0, inner0, outer0, sums)),
-            mixer_aff, result_scale,
+            *in_vmem((
+                s1, g2, low0, fired0, slope0, result0, inner0, outer0, s3, upper, fired1, outer1,
+                sums,
+            )),
+            mixer_aff, result_bias, result_scale,
         ),
-        (halves, halves, stream, vectors),
-        [hidden, vmem(rows, width), inner, outer],
+        (halves, halves, stream, vectors, hbm(*local, dtype=BF)),
+        [hidden, vmem(rows, width), inner, outer, stream],
         us=9,
     )
     sent0, sums = lax.optimization_barrier((sent0, sums, main1[-1]))[:2]
@@ -773,19 +785,15 @@
     leaving1, main1 = halve(main1, HALF // 2, mesh_shape, 2)
     sums = after(sums, leaving1)
     halves = vmem(HALF, VECTOR_ROWS, LANES)
-    input_grad, output, kept_small, sent_small = call(
+    input_grad, kept_small, sent_small = call(
         functools.partial(fourth_kernel, mesh_shape),
         "first_cross",
         (
-            *in_vmem((
-                s0, g1, kept_weight, keep, bias_columns, weight_grad1, sums, s3, upper, fired1,
-                outer1,
-            )),
-            aff_scale, aff_shift, scale, result_bias, result_scale,
+            *in_vmem((s0, g1, kept_weight, keep, bias_columns, weight_grad1, sums)),
+            aff_scale, aff_shift, scale,
         ),
-        (hbm(*local, dtype=BF), hbm(*local, dtype=BF), halves, halves),
+        (hbm(*local, dtype=BF), halves, halves),
         [
-            stream,
             stream,
             vmem(padded, padded, dtype=F32),
             vectors,
@@ -795,27 +803,29 @@
         ],
         us=5,
     )
-    sent_small = after(sent_small, main1[-1])
     small = [kept_small, exchange_bits(sent_small, mesh_shape, [0])]
     _, main0 = halve(main0, HALF, mesh_shape, 1)
     _, small = halve(small, HALF, mesh_shape, 1)
-    own1 = scatter_last([main1], mesh_shape)
+    own1 = sum_last([main1], send_last([main1], mesh_shape)[1], mesh_shape)
     main0[-1], small[-1], own1 = lax.optimization_barrier((main0[-1], small[-1], own1))
     width0 = HALF // 2
     terms0 = [[t[:width0] for t in main0], [t[:width0] for t in small]]
     _, terms0 = halve_all(terms0, width0, mesh_shape, 2)
-    four1 = gather_last(own1, mesh_shape)
-    terms0, four1 = lax.optimization_barrier((terms0, four1))
-    own0 = scatter_last(terms0, mesh_shape)
-    held1 = double(four1, mesh_shape, 2)
-    own0, held1 = lax.optimization_barrier((own0, held1))
-    four0 = gather_last(own0, mesh_shape)
+    peers1 = gather_last(own1, mesh_shape)
+    leaving0, arrived0 = send_last(terms0, mesh_shape)
+    four1 = join(own1, after(peers1, leaving0))
+    own0 = sum_last(terms0, arrived0, mesh_shape)
+    more1 = exchange_bits(four1, mesh_shape, [2])
+    peers0 = gather_last(own0, mesh_shape)
+    more1 = after(more1, own0)
+    held1 = jnp.concatenate([four1, more1], axis=0)
+    four0 = join(own0, peers0)
     late1 = exchange_bits(held1, mesh_shape, [1])
     other_held1 = exchange_bits(held1, mesh_shape, [0])
-    four0, late1 = lax.optimization_barrier((four0, late1))
+    late1 = after(late1, four0)
     held0 = double(four0, mesh_shape, 2)
     other_late1 = exchange_bits(late1, mesh_shape, [0])
-    held0, other_late1 = lax.optimization_barrier((held0, other_late1))
+    other_late1 = after(other_late1, held0)
     late0 = exchange_bits(held0, mesh_shape, [1])
     other_held0 = exchange_bits(held0, mesh_shape, [0])
     quarters1 = (held1, late1, other_held1, other_late1)

time: 105 us -> 101 us (0.962)
  waiting for transfers between devices: 34.4 us -> 28.8 us
    ppermute x28, waiting for transfers between devices: 34.4 us -> 28.8 us  [exchange_bits(): return lax.ppermute(values, AXES, [(i, partner(i)) for i in places])]
  transfers between devices with their start and end apart: 28 -> 28, of which waited for: 18 -> 16; matrix products, arithmetic and copies ran while one was open for 1% -> 1% of each run, Pallas kernels for 18% -> 20%
where the time goes in v4:
time: 101 us
  Pallas kernels  38.1 us (38%)
  starting transfers between devices  31.6 us (31%)
  waiting for transfers between devices  28.8 us (29%)
  other arithmetic  1.19 us (1%)
  between operations  1.08 us (1%)
    pallas_call x8, Pallas kernels, call(): pl.pallas_call(kernel, out_shape=outs, in_specs=[VMEM] * len(args) if in_...  38.1 us
    ppermute x28, starting transfers between devices, exchange_bits(): return lax.ppermute(values, AXES, [(i, partner(i)) for i in places])  31.6 us
    ppermute x28, waiting for transfers between devices, exchange_bits(): return lax.ppermute(values, AXES, [(i, partner(i)) for i in places])  28.8 us
  transfers between devices with their start and end apart: 28, of which 16 were waited for; matrix products, arithmetic and copies ran while one was open for 1% of the time, Pallas kernels for 20%

profile of v4, /device:TPU:0, one launch (start us, length us, event | category | flops | bytes accessed | tf_op | source)
XLA Modules:
  0.0 101.0 jit_solution(4173701512164053992)
XLA Ops:
  0.7 15.4 %forward.1 = (f32[2,384]{1,0:T(2,128)S(1)}, f32[2,384]{1,0:T(2,128)S(1)}, f32[2,384]{1,0:T(2,128)S(1)}, f32[2,384]{1,0:T(2,128)S(1)}, f32[2,384]{1,0:T(2,128)S(1...) custom-call(bf16[4,196,4,384]{3,2,1,0:T(4,128)(2,1)} %bitcast.6, ...), custom_call_target="tpu_custom_call" | custom-call | flops 17999998976 | bytes 54000000 | tf_op jit(solution)/shard_map/forward/pallas_call | solution.py:635
  16.1 0.5 collective-permute-start
  16.6 2.6 %last_layer.1 = (f32[3,784,128]{2,1,0:T(8,128)S(1)}, f32[208,208]{1,0:T(8,128)S(1)}, f32[2,16,384]{2,1,0:T(8,128)S(1)}) custom-call(f32[3,784,128]{2,1,0:T(8,128)S(1)} %get-tuple-element.89.s2, f32[3,784,128]{2,1,0:T(8,128)S(1)} %get-tuple-element.90.s3, f32[3,784,128]{2,1,0:T(8,128)S(1)} %get-tuple-element.91.g_rows, ...), custom_call_target="tpu_custom_call" | custom-call | flops 4000000000 | bytes 12000000 | tf_op jit(solution)/shard_map/last_layer/pallas_call | solution.py:635
  19.2 0.0 collective-permute-done
  19.2 0.2 add_convert_fusion.1
  19.4 2.8 %collective-permute-start.1 = (bf16[8,96,384]{2,1,0:T(8,128)(2,1)S(1)}, bf16[8,96,384]{2,1,0:T(8,128)(2,1)S(1)}, u32[]{:S(2)}, u32[]{:S(2)}) collective-permute-start(bf16[8,96,384]{2,1,0:T(8,128)(2,1)S(1)} %add_convert_fusion.1), channel_id=1, source_target_pairs={{0,2},{1,5},{2,0},{3,7},{4,6},{5,1},{6,4},{7,3},{8,10},{9,13},{10,... | collective-permute-start | bytes 1769480 | tf_op jit(solution)/shard_map/ppermute | solution.py:462
  22.1 9.0 %first_feed_forward.1 = (bf16[16,96,384]{2,1,0:T(8,128)(2,1)S(1)}, bf16[16,96,384]{2,1,0:T(8,128)(2,1)S(1)}, f32[3,784,128]{2,1,0:T(8,128)S(1)}, f32[2,16,384]{2,1,0:T(8,128)S(1)}, bf16[1,196,4,384]{3,2,1,0:T(4,128)(2,1)}) custom-call(f32[3,784,128]{2,1,0:T(8,128)S(1)} %get-tuple-element.88.s1, f32[3,784,128]{2,1,0:T(8,128)S(1)} %get-tuple-element.105.g2, ...), custom_call_target="tpu_custom_call" | custom-call | flops 8999999488 | bytes 27000000 | tf_op jit(solution)/shard_map/first_feed_forward/pallas_call | solution.py:635
  31.1 0.0 collective-permute-done.1
  31.1 0.1 collective-permute-start.2
  31.2 0.1 add_convert_fusion.3
  31.3 1.5 %collective-permute-start.6 = (bf16[4,96,384]{2,1,0:T(8,128)(2,1)S(1)}, bf16[4,96,384]{2,1,0:T(8,128)(2,1)S(1)}, u32[]{:S(2)}, u32[]{:S(2)}) collective-permute-start(bf16[4,96,384]{2,1,0:T(8,128)(2,1)S(1)} %add_convert_fusion.3), channel_id=1, source_target_pairs={{0,4},{1,3},{2,6},{3,1},{4,0},{5,7},{6,2},{7,5},{8,12},{9,11},{10,... | collective-permute-start | bytes 884744 | tf_op jit(solution)/shard_map/ppermute | solution.py:462
  32.8 2.6 %first_cross.1 = (bf16[1,196,4,384]{3,2,1,0:T(4,128)(2,1)}, bf16[16,16,384]{2,1,0:T(8,128)(2,1)S(1)}, bf16[16,16,384]{2,1,0:T(8,128)(2,1)S(1)}) custom-call(f32[3,784,128]{2,1,0:T(8,128)S(1)} %get-tuple-element.118.s0, f32[3,784,128]{2,1,0:T(8,128)S(1)} %get-tuple-element.119.g1, bf16[2,4,208,208]{3,2,1,0:T(8,128)(2,1)S(1)} %get-tuple-element.94.kept_weight, ...), custom_call_target="tpu_custom_call" | custom-call | flops 5000000000 | bytes 15000000 | tf_op jit(solution)/shard_map/first_cross/pallas_call | solution.py:635
  35.5 0.0 collective-permute-start.4
  35.5 0.0 collective-permute-done.2
  35.5 0.2 add_convert_fusion
  35.6 1.0 collective-permute-start.3
  36.6 1.5 %collective-permute-done.6 = bf16[4,96,384]{2,1,0:T(8,128)(2,1)S(1)} collective-permute-done((bf16[4,96,384]{2,1,0:T(8,128)(2,1)S(1)}, bf16[4,96,384]{2,1,0:T(8,128)(2,1)S(1)}, u32[]{:S(2)}, u32[]{:S(2)}) %collective-permute-start.6) | collective-permute-done | bytes 294944 | tf_op jit(solution)/shard_map/ppermute | solution.py:462
  38.1 0.1 add_convert_fusion.11
  38.2 2.6 %collective-permute-start.9 = (bf16[1,96,384]{2,1,0:T(8,128)(2,1)S(1)}, bf16[1,96,384]{2,1,0:T(8,128)(2,1)S(1)}, u32[]{:S(2)}, u32[]{:S(2)}) collective-permute-start(bf16[1,96,384]{2,1,0:T(8,128)(2,1)S(1)} %get-tuple-element.168), channel_id=1, source_target_pairs={{0,16},{1,17},{2,18},{3,19},{4,20},{5,21},{6,22},{7,23},{8,24},{9,... | collective-permute-start | bytes 221192 | tf_op jit(solution)/shard_map/ppermute | solution.py:462
  40.9 1.4 %collective-permute-start.8 = (bf16[1,96,384]{2,1,0:T(8,128)(2,1)S(1)}, bf16[1,96,384]{2,1,0:T(8,128)(2,1)S(1)}, u32[]{:S(2)}, u32[]{:S(2)}) collective-permute-start(bf16[1,96,384]{2,1,0:T(8,128)(2,1)S(1)} %get-tuple-element.169), channel_id=1, source_target_pairs={{0,24},{1,25},{2,26},{3,27},{4,28},{5,29},{6,30},{7,31},{8,16},{9,... | collective-permute-start | bytes 221192 | tf_op jit(solution)/shard_map/ppermute | solution.py:462
  42.2 0.2 collective-permute-start.7
  42.4 0.0 collective-permute-done.4
  42.5 1.6 %collective-permute-start.5 = (bf16[8,16,384]{2,1,0:T(8,128)(2,1)S(1)}, bf16[8,16,384]{2,1,0:T(8,128)(2,1)S(1)}, u32[]{:S(2)}, u32[]{:S(2)}) collective-permute-start(bf16[8,16,384]{2,1,0:T(8,128)(2,1)S(1)} %add_convert_fusion.4), channel_id=1, source_target_pairs={{0,2},{1,5},{2,0},{3,7},{4,6},{5,1},{6,4},{7,3},{8,10},{9,13},{10,... | collective-permute-start | bytes 294920 | tf_op jit(solution)/shard_map/ppermute | solution.py:462
  44.0 1.7 %collective-permute-done.9 = bf16[1,96,384]{2,1,0:T(8,128)(2,1)S(1)} collective-permute-done((bf16[1,96,384]{2,1,0:T(8,128)(2,1)S(1)}, bf16[1,96,384]{2,1,0:T(8,128)(2,1)S(1)}, u32[]{:S(2)}, u32[]{:S(2)}) %collective-permute-start.9) | collective-permute-done | bytes 73760 | tf_op jit(solution)/shard_map/ppermute | solution.py:462
  45.7 1.4 %collective-permute-done.8 = bf16[1,96,384]{2,1,0:T(8,128)(2,1)S(1)} collective-permute-done((bf16[1,96,384]{2,1,0:T(8,128)(2,1)S(1)}, bf16[1,96,384]{2,1,0:T(8,128)(2,1)S(1)}, u32[]{:S(2)}, u32[]{:S(2)}) %collective-permute-start.8) | collective-permute-done | bytes 73760 | tf_op jit(solution)/shard_map/ppermute | solution.py:462
  47.2 0.2 collective-permute-done.7
  47.4 0.1 add_convert_fusion.8
  47.5 0.1 add_convert_fusion.2
  47.7 1.6 %collective-permute-start.10 = (bf16[4,112,384]{2,1,0:T(8,128)(2,1)S(1)}, bf16[4,112,384]{2,1,0:T(8,128)(2,1)S(1)}, u32[]{:S(2)}, u32[]{:S(2)}) collective-permute-start(bf16[4,112,384]{2,1,0:T(8,128)(2,1)S(1)} %pad_maximum_fusion), channel_id=1, source_target_pairs={{0,4},{1,3},{2,6},{3,1},{4,0},{5,7},{6,2},{7,5},{8,12},{9,11},{10,... | collective-permute-start | bytes 1032200 | tf_op jit(solution)/shard_map/ppermute | solution.py:462
  49.3 2.9 %collective-permute-start.20 = (bf16[1,96,384]{2,1,0:T(8,128)(2,1)S(1)}, bf16[1,96,384]{2,1,0:T(8,128)(2,1)S(1)}, u32[]{:S(2)}, u32[]{:S(2)}) collective-permute-start(bf16[1,96,384]{2,1,0:T(8,128)(2,1)S(1)} %add_convert_fusion.8), channel_id=1, source_target_pairs={{0,16},{1,17},{2,18},{3,19},{4,20},{5,21},{6,22},{7,23},{8,24},{9,... | collective-permute-start | bytes 221192 | tf_op jit(solution)/shard_map/ppermute | solution.py:462
  52.2 0.7 collective-permute-start.21
  52.9 0.8 collective-permute-start.22
  53.7 1.3 %collective-permute-done.10 = bf16[4,112,384]{2,1,0:T(8,128)(2,1)S(1)} collective-permute-done((bf16[4,112,384]{2,1,0:T(8,128)(2,1)S(1)}, bf16[4,112,384]{2,1,0:T(8,128)(2,1)S(1)}, u32[]{:S(2)}, u32[]{:S(2)}) %collective-permute-start.10) | collective-permute-done | bytes 344096 | tf_op jit(solution)/shard_map/ppermute | solution.py:462
  55.0 0.1 convert_add_fusion
  55.2 3.0 %collective-permute-start.13 = (bf16[1,112,384]{2,1,0:T(8,128)(2,1)S(1)}, bf16[1,112,384]{2,1,0:T(8,128)(2,1)S(1)}, u32[]{:S(2)}, u32[]{:S(2)}) collective-permute-start(bf16[1,112,384]{2,1,0:T(8,128)(2,1)S(1)} %pad_maximum_fusion.5), channel_id=1, source_target_pairs={{0,16},{1,17},{2,18},{3,19},{4,20},{5,21},{6,22},{7,23},{8,24},{9,... | collective-permute-start | bytes 258056 | tf_op jit(solution)/shard_map/ppermute | solution.py:462
  58.2 1.0 collective-permute-start.12
  59.2 0.1 collective-permute-start.11
  59.3 0.5 collective-permute-done.22
  59.9 1.1 %collective-permute-start.23 = (bf16[4,96,384]{2,1,0:T(8,128)(2,1)S(1)}, bf16[4,96,384]{2,1,0:T(8,128)(2,1)S(1)}, u32[]{:S(2)}, u32[]{:S(2)}) collective-permute-start(bf16[4,96,384]{2,1,0:T(8,128)(2,1)S(1)} %pad_maximum_fusion.2), channel_id=1, source_target_pairs={{0,4},{1,3},{2,6},{3,1},{4,0},{5,7},{6,2},{7,5},{8,12},{9,11},{10,... | collective-permute-start | bytes 884744 | tf_op jit(solution)/shard_map/ppermute | solution.py:462
  61.0 2.7 %collective-permute-done.13 = bf16[1,112,384]{2,1,0:T(8,128)(2,1)S(1)} collective-permute-done((bf16[1,112,384]{2,1,0:T(8,128)(2,1)S(1)}, bf16[1,112,384]{2,1,0:T(8,128)(2,1)S(1)}, u32[]{:S(2)}, u32[]{:S(2)}) %collective-permute-start.13) | collective-permute-done | bytes 86048 | tf_op jit(solution)/shard_map/ppermute | solution.py:462
  63.7 1.0 collective-permute-done.12
  64.7 0.5 collective-permute-done.11
  65.3 1.8 %collective-permute-done.23 = bf16[4,96,384]{2,1,0:T(8,128)(2,1)S(1)} collective-permute-done((bf16[4,96,384]{2,1,0:T(8,128)(2,1)S(1)}, bf16[4,96,384]{2,1,0:T(8,128)(2,1)S(1)}, u32[]{:S(2)}, u32[]{:S(2)}) %collective-permute-start.23) | collective-permute-done | bytes 294944 | tf_op jit(solution)/shard_map/ppermute | solution.py:462
  67.1 1.2 %collective-permute-start.24 = (bf16[8,96,384]{2,1,0:T(8,128)(2,1)S(1)}, bf16[8,96,384]{2,1,0:T(8,128)(2,1)S(1)}, u32[]{:S(2)}, u32[]{:S(2)}) collective-permute-start(bf16[8,96,384]{2,1,0:T(8,128)(2,1)S(1)} %constant_dynamic-update-slice_fusion.5.refs_0_), channel_id=1, source_target_pairs={{0,2},{1,5},{2,0},{3,7},{4,6},{5,1},{6,4},{7,3},{8,10},{9,13},{10,... | collective-permute-start | bytes 1769480 | tf_op jit(solution)/shard_map/ppermute | solution.py:462
  68.3 2.5 %collective-permute-start.14 = (bf16[1,112,384]{2,1,0:T(8,128)(2,1)S(1)}, bf16[1,112,384]{2,1,0:T(8,128)(2,1)S(1)}, u32[]{:S(2)}, u32[]{:S(2)}) collective-permute-start(bf16[1,112,384]{2,1,0:T(8,128)(2,1)S(1)} %get-tuple-element.162), channel_id=1, source_target_pairs={{0,16},{1,17},{2,18},{3,19},{4,20},{5,21},{6,22},{7,23},{8,24},{9,... | collective-permute-start | bytes 258056 | tf_op jit(solution)/shard_map/ppermute | solution.py:462
  70.8 0.0 collective-permute-start.15
  70.9 1.8 %collective-permute-start.16 = (bf16[1,112,384]{2,1,0:T(8,128)(2,1)S(1)}, bf16[1,112,384]{2,1,0:T(8,128)(2,1)S(1)}, u32[]{:S(2)}, u32[]{:S(2)}) collective-permute-start(bf16[1,112,384]{2,1,0:T(8,128)(2,1)S(1)} %get-tuple-element.162), channel_id=1, source_target_pairs={{0,24},{1,25},{2,26},{3,27},{4,28},{5,29},{6,30},{7,31},{8,16},{9,... | collective-permute-start | bytes 258056 | tf_op jit(solution)/shard_map/ppermute | solution.py:462
  72.7 3.0 %collective-permute-done.14 = bf16[1,112,384]{2,1,0:T(8,128)(2,1)S(1)} collective-permute-done((bf16[1,112,384]{2,1,0:T(8,128)(2,1)S(1)}, bf16[1,112,384]{2,1,0:T(8,128)(2,1)S(1)}, u32[]{:S(2)}, u32[]{:S(2)}) %collective-permute-start.14) | collective-permute-done | bytes 86048 | tf_op jit(solution)/shard_map/ppermute | solution.py:462
  75.7 0.5 collective-permute-done.15
  76.1 1.1 %collective-permute-done.16 = bf16[1,112,384]{2,1,0:T(8,128)(2,1)S(1)} collective-permute-done((bf16[1,112,384]{2,1,0:T(8,128)(2,1)S(1)}, bf16[1,112,384]{2,1,0:T(8,128)(2,1)S(1)}, u32[]{:S(2)}, u32[]{:S(2)}) %collective-permute-start.16) | collective-permute-done | bytes 86048 | tf_op jit(solution)/shard_map/ppermute | solution.py:462
  77.2 0.1 pad_maximum_fusion.1
  77.3 1.6 %collective-permute-start.17 = (bf16[4,112,384]{2,1,0:T(8,128)(2,1)S(1)}, bf16[4,112,384]{2,1,0:T(8,128)(2,1)S(1)}, u32[]{:S(2)}, u32[]{:S(2)}) collective-permute-start(bf16[4,112,384]{2,1,0:T(8,128)(2,1)S(1)} %pad_maximum_fusion.1), channel_id=1, source_target_pairs={{0,4},{1,3},{2,6},{3,1},{4,0},{5,7},{6,2},{7,5},{8,12},{9,11},{10,... | collective-permute-start | bytes 1032200 | tf_op jit(solution)/shard_map/ppermute | solution.py:462
  78.9 0.1 collective-permute-start.25
  79.0 0.5 collective-permute-start.26
  79.5 5.1 %collective-permute-done.17 = bf16[4,112,384]{2,1,0:T(8,128)(2,1)S(1)} collective-permute-done((bf16[4,112,384]{2,1,0:T(8,128)(2,1)S(1)}, bf16[4,112,384]{2,1,0:T(8,128)(2,1)S(1)}, u32[]{:S(2)}, u32[]{:S(2)}) %collective-permute-start.17) | collective-permute-done | bytes 344096 | tf_op jit(solution)/shard_map/ppermute | solution.py:462
  84.6 0.1 constant_dynamic-update-slice_fusion.refs_0_.held
  84.7 0.1 collective-permute-start.19
  84.8 1.0 %collective-permute-start.18 = (bf16[8,112,384]{2,1,0:T(8,128)(2,1)S(1)}, bf16[8,112,384]{2,1,0:T(8,128)(2,1)S(1)}, u32[]{:S(2)}, u32[]{:S(2)}) collective-permute-start(bf16[8,112,384]{2,1,0:T(8,128)(2,1)S(1)} %constant_dynamic-update-slice_fusion.refs_0_.held), channel_id=1, source_target_pairs={{0,2},{1,5},{2,0},{3,7},{4,6},{5,1},{6,4},{7,3},{8,10},{9,13},{10,... | collective-permute-start | bytes 2064392 | tf_op jit(solution)/shard_map/ppermute | solution.py:462
  85.8 2.7 %unpack_last_layer.1 = (f32[2,384,1536]{2,1,0:T(8,128)}, f32[2,1536,384]{2,1,0:T(8,128)}) custom-call(bf16[8,96,384]{2,1,0:T(8,128)(2,1)S(1)} %constant_dynamic-update-slice_fusion.5.refs_0_, bf16[8,96,384]{2,1,0:T(8,128)(2,1)S(1)} %collective-permute-done.24.refs_1_, bf16[8,96,384]{2,1,0:T(8,128)(2,1)S(1)} %collective-permute-done.25.refs_2_, ...), custom_call_target="tpu_custom_call" | custom-call | flops 3000000000 | bytes 9000000 | tf_op jit(solution)/shard_map/unpack_last_layer/pallas_call | solution.py:635
  88.5 1.7 %unpack_held.1 = (f32[2,384,1536]{2,1,0:T(8,128)}, f32[2,1536,384]{2,1,0:T(8,128)}) custom-call(bf16[8,112,384]{2,1,0:T(8,128)(2,1)S(1)} %constant_dynamic-update-slice_fusion.refs_0_.held, bf16[8,112,384]{2,1,0:T(8,128)(2,1)S(1)} %collective-permute-done.19.refs_1_.other_held, ...), custom_call_target="tpu_custom_call", output_to_operand_aliasing={{0}: (2, {}), {1}: (3, {})} | custom-call | flops 2000000000 | bytes 6000000 | tf_op jit(solution)/shard_map/unpack_held/pallas_call | solution.py:635
  90.3 5.5 %collective-permute-done.18.refs_0_.late = bf16[8,112,384]{2,1,0:T(8,128)(2,1)S(1)} collective-permute-done((bf16[8,112,384]{2,1,0:T(8,128)(2,1)S(1)}, bf16[8,112,384]{2,1,0:T(8,128)(2,1)S(1)}, u32[]{:S(2)}, u32[]{:S(2)}) %collective-permute-start.18) | collective-permute-done | bytes 688160 | tf_op jit(solution)/shard_map/ppermute | solution.py:462
  95.8 1.1 %unpack_late.1 = (f32[2,384,1536]{2,1,0:T(8,128)}, f32[2,1536,384]{2,1,0:T(8,128)}) custom-call(bf16[8,112,384]{2,1,0:T(8,128)(2,1)S(1)} %collective-permute-done.18.refs_0_.late, f32[2,384,1536]{2,1,0:T(8,128)} %get-tuple-element.144.refs_1_, f32[2,1536,384]{2,1,0:T(8,128)} %get-tuple-element.145.refs_2_), custom_call_target="tpu_custom_call", output_to_operand_aliasing={{0}: (1, {}), {1}: (2, {})} | custom-call | flops 1000000000 | bytes 3000000 | tf_op jit(solution)/shard_map/unpack_late/pallas_call | solution.py:635
  96.9 1.0 collective-permute-done.27.other_late
  97.9 2.9 %unpack_rest.1 = (f32[2,384,1536]{2,1,0:T(8,128)}, f32[2,1536,384]{2,1,0:T(8,128)}, f32[196,2,196]{2,1,0:T(2,128)}, f32[2,384]{1,0:T(2,128)}, f32[2,384]{1,0:T(2...) custom-call(bf16[8,112,384]{2,1,0:T(8,128)(2,1)S(1)} %constant_dynam, ...), custom_call_target="tpu_custom_call", output_to_operand_aliasing={{0}: (4, {}), {1}: (5, {})} | custom-call | flops 2000000000 | bytes 6000000 | tf_op jit(solution)/shard_map/unpack_rest/pallas_call | solution.py:635
  (26 shorter events, 0.4 us)
Async XLA Ops:
  16.1 3.1 %collective-permute-start = (bf16[16,96,384]{2,1,0:T(8,128)(2,1)S(1)}, bf16[16,96,384]{2,1,0:T(8,128)(2,1)S(1)}, u32[]{:S(2)}, u32[]{:S(2)}) collective-permute-start(bf16[16,96,384]{2,1,0:T(8,128)(2,1)S(1)} %get-tuple-element.104), channel_id=1, source_target_pairs={{0,1},{1,0},{2,3},{3,2},{4,5},{5,4},{6,7},{7,6},{8,9},{9,8},{10,11... | collective-permute-start | bytes 3538952 | tf_op jit(solution)/shard_map/ppermute | solution.py:462
  19.4 11.7 %collective-permute-start.1 = (bf16[8,96,384]{2,1,0:T(8,128)(2,1)S(1)}, bf16[8,96,384]{2,1,0:T(8,128)(2,1)S(1)}, u32[]{:S(2)}, u32[]{:S(2)}) collective-permute-start(bf16[8,96,384]{2,1,0:T(8,128)(2,1)S(1)} %add_convert_fusion.1), channel_id=1, source_target_pairs={{0,2},{1,5},{2,0},{3,7},{4,6},{5,1},{6,4},{7,3},{8,10},{9,13},{10,... | collective-permute-start | bytes 1769480 | tf_op jit(solution)/shard_map/ppermute | solution.py:462
  31.1 4.3 %collective-permute-start.2 = (bf16[16,96,384]{2,1,0:T(8,128)(2,1)S(1)}, bf16[16,96,384]{2,1,0:T(8,128)(2,1)S(1)}, u32[]{:S(2)}, u32[]{:S(2)}) collective-permute-start(bf16[16,96,384]{2,1,0:T(8,128)(2,1)S(1)} %get-tuple-element.127), channel_id=1, source_target_pairs={{0,1},{1,0},{2,3},{3,2},{4,5},{5,4},{6,7},{7,6},{8,9},{9,8},{10,11... | collective-permute-start | bytes 3538952 | tf_op jit(solution)/shard_map/ppermute | solution.py:462
  31.3 6.8 %collective-permute-start.6 = (bf16[4,96,384]{2,1,0:T(8,128)(2,1)S(1)}, bf16[4,96,384]{2,1,0:T(8,128)(2,1)S(1)}, u32[]{:S(2)}, u32[]{:S(2)}) collective-permute-start(bf16[4,96,384]{2,1,0:T(8,128)(2,1)S(1)} %add_convert_fusion.3), channel_id=1, source_target_pairs={{0,4},{1,3},{2,6},{3,1},{4,0},{5,7},{6,2},{7,5},{8,12},{9,11},{10,... | collective-permute-start | bytes 884744 | tf_op jit(solution)/shard_map/ppermute | solution.py:462
  35.5 7.0 %collective-permute-start.4 = (bf16[16,16,384]{2,1,0:T(8,128)(2,1)S(1)}, bf16[16,16,384]{2,1,0:T(8,128)(2,1)S(1)}, u32[]{:S(2)}, u32[]{:S(2)}) collective-permute-start(bf16[16,16,384]{2,1,0:T(8,128)(2,1)S(1)} %get-tuple-element.129), channel_id=1, source_target_pairs={{0,1},{1,0},{2,3},{3,2},{4,5},{5,4},{6,7},{7,6},{8,9},{9,8},{10,11... | collective-permute-start | bytes 589832 | tf_op jit(solution)/shard_map/ppermute | solution.py:462
  35.6 11.8 %collective-permute-start.3 = (bf16[8,96,384]{2,1,0:T(8,128)(2,1)S(1)}, bf16[8,96,384]{2,1,0:T(8,128)(2,1)S(1)}, u32[]{:S(2)}, u32[]{:S(2)}) collective-permute-start(bf16[8,96,384]{2,1,0:T(8,128)(2,1)S(1)} %add_convert_fusion), channel_id=1, source_target_pairs={{0,2},{1,5},{2,0},{3,7},{4,6},{5,1},{6,4},{7,3},{8,10},{9,13},{10,... | collective-permute-start | bytes 1769480 | tf_op jit(solution)/shard_map/ppermute | solution.py:462
  38.2 7.5 %collective-permute-start.9 = (bf16[1,96,384]{2,1,0:T(8,128)(2,1)S(1)}, bf16[1,96,384]{2,1,0:T(8,128)(2,1)S(1)}, u32[]{:S(2)}, u32[]{:S(2)}) collective-permute-start(bf16[1,96,384]{2,1,0:T(8,128)(2,1)S(1)} %get-tuple-element.168), channel_id=1, source_target_pairs={{0,16},{1,17},{2,18},{3,19},{4,20},{5,21},{6,22},{7,23},{8,24},{9,... | collective-permute-start | bytes 221192 | tf_op jit(solution)/shard_map/ppermute | solution.py:462
  40.9 6.3 %collective-permute-start.8 = (bf16[1,96,384]{2,1,0:T(8,128)(2,1)S(1)}, bf16[1,96,384]{2,1,0:T(8,128)(2,1)S(1)}, u32[]{:S(2)}, u32[]{:S(2)}) collective-permute-start(bf16[1,96,384]{2,1,0:T(8,128)(2,1)S(1)} %get-tuple-element.169), channel_id=1, source_target_pairs={{0,24},{1,25},{2,26},{3,27},{4,28},{5,29},{6,30},{7,31},{8,16},{9,... | collective-permute-start | bytes 221192 | tf_op jit(solution)/shard_map/ppermute | solution.py:462
  42.2 5.1 %collective-permute-start.7 = (bf16[1,96,384]{2,1,0:T(8,128)(2,1)S(1)}, bf16[1,96,384]{2,1,0:T(8,128)(2,1)S(1)}, u32[]{:S(2)}, u32[]{:S(2)}) collective-permute-start(bf16[1,96,384]{2,1,0:T(8,128)(2,1)S(1)} %get-tuple-element.167), channel_id=1, source_target_pairs={{0,8},{1,9},{2,10},{3,11},{4,12},{5,13},{6,14},{7,15},{8,0},{9,1},... | collective-permute-start | bytes 221192 | tf_op jit(solution)/shard_map/ppermute | solution.py:462
  42.5 5.0 %collective-permute-start.5 = (bf16[8,16,384]{2,1,0:T(8,128)(2,1)S(1)}, bf16[8,16,384]{2,1,0:T(8,128)(2,1)S(1)}, u32[]{:S(2)}, u32[]{:S(2)}) collective-permute-start(bf16[8,16,384]{2,1,0:T(8,128)(2,1)S(1)} %add_convert_fusion.4), channel_id=1, source_target_pairs={{0,2},{1,5},{2,0},{3,7},{4,6},{5,1},{6,4},{7,3},{8,10},{9,13},{10,... | collective-permute-start | bytes 294920 | tf_op jit(solution)/shard_map/ppermute | solution.py:462
  47.7 7.3 %collective-permute-start.10 = (bf16[4,112,384]{2,1,0:T(8,128)(2,1)S(1)}, bf16[4,112,384]{2,1,0:T(8,128)(2,1)S(1)}, u32[]{:S(2)}, u32[]{:S(2)}) collective-permute-start(bf16[4,112,384]{2,1,0:T(8,128)(2,1)S(1)} %pad_maximum_fusion), channel_id=1, source_target_pairs={{0,4},{1,3},{2,6},{3,1},{4,0},{5,7},{6,2},{7,5},{8,12},{9,11},{10,... | collective-permute-start | bytes 1032200 | tf_op jit(solution)/shard_map/ppermute | solution.py:462
  49.3 9.9 %collective-permute-start.20 = (bf16[1,96,384]{2,1,0:T(8,128)(2,1)S(1)}, bf16[1,96,384]{2,1,0:T(8,128)(2,1)S(1)}, u32[]{:S(2)}, u32[]{:S(2)}) collective-permute-start(bf16[1,96,384]{2,1,0:T(8,128)(2,1)S(1)} %add_convert_fusion.8), channel_id=1, source_target_pairs={{0,16},{1,17},{2,18},{3,19},{4,20},{5,21},{6,22},{7,23},{8,24},{9,... | collective-permute-start | bytes 221192 | tf_op jit(solution)/shard_map/ppermute | solution.py:462
  52.2 7.1 %collective-permute-start.21 = (bf16[1,96,384]{2,1,0:T(8,128)(2,1)S(1)}, bf16[1,96,384]{2,1,0:T(8,128)(2,1)S(1)}, u32[]{:S(2)}, u32[]{:S(2)}) collective-permute-start(bf16[1,96,384]{2,1,0:T(8,128)(2,1)S(1)} %add_convert_fusion.8), channel_id=1, source_target_pairs={{0,8},{1,9},{2,10},{3,11},{4,12},{5,13},{6,14},{7,15},{8,0},{9,1},... | collective-permute-start | bytes 221192 | tf_op jit(solution)/shard_map/ppermute | solution.py:462
  52.9 6.9 %collective-permute-start.22 = (bf16[1,96,384]{2,1,0:T(8,128)(2,1)S(1)}, bf16[1,96,384]{2,1,0:T(8,128)(2,1)S(1)}, u32[]{:S(2)}, u32[]{:S(2)}) collective-permute-start(bf16[1,96,384]{2,1,0:T(8,128)(2,1)S(1)} %add_convert_fusion.8), channel_id=1, source_target_pairs={{0,24},{1,25},{2,26},{3,27},{4,28},{5,29},{6,30},{7,31},{8,16},{9,... | collective-permute-start | bytes 221192 | tf_op jit(solution)/shard_map/ppermute | solution.py:462
  55.2 8.6 %collective-permute-start.13 = (bf16[1,112,384]{2,1,0:T(8,128)(2,1)S(1)}, bf16[1,112,384]{2,1,0:T(8,128)(2,1)S(1)}, u32[]{:S(2)}, u32[]{:S(2)}) collective-permute-start(bf16[1,112,384]{2,1,0:T(8,128)(2,1)S(1)} %pad_maximum_fusion.5), channel_id=1, source_target_pairs={{0,16},{1,17},{2,18},{3,19},{4,20},{5,21},{6,22},{7,23},{8,24},{9,... | collective-permute-start | bytes 258056 | tf_op jit(solution)/shard_map/ppermute | solution.py:462
  58.2 6.5 %collective-permute-start.12 = (bf16[1,112,384]{2,1,0:T(8,128)(2,1)S(1)}, bf16[1,112,384]{2,1,0:T(8,128)(2,1)S(1)}, u32[]{:S(2)}, u32[]{:S(2)}) collective-permute-start(bf16[1,112,384]{2,1,0:T(8,128)(2,1)S(1)} %pad_maximum_fusion.4), channel_id=1, source_target_pairs={{0,24},{1,25},{2,26},{3,27},{4,28},{5,29},{6,30},{7,31},{8,16},{9,... | collective-permute-start | bytes 258056 | tf_op jit(solution)/shard_map/ppermute | solution.py:462
  59.2 6.1 %collective-permute-start.11 = (bf16[1,112,384]{2,1,0:T(8,128)(2,1)S(1)}, bf16[1,112,384]{2,1,0:T(8,128)(2,1)S(1)}, u32[]{:S(2)}, u32[]{:S(2)}) collective-permute-start(bf16[1,112,384]{2,1,0:T(8,128)(2,1)S(1)} %pad_maximum_fusion.3), channel_id=1, source_target_pairs={{0,8},{1,9},{2,10},{3,11},{4,12},{5,13},{6,14},{7,15},{8,0},{9,1},... | collective-permute-start | bytes 258056 | tf_op jit(solution)/shard_map/ppermute | solution.py:462
  59.9 7.2 %collective-permute-start.23 = (bf16[4,96,384]{2,1,0:T(8,128)(2,1)S(1)}, bf16[4,96,384]{2,1,0:T(8,128)(2,1)S(1)}, u32[]{:S(2)}, u32[]{:S(2)}) collective-permute-start(bf16[4,96,384]{2,1,0:T(8,128)(2,1)S(1)} %pad_maximum_fusion.2), channel_id=1, source_target_pairs={{0,4},{1,3},{2,6},{3,1},{4,0},{5,7},{6,2},{7,5},{8,12},{9,11},{10,... | collective-permute-start | bytes 884744 | tf_op jit(solution)/shard_map/ppermute | solution.py:462
  67.1 11.9 %collective-permute-start.24 = (bf16[8,96,384]{2,1,0:T(8,128)(2,1)S(1)}, bf16[8,96,384]{2,1,0:T(8,128)(2,1)S(1)}, u32[]{:S(2)}, u32[]{:S(2)}) collective-permute-start(bf16[8,96,384]{2,1,0:T(8,128)(2,1)S(1)} %constant_dynamic-update-slice_fusion.5.refs_0_), channel_id=1, source_target_pairs={{0,2},{1,5},{2,0},{3,7},{4,6},{5,1},{6,4},{7,3},{8,10},{9,13},{10,... | collective-permute-start | bytes 1769480 | tf_op jit(solution)/shard_map/ppermute | solution.py:462
  68.3 7.4 %collective-permute-start.14 = (bf16[1,112,384]{2,1,0:T(8,128)(2,1)S(1)}, bf16[1,112,384]{2,1,0:T(8,128)(2,1)S(1)}, u32[]{:S(2)}, u32[]{:S(2)}) collective-permute-start(bf16[1,112,384]{2,1,0:T(8,128)(2,1)S(1)} %get-tuple-element.162), channel_id=1, source_target_pairs={{0,16},{1,17},{2,18},{3,19},{4,20},{5,21},{6,22},{7,23},{8,24},{9,... | collective-permute-start | bytes 258056 | tf_op jit(solution)/shard_map/ppermute | solution.py:462
  70.8 5.3 %collective-permute-start.15 = (bf16[1,112,384]{2,1,0:T(8,128)(2,1)S(1)}, bf16[1,112,384]{2,1,0:T(8,128)(2,1)S(1)}, u32[]{:S(2)}, u32[]{:S(2)}) collective-permute-start(bf16[1,112,384]{2,1,0:T(8,128)(2,1)S(1)} %get-tuple-element.162), channel_id=1, source_target_pairs={{0,8},{1,9},{2,10},{3,11},{4,12},{5,13},{6,14},{7,15},{8,0},{9,1},... | collective-permute-start | bytes 258056 | tf_op jit(solution)/shard_map/ppermute | solution.py:462
  70.9 6.4 %collective-permute-start.16 = (bf16[1,112,384]{2,1,0:T(8,128)(2,1)S(1)}, bf16[1,112,384]{2,1,0:T(8,128)(2,1)S(1)}, u32[]{:S(2)}, u32[]{:S(2)}) collective-permute-start(bf16[1,112,384]{2,1,0:T(8,128)(2,1)S(1)} %get-tuple-element.162), channel_id=1, source_target_pairs={{0,24},{1,25},{2,26},{3,27},{4,28},{5,29},{6,30},{7,31},{8,16},{9,... | collective-permute-start | bytes 258056 | tf_op jit(solution)/shard_map/ppermute | solution.py:462
  77.3 7.3 %collective-permute-start.17 = (bf16[4,112,384]{2,1,0:T(8,128)(2,1)S(1)}, bf16[4,112,384]{2,1,0:T(8,128)(2,1)S(1)}, u32[]{:S(2)}, u32[]{:S(2)}) collective-permute-start(bf16[4,112,384]{2,1,0:T(8,128)(2,1)S(1)} %pad_maximum_fusion.1), channel_id=1, source_target_pairs={{0,4},{1,3},{2,6},{3,1},{4,0},{5,7},{6,2},{7,5},{8,12},{9,11},{10,... | collective-permute-start | bytes 1032200 | tf_op jit(solution)/shard_map/ppermute | solution.py:462
  78.9 6.8 %collective-permute-start.25 = (bf16[8,96,384]{2,1,0:T(8,128)(2,1)S(1)}, bf16[8,96,384]{2,1,0:T(8,128)(2,1)S(1)}, u32[]{:S(2)}, u32[]{:S(2)}) collective-permute-start(bf16[8,96,384]{2,1,0:T(8,128)(2,1)S(1)} %constant_dynamic-update-slice_fusion.5.refs_0_), channel_id=1, source_target_pairs={{0,1},{1,0},{2,3},{3,2},{4,5},{5,4},{6,7},{7,6},{8,9},{9,8},{10,11... | collective-permute-start | bytes 1769480 | tf_op jit(solution)/shard_map/ppermute | solution.py:462
  79.0 6.8 %collective-permute-start.26 = (bf16[8,96,384]{2,1,0:T(8,128)(2,1)S(1)}, bf16[8,96,384]{2,1,0:T(8,128)(2,1)S(1)}, u32[]{:S(2)}, u32[]{:S(2)}) collective-permute-start(bf16[8,96,384]{2,1,0:T(8,128)(2,1)S(1)} %collective-permute-done.24.refs_1_), channel_id=1, source_target_pairs={{0,1},{1,0},{2,3},{3,2},{4,5},{5,4},{6,7},{7,6},{8,9},{9,8},{10,11... | collective-permute-start | bytes 1769480 | tf_op jit(solution)/shard_map/ppermute | solution.py:462
  84.7 3.9 %collective-permute-start.19 = (bf16[8,112,384]{2,1,0:T(8,128)(2,1)S(1)}, bf16[8,112,384]{2,1,0:T(8,128)(2,1)S(1)}, u32[]{:S(2)}, u32[]{:S(2)}) collective-permute-start(bf16[8,112,384]{2,1,0:T(8,128)(2,1)S(1)} %constant_dynamic-update-slice_fusion.refs_0_.held), channel_id=1, source_target_pairs={{0,1},{1,0},{2,3},{3,2},{4,5},{5,4},{6,7},{7,6},{8,9},{9,8},{10,11... | collective-permute-start | bytes 2064392 | tf_op jit(solution)/shard_map/ppermute | solution.py:462
  84.8 11.0 %collective-permute-start.18 = (bf16[8,112,384]{2,1,0:T(8,128)(2,1)S(1)}, bf16[8,112,384]{2,1,0:T(8,128)(2,1)S(1)}, u32[]{:S(2)}, u32[]{:S(2)}) collective-permute-start(bf16[8,112,384]{2,1,0:T(8,128)(2,1)S(1)} %constant_dynamic-update-slice_fusion.refs_0_.held), channel_id=1, source_target_pairs={{0,2},{1,5},{2,0},{3,7},{4,6},{5,1},{6,4},{7,3},{8,10},{9,13},{10,... | collective-permute-start | bytes 2064392 | tf_op jit(solution)/shard_map/ppermute | solution.py:462
  95.8 2.1 %collective-permute-start.27 = (bf16[8,112,384]{2,1,0:T(8,128)(2,1)S(1)}, bf16[8,112,384]{2,1,0:T(8,128)(2,1)S(1)}, u32[]{:S(2)}, u32[]{:S(2)}) collective-permute-start(bf16[8,112,384]{2,1,0:T(8,128)(2,1)S(1)} %collective-permute-done.18.refs_0_.late), channel_id=1, source_target_pairs={{0,1},{1,0},{2,3},{3,2},{4,5},{5,4},{6,7},{7,6},{8,9},{9,8},{10,11... | collective-permute-start | bytes 2064392 | tf_op jit(solution)/shard_map/ppermute | solution.py:462

commit v5 on v4

--- a/solution.py
+++ b/solution.py
@@ -14,7 +14,8 @@
 HALF = BLOCKS // 2
 SCATTERED = 5
 LANES = 384
-VECTOR_ROWS = 16
+SMALL_ROWS = 8
+VECTOR_ROWS = 24
 BF = jnp.bfloat16
 F32 = jnp.float32
 VMEM = pl.BlockSpec(memory_space=pltpu.VMEM)
@@ -25,6 +26,7 @@
 MIXER_AFF_SCALE, MIXER_AFF_SHIFT, MIXER_OUT_BIAS, MIXER_SCALE = 4, 5, 6, 7
 MIXER_IN_BIAS = 8
 SQUARES = 12
+CROSS_REST = 16
 
 
 def dot(a, b, a_dim=1, b_dim=0):
@@ -289,7 +291,7 @@
         aff_scale_grad += row_sum(normed_grad * stream)
         aff_shift_grad += row_sum(normed_grad)
         write(target_ref, rows, rounded(upper + normed_grad * aff_scale))
-    weight_grad_ref[...] = weight_grad
+    weight_grad_ref[0:padded, 0:padded] = weight_grad
     vectors_ref[layer, CROSS_AFF_SCALE : CROSS_AFF_SCALE + 1, :] = aff_scale_grad
     vectors_ref[layer, CROSS_AFF_SHIFT : CROSS_AFF_SHIFT + 1, :] = aff_shift_grad
     vectors_ref[layer, CROSS_SCALE : CROSS_SCALE + 1, :] = scale_grad
@@ -424,6 +426,28 @@
     gather_rows(leaving, output)
 
 
+def pack_small(weight_grads, vectors_ref, small_ref, patches):
+    groups = -(-patches // SMALL_ROWS)
+    rows = groups * SMALL_ROWS
+    first, second = (grad[0:rows, 128:256] for grad in weight_grads)
+    lane = lax.broadcasted_iota(jnp.int32, (rows, 128), 1)
+    shared = jnp.where(lane < 64, first, pltpu.roll(second, 64, 1))
+    blocks = [grad[0:rows, 0:128] for grad in weight_grads] + [shared]
+    small_ref[...] = jnp.zeros_like(small_ref)
+    for part, block in enumerate(blocks):
+        small_ref[0:groups, :, part * 128 : (part + 1) * 128] = block.astype(BF).reshape(
+            groups, SMALL_ROWS, 128
+        )
+    for layer, grad in enumerate(weight_grads):
+        rest = jnp.transpose(grad[:, 128:256])[64 : 64 + SMALL_ROWS]
+        vectors_ref[layer, CROSS_REST : CROSS_REST + SMALL_ROWS, 0:256] = rest
+        for piece in range(VECTOR_ROWS // SMALL_ROWS):
+            at = groups + layer * (VECTOR_ROWS // SMALL_ROWS) + piece
+            small_ref[at] = vectors_ref[
+                layer, piece * SMALL_ROWS : (piece + 1) * SMALL_ROWS, :
+            ].astype(BF)
+
+
 def fourth_kernel(
     mesh_shape,
     s0, g1, kept_weight, keep, bias_columns, weight_grad1, vectors_in,
@@ -438,14 +462,7 @@
         0, s0, g1, g0, weight_grad0, vectors, kept_weight, keep, bias_columns,
         cross_aff_scale, cross_aff_shift, cross_scale, padded_low, padded_mixing, patches, each,
     )
-    layers, padded = kept_weight.shape[0], kept_weight.shape[2]
-    groups = padded // VECTOR_ROWS
-    small[...] = jnp.zeros_like(small)
-    for layer, weight_grad in enumerate((weight_grad0, weight_grad1)):
-        for group in range(groups):
-            rows = slice(group * VECTOR_ROWS, (group + 1) * VECTOR_ROWS)
-            small[layer * groups + group, :, 0:padded] = weight_grad[rows, :].astype(BF)
-        small[layers * groups + layer] = vectors[layer].astype(BF)
+    pack_small((weight_grad0, weight_grad1), vectors, small, patches)
     pack_halves(own_codes(mesh_shape), lambda block: (small[block],), kept, sent)
     gather_rows(g0, input_grad)
 
@@ -528,7 +545,9 @@
     return lax.optimization_barrier((values, *others))[0]
 
 
-def unpack_quarters(mesh_shape, images_all, layer, plan, quarters, inner_out, outer_out, stage, sems):
+def unpack_quarters(
+    mesh_shape, images_all, layer, plan, quarters, inner_out, outer_out, stage, sems, meanwhile=None
+):
     codes = own_codes(mesh_shape)
     quarter, depth = HALF // 2, stage.shape[2]
     columns = inner_out.shape[2]
@@ -559,6 +578,8 @@
                 stage[kind, number * quarter + slot] = block.astype(F32) / images_all
                 copy.start()
 
+    if meanwhile is not None:
+        meanwhile()
     for number in range(len(quarters)):
 
         @pl.loop(0, quarter)
@@ -570,64 +591,89 @@
 QUARTERS = ((kept_block, 0), (kept_block, HALF // 2), (sent_block, 0), (sent_block, HALF // 2))
 
 
-def unpack_first(mesh_shape, images_all, layer, numbers, *refs):
-    quarters, outs = refs[: len(numbers)], refs[len(numbers) :]
-    unpack_quarters(mesh_shape, images_all, layer, [QUARTERS[n] for n in numbers], quarters, *outs)
-
-
-def unpack_more(mesh_shape, images_all, layer, numbers, *refs):
-    quarters, outs = refs[: len(numbers)], refs[len(numbers) + 2 :]
-    unpack_quarters(mesh_shape, images_all, layer, [QUARTERS[n] for n in numbers], quarters, *outs)
+def unpack_small(mesh_shape, plan, quarters, small_rows, depth):
+    codes = own_codes(mesh_shape)
+    for (block_of, base), values in zip(plan, quarters):
+
+        @pl.loop(0, HALF // 2)
+        def _(slot):
+            small_rows[block_of(codes, slot + base)] = values[slot, 2 * depth :, :].astype(F32)
+
+
+def unpack_last_layer(mesh_shape, images_all, *refs):
+    unpack_quarters(mesh_shape, images_all, 1, QUARTERS, refs[:4], *refs[4:])
+
+
+def unpack_held(
+    mesh_shape, images_all, held, other_held, inner_in, outer_in,
+    inner_out, outer_out, small_rows, stage, sems,
+):
+    plan, quarters = (QUARTERS[0], QUARTERS[2]), (held, other_held)
+    unpack_quarters(mesh_shape, images_all, 0, plan, quarters, inner_out, outer_out, stage, sems)
+    unpack_small(mesh_shape, plan, quarters, small_rows, stage.shape[2])
+
+
+def unpack_late(
+    mesh_shape, images_all, late, inner_in, outer_in, small_in,
+    inner_out, outer_out, small_rows, stage, sems,
+):
+    plan, quarters = QUARTERS[1:2], (late,)
+    unpack_quarters(mesh_shape, images_all, 0, plan, quarters, inner_out, outer_out, stage, sems)
+    unpack_small(mesh_shape, plan, quarters, small_rows, stage.shape[2])
 
 
 def unpack_rest(
-    mesh_shape, images_all, held, late, other_held, other_late, inner_in, outer_in,
-    inner_out, outer_out, weight_out, aff_scale_out, aff_shift_out, cross_bias_out,
+    mesh_shape, images_all, other_late, inner_in, outer_in, small_in,
+    inner_out, outer_out, small_rows, weight_out, aff_scale_out, aff_shift_out, cross_bias_out,
     cross_scale_out, mixer_aff_scale_out, mixer_aff_shift_out, inner_bias_out, outer_bias_out,
     mixer_scale_out, magnitudes_out,
-    stage, weight_rows, vectors, sems,
+    stage, rest_rows, sems,
 ):
     patches, layers, _ = weight_out.shape
-    groups = weight_rows.shape[1] // VECTOR_ROWS
-    codes = own_codes(mesh_shape)
-    for values, (block_of, base) in zip((held, late, other_held, other_late), QUARTERS):
-
-        @pl.loop(0, HALF // 2)
-        def _(slot):
-            block = block_of(codes, slot + base)
-            small = values[slot, 2 * stage.shape[2] :, :].astype(F32) / images_all
-
-            @pl.when(block < layers * groups)
-            def _():
-                at = pl.multiple_of((block % groups) * VECTOR_ROWS, VECTOR_ROWS)
-                weight_rows[block // groups, pl.ds(at, VECTOR_ROWS), :] = small
-
-            @pl.when((block >= layers * groups) & (block < layers * (groups + 1)))
-            def _():
-                vectors[block - layers * groups] = small
-
-    for layer in range(layers):
-        row = slice(layer, layer + 1)
-        weight_out[:, layer, :] = weight_rows[layer, 0:patches, 0:patches]
-        aff_scale_out[row, :] = vectors[layer, CROSS_AFF_SCALE : CROSS_AFF_SCALE + 1, :]
-        aff_shift_out[row, :] = vectors[layer, CROSS_AFF_SHIFT : CROSS_AFF_SHIFT + 1, :]
-        cross_bias_out[row, :] = vectors[layer, CROSS_BIAS : CROSS_BIAS + 1, 0:patches]
-        cross_scale_out[row, :] = vectors[layer, CROSS_SCALE : CROSS_SCALE + 1, :]
-        mixer_aff_scale_out[row, :] = vectors[layer, MIXER_AFF_SCALE : MIXER_AFF_SCALE + 1, :]
-        mixer_aff_shift_out[row, :] = vectors[layer, MIXER_AFF_SHIFT : MIXER_AFF_SHIFT + 1, :]
-        outer_bias_out[row, :] = vectors[layer, MIXER_OUT_BIAS : MIXER_OUT_BIAS + 1, :]
-        mixer_scale_out[row, :] = vectors[layer, MIXER_SCALE : MIXER_SCALE + 1, :]
-        for piece in range(SQUARES - MIXER_IN_BIAS):
-            at = slice(piece * LANES, (piece + 1) * LANES)
-            inner_bias_out[row, at] = vectors[layer, MIXER_IN_BIAS + piece : MIXER_IN_BIAS + piece + 1, :]
-        squares = vectors[layer, SQUARES : SQUARES + 4, :] / (patches * LANES)
-        means = jnp.sqrt(jnp.sum(squares, axis=1, keepdims=True))
-        for kind in range(2):
-            for which in range(2):
-                at = 2 * kind + which
-                magnitudes_out[layer, kind : kind + 1, which : which + 1] = means[at : at + 1]
+    plan, quarters = QUARTERS[3:], (other_late,)
+
+    def small_gradients():
+        unpack_small(mesh_shape, plan, quarters, small_rows, stage.shape[2])
+        groups = -(-patches // SMALL_ROWS)
+        weights = (small_rows[0:groups] / images_all).reshape(groups * SMALL_ROWS, LANES)[0:patches]
+        pieces = VECTOR_ROWS // SMALL_ROWS
+        lane = lax.broadcasted_iota(jnp.int32, (patches, 128), 1)
+        for layer in range(layers):
+            row = slice(layer, layer + 1)
+            at = groups + layer * pieces
+            vectors = (small_rows[at : at + pieces] / images_all).reshape(VECTOR_ROWS, LANES)
+            rest_rows[...] = jnp.zeros_like(rest_rows)
+            rest_rows[64 : 64 + SMALL_ROWS, :] = vectors[CROSS_REST:, 0:256]
+            rest = jnp.transpose(rest_rows[...])[0:patches]
+            shared = weights[:, 256:384]
+            if layer:
+                shared = pltpu.roll(shared, 64, 1)
+            last = jnp.where(lane < 64, shared, rest)
+            weight_out[:, layer, 0:128] = weights[:, layer * 128 : (layer + 1) * 128]
+            weight_out[:, layer, 128:] = last[:, 0 : patches - 128]
+            for out, index in (
+                (aff_scale_out, CROSS_AFF_SCALE),
+                (aff_shift_out, CROSS_AFF_SHIFT),
+                (cross_scale_out, CROSS_SCALE),
+                (mixer_aff_scale_out, MIXER_AFF_SCALE),
+                (mixer_aff_shift_out, MIXER_AFF_SHIFT),
+                (outer_bias_out, MIXER_OUT_BIAS),
+                (mixer_scale_out, MIXER_SCALE),
+            ):
+                out[row, :] = vectors[index : index + 1]
+            cross_bias_out[row, :] = vectors[CROSS_BIAS : CROSS_BIAS + 1, 0:patches]
+            for piece in range(SQUARES - MIXER_IN_BIAS):
+                index = MIXER_IN_BIAS + piece
+                inner_bias_out[row, piece * LANES : (piece + 1) * LANES] = vectors[index : index + 1]
+            squares = vectors[SQUARES : SQUARES + 4] / (patches * LANES)
+            means = jnp.sqrt(jnp.sum(squares, axis=1, keepdims=True))
+            for kind in range(2):
+                for which in range(2):
+                    index = 2 * kind + which
+                    magnitudes_out[layer, kind : kind + 1, which : which + 1] = means[index : index + 1]
+
     unpack_quarters(
-        mesh_shape, images_all, 0, [QUARTERS[3]], (other_late,), inner_out, outer_out, stage, sems
+        mesh_shape, images_all, 0, plan, quarters, inner_out, outer_out, stage, sems, small_gradients
     )
 
 
@@ -758,7 +804,7 @@
             )),
             aff_scale, aff_shift, scale, mixer_aff,
         ),
-        (stream, vmem(padded, padded, dtype=F32), vectors),
+        (stream, vmem(256, 256, dtype=F32), vectors),
         [stream, padded_images, padded_images],
         us=4,
     )
@@ -784,7 +830,7 @@
     main0 = [kept0, exchange_bits(sent0, mesh_shape, [0])]
     leaving1, main1 = halve(main1, HALF // 2, mesh_shape, 2)
     sums = after(sums, leaving1)
-    halves = vmem(HALF, VECTOR_ROWS, LANES)
+    halves = vmem(HALF, SMALL_ROWS, LANES)
     input_grad, kept_small, sent_small = call(
         functools.partial(fourth_kernel, mesh_shape),
         "first_cross",
@@ -795,9 +841,9 @@
         (hbm(*local, dtype=BF), halves, halves),
         [
             stream,
-            vmem(padded, padded, dtype=F32),
+            vmem(256, 256, dtype=F32),
             vectors,
-            vmem(BLOCKS, VECTOR_ROWS, LANES),
+            vmem(BLOCKS, SMALL_ROWS, LANES),
             padded_images,
             padded_images,
         ],
@@ -816,16 +862,18 @@
     four1 = join(own1, after(peers1, leaving0))
     own0 = sum_last(terms0, arrived0, mesh_shape)
     more1 = exchange_bits(four1, mesh_shape, [2])
+    late1 = exchange_bits(four1, mesh_shape, [1])
     peers0 = gather_last(own0, mesh_shape)
     more1 = after(more1, own0)
+    latest1 = exchange_bits(more1, mesh_shape, [1])
+    four0 = join(own0, after(peers0, more1))
     held1 = jnp.concatenate([four1, more1], axis=0)
-    four0 = join(own0, peers0)
-    late1 = exchange_bits(held1, mesh_shape, [1])
     other_held1 = exchange_bits(held1, mesh_shape, [0])
-    late1 = after(late1, four0)
-    held0 = double(four0, mesh_shape, 2)
+    more0 = exchange_bits(four0, mesh_shape, [2])
+    late1, latest1 = after((late1, latest1), more0)
+    late1 = jnp.concatenate([late1, latest1], axis=0)
+    held0 = jnp.concatenate([four0, more0], axis=0)
     other_late1 = exchange_bits(late1, mesh_shape, [0])
-    other_late1 = after(other_late1, held0)
     late0 = exchange_bits(held0, mesh_shape, [1])
     other_held0 = exchange_bits(held0, mesh_shape, [0])
     quarters1 = (held1, late1, other_held1, other_late1)
@@ -838,8 +886,9 @@
             pltpu.SemaphoreType.DMA((2, quarters * quarter)),
         ]
 
+    small_rows = vmem(BLOCKS, SMALL_ROWS, LANES, dtype=F32)
     grads = call(
-        functools.partial(unpack_first, mesh_shape, images_all, 1, (0, 1, 2, 3)),
+        functools.partial(unpack_last_layer, mesh_shape, images_all),
         "unpack_last_layer",
         in_vmem(quarters1),
         (inner_out, outer_out),
@@ -847,49 +896,49 @@
         out_specs=[HBM] * 2,
         us=3,
     )
-    grads = call(
-        functools.partial(unpack_more, mesh_shape, images_all, 0, (0, 2)),
+    *grads, rows_held = call(
+        functools.partial(unpack_held, mesh_shape, images_all),
         "unpack_held",
         (*in_vmem((held0, other_held0)), *grads),
-        (inner_out, outer_out),
+        (inner_out, outer_out, small_rows),
         staging(2),
         in_specs=[VMEM] * 2 + [HBM] * 2,
-        out_specs=[HBM] * 2,
+        out_specs=[HBM] * 2 + [VMEM],
         aliases={2: 0, 3: 1},
         us=2,
     )
     late0, grads = lax.optimization_barrier((late0, grads))
     other_late0 = exchange_bits(late0, mesh_shape, [0])
-    grads = call(
-        functools.partial(unpack_more, mesh_shape, images_all, 0, (1,)),
+    *grads, rows_held = call(
+        functools.partial(unpack_late, mesh_shape, images_all),
         "unpack_late",
-        (*in_vmem((late0,)), *grads),
-        (inner_out, outer_out),
+        (*in_vmem((late0,)), *grads, *in_vmem((rows_held,))),
+        (inner_out, outer_out, small_rows),
         staging(1),
-        in_specs=[VMEM] + [HBM] * 2,
-        out_specs=[HBM] * 2,
-        aliases={1: 0, 2: 1},
+        in_specs=[VMEM] + [HBM] * 2 + [VMEM],
+        out_specs=[HBM] * 2 + [VMEM],
+        aliases={1: 0, 2: 1, 3: 2},
         us=1,
     )
     row = hbm(layers, width)
     stage, sems = staging(1)
     (
-        inner_grad, outer_grad, weight_grad, aff_scale_grad, aff_shift_grad, bias_grad,
+        inner_grad, outer_grad, _, weight_grad, aff_scale_grad, aff_shift_grad, bias_grad,
         scale_grad, mixer_aff_scale_grad, mixer_aff_shift_grad, inner_bias_grad,
         outer_bias_grad, mixer_scale_grad, magnitudes,
     ) = call(
         functools.partial(unpack_rest, mesh_shape, images_all),
         "unpack_rest",
-        (*in_vmem((held0, late0, other_held0, other_late0)), *grads),
+        (*in_vmem((other_late0,)), *grads, *in_vmem((rows_held,))),
         (
-            inner_out, outer_out, hbm(patches, layers, patches), row, row,
+            inner_out, outer_out, small_rows, hbm(patches, layers, patches), row, row,
             hbm(layers, patches), row, row, row, hbm(layers, columns), row, row,
             hbm(layers, 2, 2),
         ),
-        [stage, vmem(layers, padded, LANES, dtype=F32), vectors, sems],
-        in_specs=[VMEM] * 4 + [HBM] * 2,
-        out_specs=[HBM] * 2 + [VMEM] * 11,
-        aliases={4: 0, 5: 1},
+        [stage, vmem(128, 256, dtype=F32), sems],
+        in_specs=[VMEM] + [HBM] * 2 + [VMEM],
+        out_specs=[HBM] * 2 + [VMEM] * 12,
+        aliases={1: 0, 2: 1, 3: 2},
         us=2,
     )
     return (

time: 101 us -> 98.1 us (0.971)
  waiting for transfers between devices: 28.8 us -> 26.7 us
    ppermute x28 -> x29, waiting for transfers between devices: 28.8 us -> 26.7 us  [exchange_bits(): return lax.ppermute(values, AXES, [(i, partner(i)) for i in places])]
    ppermute x28 -> x29, starting transfers between devices: 31.6 us -> 31.6 us  [exchange_bits(): return lax.ppermute(values, AXES, [(i, partner(i)) for i in places])]
  transfers between devices with their start and end apart: 28 -> 29, of which waited for: 16 -> 16; matrix products, arithmetic and copies ran while one was open for 1% -> 1% of each run, Pallas kernels for 20% -> 20%
where the time goes in v5:
time: 98.1 us; the launch traced here: 97.9 us
  Pallas kernels  37.1 us (38%)
  starting transfers between devices  31.6 us (32%)
  waiting for transfers between devices  26.7 us (27%)
  other arithmetic  1.09 us (1%)
  between operations  1.08 us (1%)
    pallas_call x8, Pallas kernels, call(): pl.pallas_call(kernel, out_shape=outs, in_specs=[VMEM] * len(args) if in_...  37.1 us
    ppermute x29, starting transfers between devices, exchange_bits(): return lax.ppermute(values, AXES, [(i, partner(i)) for i in places])  31.6 us
    ppermute x29, waiting for transfers between devices, exchange_bits(): return lax.ppermute(values, AXES, [(i, partner(i)) for i in places])  26.7 us
  transfers between devices with their start and end apart: 29, of which 16 were waited for; matrix products, arithmetic and copies ran while one was open for 1% of the time, Pallas kernels for 20%

profile of v5, /device:TPU:0, one launch (start us, length us, event | category | flops | bytes accessed | tf_op | source)
XLA Modules:
  0.0 97.9 jit_solution(8682869621176125102)
XLA Ops:
  0.7 15.4 %forward.1 = (f32[2,384]{1,0:T(2,128)S(1)}, f32[2,384]{1,0:T(2,128)S(1)}, f32[2,384]{1,0:T(2,128)S(1)}, f32[2,384]{1,0:T(2,128)S(1)}, f32[2,384]{1,0:T(2,128)S(1...) custom-call(bf16[4,196,4,384]{3,2,1,0:T(4,128)(2,1)} %bitcast.6, ...), custom_call_target="tpu_custom_call" | custom-call | flops 17999998976 | bytes 54000000 | tf_op jit(solution)/shard_map/forward/pallas_call | solution.py:681
  16.0 0.5 collective-permute-start
  16.5 2.6 %last_layer.1 = (f32[3,784,128]{2,1,0:T(8,128)S(1)}, f32[256,256]{1,0:T(8,128)S(1)}, f32[2,24,384]{2,1,0:T(8,128)S(1)}) custom-call(f32[3,784,128]{2,1,0:T(8,128)S(1)} %get-tuple-element.94.s2, f32[3,784,128]{2,1,0:T(8,128)S(1)} %get-tuple-element.95.s3, f32[3,784,128]{2,1,0:T(8,128)S(1)} %get-tuple-element.96.g_rows, ...), custom_call_target="tpu_custom_call" | custom-call | flops 4000000000 | bytes 12000000 | tf_op jit(solution)/shard_map/last_layer/pallas_call | solution.py:681
  19.1 0.1 add_convert_fusion.1
  19.3 2.8 %collective-permute-start.1 = (bf16[8,96,384]{2,1,0:T(8,128)(2,1)S(1)}, bf16[8,96,384]{2,1,0:T(8,128)(2,1)S(1)}, u32[]{:S(2)}, u32[]{:S(2)}) collective-permute-start(bf16[8,96,384]{2,1,0:T(8,128)(2,1)S(1)} %add_convert_fusion.1), channel_id=1, source_target_pairs={{0,2},{1,5},{2,0},{3,7},{4,6},{5,1},{6,4},{7,3},{8,10},{9,13},{10,... | collective-permute-start | bytes 1769480 | tf_op jit(solution)/shard_map/ppermute | solution.py:479
  22.1 9.0 %first_feed_forward.1 = (bf16[16,96,384]{2,1,0:T(8,128)(2,1)S(1)}, bf16[16,96,384]{2,1,0:T(8,128)(2,1)S(1)}, f32[3,784,128]{2,1,0:T(8,128)S(1)}, f32[2,24,384]{2,1,0:T(8,128)S(1)}, bf16[1,196,4,384]{3,2,1,0:T(4,128)(2,1)}) custom-call(f32[3,784,128]{2,1,0:T(8,128)S(1)} %get-tuple-element.93.s1, f32[3,784,128]{2,1,0:T(8,128)S(1)} %get-tuple-element.110.g2, ...), custom_call_target="tpu_custom_call" | custom-call | flops 8999999488 | bytes 27000000 | tf_op jit(solution)/shard_map/first_feed_forward/pallas_call | solution.py:681
  31.1 0.1 add_convert_fusion.3
  31.2 1.6 %collective-permute-start.6 = (bf16[4,96,384]{2,1,0:T(8,128)(2,1)S(1)}, bf16[4,96,384]{2,1,0:T(8,128)(2,1)S(1)}, u32[]{:S(2)}, u32[]{:S(2)}) collective-permute-start(bf16[4,96,384]{2,1,0:T(8,128)(2,1)S(1)} %add_convert_fusion.3), channel_id=1, source_target_pairs={{0,4},{1,3},{2,6},{3,1},{4,0},{5,7},{6,2},{7,5},{8,12},{9,11},{10,... | collective-permute-start | bytes 884744 | tf_op jit(solution)/shard_map/ppermute | solution.py:479
  32.8 2.6 %first_cross.1 = (bf16[1,196,4,384]{3,2,1,0:T(4,128)(2,1)}, bf16[16,8,384]{2,1,0:T(8,128)(2,1)S(1)}, bf16[16,8,384]{2,1,0:T(8,128)(2,1)S(1)}) custom-call(f32[3,784,128]{2,1,0:T(8,128)S(1)} %get-tuple-element.123.s0, f32[3,784,128]{2,1,0:T(8,128)S(1)} %get-tuple-element.124.g1, bf16[2,4,208,208]{3,2,1,0:T(8,128)(2,1)S(1)} %get-tuple-element.99.kept_weight, ...), custom_call_target="tpu_custom_call" | custom-call | flops 5000000000 | bytes 15000000 | tf_op jit(solution)/shard_map/first_cross/pallas_call | solution.py:681
  35.4 0.2 add_convert_fusion
  35.5 0.9 collective-permute-start.3
  36.5 1.5 %collective-permute-done.6 = bf16[4,96,384]{2,1,0:T(8,128)(2,1)S(1)} collective-permute-done((bf16[4,96,384]{2,1,0:T(8,128)(2,1)S(1)}, bf16[4,96,384]{2,1,0:T(8,128)(2,1)S(1)}, u32[]{:S(2)}, u32[]{:S(2)}) %collective-permute-start.6) | collective-permute-done | bytes 294944 | tf_op jit(solution)/shard_map/ppermute | solution.py:479
  38.0 0.1 add_convert_fusion.10
  38.1 2.6 %collective-permute-start.9 = (bf16[1,96,384]{2,1,0:T(8,128)(2,1)S(1)}, bf16[1,96,384]{2,1,0:T(8,128)(2,1)S(1)}, u32[]{:S(2)}, u32[]{:S(2)}) collective-permute-start(bf16[1,96,384]{2,1,0:T(8,128)(2,1)S(1)} %get-tuple-element.178), channel_id=1, source_target_pairs={{0,16},{1,17},{2,18},{3,19},{4,20},{5,21},{6,22},{7,23},{8,24},{9,... | collective-permute-start | bytes 221192 | tf_op jit(solution)/shard_map/ppermute | solution.py:479
  40.8 1.3 %collective-permute-start.8 = (bf16[1,96,384]{2,1,0:T(8,128)(2,1)S(1)}, bf16[1,96,384]{2,1,0:T(8,128)(2,1)S(1)}, u32[]{:S(2)}, u32[]{:S(2)}) collective-permute-start(bf16[1,96,384]{2,1,0:T(8,128)(2,1)S(1)} %get-tuple-element.179), channel_id=1, source_target_pairs={{0,24},{1,25},{2,26},{3,27},{4,28},{5,29},{6,30},{7,31},{8,16},{9,... | collective-permute-start | bytes 221192 | tf_op jit(solution)/shard_map/ppermute | solution.py:479
  42.1 0.2 collective-permute-start.7
  42.4 1.6 %collective-permute-start.5 = (bf16[8,8,384]{2,1,0:T(8,128)(2,1)S(1)}, bf16[8,8,384]{2,1,0:T(8,128)(2,1)S(1)}, u32[]{:S(2)}, u32[]{:S(2)}) collective-permute-start(bf16[8,8,384]{2,1,0:T(8,128)(2,1)S(1)} %add_convert_fusion.11), channel_id=1, source_target_pairs={{0,2},{1,5},{2,0},{3,7},{4,6},{5,1},{6,4},{7,3},{8,10},{9,13},{10,... | collective-permute-start | bytes 147464 | tf_op jit(solution)/shard_map/ppermute | solution.py:479
  43.9 1.7 %collective-permute-done.9 = bf16[1,96,384]{2,1,0:T(8,128)(2,1)S(1)} collective-permute-done((bf16[1,96,384]{2,1,0:T(8,128)(2,1)S(1)}, bf16[1,96,384]{2,1,0:T(8,128)(2,1)S(1)}, u32[]{:S(2)}, u32[]{:S(2)}) %collective-permute-start.9) | collective-permute-done | bytes 73760 | tf_op jit(solution)/shard_map/ppermute | solution.py:479
  45.7 1.4 %collective-permute-done.8 = bf16[1,96,384]{2,1,0:T(8,128)(2,1)S(1)} collective-permute-done((bf16[1,96,384]{2,1,0:T(8,128)(2,1)S(1)}, bf16[1,96,384]{2,1,0:T(8,128)(2,1)S(1)}, u32[]{:S(2)}, u32[]{:S(2)}) %collective-permute-start.8) | collective-permute-done | bytes 73760 | tf_op jit(solution)/shard_map/ppermute | solution.py:479
  47.1 0.2 collective-permute-done.7
  47.3 0.1 add_convert_fusion.7
  47.4 0.0 collective-permute-done.3
  47.4 0.1 add_convert_fusion.2
  47.5 1.7 %collective-permute-start.10 = (bf16[4,104,384]{2,1,0:T(8,128)(2,1)S(1)}, bf16[4,104,384]{2,1,0:T(8,128)(2,1)S(1)}, u32[]{:S(2)}, u32[]{:S(2)}) collective-permute-start(bf16[4,104,384]{2,1,0:T(8,128)(2,1)S(1)} %pad_maximum_fusion), channel_id=1, source_target_pairs={{0,4},{1,3},{2,6},{3,1},{4,0},{5,7},{6,2},{7,5},{8,12},{9,11},{10,... | collective-permute-start | bytes 958472 | tf_op jit(solution)/shard_map/ppermute | solution.py:479
  49.3 2.8 %collective-permute-start.17 = (bf16[1,96,384]{2,1,0:T(8,128)(2,1)S(1)}, bf16[1,96,384]{2,1,0:T(8,128)(2,1)S(1)}, u32[]{:S(2)}, u32[]{:S(2)}) collective-permute-start(bf16[1,96,384]{2,1,0:T(8,128)(2,1)S(1)} %add_convert_fusion.7), channel_id=1, source_target_pairs={{0,16},{1,17},{2,18},{3,19},{4,20},{5,21},{6,22},{7,23},{8,24},{9,... | collective-permute-start | bytes 221192 | tf_op jit(solution)/shard_map/ppermute | solution.py:479
  52.1 0.7 collective-permute-start.18
  52.8 0.9 collective-permute-start.19
  53.7 0.9 collective-permute-done.10
  54.6 0.2 convert_add_fusion
  54.8 3.0 %collective-permute-start.13 = (bf16[1,104,384]{2,1,0:T(8,128)(2,1)S(1)}, bf16[1,104,384]{2,1,0:T(8,128)(2,1)S(1)}, u32[]{:S(2)}, u32[]{:S(2)}) collective-permute-start(bf16[1,104,384]{2,1,0:T(8,128)(2,1)S(1)} %pad_maximum_fusion.4), channel_id=1, source_target_pairs={{0,16},{1,17},{2,18},{3,19},{4,20},{5,21},{6,22},{7,23},{8,24},{9,... | collective-permute-start | bytes 239624 | tf_op jit(solution)/shard_map/ppermute | solution.py:479
  57.9 0.6 collective-permute-start.12
  58.5 0.0 collective-permute-done.17
  58.5 0.3 collective-permute-start.11
  58.8 1.1 %collective-permute-done.19 = bf16[1,96,384]{2,1,0:T(8,128)(2,1)S(1)} collective-permute-done((bf16[1,96,384]{2,1,0:T(8,128)(2,1)S(1)}, bf16[1,96,384]{2,1,0:T(8,128)(2,1)S(1)}, u32[]{:S(2)}, u32[]{:S(2)}) %collective-permute-start.19) | collective-permute-done | bytes 73760 | tf_op jit(solution)/shard_map/ppermute | solution.py:479
  60.0 0.4 collective-permute-start.20
  60.4 2.9 %collective-permute-done.13 = bf16[1,104,384]{2,1,0:T(8,128)(2,1)S(1)} collective-permute-done((bf16[1,104,384]{2,1,0:T(8,128)(2,1)S(1)}, bf16[1,104,384]{2,1,0:T(8,128)(2,1)S(1)}, u32[]{:S(2)}, u32[]{:S(2)}) %collective-permute-start.13) | collective-permute-done | bytes 79904 | tf_op jit(solution)/shard_map/ppermute | solution.py:479
  63.3 1.0 %collective-permute-done.12 = bf16[1,104,384]{2,1,0:T(8,128)(2,1)S(1)} collective-permute-done((bf16[1,104,384]{2,1,0:T(8,128)(2,1)S(1)}, bf16[1,104,384]{2,1,0:T(8,128)(2,1)S(1)}, u32[]{:S(2)}, u32[]{:S(2)}) %collective-permute-start.12) | collective-permute-done | bytes 79904 | tf_op jit(solution)/shard_map/ppermute | solution.py:479
  64.3 0.4 collective-permute-done.11
  64.7 2.4 %collective-permute-start.14 = (bf16[1,104,384]{2,1,0:T(8,128)(2,1)S(1)}, bf16[1,104,384]{2,1,0:T(8,128)(2,1)S(1)}, u32[]{:S(2)}, u32[]{:S(2)}) collective-permute-start(bf16[1,104,384]{2,1,0:T(8,128)(2,1)S(1)} %get-tuple-element.172), channel_id=1, source_target_pairs={{0,16},{1,17},{2,18},{3,19},{4,20},{5,21},{6,22},{7,23},{8,24},{9,... | collective-permute-start | bytes 239624 | tf_op jit(solution)/shard_map/ppermute | solution.py:479
  67.1 0.6 collective-permute-start.15
  67.7 1.5 %collective-permute-start.16 = (bf16[1,104,384]{2,1,0:T(8,128)(2,1)S(1)}, bf16[1,104,384]{2,1,0:T(8,128)(2,1)S(1)}, u32[]{:S(2)}, u32[]{:S(2)}) collective-permute-start(bf16[1,104,384]{2,1,0:T(8,128)(2,1)S(1)} %get-tuple-element.172), channel_id=1, source_target_pairs={{0,24},{1,25},{2,26},{3,27},{4,28},{5,29},{6,30},{7,31},{8,16},{9,... | collective-permute-start | bytes 239624 | tf_op jit(solution)/shard_map/ppermute | solution.py:479
  69.2 0.9 collective-permute-start.24
  70.1 0.0 collective-permute-done.20
  70.1 1.1 %collective-permute-start.25 = (bf16[4,96,384]{2,1,0:T(8,128)(2,1)S(1)}, bf16[4,96,384]{2,1,0:T(8,128)(2,1)S(1)}, u32[]{:S(2)}, u32[]{:S(2)}) collective-permute-start(bf16[4,96,384]{2,1,0:T(8,128)(2,1)S(1)} %collective-permute-done.20), channel_id=1, source_target_pairs={{0,2},{1,5},{2,0},{3,7},{4,6},{5,1},{6,4},{7,3},{8,10},{9,13},{10,... | collective-permute-start | bytes 884744 | tf_op jit(solution)/shard_map/ppermute | solution.py:479
  71.2 1.7 %collective-permute-done.14 = bf16[1,104,384]{2,1,0:T(8,128)(2,1)S(1)} collective-permute-done((bf16[1,104,384]{2,1,0:T(8,128)(2,1)S(1)}, bf16[1,104,384]{2,1,0:T(8,128)(2,1)S(1)}, u32[]{:S(2)}, u32[]{:S(2)}) %collective-permute-start.14) | collective-permute-done | bytes 79904 | tf_op jit(solution)/shard_map/ppermute | solution.py:479
  72.9 0.0 collective-permute-done.15
  72.9 1.2 %collective-permute-done.16 = bf16[1,104,384]{2,1,0:T(8,128)(2,1)S(1)} collective-permute-done((bf16[1,104,384]{2,1,0:T(8,128)(2,1)S(1)}, bf16[1,104,384]{2,1,0:T(8,128)(2,1)S(1)}, u32[]{:S(2)}, u32[]{:S(2)}) %collective-permute-start.16) | collective-permute-done | bytes 79904 | tf_op jit(solution)/shard_map/ppermute | solution.py:479
  74.1 0.1 pad_maximum_fusion.1
  74.2 1.5 %collective-permute-start.21 = (bf16[4,104,384]{2,1,0:T(8,128)(2,1)S(1)}, bf16[4,104,384]{2,1,0:T(8,128)(2,1)S(1)}, u32[]{:S(2)}, u32[]{:S(2)}) collective-permute-start(bf16[4,104,384]{2,1,0:T(8,128)(2,1)S(1)} %pad_maximum_fusion.1), channel_id=1, source_target_pairs={{0,4},{1,3},{2,6},{3,1},{4,0},{5,7},{6,2},{7,5},{8,12},{9,11},{10,... | collective-permute-start | bytes 958472 | tf_op jit(solution)/shard_map/ppermute | solution.py:479
  75.7 0.1 collective-permute-start.26
  75.8 0.5 collective-permute-done.24
  76.3 6.2 %collective-permute-done.25 = bf16[4,96,384]{2,1,0:T(8,128)(2,1)S(1)} collective-permute-done((bf16[4,96,384]{2,1,0:T(8,128)(2,1)S(1)}, bf16[4,96,384]{2,1,0:T(8,128)(2,1)S(1)}, u32[]{:S(2)}, u32[]{:S(2)}) %collective-permute-start.25) | collective-permute-done | bytes 294944 | tf_op jit(solution)/shard_map/ppermute | solution.py:479
  82.5 0.0 collective-permute-done.21
  82.6 0.1 collective-permute-start.27
  82.7 0.1 constant_dynamic-update-slice_fusion.4.held
  82.8 0.6 collective-permute-start.23
  83.3 0.9 collective-permute-start.22
  84.2 0.4 collective-permute-done.27.refs_3_
  84.7 2.7 %unpack_last_layer.1 = (f32[2,384,1536]{2,1,0:T(8,128)}, f32[2,1536,384]{2,1,0:T(8,128)}) custom-call(bf16[8,96,384]{2,1,0:T(8,128)(2,1)S(1)} %constant_dynamic-update-slice_fusion.9.refs_0_, bf16[8,96,384]{2,1,0:T(8,128)(2,1)S(1)} %constant_dynamic-update-slice_fusion.14.refs_1_, bf16[8,96,384]{2,1,0:T(8,128)(2,1)S(1)} %collective-permute-done.26.refs_2_, ...), custom_call_target="tpu_custom_call" | custom-call | flops 3000000000 | bytes 9000000 | tf_op jit(solution)/shard_map/unpack_last_layer/pallas_call | solution.py:681
  87.4 1.8 %unpack_held.1 = (f32[2,384,1536]{2,1,0:T(8,128)}, f32[2,1536,384]{2,1,0:T(8,128)}, f32[32,8,384]{2,1,0:T(8,128)S(1)}) custom-call(bf16[8,104,384]{2,1,0:T(8,128)(2,1)S(1)} %constant_dynamic-update-slice_fusion.4.held, bf16[8,104,384]{2,1,0:T(8,128)(2,1)S(1)} %collective-permute-done.23.other_held, ...), custom_call_target="tpu_custom_call", output_to_operand_aliasing={{0}: (2, {}), {1}: (3, {})} | custom-call | flops 2000000000 | bytes 6000000 | tf_op jit(solution)/shard_map/unpack_held/pallas_call | solution.py:681
  89.2 4.5 %collective-permute-done.22.late = bf16[8,104,384]{2,1,0:T(8,128)(2,1)S(1)} collective-permute-done((bf16[8,104,384]{2,1,0:T(8,128)(2,1)S(1)}, bf16[8,104,384]{2,1,0:T(8,128)(2,1)S(1)}, u32[]{:S(2)}, u32[]{:S(2)}) %collective-permute-start.22) | collective-permute-done | bytes 639008 | tf_op jit(solution)/shard_map/ppermute | solution.py:479
  93.7 1.2 %unpack_late.1 = (f32[2,384,1536]{2,1,0:T(8,128)}, f32[2,1536,384]{2,1,0:T(8,128)}, f32[32,8,384]{2,1,0:T(8,128)S(1)}) custom-call(bf16[8,104,384]{2,1,0:T(8,128)(2,1)S(1)} %collective-permute-done.22.late, f32[2,384,1536]{2,1,0:T(8,128)} %get-tuple-element.152.inner_in, ...), custom_call_target="tpu_custom_call", output_to_operand_aliasing={{0}: (1, {}), {1}: (2, {}), {2}: (3, {})} | custom-call | flops 1000000000 | bytes 3000000 | tf_op jit(solution)/shard_map/unpack_late/pallas_call | solution.py:681
  94.9 0.9 collective-permute-done.28.other_late
  95.8 1.9 %unpack_rest.1 = (f32[2,384,1536]{2,1,0:T(8,128)}, f32[2,1536,384]{2,1,0:T(8,128)}, f32[32,8,384]{2,1,0:T(8,128)S(1)}, f32[196,2,196]{2,1,0:T(2,128)}, f32[2,384...) custom-call(bf16[8,104,384]{2,1,0:T(8,128)(2,1)S(1)} %collective-per, ...), custom_call_target="tpu_custom_call", output_to_operand_aliasing={{0}: (1, {}), {1}: (2, {}), {2}: (3, {})} | custom-call | flops 2000000000 | bytes 6000000 | tf_op jit(solution)/shard_map/unpack_rest/pallas_call | solution.py:681
  (29 shorter events, 0.5 us)
Async XLA Ops:
  16.0 3.1 %collective-permute-start = (bf16[16,96,384]{2,1,0:T(8,128)(2,1)S(1)}, bf16[16,96,384]{2,1,0:T(8,128)(2,1)S(1)}, u32[]{:S(2)}, u32[]{:S(2)}) collective-permute-start(bf16[16,96,384]{2,1,0:T(8,128)(2,1)S(1)} %get-tuple-element.109), channel_id=1, source_target_pairs={{0,1},{1,0},{2,3},{3,2},{4,5},{5,4},{6,7},{7,6},{8,9},{9,8},{10,11... | collective-permute-start | bytes 3538952 | tf_op jit(solution)/shard_map/ppermute | solution.py:479
  19.3 11.8 %collective-permute-start.1 = (bf16[8,96,384]{2,1,0:T(8,128)(2,1)S(1)}, bf16[8,96,384]{2,1,0:T(8,128)(2,1)S(1)}, u32[]{:S(2)}, u32[]{:S(2)}) collective-permute-start(bf16[8,96,384]{2,1,0:T(8,128)(2,1)S(1)} %add_convert_fusion.1), channel_id=1, source_target_pairs={{0,2},{1,5},{2,0},{3,7},{4,6},{5,1},{6,4},{7,3},{8,10},{9,13},{10,... | collective-permute-start | bytes 1769480 | tf_op jit(solution)/shard_map/ppermute | solution.py:479
  31.1 4.3 %collective-permute-start.2 = (bf16[16,96,384]{2,1,0:T(8,128)(2,1)S(1)}, bf16[16,96,384]{2,1,0:T(8,128)(2,1)S(1)}, u32[]{:S(2)}, u32[]{:S(2)}) collective-permute-start(bf16[16,96,384]{2,1,0:T(8,128)(2,1)S(1)} %get-tuple-element.132), channel_id=1, source_target_pairs={{0,1},{1,0},{2,3},{3,2},{4,5},{5,4},{6,7},{7,6},{8,9},{9,8},{10,11... | collective-permute-start | bytes 3538952 | tf_op jit(solution)/shard_map/ppermute | solution.py:479
  31.2 6.8 %collective-permute-start.6 = (bf16[4,96,384]{2,1,0:T(8,128)(2,1)S(1)}, bf16[4,96,384]{2,1,0:T(8,128)(2,1)S(1)}, u32[]{:S(2)}, u32[]{:S(2)}) collective-permute-start(bf16[4,96,384]{2,1,0:T(8,128)(2,1)S(1)} %add_convert_fusion.3), channel_id=1, source_target_pairs={{0,4},{1,3},{2,6},{3,1},{4,0},{5,7},{6,2},{7,5},{8,12},{9,11},{10,... | collective-permute-start | bytes 884744 | tf_op jit(solution)/shard_map/ppermute | solution.py:479
  35.4 7.0 %collective-permute-start.4 = (bf16[16,8,384]{2,1,0:T(8,128)(2,1)S(1)}, bf16[16,8,384]{2,1,0:T(8,128)(2,1)S(1)}, u32[]{:S(2)}, u32[]{:S(2)}) collective-permute-start(bf16[16,8,384]{2,1,0:T(8,128)(2,1)S(1)} %get-tuple-element.134), channel_id=1, source_target_pairs={{0,1},{1,0},{2,3},{3,2},{4,5},{5,4},{6,7},{7,6},{8,9},{9,8},{10,11... | collective-permute-start | bytes 294920 | tf_op jit(solution)/shard_map/ppermute | solution.py:479
  35.5 11.8 %collective-permute-start.3 = (bf16[8,96,384]{2,1,0:T(8,128)(2,1)S(1)}, bf16[8,96,384]{2,1,0:T(8,128)(2,1)S(1)}, u32[]{:S(2)}, u32[]{:S(2)}) collective-permute-start(bf16[8,96,384]{2,1,0:T(8,128)(2,1)S(1)} %add_convert_fusion), channel_id=1, source_target_pairs={{0,2},{1,5},{2,0},{3,7},{4,6},{5,1},{6,4},{7,3},{8,10},{9,13},{10,... | collective-permute-start | bytes 1769480 | tf_op jit(solution)/shard_map/ppermute | solution.py:479
  38.1 7.5 %collective-permute-start.9 = (bf16[1,96,384]{2,1,0:T(8,128)(2,1)S(1)}, bf16[1,96,384]{2,1,0:T(8,128)(2,1)S(1)}, u32[]{:S(2)}, u32[]{:S(2)}) collective-permute-start(bf16[1,96,384]{2,1,0:T(8,128)(2,1)S(1)} %get-tuple-element.178), channel_id=1, source_target_pairs={{0,16},{1,17},{2,18},{3,19},{4,20},{5,21},{6,22},{7,23},{8,24},{9,... | collective-permute-start | bytes 221192 | tf_op jit(solution)/shard_map/ppermute | solution.py:479
  40.8 6.3 %collective-permute-start.8 = (bf16[1,96,384]{2,1,0:T(8,128)(2,1)S(1)}, bf16[1,96,384]{2,1,0:T(8,128)(2,1)S(1)}, u32[]{:S(2)}, u32[]{:S(2)}) collective-permute-start(bf16[1,96,384]{2,1,0:T(8,128)(2,1)S(1)} %get-tuple-element.179), channel_id=1, source_target_pairs={{0,24},{1,25},{2,26},{3,27},{4,28},{5,29},{6,30},{7,31},{8,16},{9,... | collective-permute-start | bytes 221192 | tf_op jit(solution)/shard_map/ppermute | solution.py:479
  42.1 5.1 %collective-permute-start.7 = (bf16[1,96,384]{2,1,0:T(8,128)(2,1)S(1)}, bf16[1,96,384]{2,1,0:T(8,128)(2,1)S(1)}, u32[]{:S(2)}, u32[]{:S(2)}) collective-permute-start(bf16[1,96,384]{2,1,0:T(8,128)(2,1)S(1)} %get-tuple-element.177), channel_id=1, source_target_pairs={{0,8},{1,9},{2,10},{3,11},{4,12},{5,13},{6,14},{7,15},{8,0},{9,1},... | collective-permute-start | bytes 221192 | tf_op jit(solution)/shard_map/ppermute | solution.py:479
  42.4 5.0 %collective-permute-start.5 = (bf16[8,8,384]{2,1,0:T(8,128)(2,1)S(1)}, bf16[8,8,384]{2,1,0:T(8,128)(2,1)S(1)}, u32[]{:S(2)}, u32[]{:S(2)}) collective-permute-start(bf16[8,8,384]{2,1,0:T(8,128)(2,1)S(1)} %add_convert_fusion.11), channel_id=1, source_target_pairs={{0,2},{1,5},{2,0},{3,7},{4,6},{5,1},{6,4},{7,3},{8,10},{9,13},{10,... | collective-permute-start | bytes 147464 | tf_op jit(solution)/shard_map/ppermute | solution.py:479
  47.5 7.1 %collective-permute-start.10 = (bf16[4,104,384]{2,1,0:T(8,128)(2,1)S(1)}, bf16[4,104,384]{2,1,0:T(8,128)(2,1)S(1)}, u32[]{:S(2)}, u32[]{:S(2)}) collective-permute-start(bf16[4,104,384]{2,1,0:T(8,128)(2,1)S(1)} %pad_maximum_fusion), channel_id=1, source_target_pairs={{0,4},{1,3},{2,6},{3,1},{4,0},{5,7},{6,2},{7,5},{8,12},{9,11},{10,... | collective-permute-start | bytes 958472 | tf_op jit(solution)/shard_map/ppermute | solution.py:479
  49.3 9.2 %collective-permute-start.17 = (bf16[1,96,384]{2,1,0:T(8,128)(2,1)S(1)}, bf16[1,96,384]{2,1,0:T(8,128)(2,1)S(1)}, u32[]{:S(2)}, u32[]{:S(2)}) collective-permute-start(bf16[1,96,384]{2,1,0:T(8,128)(2,1)S(1)} %add_convert_fusion.7), channel_id=1, source_target_pairs={{0,16},{1,17},{2,18},{3,19},{4,20},{5,21},{6,22},{7,23},{8,24},{9,... | collective-permute-start | bytes 221192 | tf_op jit(solution)/shard_map/ppermute | solution.py:479
  52.1 6.7 %collective-permute-start.18 = (bf16[1,96,384]{2,1,0:T(8,128)(2,1)S(1)}, bf16[1,96,384]{2,1,0:T(8,128)(2,1)S(1)}, u32[]{:S(2)}, u32[]{:S(2)}) collective-permute-start(bf16[1,96,384]{2,1,0:T(8,128)(2,1)S(1)} %add_convert_fusion.7), channel_id=1, source_target_pairs={{0,8},{1,9},{2,10},{3,11},{4,12},{5,13},{6,14},{7,15},{8,0},{9,1},... | collective-permute-start | bytes 221192 | tf_op jit(solution)/shard_map/ppermute | solution.py:479
  52.8 7.1 %collective-permute-start.19 = (bf16[1,96,384]{2,1,0:T(8,128)(2,1)S(1)}, bf16[1,96,384]{2,1,0:T(8,128)(2,1)S(1)}, u32[]{:S(2)}, u32[]{:S(2)}) collective-permute-start(bf16[1,96,384]{2,1,0:T(8,128)(2,1)S(1)} %add_convert_fusion.7), channel_id=1, source_target_pairs={{0,24},{1,25},{2,26},{3,27},{4,28},{5,29},{6,30},{7,31},{8,16},{9,... | collective-permute-start | bytes 221192 | tf_op jit(solution)/shard_map/ppermute | solution.py:479
  54.8 8.5 %collective-permute-start.13 = (bf16[1,104,384]{2,1,0:T(8,128)(2,1)S(1)}, bf16[1,104,384]{2,1,0:T(8,128)(2,1)S(1)}, u32[]{:S(2)}, u32[]{:S(2)}) collective-permute-start(bf16[1,104,384]{2,1,0:T(8,128)(2,1)S(1)} %pad_maximum_fusion.4), channel_id=1, source_target_pairs={{0,16},{1,17},{2,18},{3,19},{4,20},{5,21},{6,22},{7,23},{8,24},{9,... | collective-permute-start | bytes 239624 | tf_op jit(solution)/shard_map/ppermute | solution.py:479
  57.9 6.4 %collective-permute-start.12 = (bf16[1,104,384]{2,1,0:T(8,128)(2,1)S(1)}, bf16[1,104,384]{2,1,0:T(8,128)(2,1)S(1)}, u32[]{:S(2)}, u32[]{:S(2)}) collective-permute-start(bf16[1,104,384]{2,1,0:T(8,128)(2,1)S(1)} %pad_maximum_fusion.3), channel_id=1, source_target_pairs={{0,24},{1,25},{2,26},{3,27},{4,28},{5,29},{6,30},{7,31},{8,16},{9,... | collective-permute-start | bytes 239624 | tf_op jit(solution)/shard_map/ppermute | solution.py:479
  58.5 6.2 %collective-permute-start.11 = (bf16[1,104,384]{2,1,0:T(8,128)(2,1)S(1)}, bf16[1,104,384]{2,1,0:T(8,128)(2,1)S(1)}, u32[]{:S(2)}, u32[]{:S(2)}) collective-permute-start(bf16[1,104,384]{2,1,0:T(8,128)(2,1)S(1)} %pad_maximum_fusion.2), channel_id=1, source_target_pairs={{0,8},{1,9},{2,10},{3,11},{4,12},{5,13},{6,14},{7,15},{8,0},{9,1},... | collective-permute-start | bytes 239624 | tf_op jit(solution)/shard_map/ppermute | solution.py:479
  60.0 10.1 %collective-permute-start.20 = (bf16[4,96,384]{2,1,0:T(8,128)(2,1)S(1)}, bf16[4,96,384]{2,1,0:T(8,128)(2,1)S(1)}, u32[]{:S(2)}, u32[]{:S(2)}) collective-permute-start(bf16[4,96,384]{2,1,0:T(8,128)(2,1)S(1)} %get-tuple-element.185), channel_id=1, source_target_pairs={{0,4},{1,3},{2,6},{3,1},{4,0},{5,7},{6,2},{7,5},{8,12},{9,11},{10,... | collective-permute-start | bytes 884744 | tf_op jit(solution)/shard_map/ppermute | solution.py:479
  64.7 8.2 %collective-permute-start.14 = (bf16[1,104,384]{2,1,0:T(8,128)(2,1)S(1)}, bf16[1,104,384]{2,1,0:T(8,128)(2,1)S(1)}, u32[]{:S(2)}, u32[]{:S(2)}) collective-permute-start(bf16[1,104,384]{2,1,0:T(8,128)(2,1)S(1)} %get-tuple-element.172), channel_id=1, source_target_pairs={{0,16},{1,17},{2,18},{3,19},{4,20},{5,21},{6,22},{7,23},{8,24},{9,... | collective-permute-start | bytes 239624 | tf_op jit(solution)/shard_map/ppermute | solution.py:479
  67.1 5.8 %collective-permute-start.15 = (bf16[1,104,384]{2,1,0:T(8,128)(2,1)S(1)}, bf16[1,104,384]{2,1,0:T(8,128)(2,1)S(1)}, u32[]{:S(2)}, u32[]{:S(2)}) collective-permute-start(bf16[1,104,384]{2,1,0:T(8,128)(2,1)S(1)} %get-tuple-element.172), channel_id=1, source_target_pairs={{0,8},{1,9},{2,10},{3,11},{4,12},{5,13},{6,14},{7,15},{8,0},{9,1},... | collective-permute-start | bytes 239624 | tf_op jit(solution)/shard_map/ppermute | solution.py:479
  67.7 6.4 %collective-permute-start.16 = (bf16[1,104,384]{2,1,0:T(8,128)(2,1)S(1)}, bf16[1,104,384]{2,1,0:T(8,128)(2,1)S(1)}, u32[]{:S(2)}, u32[]{:S(2)}) collective-permute-start(bf16[1,104,384]{2,1,0:T(8,128)(2,1)S(1)} %get-tuple-element.172), channel_id=1, source_target_pairs={{0,24},{1,25},{2,26},{3,27},{4,28},{5,29},{6,30},{7,31},{8,16},{9,... | collective-permute-start | bytes 239624 | tf_op jit(solution)/shard_map/ppermute | solution.py:479
  69.2 7.1 %collective-permute-start.24 = (bf16[4,96,384]{2,1,0:T(8,128)(2,1)S(1)}, bf16[4,96,384]{2,1,0:T(8,128)(2,1)S(1)}, u32[]{:S(2)}, u32[]{:S(2)}) collective-permute-start(bf16[4,96,384]{2,1,0:T(8,128)(2,1)S(1)} %get-tuple-element.185), channel_id=1, source_target_pairs={{0,2},{1,5},{2,0},{3,7},{4,6},{5,1},{6,4},{7,3},{8,10},{9,13},{10,... | collective-permute-start | bytes 884744 | tf_op jit(solution)/shard_map/ppermute | solution.py:479
  70.1 12.4 %collective-permute-start.25 = (bf16[4,96,384]{2,1,0:T(8,128)(2,1)S(1)}, bf16[4,96,384]{2,1,0:T(8,128)(2,1)S(1)}, u32[]{:S(2)}, u32[]{:S(2)}) collective-permute-start(bf16[4,96,384]{2,1,0:T(8,128)(2,1)S(1)} %collective-permute-done.20), channel_id=1, source_target_pairs={{0,2},{1,5},{2,0},{3,7},{4,6},{5,1},{6,4},{7,3},{8,10},{9,13},{10,... | collective-permute-start | bytes 884744 | tf_op jit(solution)/shard_map/ppermute | solution.py:479
  74.2 8.3 %collective-permute-start.21 = (bf16[4,104,384]{2,1,0:T(8,128)(2,1)S(1)}, bf16[4,104,384]{2,1,0:T(8,128)(2,1)S(1)}, u32[]{:S(2)}, u32[]{:S(2)}) collective-permute-start(bf16[4,104,384]{2,1,0:T(8,128)(2,1)S(1)} %pad_maximum_fusion.1), channel_id=1, source_target_pairs={{0,4},{1,3},{2,6},{3,1},{4,0},{5,7},{6,2},{7,5},{8,12},{9,11},{10,... | collective-permute-start | bytes 958472 | tf_op jit(solution)/shard_map/ppermute | solution.py:479
  75.7 8.5 %collective-permute-start.26 = (bf16[8,96,384]{2,1,0:T(8,128)(2,1)S(1)}, bf16[8,96,384]{2,1,0:T(8,128)(2,1)S(1)}, u32[]{:S(2)}, u32[]{:S(2)}) collective-permute-start(bf16[8,96,384]{2,1,0:T(8,128)(2,1)S(1)} %constant_dynamic-update-slice_fusion.9.refs_0_), channel_id=1, source_target_pairs={{0,1},{1,0},{2,3},{3,2},{4,5},{5,4},{6,7},{7,6},{8,9},{9,8},{10,11... | collective-permute-start | bytes 1769480 | tf_op jit(solution)/shard_map/ppermute | solution.py:479
  82.6 2.1 %collective-permute-start.27 = (bf16[8,96,384]{2,1,0:T(8,128)(2,1)S(1)}, bf16[8,96,384]{2,1,0:T(8,128)(2,1)S(1)}, u32[]{:S(2)}, u32[]{:S(2)}) collective-permute-start(bf16[8,96,384]{2,1,0:T(8,128)(2,1)S(1)} %constant_dynamic-update-slice_fusion.14.refs_1_), channel_id=1, source_target_pairs={{0,1},{1,0},{2,3},{3,2},{4,5},{5,4},{6,7},{7,6},{8,9},{9,8},{10,11... | collective-permute-start | bytes 1769480 | tf_op jit(solution)/shard_map/ppermute | solution.py:479
  82.8 4.6 %collective-permute-start.23 = (bf16[8,104,384]{2,1,0:T(8,128)(2,1)S(1)}, bf16[8,104,384]{2,1,0:T(8,128)(2,1)S(1)}, u32[]{:S(2)}, u32[]{:S(2)}) collective-permute-start(bf16[8,104,384]{2,1,0:T(8,128)(2,1)S(1)} %constant_dynamic-update-slice_fusion.4.held), channel_id=1, source_target_pairs={{0,1},{1,0},{2,3},{3,2},{4,5},{5,4},{6,7},{7,6},{8,9},{9,8},{10,11... | collective-permute-start | bytes 1916936 | tf_op jit(solution)/shard_map/ppermute | solution.py:479
  83.3 10.4 %collective-permute-start.22 = (bf16[8,104,384]{2,1,0:T(8,128)(2,1)S(1)}, bf16[8,104,384]{2,1,0:T(8,128)(2,1)S(1)}, u32[]{:S(2)}, u32[]{:S(2)}) collective-permute-start(bf16[8,104,384]{2,1,0:T(8,128)(2,1)S(1)} %constant_dynamic-update-slice_fusion.4.held), channel_id=1, source_target_pairs={{0,2},{1,5},{2,0},{3,7},{4,6},{5,1},{6,4},{7,3},{8,10},{9,13},{10,... | collective-permute-start | bytes 1916936 | tf_op jit(solution)/shard_map/ppermute | solution.py:479
  93.7 2.1 %collective-permute-start.28 = (bf16[8,104,384]{2,1,0:T(8,128)(2,1)S(1)}, bf16[8,104,384]{2,1,0:T(8,128)(2,1)S(1)}, u32[]{:S(2)}, u32[]{:S(2)}) collective-permute-start(bf16[8,104,384]{2,1,0:T(8,128)(2,1)S(1)} %collective-permute-done.22.late), channel_id=1, source_target_pairs={{0,1},{1,0},{2,3},{3,2},{4,5},{5,4},{6,7},{7,6},{8,9},{9,8},{10,11... | collective-permute-start | bytes 1916936 | tf_op jit(solution)/shard_map/ppermute | solution.py:479

commit v6 on v5

--- a/solution.py
+++ b/solution.py
@@ -20,7 +20,7 @@
 F32 = jnp.float32
 VMEM = pl.BlockSpec(memory_space=pltpu.VMEM)
 HBM = pl.BlockSpec(memory_space=pltpu.HBM)
-VMEM_LIMIT = 28 * 2**20
+VMEM_LIMIT = 20 * 2**20
 
 CROSS_AFF_SCALE, CROSS_AFF_SHIFT, CROSS_SCALE, CROSS_BIAS = 0, 1, 2, 3
 MIXER_AFF_SCALE, MIXER_AFF_SHIFT, MIXER_OUT_BIAS, MIXER_SCALE = 4, 5, 6, 7
@@ -213,8 +213,8 @@
 
 
 def mixer_backward(
-    layer, upper_ref, low_ref, fired_ref, slope_ref, scaled_ref, inner_ref, outer_ref,
-    inner_grad_ref, outer_grad_ref, vectors_ref, scale_ref,
+    layer, upper_ref, low_ref, fired_ref, slope_ref, hidden_grad_ref, scaled_ref, inner_ref,
+    outer_ref, inner_grad_ref, outer_grad_ref, vectors_ref, scale_ref,
 ):
     scale = scale_ref[layer : layer + 1, :]
     tiles = row_tiles(upper_ref.shape[1])
@@ -236,11 +236,11 @@
                 rows, at
             ].astype(F32)
             inner_bias += row_sum(hidden_grad)
-            slope_ref[rows, at] = hidden_grad.astype(BF)
+            hidden_grad_ref[rows, at] = hidden_grad.astype(BF)
         for piece in range(step // LANES):
             row = MIXER_IN_BIAS + part * (step // LANES) + piece
             vectors_ref[layer, row : row + 1, :] = inner_bias[:, piece * LANES : (piece + 1) * LANES]
-        inner_grad_ref[:, at] = dot(low_ref[...], slope_ref[:, at], 0, 0).astype(BF)
+        inner_grad_ref[:, at] = dot(low_ref[...], hidden_grad_ref[:, at], 0, 0).astype(BF)
 
 
 def mixer_input_grad(
@@ -322,41 +322,45 @@
     _, patches, each, _ = x_in.shape
     per = x_in.shape[0]
     own = lax.axis_index("pipe") * per
-    sources = (
-        (cross_weight_hbm, cross_weight),
-        (cross_bias_hbm, cross_bias),
-        (inner_bias_hbm, inner_bias),
-        (mixer_aff_shift_hbm, mixer_aff_shift),
-        *zip(parameters_hbm, parameters),
-        (mask_hbm.at[pl.ds(own, per)], mask_in),
-        (x_hbm.at[pl.ds(own, per)], x_in),
-        (inner_hbm.at[0], inner0),
-        (outer_hbm.at[0], outer0),
-        (inner_hbm.at[1], inner1),
-        (g_hbm.at[pl.ds(own, per)], g_in),
-        (outer_hbm.at[1], outer1),
-    )
-    copies = [
-        pltpu.make_async_copy(source, target, sems.at[number])
-        for number, (source, target) in enumerate(sources)
-    ]
-    for copy in copies:
-        copy.start()
+    mine = pl.ds(own, per)
+    groups = (
+        ((cross_weight_hbm, cross_weight), (mask_hbm.at[mine], mask_in), (cross_bias_hbm, cross_bias)),
+        ((x_hbm.at[mine], x_in), *zip(parameters_hbm, parameters)),
+        (
+            (inner_hbm.at[0], inner0),
+            (inner_bias_hbm, inner_bias),
+            (mixer_aff_shift_hbm, mixer_aff_shift),
+        ),
+        ((outer_hbm.at[0], outer0),),
+        ((inner_hbm.at[1], inner1),),
+        ((g_hbm.at[mine], g_in), (outer_hbm.at[1], outer1)),
+    )
+    arrivals, number = [], 0
+    for group in groups:
+        arrivals.append([])
+        for source, target in group:
+            copy = pltpu.make_async_copy(source, target, sems.at[number])
+            copy.start()
+            arrivals[-1].append(copy)
+            number += 1
+
+    def wait_for(group):
+        for copy in arrivals[group]:
+            copy.wait()
+
     vectors[...] = jnp.zeros_like(vectors)
     clear_padding(padded_low, patches=patches)
-    for copy in copies[:-6]:
-        copy.wait()
-    copies = copies[-7:]
+    wait_for(0)
     masks = mask_in[...].reshape((per * each,) + mask_in.shape[2:])
     cross_setup(masks, cross_weight, cross_bias, kept_weight, keep, bias_columns, weight_rows)
-    copies[1].wait()
+    wait_for(1)
     spread_rows(x_in, s0)
     cross = (kept_weight, bias_columns, cross_aff_scale, cross_aff_shift, cross_scale, padded_low)
     cross_forward(0, s0, s1, vectors, *cross, patches, each)
-    copies[2].wait()
+    wait_for(2)
     mixer = (mixer_aff_scale, mixer_aff_shift)
     mixer_hidden(0, s1, low0, fired0, slope0, vectors, *mixer, inner0, inner_bias)
-    copies[3].wait()
+    wait_for(3)
     squares = jnp.zeros((1, LANES), F32)
     for rows in row_halves(s1.shape[1]):
         result = dot(fired0[rows, :], outer0[...]) + outer_bias[0:1, :]
@@ -366,13 +370,12 @@
         squares += row_sum(branch * branch)
     vectors[0, SQUARES + 2 : SQUARES + 3, :] = squares
     cross_forward(1, s2, s3, vectors, *cross, patches, each)
-    copies[4].wait()
+    wait_for(4)
     mixer_hidden(1, s3, low1, fired1, slope1, vectors, *mixer, inner1, inner_bias)
-    copies[5].wait()
+    wait_for(5)
     spread_rows(g_in, g_rows)
-    copies[6].wait()
     mixer_backward(
-        1, g_rows, low1, fired1, slope1, scaled, inner1, outer1, inner_grad, outer_grad,
+        1, g_rows, low1, fired1, slope1, slope1, scaled, inner1, outer1, inner_grad, outer_grad,
         vectors, mixer_scale,
     )
     pack_products(own_codes(mesh_shape), inner_grad, outer_grad, kept, sent)
@@ -396,22 +399,17 @@
 
 def third_kernel(
     mesh_shape,
-    s1, g2, low0, fired0, slope0, result0, inner0, outer0, s3, g_rows, fired1, outer1, vectors_in,
+    s1, g2, low0, fired0, slope0, inner0, outer0, s3, g_rows, fired1, outer1, vectors_in,
     mixer_aff_scale, outer_bias, mixer_scale,
-    kept, sent, g1, vectors, output,
-    hidden_grad, scaled, inner_grad, outer_grad, leaving,
+    kept, sent, g1, vectors, leaving,
+    hidden_grad, scaled, inner_grad, outer_grad,
 ):
     vectors[...] = vectors_in[...]
-    hidden_grad[...] = slope0[...]
     mixer_backward(
-        0, g2, low0, fired0, hidden_grad, scaled, inner0, outer0, inner_grad, outer_grad,
+        0, g2, low0, fired0, slope0, hidden_grad, scaled, inner0, outer0, inner_grad, outer_grad,
         vectors, mixer_scale,
     )
     pack_products(own_codes(mesh_shape), inner_grad, outer_grad, kept, sent)
-    scale_grad = jnp.zeros((1, LANES), F32)
-    for rows in row_tiles(g2.shape[1]):
-        scale_grad += row_sum(read(g2, rows) * result0[rows, :].astype(F32))
-    vectors[0, MIXER_SCALE : MIXER_SCALE + 1, :] = scale_grad
     mixer_input_grad(0, g2, s1, hidden_grad, g1, inner0, vectors, mixer_aff_scale)
     squares = jnp.zeros((1, LANES), F32)
     scale_grad = jnp.zeros((1, LANES), F32)
@@ -423,7 +421,6 @@
         squares += row_sum(branch * branch)
     vectors[1, SQUARES + 2 : SQUARES + 3, :] = squares
     vectors[1, MIXER_SCALE : MIXER_SCALE + 1, :] = scale_grad
-    gather_rows(leaving, output)
 
 
 def pack_small(weight_grads, vectors_ref, small_ref, patches):
@@ -450,9 +447,9 @@
 
 def fourth_kernel(
     mesh_shape,
-    s0, g1, kept_weight, keep, bias_columns, weight_grad1, vectors_in,
+    s0, g1, kept_weight, keep, bias_columns, weight_grad1, vectors_in, g2, result0, leaving,
     cross_aff_scale, cross_aff_shift, cross_scale,
-    input_grad, kept, sent,
+    input_grad, output, kept, sent,
     g0, weight_grad0, vectors, small, padded_low, padded_mixing,
 ):
     _, patches, each, _ = input_grad.shape
@@ -462,9 +459,14 @@
         0, s0, g1, g0, weight_grad0, vectors, kept_weight, keep, bias_columns,
         cross_aff_scale, cross_aff_shift, cross_scale, padded_low, padded_mixing, patches, each,
     )
+    scale_grad = jnp.zeros((1, LANES), F32)
+    for rows in row_tiles(g2.shape[1]):
+        scale_grad += row_sum(read(g2, rows) * result0[rows, :].astype(F32))
+    vectors[0, MIXER_SCALE : MIXER_SCALE + 1, :] = scale_grad
     pack_small((weight_grad0, weight_grad1), vectors, small, patches)
     pack_halves(own_codes(mesh_shape), lambda block: (small[block],), kept, sent)
     gather_rows(g0, input_grad)
+    gather_rows(leaving, output)
 
 
 def exchange_bits(values, mesh_shape, phases):
@@ -509,13 +511,10 @@
     return arrived, grown
 
 
-LAST_SLOTS = (2, 3, 1)
-
-
-def send_last(families, mesh_shape):
-    leaving = [joint_sum(families, slot, slot + 1) for slot in LAST_SLOTS]
+def send_last(families, mesh_shape, slots):
+    leaving = [joint_sum(families, slot, slot + 1) for slot in slots]
     return leaving, [
-        exchange_bits(block, mesh_shape, across(slot)) for slot, block in zip(LAST_SLOTS, leaving)
+        exchange_bits(block, mesh_shape, across(slot)) for slot, block in zip(slots, leaving)
     ]
 
 
@@ -529,8 +528,8 @@
     return total.astype(BF)
 
 
-def gather_last(own, mesh_shape):
-    return {slot: exchange_bits(own, mesh_shape, across(slot)) for slot in LAST_SLOTS}
+def gather_last(own, mesh_shape, slots):
+    return {slot: exchange_bits(own, mesh_shape, across(slot)) for slot in slots}
 
 
 def join(own, arrived):
@@ -545,19 +544,22 @@
     return lax.optimization_barrier((values, *others))[0]
 
 
-def unpack_quarters(
-    mesh_shape, images_all, layer, plan, quarters, inner_out, outer_out, stage, sems, meanwhile=None
+def unpack_pieces(
+    mesh_shape, images_all, plan, pieces, inner_out, outer_out, stage, sems, meanwhile=None
 ):
     codes = own_codes(mesh_shape)
-    quarter, depth = HALF // 2, stage.shape[2]
+    depth = stage.shape[2]
     columns = inner_out.shape[2]
+    first = [0]
+    for values in pieces:
+        first.append(first[-1] + values.shape[0])
 
     def copies(number, slot):
-        block_of, base = plan[number]
+        layer, block_of, base = plan[number]
         block = block_of(codes, slot + base)
         row_at, column_at = inner_spot(block, depth, columns)
         outer_at = pl.multiple_of(block * depth, depth)
-        index = number * quarter + slot
+        index = first[number] + slot
         return (
             pltpu.make_async_copy(
                 stage.at[0, index],
@@ -569,79 +571,74 @@
             ),
         )
 
-    for number, values in enumerate(quarters):
-
-        @pl.loop(0, quarter)
+    for number, values in enumerate(pieces):
+
+        @pl.loop(0, values.shape[0])
         def _(slot):
             for kind, copy in enumerate(copies(number, slot)):
                 block = values[slot, kind * depth : (kind + 1) * depth, :]
-                stage[kind, number * quarter + slot] = block.astype(F32) / images_all
+                stage[kind, first[number] + slot] = block.astype(F32) / images_all
                 copy.start()
 
     if meanwhile is not None:
         meanwhile()
-    for number in range(len(quarters)):
-
-        @pl.loop(0, quarter)
+    for number, values in enumerate(pieces):
+
+        @pl.loop(0, values.shape[0])
         def _(slot):
             for copy in copies(number, slot):
                 copy.wait()
 
 
-QUARTERS = ((kept_block, 0), (kept_block, HALF // 2), (sent_block, 0), (sent_block, HALF // 2))
-
-
-def unpack_small(mesh_shape, plan, quarters, small_rows, depth):
+QUARTER, EIGHTH = HALF // 2, HALF // 4
+SMALL_OUTS = 11
+
+
+def unpack_small(mesh_shape, plan, pieces, small_rows, depth):
     codes = own_codes(mesh_shape)
-    for (block_of, base), values in zip(plan, quarters):
-
-        @pl.loop(0, HALF // 2)
-        def _(slot):
-            small_rows[block_of(codes, slot + base)] = values[slot, 2 * depth :, :].astype(F32)
-
-
-def unpack_last_layer(mesh_shape, images_all, *refs):
-    unpack_quarters(mesh_shape, images_all, 1, QUARTERS, refs[:4], *refs[4:])
-
-
-def unpack_held(
-    mesh_shape, images_all, held, other_held, inner_in, outer_in,
-    inner_out, outer_out, small_rows, stage, sems,
-):
-    plan, quarters = (QUARTERS[0], QUARTERS[2]), (held, other_held)
-    unpack_quarters(mesh_shape, images_all, 0, plan, quarters, inner_out, outer_out, stage, sems)
-    unpack_small(mesh_shape, plan, quarters, small_rows, stage.shape[2])
-
-
-def unpack_late(
-    mesh_shape, images_all, late, inner_in, outer_in, small_in,
-    inner_out, outer_out, small_rows, stage, sems,
-):
-    plan, quarters = QUARTERS[1:2], (late,)
-    unpack_quarters(mesh_shape, images_all, 0, plan, quarters, inner_out, outer_out, stage, sems)
-    unpack_small(mesh_shape, plan, quarters, small_rows, stage.shape[2])
+    for (layer, block_of, base), values in zip(plan, pieces):
+        if layer == 0:
+
+            @pl.loop(0, values.shape[0])
+            def _(slot):
+                small_rows[block_of(codes, slot + base)] = values[slot, 2 * depth :, :].astype(F32)
+
+
+def unpack_some(mesh_shape, images_all, plan, *refs):
+    inner_out, outer_out, small_rows, stage, sems = refs[-5:]
+    pieces = refs[: len(plan)]
+    unpack_pieces(mesh_shape, images_all, plan, pieces, inner_out, outer_out, stage, sems)
+    unpack_small(mesh_shape, plan, pieces, small_rows, stage.shape[2])
 
 
 def unpack_rest(
     mesh_shape, images_all, other_late, inner_in, outer_in, small_in,
-    inner_out, outer_out, small_rows, weight_out, aff_scale_out, aff_shift_out, cross_bias_out,
-    cross_scale_out, mixer_aff_scale_out, mixer_aff_shift_out, inner_bias_out, outer_bias_out,
-    mixer_scale_out, magnitudes_out,
-    stage, rest_rows, sems,
-):
+    inner_out, outer_out, small_rows, *small_outs_and_rest,
+):
+    small_outs, rest = small_outs_and_rest[:SMALL_OUTS], small_outs_and_rest[SMALL_OUTS:]
+    buffers, (stage, rest_rows, sems, small_sems) = rest[:SMALL_OUTS], rest[SMALL_OUTS:]
+    (
+        weight_out, aff_scale_out, aff_shift_out, cross_bias_out, cross_scale_out,
+        mixer_aff_scale_out, mixer_aff_shift_out, inner_bias_out, outer_bias_out,
+        mixer_scale_out, magnitudes_out,
+    ) = buffers
+    small_copies = [
+        pltpu.make_async_copy(buffer, out, small_sems.at[number])
+        for number, (buffer, out) in enumerate(zip(buffers, small_outs))
+    ]
     patches, layers, _ = weight_out.shape
-    plan, quarters = QUARTERS[3:], (other_late,)
+    plan, pieces = ((0, sent_block, QUARTER + EIGHTH),), (other_late,)
 
     def small_gradients():
-        unpack_small(mesh_shape, plan, quarters, small_rows, stage.shape[2])
+        unpack_small(mesh_shape, plan, pieces, small_rows, stage.shape[2])
         groups = -(-patches // SMALL_ROWS)
         weights = (small_rows[0:groups] / images_all).reshape(groups * SMALL_ROWS, LANES)[0:patches]
-        pieces = VECTOR_ROWS // SMALL_ROWS
+        parts = VECTOR_ROWS // SMALL_ROWS
         lane = lax.broadcasted_iota(jnp.int32, (patches, 128), 1)
         for layer in range(layers):
             row = slice(layer, layer + 1)
-            at = groups + layer * pieces
-            vectors = (small_rows[at : at + pieces] / images_all).reshape(VECTOR_ROWS, LANES)
+            at = groups + layer * parts
+            vectors = (small_rows[at : at + parts] / images_all).reshape(VECTOR_ROWS, LANES)
             rest_rows[...] = jnp.zeros_like(rest_rows)
             rest_rows[64 : 64 + SMALL_ROWS, :] = vectors[CROSS_REST:, 0:256]
             rest = jnp.transpose(rest_rows[...])[0:patches]
@@ -671,10 +668,14 @@
                 for which in range(2):
                     index = 2 * kind + which
                     magnitudes_out[layer, kind : kind + 1, which : which + 1] = means[index : index + 1]
-
-    unpack_quarters(
-        mesh_shape, images_all, 0, plan, quarters, inner_out, outer_out, stage, sems, small_gradients
-    )
+        for copy in small_copies:
+            copy.start()
+
+    unpack_pieces(
+        mesh_shape, images_all, plan, pieces, inner_out, outer_out, stage, sems, small_gradients
+    )
+    for copy in small_copies:
+        copy.wait()
 
 
 def call(kernel, name, args, outs, scratch, in_specs=None, out_specs=None, aliases=None, us=1):
@@ -812,18 +813,17 @@
     leaving1, main1 = halve(main1, HALF, mesh_shape, 1)
     g2 = after(g2, leaving1)
     halves = vmem(HALF, 2 * depth, LANES)
-    kept0, sent0, g1, sums, output = call(
+    kept0, sent0, g1, sums, leaving = call(
         functools.partial(third_kernel, mesh_shape),
         "first_feed_forward",
         (
             *in_vmem((
-                s1, g2, low0, fired0, slope0, result0, inner0, outer0, s3, upper, fired1, outer1,
-                sums,
+                s1, g2, low0, fired0, slope0, inner0, outer0, s3, upper, fired1, outer1, sums,
             )),
             mixer_aff, result_bias, result_scale,
         ),
-        (halves, halves, stream, vectors, hbm(*local, dtype=BF)),
-        [hidden, vmem(rows, width), inner, outer, stream],
+        (halves, halves, stream, vectors, stream),
+        [hidden, vmem(rows, width), inner, outer],
         us=9,
     )
     sent0, sums = lax.optimization_barrier((sent0, sums, main1[-1]))[:2]
@@ -831,14 +831,16 @@
     leaving1, main1 = halve(main1, HALF // 2, mesh_shape, 2)
     sums = after(sums, leaving1)
     halves = vmem(HALF, SMALL_ROWS, LANES)
-    input_grad, kept_small, sent_small = call(
+    input_grad, output, kept_small, sent_small = call(
         functools.partial(fourth_kernel, mesh_shape),
         "first_cross",
         (
-            *in_vmem((s0, g1, kept_weight, keep, bias_columns, weight_grad1, sums)),
+            *in_vmem((
+                s0, g1, kept_weight, keep, bias_columns, weight_grad1, sums, g2, result0, leaving,
+            )),
             aff_scale, aff_shift, scale,
         ),
-        (hbm(*local, dtype=BF), halves, halves),
+        (hbm(*local, dtype=BF), hbm(*local, dtype=BF), halves, halves),
         [
             stream,
             vmem(256, 256, dtype=F32),
@@ -852,76 +854,83 @@
     small = [kept_small, exchange_bits(sent_small, mesh_shape, [0])]
     _, main0 = halve(main0, HALF, mesh_shape, 1)
     _, small = halve(small, HALF, mesh_shape, 1)
-    own1 = sum_last([main1], send_last([main1], mesh_shape)[1], mesh_shape)
+    own1 = sum_last([main1], send_last([main1], mesh_shape, (1, 3, 2))[1], mesh_shape)
     main0[-1], small[-1], own1 = lax.optimization_barrier((main0[-1], small[-1], own1))
     width0 = HALF // 2
     terms0 = [[t[:width0] for t in main0], [t[:width0] for t in small]]
     _, terms0 = halve_all(terms0, width0, mesh_shape, 2)
-    peers1 = gather_last(own1, mesh_shape)
-    leaving0, arrived0 = send_last(terms0, mesh_shape)
+    peers1 = gather_last(own1, mesh_shape, (1, 2, 3))
+    leaving0, arrived0 = send_last(terms0, mesh_shape, (1, 3, 2))
     four1 = join(own1, after(peers1, leaving0))
     own0 = sum_last(terms0, arrived0, mesh_shape)
     more1 = exchange_bits(four1, mesh_shape, [2])
     late1 = exchange_bits(four1, mesh_shape, [1])
-    peers0 = gather_last(own0, mesh_shape)
+    peers0 = gather_last(own0, mesh_shape, (3, 1, 2))
     more1 = after(more1, own0)
     latest1 = exchange_bits(more1, mesh_shape, [1])
-    four0 = join(own0, after(peers0, more1))
+    four0 = join(own0, after(peers0, more1, late1))
     held1 = jnp.concatenate([four1, more1], axis=0)
     other_held1 = exchange_bits(held1, mesh_shape, [0])
     more0 = exchange_bits(four0, mesh_shape, [2])
+    late0 = exchange_bits(four0, mesh_shape, [1])
+    inner_out, outer_out = hbm(layers, width, columns), hbm(layers, columns, width)
+
+    def staging(blocks):
+        return [
+            vmem(2, blocks, depth, LANES, dtype=F32),
+            pltpu.SemaphoreType.DMA((2, blocks)),
+        ]
+
+    small_rows = vmem(BLOCKS, SMALL_ROWS, LANES, dtype=F32)
+
+    def unpack(name, plan, pieces, grads=()):
+        count, blocks = len(pieces), sum(p.shape[0] for p in pieces)
+        return call(
+            functools.partial(unpack_some, mesh_shape, images_all, plan),
+            name,
+            (*in_vmem(pieces), *grads[:2], *in_vmem(grads[2:])),
+            (inner_out, outer_out, small_rows),
+            staging(blocks),
+            in_specs=[VMEM] * count + ([HBM, HBM, VMEM] if grads else []),
+            out_specs=[HBM] * 2 + [VMEM],
+            aliases={count + number: number for number in range(len(grads))},
+            us=blocks / 8,
+        )
+
+    more0, late0 = lax.optimization_barrier((more0, late0))
     late1, latest1 = after((late1, latest1), more0)
+    latest0 = exchange_bits(more0, mesh_shape, [1])
     late1 = jnp.concatenate([late1, latest1], axis=0)
+    other_late1 = exchange_bits(late1, mesh_shape, [0])
     held0 = jnp.concatenate([four0, more0], axis=0)
-    other_late1 = exchange_bits(late1, mesh_shape, [0])
-    late0 = exchange_bits(held0, mesh_shape, [1])
     other_held0 = exchange_bits(held0, mesh_shape, [0])
-    quarters1 = (held1, late1, other_held1, other_late1)
-    inner_out, outer_out = hbm(layers, width, columns), hbm(layers, columns, width)
-    quarter = HALF // 2
-
-    def staging(quarters):
-        return [
-            vmem(2, quarters * quarter, depth, LANES, dtype=F32),
-            pltpu.SemaphoreType.DMA((2, quarters * quarter)),
-        ]
-
-    small_rows = vmem(BLOCKS, SMALL_ROWS, LANES, dtype=F32)
-    grads = call(
-        functools.partial(unpack_last_layer, mesh_shape, images_all),
-        "unpack_last_layer",
-        in_vmem(quarters1),
-        (inner_out, outer_out),
-        staging(4),
-        out_specs=[HBM] * 2,
-        us=3,
-    )
-    *grads, rows_held = call(
-        functools.partial(unpack_held, mesh_shape, images_all),
-        "unpack_held",
-        (*in_vmem((held0, other_held0)), *grads),
-        (inner_out, outer_out, small_rows),
-        staging(2),
-        in_specs=[VMEM] * 2 + [HBM] * 2,
-        out_specs=[HBM] * 2 + [VMEM],
-        aliases={2: 0, 3: 1},
-        us=2,
-    )
-    late0, grads = lax.optimization_barrier((late0, grads))
     other_late0 = exchange_bits(late0, mesh_shape, [0])
-    *grads, rows_held = call(
-        functools.partial(unpack_late, mesh_shape, images_all),
-        "unpack_late",
-        (*in_vmem((late0,)), *grads, *in_vmem((rows_held,))),
-        (inner_out, outer_out, small_rows),
-        staging(1),
-        in_specs=[VMEM] + [HBM] * 2 + [VMEM],
-        out_specs=[HBM] * 2 + [VMEM],
-        aliases={1: 0, 2: 1, 3: 2},
-        us=1,
-    )
-    row = hbm(layers, width)
-    stage, sems = staging(1)
+    grads = unpack(
+        "unpack_kept",
+        (
+            (1, kept_block, 0),
+            (1, sent_block, 0),
+            (1, kept_block, QUARTER),
+            (0, kept_block, 0),
+            (0, kept_block, QUARTER),
+        ),
+        (held1, other_held1, late1, held0, late0),
+    )
+    grads = unpack(
+        "unpack_others",
+        ((1, sent_block, QUARTER), (0, sent_block, 0), (0, sent_block, QUARTER)),
+        (other_late1, other_held0, other_late0),
+        grads,
+    )
+    latest0, grads = lax.optimization_barrier((latest0, grads))
+    other_latest0 = exchange_bits(latest0, mesh_shape, [0])
+    grads = unpack("unpack_latest", ((0, kept_block, QUARTER + EIGHTH),), (latest0,), grads)
+    row = (layers, width)
+    small_shapes = (
+        (patches, layers, patches), row, row, (layers, patches), row, row, row,
+        (layers, columns), row, row, (layers, 2, 2),
+    )
+    stage, sems = staging(EIGHTH)
     (
         inner_grad, outer_grad, _, weight_grad, aff_scale_grad, aff_shift_grad, bias_grad,
         scale_grad, mixer_aff_scale_grad, mixer_aff_shift_grad, inner_bias_grad,
@@ -929,15 +938,17 @@
     ) = call(
         functools.partial(unpack_rest, mesh_shape, images_all),
         "unpack_rest",
-        (*in_vmem((other_late0,)), *grads, *in_vmem((rows_held,))),
-        (
-            inner_out, outer_out, small_rows, hbm(patches, layers, patches), row, row,
-            hbm(layers, patches), row, row, row, hbm(layers, columns), row, row,
-            hbm(layers, 2, 2),
-        ),
-        [stage, vmem(128, 256, dtype=F32), sems],
+        (*in_vmem((other_latest0,)), *grads[:2], *in_vmem(grads[2:])),
+        (inner_out, outer_out, small_rows, *(hbm(*shape) for shape in small_shapes)),
+        [
+            *(vmem(*shape, dtype=F32) for shape in small_shapes),
+            stage,
+            vmem(128, 256, dtype=F32),
+            sems,
+            pltpu.SemaphoreType.DMA((SMALL_OUTS,)),
+        ],
         in_specs=[VMEM] + [HBM] * 2 + [VMEM],
-        out_specs=[HBM] * 2 + [VMEM] * 12,
+        out_specs=[HBM] * 2 + [VMEM] + [HBM] * SMALL_OUTS,
         aliases={1: 0, 2: 1, 3: 2},
         us=2,
     )

time: 98.1 us -> 94.4 us (0.962)
  waiting for transfers between devices: 26.7 us -> 22.5 us
  starting transfers between devices: 31.6 us -> 33.5 us
  Pallas kernels: 37.1 us -> 35.8 us
    ppermute x29 -> x31, waiting for transfers between devices: 26.7 us -> 22.5 us  [exchange_bits(): return lax.ppermute(values, AXES, [(i, partner(i)) for i in places])]
    ppermute x29 -> x31, starting transfers between devices: 31.6 us -> 33.5 us  [exchange_bits(): return lax.ppermute(values, AXES, [(i, partner(i)) for i in places])]
    pallas_call x8, Pallas kernels: 37.1 us -> 35.8 us  [call(): pl.pallas_call(kernel, out_shape=outs, in_specs=[VMEM] * len(args) if in_...]
  transfers between devices with their start and end apart: 29 -> 31, of which waited for: 16 -> 14; matrix products, arithmetic and copies ran while one was open for 1% -> 1% of each run, Pallas kernels for 20% -> 20%
where the time goes in v6:
time: 94.4 us; the launch traced here: 94.3 us
  Pallas kernels  35.8 us (38%)
  starting transfers between devices  33.5 us (35%)
  waiting for transfers between devices  22.5 us (24%)
  between operations  1.11 us (1%)
  other arithmetic  1.06 us (1%)
    pallas_call x8, Pallas kernels, call(): pl.pallas_call(kernel, out_shape=outs, in_specs=[VMEM] * len(args) if in_...  35.8 us
    ppermute x31, starting transfers between devices, exchange_bits(): return lax.ppermute(values, AXES, [(i, partner(i)) for i in places])  33.5 us
    ppermute x31, waiting for transfers between devices, exchange_bits(): return lax.ppermute(values, AXES, [(i, partner(i)) for i in places])  22.5 us
  transfers between devices with their start and end apart: 31, of which 14 were waited for; matrix products, arithmetic and copies ran while one was open for 1% of the time, Pallas kernels for 20%

profile of v6, /device:TPU:0, one launch (start us, length us, event | category | flops | bytes accessed | tf_op | source)
XLA Modules:
  0.0 94.3 jit_solution(2451713014212559178)
XLA Ops:
  0.7 15.3 %forward.1 = (f32[2,384]{1,0:T(2,128)S(1)}, f32[2,384]{1,0:T(2,128)S(1)}, f32[2,384]{1,0:T(2,128)S(1)}, f32[2,384]{1,0:T(2,128)S(1)}, f32[2,384]{1,0:T(2,128)S(1...) custom-call(bf16[4,196,4,384]{3,2,1,0:T(4,128)(2,1)} %bitcast.6, ...), custom_call_target="tpu_custom_call" | custom-call | flops 17999998976 | bytes 54000000 | tf_op jit(solution)/shard_map/forward/pallas_call | solution.py:682
  15.9 0.5 collective-permute-start
  16.4 2.6 %last_layer.1 = (f32[3,784,128]{2,1,0:T(8,128)S(1)}, f32[256,256]{1,0:T(8,128)S(1)}, f32[2,24,384]{2,1,0:T(8,128)S(1)}) custom-call(f32[3,784,128]{2,1,0:T(8,128)S(1)} %get-tuple-element.100.s2, f32[3,784,128]{2,1,0:T(8,128)S(1)} %get-tuple-element.101.s3, f32[3,784,128]{2,1,0:T(8,128)S(1)} %get-tuple-element.102.g_rows, ...), custom_call_target="tpu_custom_call" | custom-call | flops 4000000000 | bytes 12000000 | tf_op jit(solution)/shard_map/last_layer/pallas_call | solution.py:682
  19.0 0.1 add_convert_fusion.1
  19.2 2.8 %collective-permute-start.1 = (bf16[8,96,384]{2,1,0:T(8,128)(2,1)S(1)}, bf16[8,96,384]{2,1,0:T(8,128)(2,1)S(1)}, u32[]{:S(2)}, u32[]{:S(2)}) collective-permute-start(bf16[8,96,384]{2,1,0:T(8,128)(2,1)S(1)} %add_convert_fusion.1), channel_id=1, source_target_pairs={{0,2},{1,5},{2,0},{3,7},{4,6},{5,1},{6,4},{7,3},{8,10},{9,13},{10,... | collective-permute-start | bytes 1769480 | tf_op jit(solution)/shard_map/ppermute | solution.py:481
  22.0 7.7 %first_feed_forward.1 = (bf16[16,96,384]{2,1,0:T(8,128)(2,1)S(1)}, bf16[16,96,384]{2,1,0:T(8,128)(2,1)S(1)}, f32[3,784,128]{2,1,0:T(8,128)S(1)}, f32[2,24,384]{2,1,0:T(8,128)S(1)}, f32[3,784,128]{2,1,0:T(8,128)S(1)}) custom-call(f32[3,784,128]{2,1,0:T(8,128)S(1)} %get-tuple-element.99.s1, f32[3,784,128]{2,1,0:T(8,128)S(1)} %get-tuple-element.116.g2, ...), custom_call_target="tpu_custom_call" | custom-call | flops 8999999488 | bytes 27000000 | tf_op jit(solution)/shard_map/first_feed_forward/pallas_call | solution.py:682
  29.7 0.2 collective-permute-done.1
  29.9 0.0 collective-permute-start.2
  29.9 0.1 add_convert_fusion.3
  30.0 2.1 %collective-permute-start.6 = (bf16[4,96,384]{2,1,0:T(8,128)(2,1)S(1)}, bf16[4,96,384]{2,1,0:T(8,128)(2,1)S(1)}, u32[]{:S(2)}, u32[]{:S(2)}) collective-permute-start(bf16[4,96,384]{2,1,0:T(8,128)(2,1)S(1)} %add_convert_fusion.3), channel_id=1, source_target_pairs={{0,4},{1,3},{2,6},{3,1},{4,0},{5,7},{6,2},{7,5},{8,12},{9,11},{10,... | collective-permute-start | bytes 884744 | tf_op jit(solution)/shard_map/ppermute | solution.py:481
  32.1 3.0 %first_cross.1 = (bf16[1,196,4,384]{3,2,1,0:T(4,128)(2,1)}, bf16[1,196,4,384]{3,2,1,0:T(4,128)(2,1)}, bf16[16,8,384]{2,1,0:T(8,128)(2,1)S(1)}, bf16[16,8,384]{2,1,0:T(8,128)(2,1)S(1)}) custom-call(f32[3,784,128]{2,1,0:T(8,128)S(1)} %get-tuple-element.98.s0, f32[3,784,128]{2,1,0:T(8,128)S(1)} %get-tuple-element.127.g1, ...), custom_call_target="tpu_custom_call" | custom-call | flops 5000000000 | bytes 15000000 | tf_op jit(solution)/shard_map/first_cross/pallas_call | solution.py:682
  35.1 0.2 collective-permute-start.4
  35.3 0.1 add_convert_fusion
  35.4 1.4 %collective-permute-start.3 = (bf16[8,96,384]{2,1,0:T(8,128)(2,1)S(1)}, bf16[8,96,384]{2,1,0:T(8,128)(2,1)S(1)}, u32[]{:S(2)}, u32[]{:S(2)}) collective-permute-start(bf16[8,96,384]{2,1,0:T(8,128)(2,1)S(1)} %add_convert_fusion), channel_id=1, source_target_pairs={{0,2},{1,5},{2,0},{3,7},{4,6},{5,1},{6,4},{7,3},{8,10},{9,13},{10,... | collective-permute-start | bytes 1769480 | tf_op jit(solution)/shard_map/ppermute | solution.py:481
  36.8 0.0 collective-permute-done.6
  36.8 0.1 add_convert_fusion.10
  36.9 3.1 %collective-permute-start.7 = (bf16[1,96,384]{2,1,0:T(8,128)(2,1)S(1)}, bf16[1,96,384]{2,1,0:T(8,128)(2,1)S(1)}, u32[]{:S(2)}, u32[]{:S(2)}) collective-permute-start(bf16[1,96,384]{2,1,0:T(8,128)(2,1)S(1)} %get-tuple-element.187), channel_id=1, source_target_pairs={{0,16},{1,17},{2,18},{3,19},{4,20},{5,21},{6,22},{7,23},{8,24},{9,... | collective-permute-start | bytes 221192 | tf_op jit(solution)/shard_map/ppermute | solution.py:481
  40.1 1.6 %collective-permute-start.9 = (bf16[1,96,384]{2,1,0:T(8,128)(2,1)S(1)}, bf16[1,96,384]{2,1,0:T(8,128)(2,1)S(1)}, u32[]{:S(2)}, u32[]{:S(2)}) collective-permute-start(bf16[1,96,384]{2,1,0:T(8,128)(2,1)S(1)} %get-tuple-element.188), channel_id=1, source_target_pairs={{0,8},{1,9},{2,10},{3,11},{4,12},{5,13},{6,14},{7,15},{8,0},{9,1},... | collective-permute-start | bytes 221192 | tf_op jit(solution)/shard_map/ppermute | solution.py:481
  41.6 0.0 collective-permute-start.8
  41.6 0.0 collective-permute-done.4
  41.7 1.8 %collective-permute-start.5 = (bf16[8,8,384]{2,1,0:T(8,128)(2,1)S(1)}, bf16[8,8,384]{2,1,0:T(8,128)(2,1)S(1)}, u32[]{:S(2)}, u32[]{:S(2)}) collective-permute-start(bf16[8,8,384]{2,1,0:T(8,128)(2,1)S(1)} %add_convert_fusion.11), channel_id=1, source_target_pairs={{0,2},{1,5},{2,0},{3,7},{4,6},{5,1},{6,4},{7,3},{8,10},{9,13},{10,... | collective-permute-start | bytes 147464 | tf_op jit(solution)/shard_map/ppermute | solution.py:481
  43.4 0.0 collective-permute-done.7
  43.4 1.0 %collective-permute-done.9 = bf16[1,96,384]{2,1,0:T(8,128)(2,1)S(1)} collective-permute-done((bf16[1,96,384]{2,1,0:T(8,128)(2,1)S(1)}, bf16[1,96,384]{2,1,0:T(8,128)(2,1)S(1)}, u32[]{:S(2)}, u32[]{:S(2)}) %collective-permute-start.9) | collective-permute-done | bytes 73760 | tf_op jit(solution)/shard_map/ppermute | solution.py:481
  44.4 3.4 %collective-permute-done.8 = bf16[1,96,384]{2,1,0:T(8,128)(2,1)S(1)} collective-permute-done((bf16[1,96,384]{2,1,0:T(8,128)(2,1)S(1)}, bf16[1,96,384]{2,1,0:T(8,128)(2,1)S(1)}, u32[]{:S(2)}, u32[]{:S(2)}) %collective-permute-start.8) | collective-permute-done | bytes 73760 | tf_op jit(solution)/shard_map/ppermute | solution.py:481
  47.8 0.1 add_convert_fusion.7
  47.9 0.0 collective-permute-done.3
  47.9 0.1 add_convert_fusion.2
  48.1 1.6 %collective-permute-start.10 = (bf16[4,104,384]{2,1,0:T(8,128)(2,1)S(1)}, bf16[4,104,384]{2,1,0:T(8,128)(2,1)S(1)}, u32[]{:S(2)}, u32[]{:S(2)}) collective-permute-start(bf16[4,104,384]{2,1,0:T(8,128)(2,1)S(1)} %pad_maximum_fusion), channel_id=1, source_target_pairs={{0,4},{1,3},{2,6},{3,1},{4,0},{5,7},{6,2},{7,5},{8,12},{9,11},{10,... | collective-permute-start | bytes 958472 | tf_op jit(solution)/shard_map/ppermute | solution.py:481
  49.6 1.8 %collective-permute-start.19 = (bf16[1,96,384]{2,1,0:T(8,128)(2,1)S(1)}, bf16[1,96,384]{2,1,0:T(8,128)(2,1)S(1)}, u32[]{:S(2)}, u32[]{:S(2)}) collective-permute-start(bf16[1,96,384]{2,1,0:T(8,128)(2,1)S(1)} %add_convert_fusion.7), channel_id=1, source_target_pairs={{0,24},{1,25},{2,26},{3,27},{4,28},{5,29},{6,30},{7,31},{8,16},{9,... | collective-permute-start | bytes 221192 | tf_op jit(solution)/shard_map/ppermute | solution.py:481
  51.4 0.5 collective-permute-start.18
  51.9 2.1 %collective-permute-start.17 = (bf16[1,96,384]{2,1,0:T(8,128)(2,1)S(1)}, bf16[1,96,384]{2,1,0:T(8,128)(2,1)S(1)}, u32[]{:S(2)}, u32[]{:S(2)}) collective-permute-start(bf16[1,96,384]{2,1,0:T(8,128)(2,1)S(1)} %add_convert_fusion.7), channel_id=1, source_target_pairs={{0,16},{1,17},{2,18},{3,19},{4,20},{5,21},{6,22},{7,23},{8,24},{9,... | collective-permute-start | bytes 221192 | tf_op jit(solution)/shard_map/ppermute | solution.py:481
  54.1 1.1 %collective-permute-done.10 = bf16[4,104,384]{2,1,0:T(8,128)(2,1)S(1)} collective-permute-done((bf16[4,104,384]{2,1,0:T(8,128)(2,1)S(1)}, bf16[4,104,384]{2,1,0:T(8,128)(2,1)S(1)}, u32[]{:S(2)}, u32[]{:S(2)}) %collective-permute-start.10) | collective-permute-done | bytes 319520 | tf_op jit(solution)/shard_map/ppermute | solution.py:481
  55.1 0.1 convert_add_fusion
  55.3 1.8 %collective-permute-start.11 = (bf16[1,104,384]{2,1,0:T(8,128)(2,1)S(1)}, bf16[1,104,384]{2,1,0:T(8,128)(2,1)S(1)}, u32[]{:S(2)}, u32[]{:S(2)}) collective-permute-start(bf16[1,104,384]{2,1,0:T(8,128)(2,1)S(1)} %pad_maximum_fusion.2), channel_id=1, source_target_pairs={{0,16},{1,17},{2,18},{3,19},{4,20},{5,21},{6,22},{7,23},{8,24},{9,... | collective-permute-start | bytes 239624 | tf_op jit(solution)/shard_map/ppermute | solution.py:481
  57.1 0.5 collective-permute-start.12
  57.7 1.4 %collective-permute-start.13 = (bf16[1,104,384]{2,1,0:T(8,128)(2,1)S(1)}, bf16[1,104,384]{2,1,0:T(8,128)(2,1)S(1)}, u32[]{:S(2)}, u32[]{:S(2)}) collective-permute-start(bf16[1,104,384]{2,1,0:T(8,128)(2,1)S(1)} %pad_maximum_fusion.4), channel_id=1, source_target_pairs={{0,8},{1,9},{2,10},{3,11},{4,12},{5,13},{6,14},{7,15},{8,0},{9,1},... | collective-permute-start | bytes 239624 | tf_op jit(solution)/shard_map/ppermute | solution.py:481
  59.0 2.1 %collective-permute-done.17 = bf16[1,96,384]{2,1,0:T(8,128)(2,1)S(1)} collective-permute-done((bf16[1,96,384]{2,1,0:T(8,128)(2,1)S(1)}, bf16[1,96,384]{2,1,0:T(8,128)(2,1)S(1)}, u32[]{:S(2)}, u32[]{:S(2)}) %collective-permute-start.17) | collective-permute-done | bytes 73760 | tf_op jit(solution)/shard_map/ppermute | solution.py:481
  61.3 1.5 %collective-permute-start.21 = (bf16[4,96,384]{2,1,0:T(8,128)(2,1)S(1)}, bf16[4,96,384]{2,1,0:T(8,128)(2,1)S(1)}, u32[]{:S(2)}, u32[]{:S(2)}) collective-permute-start(bf16[4,96,384]{2,1,0:T(8,128)(2,1)S(1)} %get-tuple-element.195), channel_id=1, source_target_pairs={{0,2},{1,5},{2,0},{3,7},{4,6},{5,1},{6,4},{7,3},{8,10},{9,13},{10,... | collective-permute-start | bytes 884744 | tf_op jit(solution)/shard_map/ppermute | solution.py:481
  62.8 0.9 collective-permute-done.11
  63.7 0.2 collective-permute-done.13
  64.0 2.4 %collective-permute-start.16 = (bf16[1,104,384]{2,1,0:T(8,128)(2,1)S(1)}, bf16[1,104,384]{2,1,0:T(8,128)(2,1)S(1)}, u32[]{:S(2)}, u32[]{:S(2)}) collective-permute-start(bf16[1,104,384]{2,1,0:T(8,128)(2,1)S(1)} %get-tuple-element.182), channel_id=1, source_target_pairs={{0,24},{1,25},{2,26},{3,27},{4,28},{5,29},{6,30},{7,31},{8,16},{9,... | collective-permute-start | bytes 239624 | tf_op jit(solution)/shard_map/ppermute | solution.py:481
  66.5 0.5 collective-permute-start.15
  67.0 1.5 %collective-permute-start.14 = (bf16[1,104,384]{2,1,0:T(8,128)(2,1)S(1)}, bf16[1,104,384]{2,1,0:T(8,128)(2,1)S(1)}, u32[]{:S(2)}, u32[]{:S(2)}) collective-permute-start(bf16[1,104,384]{2,1,0:T(8,128)(2,1)S(1)} %get-tuple-element.182), channel_id=1, source_target_pairs={{0,16},{1,17},{2,18},{3,19},{4,20},{5,21},{6,22},{7,23},{8,24},{9,... | collective-permute-start | bytes 239624 | tf_op jit(solution)/shard_map/ppermute | solution.py:481
  68.5 1.0 %collective-permute-done.20 = bf16[4,96,384]{2,1,0:T(8,128)(2,1)S(1)} collective-permute-done((bf16[4,96,384]{2,1,0:T(8,128)(2,1)S(1)}, bf16[4,96,384]{2,1,0:T(8,128)(2,1)S(1)}, u32[]{:S(2)}, u32[]{:S(2)}) %collective-permute-start.20) | collective-permute-done | bytes 294944 | tf_op jit(solution)/shard_map/ppermute | solution.py:481
  69.5 0.5 collective-permute-start.25
  70.1 0.9 collective-permute-done.16
  71.0 1.6 %collective-permute-done.15 = bf16[1,104,384]{2,1,0:T(8,128)(2,1)S(1)} collective-permute-done((bf16[1,104,384]{2,1,0:T(8,128)(2,1)S(1)}, bf16[1,104,384]{2,1,0:T(8,128)(2,1)S(1)}, u32[]{:S(2)}, u32[]{:S(2)}) %collective-permute-start.15) | collective-permute-done | bytes 79904 | tf_op jit(solution)/shard_map/ppermute | solution.py:481
  72.6 1.1 %collective-permute-done.14 = bf16[1,104,384]{2,1,0:T(8,128)(2,1)S(1)} collective-permute-done((bf16[1,104,384]{2,1,0:T(8,128)(2,1)S(1)}, bf16[1,104,384]{2,1,0:T(8,128)(2,1)S(1)}, u32[]{:S(2)}, u32[]{:S(2)}) %collective-permute-start.14) | collective-permute-done | bytes 79904 | tf_op jit(solution)/shard_map/ppermute | solution.py:481
  73.7 0.1 pad_maximum_fusion.1
  73.8 1.5 %collective-permute-start.23 = (bf16[4,104,384]{2,1,0:T(8,128)(2,1)S(1)}, bf16[4,104,384]{2,1,0:T(8,128)(2,1)S(1)}, u32[]{:S(2)}, u32[]{:S(2)}) collective-permute-start(bf16[4,104,384]{2,1,0:T(8,128)(2,1)S(1)} %pad_maximum_fusion.1), channel_id=1, source_target_pairs={{0,2},{1,5},{2,0},{3,7},{4,6},{5,1},{6,4},{7,3},{8,10},{9,13},{10,... | collective-permute-start | bytes 958472 | tf_op jit(solution)/shard_map/ppermute | solution.py:481
  75.3 0.3 collective-permute-start.22
  75.6 0.1 collective-permute-start.29
  75.7 7.6 %collective-permute-done.23.refs_4_ = bf16[4,104,384]{2,1,0:T(8,128)(2,1)S(1)} collective-permute-done((bf16[4,104,384]{2,1,0:T(8,128)(2,1)S(1)}, bf16[4,104,384]{2,1,0:T(8,128)(2,1)S(1)}, u32[]{:S(2)}, u32[]{:S(2)}) %collective-permute-start.23) | collective-permute-done | bytes 319520 | tf_op jit(solution)/shard_map/ppermute | solution.py:481
  83.3 0.1 constant_dynamic-update-slice_fusion.6.refs_3_
  83.4 0.1 collective-permute-start.27
  83.6 0.6 collective-permute-start.26
  84.1 1.2 %collective-permute-start.24 = (bf16[4,104,384]{2,1,0:T(8,128)(2,1)S(1)}, bf16[4,104,384]{2,1,0:T(8,128)(2,1)S(1)}, u32[]{:S(2)}, u32[]{:S(2)}) collective-permute-start(bf16[4,104,384]{2,1,0:T(8,128)(2,1)S(1)} %collective-permute-done.22), channel_id=1, source_target_pairs={{0,2},{1,5},{2,0},{3,7},{4,6},{5,1},{6,4},{7,3},{8,10},{9,13},{10,... | collective-permute-start | bytes 958472 | tf_op jit(solution)/shard_map/ppermute | solution.py:481
  85.3 0.1 collective-permute-start.28
  85.5 3.0 %unpack_kept.1 = (f32[2,384,1536]{2,1,0:T(8,128)}, f32[2,1536,384]{2,1,0:T(8,128)}, f32[32,8,384]{2,1,0:T(8,128)S(1)}) custom-call(bf16[8,96,384]{2,1,0:T(8,128)(2,1)S(1)} %constant_dynamic-update-slice_fusion.11.refs_0_, bf16[8,96,384]{2,1,0:T(8,128)(2,1)S(1)} %collective-permute-done.29.refs_1_, ...), custom_call_target="tpu_custom_call" | custom-call | flops 4499999744 | bytes 13500000 | tf_op jit(solution)/shard_map/unpack_kept/pallas_call | solution.py:682
  88.5 2.0 %unpack_others.1 = (f32[2,384,1536]{2,1,0:T(8,128)}, f32[2,1536,384]{2,1,0:T(8,128)}, f32[32,8,384]{2,1,0:T(8,128)S(1)}) custom-call(bf16[8,96,384]{2,1,0:T(8,128)(2,1)S(1)} %collective-permute-done.26.refs_0_, bf16[8,104,384]{2,1,0:T(8,128)(2,1)S(1)} %collective-permute-done.27.refs_1_, ...), custom_call_target="tpu_custom_call", output_to_operand_aliasing={{0}: (3, {}), {1}: (4, {}), {2}: (5, {})} | custom-call | flops 2500000000 | bytes 7500000 | tf_op jit(solution)/shard_map/unpack_others/pallas_call | solution.py:682
  90.6 0.5 collective-permute-done.24.refs_0_
  91.1 0.9 unpack_latest.1
  92.0 0.7 collective-permute-done.30.other_late
  92.7 1.3 %unpack_rest.1 = (f32[2,384,1536]{2,1,0:T(8,128)}, f32[2,1536,384]{2,1,0:T(8,128)}, f32[32,8,384]{2,1,0:T(8,128)S(1)}, f32[196,2,196]{2,1,0:T(2,128)}, f32[2,384...) custom-call(bf16[4,104,384]{2,1,0:T(8,128)(2,1)S(1)} %collective-per, ...), custom_call_target="tpu_custom_call", output_to_operand_aliasing={{0}: (1, {}), {1}: (2, {}), {2}: (3, {})} | custom-call | flops 2000000000 | bytes 6000000 | tf_op jit(solution)/shard_map/unpack_rest/pallas_call | solution.py:682
  (33 shorter events, 0.5 us)
Async XLA Ops:
  15.9 3.1 %collective-permute-start = (bf16[16,96,384]{2,1,0:T(8,128)(2,1)S(1)}, bf16[16,96,384]{2,1,0:T(8,128)(2,1)S(1)}, u32[]{:S(2)}, u32[]{:S(2)}) collective-permute-start(bf16[16,96,384]{2,1,0:T(8,128)(2,1)S(1)} %get-tuple-element.115), channel_id=1, source_target_pairs={{0,1},{1,0},{2,3},{3,2},{4,5},{5,4},{6,7},{7,6},{8,9},{9,8},{10,11... | collective-permute-start | bytes 3538952 | tf_op jit(solution)/shard_map/ppermute | solution.py:481
  19.2 10.7 %collective-permute-start.1 = (bf16[8,96,384]{2,1,0:T(8,128)(2,1)S(1)}, bf16[8,96,384]{2,1,0:T(8,128)(2,1)S(1)}, u32[]{:S(2)}, u32[]{:S(2)}) collective-permute-start(bf16[8,96,384]{2,1,0:T(8,128)(2,1)S(1)} %add_convert_fusion.1), channel_id=1, source_target_pairs={{0,2},{1,5},{2,0},{3,7},{4,6},{5,1},{6,4},{7,3},{8,10},{9,13},{10,... | collective-permute-start | bytes 1769480 | tf_op jit(solution)/shard_map/ppermute | solution.py:481
  29.9 5.4 %collective-permute-start.2 = (bf16[16,96,384]{2,1,0:T(8,128)(2,1)S(1)}, bf16[16,96,384]{2,1,0:T(8,128)(2,1)S(1)}, u32[]{:S(2)}, u32[]{:S(2)}) collective-permute-start(bf16[16,96,384]{2,1,0:T(8,128)(2,1)S(1)} %get-tuple-element.138), channel_id=1, source_target_pairs={{0,1},{1,0},{2,3},{3,2},{4,5},{5,4},{6,7},{7,6},{8,9},{9,8},{10,11... | collective-permute-start | bytes 3538952 | tf_op jit(solution)/shard_map/ppermute | solution.py:481
  30.0 6.8 %collective-permute-start.6 = (bf16[4,96,384]{2,1,0:T(8,128)(2,1)S(1)}, bf16[4,96,384]{2,1,0:T(8,128)(2,1)S(1)}, u32[]{:S(2)}, u32[]{:S(2)}) collective-permute-start(bf16[4,96,384]{2,1,0:T(8,128)(2,1)S(1)} %add_convert_fusion.3), channel_id=1, source_target_pairs={{0,4},{1,3},{2,6},{3,1},{4,0},{5,7},{6,2},{7,5},{8,12},{9,11},{10,... | collective-permute-start | bytes 884744 | tf_op jit(solution)/shard_map/ppermute | solution.py:481
  35.1 6.5 %collective-permute-start.4 = (bf16[16,8,384]{2,1,0:T(8,128)(2,1)S(1)}, bf16[16,8,384]{2,1,0:T(8,128)(2,1)S(1)}, u32[]{:S(2)}, u32[]{:S(2)}) collective-permute-start(bf16[16,8,384]{2,1,0:T(8,128)(2,1)S(1)} %get-tuple-element.140), channel_id=1, source_target_pairs={{0,1},{1,0},{2,3},{3,2},{4,5},{5,4},{6,7},{7,6},{8,9},{9,8},{10,11... | collective-permute-start | bytes 294920 | tf_op jit(solution)/shard_map/ppermute | solution.py:481
  35.4 12.4 %collective-permute-start.3 = (bf16[8,96,384]{2,1,0:T(8,128)(2,1)S(1)}, bf16[8,96,384]{2,1,0:T(8,128)(2,1)S(1)}, u32[]{:S(2)}, u32[]{:S(2)}) collective-permute-start(bf16[8,96,384]{2,1,0:T(8,128)(2,1)S(1)} %add_convert_fusion), channel_id=1, source_target_pairs={{0,2},{1,5},{2,0},{3,7},{4,6},{5,1},{6,4},{7,3},{8,10},{9,13},{10,... | collective-permute-start | bytes 1769480 | tf_op jit(solution)/shard_map/ppermute | solution.py:481
  36.9 6.5 %collective-permute-start.7 = (bf16[1,96,384]{2,1,0:T(8,128)(2,1)S(1)}, bf16[1,96,384]{2,1,0:T(8,128)(2,1)S(1)}, u32[]{:S(2)}, u32[]{:S(2)}) collective-permute-start(bf16[1,96,384]{2,1,0:T(8,128)(2,1)S(1)} %get-tuple-element.187), channel_id=1, source_target_pairs={{0,16},{1,17},{2,18},{3,19},{4,20},{5,21},{6,22},{7,23},{8,24},{9,... | collective-permute-start | bytes 221192 | tf_op jit(solution)/shard_map/ppermute | solution.py:481
  40.1 4.4 %collective-permute-start.9 = (bf16[1,96,384]{2,1,0:T(8,128)(2,1)S(1)}, bf16[1,96,384]{2,1,0:T(8,128)(2,1)S(1)}, u32[]{:S(2)}, u32[]{:S(2)}) collective-permute-start(bf16[1,96,384]{2,1,0:T(8,128)(2,1)S(1)} %get-tuple-element.188), channel_id=1, source_target_pairs={{0,8},{1,9},{2,10},{3,11},{4,12},{5,13},{6,14},{7,15},{8,0},{9,1},... | collective-permute-start | bytes 221192 | tf_op jit(solution)/shard_map/ppermute | solution.py:481
  41.6 6.2 %collective-permute-start.8 = (bf16[1,96,384]{2,1,0:T(8,128)(2,1)S(1)}, bf16[1,96,384]{2,1,0:T(8,128)(2,1)S(1)}, u32[]{:S(2)}, u32[]{:S(2)}) collective-permute-start(bf16[1,96,384]{2,1,0:T(8,128)(2,1)S(1)} %get-tuple-element.189), channel_id=1, source_target_pairs={{0,24},{1,25},{2,26},{3,27},{4,28},{5,29},{6,30},{7,31},{8,16},{9,... | collective-permute-start | bytes 221192 | tf_op jit(solution)/shard_map/ppermute | solution.py:481
  41.7 6.2 %collective-permute-start.5 = (bf16[8,8,384]{2,1,0:T(8,128)(2,1)S(1)}, bf16[8,8,384]{2,1,0:T(8,128)(2,1)S(1)}, u32[]{:S(2)}, u32[]{:S(2)}) collective-permute-start(bf16[8,8,384]{2,1,0:T(8,128)(2,1)S(1)} %add_convert_fusion.11), channel_id=1, source_target_pairs={{0,2},{1,5},{2,0},{3,7},{4,6},{5,1},{6,4},{7,3},{8,10},{9,13},{10,... | collective-permute-start | bytes 147464 | tf_op jit(solution)/shard_map/ppermute | solution.py:481
  48.1 7.1 %collective-permute-start.10 = (bf16[4,104,384]{2,1,0:T(8,128)(2,1)S(1)}, bf16[4,104,384]{2,1,0:T(8,128)(2,1)S(1)}, u32[]{:S(2)}, u32[]{:S(2)}) collective-permute-start(bf16[4,104,384]{2,1,0:T(8,128)(2,1)S(1)} %pad_maximum_fusion), channel_id=1, source_target_pairs={{0,4},{1,3},{2,6},{3,1},{4,0},{5,7},{6,2},{7,5},{8,12},{9,11},{10,... | collective-permute-start | bytes 958472 | tf_op jit(solution)/shard_map/ppermute | solution.py:481
  49.6 8.0 %collective-permute-start.19 = (bf16[1,96,384]{2,1,0:T(8,128)(2,1)S(1)}, bf16[1,96,384]{2,1,0:T(8,128)(2,1)S(1)}, u32[]{:S(2)}, u32[]{:S(2)}) collective-permute-start(bf16[1,96,384]{2,1,0:T(8,128)(2,1)S(1)} %add_convert_fusion.7), channel_id=1, source_target_pairs={{0,24},{1,25},{2,26},{3,27},{4,28},{5,29},{6,30},{7,31},{8,16},{9,... | collective-permute-start | bytes 221192 | tf_op jit(solution)/shard_map/ppermute | solution.py:481
  51.4 7.6 %collective-permute-start.18 = (bf16[1,96,384]{2,1,0:T(8,128)(2,1)S(1)}, bf16[1,96,384]{2,1,0:T(8,128)(2,1)S(1)}, u32[]{:S(2)}, u32[]{:S(2)}) collective-permute-start(bf16[1,96,384]{2,1,0:T(8,128)(2,1)S(1)} %add_convert_fusion.7), channel_id=1, source_target_pairs={{0,8},{1,9},{2,10},{3,11},{4,12},{5,13},{6,14},{7,15},{8,0},{9,1},... | collective-permute-start | bytes 221192 | tf_op jit(solution)/shard_map/ppermute | solution.py:481
  51.9 9.2 %collective-permute-start.17 = (bf16[1,96,384]{2,1,0:T(8,128)(2,1)S(1)}, bf16[1,96,384]{2,1,0:T(8,128)(2,1)S(1)}, u32[]{:S(2)}, u32[]{:S(2)}) collective-permute-start(bf16[1,96,384]{2,1,0:T(8,128)(2,1)S(1)} %add_convert_fusion.7), channel_id=1, source_target_pairs={{0,16},{1,17},{2,18},{3,19},{4,20},{5,21},{6,22},{7,23},{8,24},{9,... | collective-permute-start | bytes 221192 | tf_op jit(solution)/shard_map/ppermute | solution.py:481
  55.3 8.4 %collective-permute-start.11 = (bf16[1,104,384]{2,1,0:T(8,128)(2,1)S(1)}, bf16[1,104,384]{2,1,0:T(8,128)(2,1)S(1)}, u32[]{:S(2)}, u32[]{:S(2)}) collective-permute-start(bf16[1,104,384]{2,1,0:T(8,128)(2,1)S(1)} %pad_maximum_fusion.2), channel_id=1, source_target_pairs={{0,16},{1,17},{2,18},{3,19},{4,20},{5,21},{6,22},{7,23},{8,24},{9,... | collective-permute-start | bytes 239624 | tf_op jit(solution)/shard_map/ppermute | solution.py:481
  57.1 6.6 %collective-permute-start.12 = (bf16[1,104,384]{2,1,0:T(8,128)(2,1)S(1)}, bf16[1,104,384]{2,1,0:T(8,128)(2,1)S(1)}, u32[]{:S(2)}, u32[]{:S(2)}) collective-permute-start(bf16[1,104,384]{2,1,0:T(8,128)(2,1)S(1)} %pad_maximum_fusion.3), channel_id=1, source_target_pairs={{0,24},{1,25},{2,26},{3,27},{4,28},{5,29},{6,30},{7,31},{8,16},{9,... | collective-permute-start | bytes 239624 | tf_op jit(solution)/shard_map/ppermute | solution.py:481
  57.7 6.3 %collective-permute-start.13 = (bf16[1,104,384]{2,1,0:T(8,128)(2,1)S(1)}, bf16[1,104,384]{2,1,0:T(8,128)(2,1)S(1)}, u32[]{:S(2)}, u32[]{:S(2)}) collective-permute-start(bf16[1,104,384]{2,1,0:T(8,128)(2,1)S(1)} %pad_maximum_fusion.4), channel_id=1, source_target_pairs={{0,8},{1,9},{2,10},{3,11},{4,12},{5,13},{6,14},{7,15},{8,0},{9,1},... | collective-permute-start | bytes 239624 | tf_op jit(solution)/shard_map/ppermute | solution.py:481
  61.3 12.5 %collective-permute-start.21 = (bf16[4,96,384]{2,1,0:T(8,128)(2,1)S(1)}, bf16[4,96,384]{2,1,0:T(8,128)(2,1)S(1)}, u32[]{:S(2)}, u32[]{:S(2)}) collective-permute-start(bf16[4,96,384]{2,1,0:T(8,128)(2,1)S(1)} %get-tuple-element.195), channel_id=1, source_target_pairs={{0,2},{1,5},{2,0},{3,7},{4,6},{5,1},{6,4},{7,3},{8,10},{9,13},{10,... | collective-permute-start | bytes 884744 | tf_op jit(solution)/shard_map/ppermute | solution.py:481
  62.8 6.7 %collective-permute-start.20 = (bf16[4,96,384]{2,1,0:T(8,128)(2,1)S(1)}, bf16[4,96,384]{2,1,0:T(8,128)(2,1)S(1)}, u32[]{:S(2)}, u32[]{:S(2)}) collective-permute-start(bf16[4,96,384]{2,1,0:T(8,128)(2,1)S(1)} %get-tuple-element.195), channel_id=1, source_target_pairs={{0,4},{1,3},{2,6},{3,1},{4,0},{5,7},{6,2},{7,5},{8,12},{9,11},{10,... | collective-permute-start | bytes 884744 | tf_op jit(solution)/shard_map/ppermute | solution.py:481
  64.0 7.0 %collective-permute-start.16 = (bf16[1,104,384]{2,1,0:T(8,128)(2,1)S(1)}, bf16[1,104,384]{2,1,0:T(8,128)(2,1)S(1)}, u32[]{:S(2)}, u32[]{:S(2)}) collective-permute-start(bf16[1,104,384]{2,1,0:T(8,128)(2,1)S(1)} %get-tuple-element.182), channel_id=1, source_target_pairs={{0,24},{1,25},{2,26},{3,27},{4,28},{5,29},{6,30},{7,31},{8,16},{9,... | collective-permute-start | bytes 239624 | tf_op jit(solution)/shard_map/ppermute | solution.py:481
  66.5 6.2 %collective-permute-start.15 = (bf16[1,104,384]{2,1,0:T(8,128)(2,1)S(1)}, bf16[1,104,384]{2,1,0:T(8,128)(2,1)S(1)}, u32[]{:S(2)}, u32[]{:S(2)}) collective-permute-start(bf16[1,104,384]{2,1,0:T(8,128)(2,1)S(1)} %get-tuple-element.182), channel_id=1, source_target_pairs={{0,8},{1,9},{2,10},{3,11},{4,12},{5,13},{6,14},{7,15},{8,0},{9,1},... | collective-permute-start | bytes 239624 | tf_op jit(solution)/shard_map/ppermute | solution.py:481
  67.0 6.7 %collective-permute-start.14 = (bf16[1,104,384]{2,1,0:T(8,128)(2,1)S(1)}, bf16[1,104,384]{2,1,0:T(8,128)(2,1)S(1)}, u32[]{:S(2)}, u32[]{:S(2)}) collective-permute-start(bf16[1,104,384]{2,1,0:T(8,128)(2,1)S(1)} %get-tuple-element.182), channel_id=1, source_target_pairs={{0,16},{1,17},{2,18},{3,19},{4,20},{5,21},{6,22},{7,23},{8,24},{9,... | collective-permute-start | bytes 239624 | tf_op jit(solution)/shard_map/ppermute | solution.py:481
  69.5 13.8 %collective-permute-start.25 = (bf16[4,96,384]{2,1,0:T(8,128)(2,1)S(1)}, bf16[4,96,384]{2,1,0:T(8,128)(2,1)S(1)}, u32[]{:S(2)}, u32[]{:S(2)}) collective-permute-start(bf16[4,96,384]{2,1,0:T(8,128)(2,1)S(1)} %collective-permute-done.20), channel_id=1, source_target_pairs={{0,2},{1,5},{2,0},{3,7},{4,6},{5,1},{6,4},{7,3},{8,10},{9,13},{10,... | collective-permute-start | bytes 884744 | tf_op jit(solution)/shard_map/ppermute | solution.py:481
  73.8 9.5 %collective-permute-start.23 = (bf16[4,104,384]{2,1,0:T(8,128)(2,1)S(1)}, bf16[4,104,384]{2,1,0:T(8,128)(2,1)S(1)}, u32[]{:S(2)}, u32[]{:S(2)}) collective-permute-start(bf16[4,104,384]{2,1,0:T(8,128)(2,1)S(1)} %pad_maximum_fusion.1), channel_id=1, source_target_pairs={{0,2},{1,5},{2,0},{3,7},{4,6},{5,1},{6,4},{7,3},{8,10},{9,13},{10,... | collective-permute-start | bytes 958472 | tf_op jit(solution)/shard_map/ppermute | solution.py:481
  75.3 8.1 %collective-permute-start.22 = (bf16[4,104,384]{2,1,0:T(8,128)(2,1)S(1)}, bf16[4,104,384]{2,1,0:T(8,128)(2,1)S(1)}, u32[]{:S(2)}, u32[]{:S(2)}) collective-permute-start(bf16[4,104,384]{2,1,0:T(8,128)(2,1)S(1)} %pad_maximum_fusion.1), channel_id=1, source_target_pairs={{0,4},{1,3},{2,6},{3,1},{4,0},{5,7},{6,2},{7,5},{8,12},{9,11},{10,... | collective-permute-start | bytes 958472 | tf_op jit(solution)/shard_map/ppermute | solution.py:481
  75.6 9.9 %collective-permute-start.29 = (bf16[8,96,384]{2,1,0:T(8,128)(2,1)S(1)}, bf16[8,96,384]{2,1,0:T(8,128)(2,1)S(1)}, u32[]{:S(2)}, u32[]{:S(2)}) collective-permute-start(bf16[8,96,384]{2,1,0:T(8,128)(2,1)S(1)} %constant_dynamic-update-slice_fusion.11.refs_0_), channel_id=1, source_target_pairs={{0,1},{1,0},{2,3},{3,2},{4,5},{5,4},{6,7},{7,6},{8,9},{9,8},{10,11... | collective-permute-start | bytes 1769480 | tf_op jit(solution)/shard_map/ppermute | solution.py:481
  83.4 5.1 %collective-permute-start.27 = (bf16[8,104,384]{2,1,0:T(8,128)(2,1)S(1)}, bf16[8,104,384]{2,1,0:T(8,128)(2,1)S(1)}, u32[]{:S(2)}, u32[]{:S(2)}) collective-permute-start(bf16[8,104,384]{2,1,0:T(8,128)(2,1)S(1)} %constant_dynamic-update-slice_fusion.6.refs_3_), channel_id=1, source_target_pairs={{0,1},{1,0},{2,3},{3,2},{4,5},{5,4},{6,7},{7,6},{8,9},{9,8},{10,11... | collective-permute-start | bytes 1916936 | tf_op jit(solution)/shard_map/ppermute | solution.py:481
  83.6 4.9 %collective-permute-start.26 = (bf16[8,96,384]{2,1,0:T(8,128)(2,1)S(1)}, bf16[8,96,384]{2,1,0:T(8,128)(2,1)S(1)}, u32[]{:S(2)}, u32[]{:S(2)}) collective-permute-start(bf16[8,96,384]{2,1,0:T(8,128)(2,1)S(1)} %constant_dynamic-update-slice_fusion.4.refs_2_), channel_id=1, source_target_pairs={{0,1},{1,0},{2,3},{3,2},{4,5},{5,4},{6,7},{7,6},{8,9},{9,8},{10,11... | collective-permute-start | bytes 1769480 | tf_op jit(solution)/shard_map/ppermute | solution.py:481
  84.1 7.0 %collective-permute-start.24 = (bf16[4,104,384]{2,1,0:T(8,128)(2,1)S(1)}, bf16[4,104,384]{2,1,0:T(8,128)(2,1)S(1)}, u32[]{:S(2)}, u32[]{:S(2)}) collective-permute-start(bf16[4,104,384]{2,1,0:T(8,128)(2,1)S(1)} %collective-permute-done.22), channel_id=1, source_target_pairs={{0,2},{1,5},{2,0},{3,7},{4,6},{5,1},{6,4},{7,3},{8,10},{9,13},{10,... | collective-permute-start | bytes 958472 | tf_op jit(solution)/shard_map/ppermute | solution.py:481
  85.3 3.2 %collective-permute-start.28 = (bf16[4,104,384]{2,1,0:T(8,128)(2,1)S(1)}, bf16[4,104,384]{2,1,0:T(8,128)(2,1)S(1)}, u32[]{:S(2)}, u32[]{:S(2)}) collective-permute-start(bf16[4,104,384]{2,1,0:T(8,128)(2,1)S(1)} %collective-permute-done.23.refs_4_), channel_id=1, source_target_pairs={{0,1},{1,0},{2,3},{3,2},{4,5},{5,4},{6,7},{7,6},{8,9},{9,8},{10,11... | collective-permute-start | bytes 958472 | tf_op jit(solution)/shard_map/ppermute | solution.py:481
  91.1 1.6 %collective-permute-start.30 = (bf16[4,104,384]{2,1,0:T(8,128)(2,1)S(1)}, bf16[4,104,384]{2,1,0:T(8,128)(2,1)S(1)}, u32[]{:S(2)}, u32[]{:S(2)}) collective-permute-start(bf16[4,104,384]{2,1,0:T(8,128)(2,1)S(1)} %collective-permute-done.24.refs_0_), channel_id=1, source_target_pairs={{0,1},{1,0},{2,3},{3,2},{4,5},{5,4},{6,7},{7,6},{8,9},{9,8},{10,11... | collective-permute-start | bytes 958472 | tf_op jit(solution)/shard_map/ppermute | solution.py:481

commit v7 on v6

--- a/solution.py
+++ b/solution.py
@@ -78,7 +78,7 @@
 
 
 def pack_halves(codes, block_at, kept_ref, sent_ref):
-    @pl.loop(0, HALF)
+    @pl.loop(0, HALF, unroll=4)
     def _(slot):
         for block, out_ref in ((sent_block(codes, slot), sent_ref), (kept_block(codes, slot), kept_ref)):
             at = 0

time: 94.4 us -> 94.4 us (level)
  transfers between devices with their start and end apart: 31 -> 31, of which waited for: 14 -> 15; matrix products, arithmetic and copies ran while one was open for 1% -> 1% of each run, Pallas kernels for 20% -> 20%
where the time goes in v7:
time: 94.4 us; the launch traced here: 94.2 us
  Pallas kernels  35.7 us (38%)
  starting transfers between devices  33.5 us (35%)
  waiting for transfers between devices  22.6 us (24%)
  between operations  1.11 us (1%)
  other arithmetic  1.06 us (1%)
    pallas_call x8, Pallas kernels, call(): pl.pallas_call(kernel, out_shape=outs, in_specs=[VMEM] * len(args) if in_...  35.7 us
    ppermute x31, starting transfers between devices, exchange_bits(): return lax.ppermute(values, AXES, [(i, partner(i)) for i in places])  33.5 us
    ppermute x31, waiting for transfers between devices, exchange_bits(): return lax.ppermute(values, AXES, [(i, partner(i)) for i in places])  22.6 us
  transfers between devices with their start and end apart: 31, of which 15 were waited for; matrix products, arithmetic and copies ran while one was open for 1% of the time, Pallas kernels for 20%

profile of v7, /device:TPU:0, one launch (start us, length us, event | category | flops | bytes accessed | tf_op | source)
XLA Modules:
  0.0 94.2 jit_solution(7231129762252874944)
XLA Ops:
  0.7 15.2 %forward.1 = (f32[2,384]{1,0:T(2,128)S(1)}, f32[2,384]{1,0:T(2,128)S(1)}, f32[2,384]{1,0:T(2,128)S(1)}, f32[2,384]{1,0:T(2,128)S(1)}, f32[2,384]{1,0:T(2,128)S(1...) custom-call(bf16[4,196,4,384]{3,2,1,0:T(4,128)(2,1)} %bitcast.6, ...), custom_call_target="tpu_custom_call" | custom-call | flops 17999998976 | bytes 54000000 | tf_op jit(solution)/shard_map/forward/pallas_call | solution.py:682
  15.9 0.5 collective-permute-start
  16.4 2.6 %last_layer.1 = (f32[3,784,128]{2,1,0:T(8,128)S(1)}, f32[256,256]{1,0:T(8,128)S(1)}, f32[2,24,384]{2,1,0:T(8,128)S(1)}) custom-call(f32[3,784,128]{2,1,0:T(8,128)S(1)} %get-tuple-element.100.s2, f32[3,784,128]{2,1,0:T(8,128)S(1)} %get-tuple-element.101.s3, f32[3,784,128]{2,1,0:T(8,128)S(1)} %get-tuple-element.102.g_rows, ...), custom_call_target="tpu_custom_call" | custom-call | flops 4000000000 | bytes 12000000 | tf_op jit(solution)/shard_map/last_layer/pallas_call | solution.py:682
  19.0 0.0 collective-permute-done
  19.0 0.1 add_convert_fusion.1
  19.1 2.8 %collective-permute-start.1 = (bf16[8,96,384]{2,1,0:T(8,128)(2,1)S(1)}, bf16[8,96,384]{2,1,0:T(8,128)(2,1)S(1)}, u32[]{:S(2)}, u32[]{:S(2)}) collective-permute-start(bf16[8,96,384]{2,1,0:T(8,128)(2,1)S(1)} %add_convert_fusion.1), channel_id=1, source_target_pairs={{0,2},{1,5},{2,0},{3,7},{4,6},{5,1},{6,4},{7,3},{8,10},{9,13},{10,... | collective-permute-start | bytes 1769480 | tf_op jit(solution)/shard_map/ppermute | solution.py:481
  21.9 7.7 %first_feed_forward.1 = (bf16[16,96,384]{2,1,0:T(8,128)(2,1)S(1)}, bf16[16,96,384]{2,1,0:T(8,128)(2,1)S(1)}, f32[3,784,128]{2,1,0:T(8,128)S(1)}, f32[2,24,384]{2,1,0:T(8,128)S(1)}, f32[3,784,128]{2,1,0:T(8,128)S(1)}) custom-call(f32[3,784,128]{2,1,0:T(8,128)S(1)} %get-tuple-element.99.s1, f32[3,784,128]{2,1,0:T(8,128)S(1)} %get-tuple-element.116.g2, ...), custom_call_target="tpu_custom_call" | custom-call | flops 8999999488 | bytes 27000000 | tf_op jit(solution)/shard_map/first_feed_forward/pallas_call | solution.py:682
  29.6 0.2 collective-permute-done.1
  29.8 0.0 collective-permute-start.2
  29.8 0.1 add_convert_fusion.3
  29.9 2.1 %collective-permute-start.6 = (bf16[4,96,384]{2,1,0:T(8,128)(2,1)S(1)}, bf16[4,96,384]{2,1,0:T(8,128)(2,1)S(1)}, u32[]{:S(2)}, u32[]{:S(2)}) collective-permute-start(bf16[4,96,384]{2,1,0:T(8,128)(2,1)S(1)} %add_convert_fusion.3), channel_id=1, source_target_pairs={{0,4},{1,3},{2,6},{3,1},{4,0},{5,7},{6,2},{7,5},{8,12},{9,11},{10,... | collective-permute-start | bytes 884744 | tf_op jit(solution)/shard_map/ppermute | solution.py:481
  32.0 2.9 %first_cross.1 = (bf16[1,196,4,384]{3,2,1,0:T(4,128)(2,1)}, bf16[1,196,4,384]{3,2,1,0:T(4,128)(2,1)}, bf16[16,8,384]{2,1,0:T(8,128)(2,1)S(1)}, bf16[16,8,384]{2,1,0:T(8,128)(2,1)S(1)}) custom-call(f32[3,784,128]{2,1,0:T(8,128)S(1)} %get-tuple-element.98.s0, f32[3,784,128]{2,1,0:T(8,128)S(1)} %get-tuple-element.127.g1, ...), custom_call_target="tpu_custom_call" | custom-call | flops 5000000000 | bytes 15000000 | tf_op jit(solution)/shard_map/first_cross/pallas_call | solution.py:682
  35.0 0.2 collective-permute-start.4
  35.2 0.0 collective-permute-done.2
  35.2 0.1 add_convert_fusion
  35.3 1.4 %collective-permute-start.3 = (bf16[8,96,384]{2,1,0:T(8,128)(2,1)S(1)}, bf16[8,96,384]{2,1,0:T(8,128)(2,1)S(1)}, u32[]{:S(2)}, u32[]{:S(2)}) collective-permute-start(bf16[8,96,384]{2,1,0:T(8,128)(2,1)S(1)} %add_convert_fusion), channel_id=1, source_target_pairs={{0,2},{1,5},{2,0},{3,7},{4,6},{5,1},{6,4},{7,3},{8,10},{9,13},{10,... | collective-permute-start | bytes 1769480 | tf_op jit(solution)/shard_map/ppermute | solution.py:481
  36.7 0.1 collective-permute-done.6
  36.7 0.1 add_convert_fusion.10
  36.9 3.2 %collective-permute-start.7 = (bf16[1,96,384]{2,1,0:T(8,128)(2,1)S(1)}, bf16[1,96,384]{2,1,0:T(8,128)(2,1)S(1)}, u32[]{:S(2)}, u32[]{:S(2)}) collective-permute-start(bf16[1,96,384]{2,1,0:T(8,128)(2,1)S(1)} %get-tuple-element.187), channel_id=1, source_target_pairs={{0,16},{1,17},{2,18},{3,19},{4,20},{5,21},{6,22},{7,23},{8,24},{9,... | collective-permute-start | bytes 221192 | tf_op jit(solution)/shard_map/ppermute | solution.py:481
  40.0 1.6 %collective-permute-start.9 = (bf16[1,96,384]{2,1,0:T(8,128)(2,1)S(1)}, bf16[1,96,384]{2,1,0:T(8,128)(2,1)S(1)}, u32[]{:S(2)}, u32[]{:S(2)}) collective-permute-start(bf16[1,96,384]{2,1,0:T(8,128)(2,1)S(1)} %get-tuple-element.188), channel_id=1, source_target_pairs={{0,8},{1,9},{2,10},{3,11},{4,12},{5,13},{6,14},{7,15},{8,0},{9,1},... | collective-permute-start | bytes 221192 | tf_op jit(solution)/shard_map/ppermute | solution.py:481
  41.6 0.0 collective-permute-start.8
  41.6 1.8 %collective-permute-start.5 = (bf16[8,8,384]{2,1,0:T(8,128)(2,1)S(1)}, bf16[8,8,384]{2,1,0:T(8,128)(2,1)S(1)}, u32[]{:S(2)}, u32[]{:S(2)}) collective-permute-start(bf16[8,8,384]{2,1,0:T(8,128)(2,1)S(1)} %add_convert_fusion.11), channel_id=1, source_target_pairs={{0,2},{1,5},{2,0},{3,7},{4,6},{5,1},{6,4},{7,3},{8,10},{9,13},{10,... | collective-permute-start | bytes 147464 | tf_op jit(solution)/shard_map/ppermute | solution.py:481
  43.4 1.0 %collective-permute-done.9 = bf16[1,96,384]{2,1,0:T(8,128)(2,1)S(1)} collective-permute-done((bf16[1,96,384]{2,1,0:T(8,128)(2,1)S(1)}, bf16[1,96,384]{2,1,0:T(8,128)(2,1)S(1)}, u32[]{:S(2)}, u32[]{:S(2)}) %collective-permute-start.9) | collective-permute-done | bytes 73760 | tf_op jit(solution)/shard_map/ppermute | solution.py:481
  44.4 3.4 %collective-permute-done.8 = bf16[1,96,384]{2,1,0:T(8,128)(2,1)S(1)} collective-permute-done((bf16[1,96,384]{2,1,0:T(8,128)(2,1)S(1)}, bf16[1,96,384]{2,1,0:T(8,128)(2,1)S(1)}, u32[]{:S(2)}, u32[]{:S(2)}) %collective-permute-start.8) | collective-permute-done | bytes 73760 | tf_op jit(solution)/shard_map/ppermute | solution.py:481
  47.7 0.1 add_convert_fusion.7
  47.8 0.0 collective-permute-done.3
  47.9 0.1 add_convert_fusion.2
  48.0 1.6 %collective-permute-start.10 = (bf16[4,104,384]{2,1,0:T(8,128)(2,1)S(1)}, bf16[4,104,384]{2,1,0:T(8,128)(2,1)S(1)}, u32[]{:S(2)}, u32[]{:S(2)}) collective-permute-start(bf16[4,104,384]{2,1,0:T(8,128)(2,1)S(1)} %pad_maximum_fusion), channel_id=1, source_target_pairs={{0,4},{1,3},{2,6},{3,1},{4,0},{5,7},{6,2},{7,5},{8,12},{9,11},{10,... | collective-permute-start | bytes 958472 | tf_op jit(solution)/shard_map/ppermute | solution.py:481
  49.6 1.8 %collective-permute-start.19 = (bf16[1,96,384]{2,1,0:T(8,128)(2,1)S(1)}, bf16[1,96,384]{2,1,0:T(8,128)(2,1)S(1)}, u32[]{:S(2)}, u32[]{:S(2)}) collective-permute-start(bf16[1,96,384]{2,1,0:T(8,128)(2,1)S(1)} %add_convert_fusion.7), channel_id=1, source_target_pairs={{0,24},{1,25},{2,26},{3,27},{4,28},{5,29},{6,30},{7,31},{8,16},{9,... | collective-permute-start | bytes 221192 | tf_op jit(solution)/shard_map/ppermute | solution.py:481
  51.4 0.5 collective-permute-start.18
  51.9 2.1 %collective-permute-start.17 = (bf16[1,96,384]{2,1,0:T(8,128)(2,1)S(1)}, bf16[1,96,384]{2,1,0:T(8,128)(2,1)S(1)}, u32[]{:S(2)}, u32[]{:S(2)}) collective-permute-start(bf16[1,96,384]{2,1,0:T(8,128)(2,1)S(1)} %add_convert_fusion.7), channel_id=1, source_target_pairs={{0,16},{1,17},{2,18},{3,19},{4,20},{5,21},{6,22},{7,23},{8,24},{9,... | collective-permute-start | bytes 221192 | tf_op jit(solution)/shard_map/ppermute | solution.py:481
  54.0 1.1 %collective-permute-done.10 = bf16[4,104,384]{2,1,0:T(8,128)(2,1)S(1)} collective-permute-done((bf16[4,104,384]{2,1,0:T(8,128)(2,1)S(1)}, bf16[4,104,384]{2,1,0:T(8,128)(2,1)S(1)}, u32[]{:S(2)}, u32[]{:S(2)}) %collective-permute-start.10) | collective-permute-done | bytes 319520 | tf_op jit(solution)/shard_map/ppermute | solution.py:481
  55.1 0.1 convert_add_fusion
  55.3 1.8 %collective-permute-start.11 = (bf16[1,104,384]{2,1,0:T(8,128)(2,1)S(1)}, bf16[1,104,384]{2,1,0:T(8,128)(2,1)S(1)}, u32[]{:S(2)}, u32[]{:S(2)}) collective-permute-start(bf16[1,104,384]{2,1,0:T(8,128)(2,1)S(1)} %pad_maximum_fusion.2), channel_id=1, source_target_pairs={{0,16},{1,17},{2,18},{3,19},{4,20},{5,21},{6,22},{7,23},{8,24},{9,... | collective-permute-start | bytes 239624 | tf_op jit(solution)/shard_map/ppermute | solution.py:481
  57.1 0.5 collective-permute-start.12
  57.6 1.4 %collective-permute-start.13 = (bf16[1,104,384]{2,1,0:T(8,128)(2,1)S(1)}, bf16[1,104,384]{2,1,0:T(8,128)(2,1)S(1)}, u32[]{:S(2)}, u32[]{:S(2)}) collective-permute-start(bf16[1,104,384]{2,1,0:T(8,128)(2,1)S(1)} %pad_maximum_fusion.4), channel_id=1, source_target_pairs={{0,8},{1,9},{2,10},{3,11},{4,12},{5,13},{6,14},{7,15},{8,0},{9,1},... | collective-permute-start | bytes 239624 | tf_op jit(solution)/shard_map/ppermute | solution.py:481
  59.0 2.1 %collective-permute-done.17 = bf16[1,96,384]{2,1,0:T(8,128)(2,1)S(1)} collective-permute-done((bf16[1,96,384]{2,1,0:T(8,128)(2,1)S(1)}, bf16[1,96,384]{2,1,0:T(8,128)(2,1)S(1)}, u32[]{:S(2)}, u32[]{:S(2)}) %collective-permute-start.17) | collective-permute-done | bytes 73760 | tf_op jit(solution)/shard_map/ppermute | solution.py:481
  61.2 1.5 %collective-permute-start.21 = (bf16[4,96,384]{2,1,0:T(8,128)(2,1)S(1)}, bf16[4,96,384]{2,1,0:T(8,128)(2,1)S(1)}, u32[]{:S(2)}, u32[]{:S(2)}) collective-permute-start(bf16[4,96,384]{2,1,0:T(8,128)(2,1)S(1)} %get-tuple-element.195), channel_id=1, source_target_pairs={{0,2},{1,5},{2,0},{3,7},{4,6},{5,1},{6,4},{7,3},{8,10},{9,13},{10,... | collective-permute-start | bytes 884744 | tf_op jit(solution)/shard_map/ppermute | solution.py:481
  62.8 0.9 collective-permute-done.11
  63.7 0.2 collective-permute-done.13
  64.0 2.4 %collective-permute-start.16 = (bf16[1,104,384]{2,1,0:T(8,128)(2,1)S(1)}, bf16[1,104,384]{2,1,0:T(8,128)(2,1)S(1)}, u32[]{:S(2)}, u32[]{:S(2)}) collective-permute-start(bf16[1,104,384]{2,1,0:T(8,128)(2,1)S(1)} %get-tuple-element.182), channel_id=1, source_target_pairs={{0,24},{1,25},{2,26},{3,27},{4,28},{5,29},{6,30},{7,31},{8,16},{9,... | collective-permute-start | bytes 239624 | tf_op jit(solution)/shard_map/ppermute | solution.py:481
  66.4 0.5 collective-permute-start.15
  66.9 1.5 %collective-permute-start.14 = (bf16[1,104,384]{2,1,0:T(8,128)(2,1)S(1)}, bf16[1,104,384]{2,1,0:T(8,128)(2,1)S(1)}, u32[]{:S(2)}, u32[]{:S(2)}) collective-permute-start(bf16[1,104,384]{2,1,0:T(8,128)(2,1)S(1)} %get-tuple-element.182), channel_id=1, source_target_pairs={{0,16},{1,17},{2,18},{3,19},{4,20},{5,21},{6,22},{7,23},{8,24},{9,... | collective-permute-start | bytes 239624 | tf_op jit(solution)/shard_map/ppermute | solution.py:481
  68.4 1.0 %collective-permute-done.20 = bf16[4,96,384]{2,1,0:T(8,128)(2,1)S(1)} collective-permute-done((bf16[4,96,384]{2,1,0:T(8,128)(2,1)S(1)}, bf16[4,96,384]{2,1,0:T(8,128)(2,1)S(1)}, u32[]{:S(2)}, u32[]{:S(2)}) %collective-permute-start.20) | collective-permute-done | bytes 294944 | tf_op jit(solution)/shard_map/ppermute | solution.py:481
  69.5 0.5 collective-permute-start.25
  70.0 1.0 %collective-permute-done.16 = bf16[1,104,384]{2,1,0:T(8,128)(2,1)S(1)} collective-permute-done((bf16[1,104,384]{2,1,0:T(8,128)(2,1)S(1)}, bf16[1,104,384]{2,1,0:T(8,128)(2,1)S(1)}, u32[]{:S(2)}, u32[]{:S(2)}) %collective-permute-start.16) | collective-permute-done | bytes 79904 | tf_op jit(solution)/shard_map/ppermute | solution.py:481
  71.0 1.6 %collective-permute-done.15 = bf16[1,104,384]{2,1,0:T(8,128)(2,1)S(1)} collective-permute-done((bf16[1,104,384]{2,1,0:T(8,128)(2,1)S(1)}, bf16[1,104,384]{2,1,0:T(8,128)(2,1)S(1)}, u32[]{:S(2)}, u32[]{:S(2)}) %collective-permute-start.15) | collective-permute-done | bytes 79904 | tf_op jit(solution)/shard_map/ppermute | solution.py:481
  72.6 1.1 %collective-permute-done.14 = bf16[1,104,384]{2,1,0:T(8,128)(2,1)S(1)} collective-permute-done((bf16[1,104,384]{2,1,0:T(8,128)(2,1)S(1)}, bf16[1,104,384]{2,1,0:T(8,128)(2,1)S(1)}, u32[]{:S(2)}, u32[]{:S(2)}) %collective-permute-start.14) | collective-permute-done | bytes 79904 | tf_op jit(solution)/shard_map/ppermute | solution.py:481
  73.7 0.1 pad_maximum_fusion.1
  73.8 1.5 %collective-permute-start.23 = (bf16[4,104,384]{2,1,0:T(8,128)(2,1)S(1)}, bf16[4,104,384]{2,1,0:T(8,128)(2,1)S(1)}, u32[]{:S(2)}, u32[]{:S(2)}) collective-permute-start(bf16[4,104,384]{2,1,0:T(8,128)(2,1)S(1)} %pad_maximum_fusion.1), channel_id=1, source_target_pairs={{0,2},{1,5},{2,0},{3,7},{4,6},{5,1},{6,4},{7,3},{8,10},{9,13},{10,... | collective-permute-start | bytes 958472 | tf_op jit(solution)/shard_map/ppermute | solution.py:481
  75.2 0.3 collective-permute-start.22
  75.6 0.1 collective-permute-start.29
  75.7 7.6 %collective-permute-done.23.refs_4_ = bf16[4,104,384]{2,1,0:T(8,128)(2,1)S(1)} collective-permute-done((bf16[4,104,384]{2,1,0:T(8,128)(2,1)S(1)}, bf16[4,104,384]{2,1,0:T(8,128)(2,1)S(1)}, u32[]{:S(2)}, u32[]{:S(2)}) %collective-permute-start.23) | collective-permute-done | bytes 319520 | tf_op jit(solution)/shard_map/ppermute | solution.py:481
  83.3 0.1 constant_dynamic-update-slice_fusion.6.refs_3_
  83.4 0.1 collective-permute-start.27
  83.5 0.6 collective-permute-start.26
  84.1 1.1 %collective-permute-start.24 = (bf16[4,104,384]{2,1,0:T(8,128)(2,1)S(1)}, bf16[4,104,384]{2,1,0:T(8,128)(2,1)S(1)}, u32[]{:S(2)}, u32[]{:S(2)}) collective-permute-start(bf16[4,104,384]{2,1,0:T(8,128)(2,1)S(1)} %collective-permute-done.22), channel_id=1, source_target_pairs={{0,2},{1,5},{2,0},{3,7},{4,6},{5,1},{6,4},{7,3},{8,10},{9,13},{10,... | collective-permute-start | bytes 958472 | tf_op jit(solution)/shard_map/ppermute | solution.py:481
  85.2 0.3 collective-permute-start.28
  85.4 3.0 %unpack_kept.1 = (f32[2,384,1536]{2,1,0:T(8,128)}, f32[2,1536,384]{2,1,0:T(8,128)}, f32[32,8,384]{2,1,0:T(8,128)S(1)}) custom-call(bf16[8,96,384]{2,1,0:T(8,128)(2,1)S(1)} %constant_dynamic-update-slice_fusion.11.refs_0_, bf16[8,96,384]{2,1,0:T(8,128)(2,1)S(1)} %collective-permute-done.29.refs_1_, ...), custom_call_target="tpu_custom_call" | custom-call | flops 4499999744 | bytes 13500000 | tf_op jit(solution)/shard_map/unpack_kept/pallas_call | solution.py:682
  88.5 2.0 %unpack_others.1 = (f32[2,384,1536]{2,1,0:T(8,128)}, f32[2,1536,384]{2,1,0:T(8,128)}, f32[32,8,384]{2,1,0:T(8,128)S(1)}) custom-call(bf16[8,96,384]{2,1,0:T(8,128)(2,1)S(1)} %collective-permute-done.26.refs_0_, bf16[8,104,384]{2,1,0:T(8,128)(2,1)S(1)} %collective-permute-done.27.refs_1_, ...), custom_call_target="tpu_custom_call", output_to_operand_aliasing={{0}: (3, {}), {1}: (4, {}), {2}: (5, {})} | custom-call | flops 2500000000 | bytes 7500000 | tf_op jit(solution)/shard_map/unpack_others/pallas_call | solution.py:682
  90.5 0.5 collective-permute-done.24.refs_0_
  91.1 0.9 unpack_latest.1
  92.0 0.7 collective-permute-done.30.other_late
  92.7 1.3 %unpack_rest.1 = (f32[2,384,1536]{2,1,0:T(8,128)}, f32[2,1536,384]{2,1,0:T(8,128)}, f32[32,8,384]{2,1,0:T(8,128)S(1)}, f32[196,2,196]{2,1,0:T(2,128)}, f32[2,384...) custom-call(bf16[4,104,384]{2,1,0:T(8,128)(2,1)S(1)} %collective-per, ...), custom_call_target="tpu_custom_call", output_to_operand_aliasing={{0}: (1, {}), {1}: (2, {}), {2}: (3, {})} | custom-call | flops 2000000000 | bytes 6000000 | tf_op jit(solution)/shard_map/unpack_rest/pallas_call | solution.py:682
  (33 shorter events, 0.5 us)
Async XLA Ops:
  15.9 3.1 %collective-permute-start = (bf16[16,96,384]{2,1,0:T(8,128)(2,1)S(1)}, bf16[16,96,384]{2,1,0:T(8,128)(2,1)S(1)}, u32[]{:S(2)}, u32[]{:S(2)}) collective-permute-start(bf16[16,96,384]{2,1,0:T(8,128)(2,1)S(1)} %get-tuple-element.115), channel_id=1, source_target_pairs={{0,1},{1,0},{2,3},{3,2},{4,5},{5,4},{6,7},{7,6},{8,9},{9,8},{10,11... | collective-permute-start | bytes 3538952 | tf_op jit(solution)/shard_map/ppermute | solution.py:481
  19.1 10.7 %collective-permute-start.1 = (bf16[8,96,384]{2,1,0:T(8,128)(2,1)S(1)}, bf16[8,96,384]{2,1,0:T(8,128)(2,1)S(1)}, u32[]{:S(2)}, u32[]{:S(2)}) collective-permute-start(bf16[8,96,384]{2,1,0:T(8,128)(2,1)S(1)} %add_convert_fusion.1), channel_id=1, source_target_pairs={{0,2},{1,5},{2,0},{3,7},{4,6},{5,1},{6,4},{7,3},{8,10},{9,13},{10,... | collective-permute-start | bytes 1769480 | tf_op jit(solution)/shard_map/ppermute | solution.py:481
  29.8 5.4 %collective-permute-start.2 = (bf16[16,96,384]{2,1,0:T(8,128)(2,1)S(1)}, bf16[16,96,384]{2,1,0:T(8,128)(2,1)S(1)}, u32[]{:S(2)}, u32[]{:S(2)}) collective-permute-start(bf16[16,96,384]{2,1,0:T(8,128)(2,1)S(1)} %get-tuple-element.138), channel_id=1, source_target_pairs={{0,1},{1,0},{2,3},{3,2},{4,5},{5,4},{6,7},{7,6},{8,9},{9,8},{10,11... | collective-permute-start | bytes 3538952 | tf_op jit(solution)/shard_map/ppermute | solution.py:481
  29.9 6.8 %collective-permute-start.6 = (bf16[4,96,384]{2,1,0:T(8,128)(2,1)S(1)}, bf16[4,96,384]{2,1,0:T(8,128)(2,1)S(1)}, u32[]{:S(2)}, u32[]{:S(2)}) collective-permute-start(bf16[4,96,384]{2,1,0:T(8,128)(2,1)S(1)} %add_convert_fusion.3), channel_id=1, source_target_pairs={{0,4},{1,3},{2,6},{3,1},{4,0},{5,7},{6,2},{7,5},{8,12},{9,11},{10,... | collective-permute-start | bytes 884744 | tf_op jit(solution)/shard_map/ppermute | solution.py:481
  35.0 6.6 %collective-permute-start.4 = (bf16[16,8,384]{2,1,0:T(8,128)(2,1)S(1)}, bf16[16,8,384]{2,1,0:T(8,128)(2,1)S(1)}, u32[]{:S(2)}, u32[]{:S(2)}) collective-permute-start(bf16[16,8,384]{2,1,0:T(8,128)(2,1)S(1)} %get-tuple-element.140), channel_id=1, source_target_pairs={{0,1},{1,0},{2,3},{3,2},{4,5},{5,4},{6,7},{7,6},{8,9},{9,8},{10,11... | collective-permute-start | bytes 294920 | tf_op jit(solution)/shard_map/ppermute | solution.py:481
  35.3 12.5 %collective-permute-start.3 = (bf16[8,96,384]{2,1,0:T(8,128)(2,1)S(1)}, bf16[8,96,384]{2,1,0:T(8,128)(2,1)S(1)}, u32[]{:S(2)}, u32[]{:S(2)}) collective-permute-start(bf16[8,96,384]{2,1,0:T(8,128)(2,1)S(1)} %add_convert_fusion), channel_id=1, source_target_pairs={{0,2},{1,5},{2,0},{3,7},{4,6},{5,1},{6,4},{7,3},{8,10},{9,13},{10,... | collective-permute-start | bytes 1769480 | tf_op jit(solution)/shard_map/ppermute | solution.py:481
  36.9 6.5 %collective-permute-start.7 = (bf16[1,96,384]{2,1,0:T(8,128)(2,1)S(1)}, bf16[1,96,384]{2,1,0:T(8,128)(2,1)S(1)}, u32[]{:S(2)}, u32[]{:S(2)}) collective-permute-start(bf16[1,96,384]{2,1,0:T(8,128)(2,1)S(1)} %get-tuple-element.187), channel_id=1, source_target_pairs={{0,16},{1,17},{2,18},{3,19},{4,20},{5,21},{6,22},{7,23},{8,24},{9,... | collective-permute-start | bytes 221192 | tf_op jit(solution)/shard_map/ppermute | solution.py:481
  40.0 4.4 %collective-permute-start.9 = (bf16[1,96,384]{2,1,0:T(8,128)(2,1)S(1)}, bf16[1,96,384]{2,1,0:T(8,128)(2,1)S(1)}, u32[]{:S(2)}, u32[]{:S(2)}) collective-permute-start(bf16[1,96,384]{2,1,0:T(8,128)(2,1)S(1)} %get-tuple-element.188), channel_id=1, source_target_pairs={{0,8},{1,9},{2,10},{3,11},{4,12},{5,13},{6,14},{7,15},{8,0},{9,1},... | collective-permute-start | bytes 221192 | tf_op jit(solution)/shard_map/ppermute | solution.py:481
  41.6 6.2 %collective-permute-start.8 = (bf16[1,96,384]{2,1,0:T(8,128)(2,1)S(1)}, bf16[1,96,384]{2,1,0:T(8,128)(2,1)S(1)}, u32[]{:S(2)}, u32[]{:S(2)}) collective-permute-start(bf16[1,96,384]{2,1,0:T(8,128)(2,1)S(1)} %get-tuple-element.189), channel_id=1, source_target_pairs={{0,24},{1,25},{2,26},{3,27},{4,28},{5,29},{6,30},{7,31},{8,16},{9,... | collective-permute-start | bytes 221192 | tf_op jit(solution)/shard_map/ppermute | solution.py:481
  41.6 6.2 %collective-permute-start.5 = (bf16[8,8,384]{2,1,0:T(8,128)(2,1)S(1)}, bf16[8,8,384]{2,1,0:T(8,128)(2,1)S(1)}, u32[]{:S(2)}, u32[]{:S(2)}) collective-permute-start(bf16[8,8,384]{2,1,0:T(8,128)(2,1)S(1)} %add_convert_fusion.11), channel_id=1, source_target_pairs={{0,2},{1,5},{2,0},{3,7},{4,6},{5,1},{6,4},{7,3},{8,10},{9,13},{10,... | collective-permute-start | bytes 147464 | tf_op jit(solution)/shard_map/ppermute | solution.py:481
  48.0 7.1 %collective-permute-start.10 = (bf16[4,104,384]{2,1,0:T(8,128)(2,1)S(1)}, bf16[4,104,384]{2,1,0:T(8,128)(2,1)S(1)}, u32[]{:S(2)}, u32[]{:S(2)}) collective-permute-start(bf16[4,104,384]{2,1,0:T(8,128)(2,1)S(1)} %pad_maximum_fusion), channel_id=1, source_target_pairs={{0,4},{1,3},{2,6},{3,1},{4,0},{5,7},{6,2},{7,5},{8,12},{9,11},{10,... | collective-permute-start | bytes 958472 | tf_op jit(solution)/shard_map/ppermute | solution.py:481
  49.6 8.0 %collective-permute-start.19 = (bf16[1,96,384]{2,1,0:T(8,128)(2,1)S(1)}, bf16[1,96,384]{2,1,0:T(8,128)(2,1)S(1)}, u32[]{:S(2)}, u32[]{:S(2)}) collective-permute-start(bf16[1,96,384]{2,1,0:T(8,128)(2,1)S(1)} %add_convert_fusion.7), channel_id=1, source_target_pairs={{0,24},{1,25},{2,26},{3,27},{4,28},{5,29},{6,30},{7,31},{8,16},{9,... | collective-permute-start | bytes 221192 | tf_op jit(solution)/shard_map/ppermute | solution.py:481
  51.4 7.6 %collective-permute-start.18 = (bf16[1,96,384]{2,1,0:T(8,128)(2,1)S(1)}, bf16[1,96,384]{2,1,0:T(8,128)(2,1)S(1)}, u32[]{:S(2)}, u32[]{:S(2)}) collective-permute-start(bf16[1,96,384]{2,1,0:T(8,128)(2,1)S(1)} %add_convert_fusion.7), channel_id=1, source_target_pairs={{0,8},{1,9},{2,10},{3,11},{4,12},{5,13},{6,14},{7,15},{8,0},{9,1},... | collective-permute-start | bytes 221192 | tf_op jit(solution)/shard_map/ppermute | solution.py:481
  51.9 9.2 %collective-permute-start.17 = (bf16[1,96,384]{2,1,0:T(8,128)(2,1)S(1)}, bf16[1,96,384]{2,1,0:T(8,128)(2,1)S(1)}, u32[]{:S(2)}, u32[]{:S(2)}) collective-permute-start(bf16[1,96,384]{2,1,0:T(8,128)(2,1)S(1)} %add_convert_fusion.7), channel_id=1, source_target_pairs={{0,16},{1,17},{2,18},{3,19},{4,20},{5,21},{6,22},{7,23},{8,24},{9,... | collective-permute-start | bytes 221192 | tf_op jit(solution)/shard_map/ppermute | solution.py:481
  55.3 8.4 %collective-permute-start.11 = (bf16[1,104,384]{2,1,0:T(8,128)(2,1)S(1)}, bf16[1,104,384]{2,1,0:T(8,128)(2,1)S(1)}, u32[]{:S(2)}, u32[]{:S(2)}) collective-permute-start(bf16[1,104,384]{2,1,0:T(8,128)(2,1)S(1)} %pad_maximum_fusion.2), channel_id=1, source_target_pairs={{0,16},{1,17},{2,18},{3,19},{4,20},{5,21},{6,22},{7,23},{8,24},{9,... | collective-permute-start | bytes 239624 | tf_op jit(solution)/shard_map/ppermute | solution.py:481
  57.1 6.6 %collective-permute-start.12 = (bf16[1,104,384]{2,1,0:T(8,128)(2,1)S(1)}, bf16[1,104,384]{2,1,0:T(8,128)(2,1)S(1)}, u32[]{:S(2)}, u32[]{:S(2)}) collective-permute-start(bf16[1,104,384]{2,1,0:T(8,128)(2,1)S(1)} %pad_maximum_fusion.3), channel_id=1, source_target_pairs={{0,24},{1,25},{2,26},{3,27},{4,28},{5,29},{6,30},{7,31},{8,16},{9,... | collective-permute-start | bytes 239624 | tf_op jit(solution)/shard_map/ppermute | solution.py:481
  57.6 6.3 %collective-permute-start.13 = (bf16[1,104,384]{2,1,0:T(8,128)(2,1)S(1)}, bf16[1,104,384]{2,1,0:T(8,128)(2,1)S(1)}, u32[]{:S(2)}, u32[]{:S(2)}) collective-permute-start(bf16[1,104,384]{2,1,0:T(8,128)(2,1)S(1)} %pad_maximum_fusion.4), channel_id=1, source_target_pairs={{0,8},{1,9},{2,10},{3,11},{4,12},{5,13},{6,14},{7,15},{8,0},{9,1},... | collective-permute-start | bytes 239624 | tf_op jit(solution)/shard_map/ppermute | solution.py:481
  61.2 12.5 %collective-permute-start.21 = (bf16[4,96,384]{2,1,0:T(8,128)(2,1)S(1)}, bf16[4,96,384]{2,1,0:T(8,128)(2,1)S(1)}, u32[]{:S(2)}, u32[]{:S(2)}) collective-permute-start(bf16[4,96,384]{2,1,0:T(8,128)(2,1)S(1)} %get-tuple-element.195), channel_id=1, source_target_pairs={{0,2},{1,5},{2,0},{3,7},{4,6},{5,1},{6,4},{7,3},{8,10},{9,13},{10,... | collective-permute-start | bytes 884744 | tf_op jit(solution)/shard_map/ppermute | solution.py:481
  62.8 6.7 %collective-permute-start.20 = (bf16[4,96,384]{2,1,0:T(8,128)(2,1)S(1)}, bf16[4,96,384]{2,1,0:T(8,128)(2,1)S(1)}, u32[]{:S(2)}, u32[]{:S(2)}) collective-permute-start(bf16[4,96,384]{2,1,0:T(8,128)(2,1)S(1)} %get-tuple-element.195), channel_id=1, source_target_pairs={{0,4},{1,3},{2,6},{3,1},{4,0},{5,7},{6,2},{7,5},{8,12},{9,11},{10,... | collective-permute-start | bytes 884744 | tf_op jit(solution)/shard_map/ppermute | solution.py:481
  64.0 7.1 %collective-permute-start.16 = (bf16[1,104,384]{2,1,0:T(8,128)(2,1)S(1)}, bf16[1,104,384]{2,1,0:T(8,128)(2,1)S(1)}, u32[]{:S(2)}, u32[]{:S(2)}) collective-permute-start(bf16[1,104,384]{2,1,0:T(8,128)(2,1)S(1)} %get-tuple-element.182), channel_id=1, source_target_pairs={{0,24},{1,25},{2,26},{3,27},{4,28},{5,29},{6,30},{7,31},{8,16},{9,... | collective-permute-start | bytes 239624 | tf_op jit(solution)/shard_map/ppermute | solution.py:481
  66.4 6.2 %collective-permute-start.15 = (bf16[1,104,384]{2,1,0:T(8,128)(2,1)S(1)}, bf16[1,104,384]{2,1,0:T(8,128)(2,1)S(1)}, u32[]{:S(2)}, u32[]{:S(2)}) collective-permute-start(bf16[1,104,384]{2,1,0:T(8,128)(2,1)S(1)} %get-tuple-element.182), channel_id=1, source_target_pairs={{0,8},{1,9},{2,10},{3,11},{4,12},{5,13},{6,14},{7,15},{8,0},{9,1},... | collective-permute-start | bytes 239624 | tf_op jit(solution)/shard_map/ppermute | solution.py:481
  66.9 6.7 %collective-permute-start.14 = (bf16[1,104,384]{2,1,0:T(8,128)(2,1)S(1)}, bf16[1,104,384]{2,1,0:T(8,128)(2,1)S(1)}, u32[]{:S(2)}, u32[]{:S(2)}) collective-permute-start(bf16[1,104,384]{2,1,0:T(8,128)(2,1)S(1)} %get-tuple-element.182), channel_id=1, source_target_pairs={{0,16},{1,17},{2,18},{3,19},{4,20},{5,21},{6,22},{7,23},{8,24},{9,... | collective-permute-start | bytes 239624 | tf_op jit(solution)/shard_map/ppermute | solution.py:481
  69.5 13.8 %collective-permute-start.25 = (bf16[4,96,384]{2,1,0:T(8,128)(2,1)S(1)}, bf16[4,96,384]{2,1,0:T(8,128)(2,1)S(1)}, u32[]{:S(2)}, u32[]{:S(2)}) collective-permute-start(bf16[4,96,384]{2,1,0:T(8,128)(2,1)S(1)} %collective-permute-done.20), channel_id=1, source_target_pairs={{0,2},{1,5},{2,0},{3,7},{4,6},{5,1},{6,4},{7,3},{8,10},{9,13},{10,... | collective-permute-start | bytes 884744 | tf_op jit(solution)/shard_map/ppermute | solution.py:481
  73.8 9.5 %collective-permute-start.23 = (bf16[4,104,384]{2,1,0:T(8,128)(2,1)S(1)}, bf16[4,104,384]{2,1,0:T(8,128)(2,1)S(1)}, u32[]{:S(2)}, u32[]{:S(2)}) collective-permute-start(bf16[4,104,384]{2,1,0:T(8,128)(2,1)S(1)} %pad_maximum_fusion.1), channel_id=1, source_target_pairs={{0,2},{1,5},{2,0},{3,7},{4,6},{5,1},{6,4},{7,3},{8,10},{9,13},{10,... | collective-permute-start | bytes 958472 | tf_op jit(solution)/shard_map/ppermute | solution.py:481
  75.2 8.1 %collective-permute-start.22 = (bf16[4,104,384]{2,1,0:T(8,128)(2,1)S(1)}, bf16[4,104,384]{2,1,0:T(8,128)(2,1)S(1)}, u32[]{:S(2)}, u32[]{:S(2)}) collective-permute-start(bf16[4,104,384]{2,1,0:T(8,128)(2,1)S(1)} %pad_maximum_fusion.1), channel_id=1, source_target_pairs={{0,4},{1,3},{2,6},{3,1},{4,0},{5,7},{6,2},{7,5},{8,12},{9,11},{10,... | collective-permute-start | bytes 958472 | tf_op jit(solution)/shard_map/ppermute | solution.py:481
  75.6 9.9 %collective-permute-start.29 = (bf16[8,96,384]{2,1,0:T(8,128)(2,1)S(1)}, bf16[8,96,384]{2,1,0:T(8,128)(2,1)S(1)}, u32[]{:S(2)}, u32[]{:S(2)}) collective-permute-start(bf16[8,96,384]{2,1,0:T(8,128)(2,1)S(1)} %constant_dynamic-update-slice_fusion.11.refs_0_), channel_id=1, source_target_pairs={{0,1},{1,0},{2,3},{3,2},{4,5},{5,4},{6,7},{7,6},{8,9},{9,8},{10,11... | collective-permute-start | bytes 1769480 | tf_op jit(solution)/shard_map/ppermute | solution.py:481
  83.4 5.1 %collective-permute-start.27 = (bf16[8,104,384]{2,1,0:T(8,128)(2,1)S(1)}, bf16[8,104,384]{2,1,0:T(8,128)(2,1)S(1)}, u32[]{:S(2)}, u32[]{:S(2)}) collective-permute-start(bf16[8,104,384]{2,1,0:T(8,128)(2,1)S(1)} %constant_dynamic-update-slice_fusion.6.refs_3_), channel_id=1, source_target_pairs={{0,1},{1,0},{2,3},{3,2},{4,5},{5,4},{6,7},{7,6},{8,9},{9,8},{10,11... | collective-permute-start | bytes 1916936 | tf_op jit(solution)/shard_map/ppermute | solution.py:481
  83.5 4.9 %collective-permute-start.26 = (bf16[8,96,384]{2,1,0:T(8,128)(2,1)S(1)}, bf16[8,96,384]{2,1,0:T(8,128)(2,1)S(1)}, u32[]{:S(2)}, u32[]{:S(2)}) collective-permute-start(bf16[8,96,384]{2,1,0:T(8,128)(2,1)S(1)} %constant_dynamic-update-slice_fusion.4.refs_2_), channel_id=1, source_target_pairs={{0,1},{1,0},{2,3},{3,2},{4,5},{5,4},{6,7},{7,6},{8,9},{9,8},{10,11... | collective-permute-start | bytes 1769480 | tf_op jit(solution)/shard_map/ppermute | solution.py:481
  84.1 7.0 %collective-permute-start.24 = (bf16[4,104,384]{2,1,0:T(8,128)(2,1)S(1)}, bf16[4,104,384]{2,1,0:T(8,128)(2,1)S(1)}, u32[]{:S(2)}, u32[]{:S(2)}) collective-permute-start(bf16[4,104,384]{2,1,0:T(8,128)(2,1)S(1)} %collective-permute-done.22), channel_id=1, source_target_pairs={{0,2},{1,5},{2,0},{3,7},{4,6},{5,1},{6,4},{7,3},{8,10},{9,13},{10,... | collective-permute-start | bytes 958472 | tf_op jit(solution)/shard_map/ppermute | solution.py:481
  85.2 3.3 %collective-permute-start.28 = (bf16[4,104,384]{2,1,0:T(8,128)(2,1)S(1)}, bf16[4,104,384]{2,1,0:T(8,128)(2,1)S(1)}, u32[]{:S(2)}, u32[]{:S(2)}) collective-permute-start(bf16[4,104,384]{2,1,0:T(8,128)(2,1)S(1)} %collective-permute-done.23.refs_4_), channel_id=1, source_target_pairs={{0,1},{1,0},{2,3},{3,2},{4,5},{5,4},{6,7},{7,6},{8,9},{9,8},{10,11... | collective-permute-start | bytes 958472 | tf_op jit(solution)/shard_map/ppermute | solution.py:481
  91.1 1.6 %collective-permute-start.30 = (bf16[4,104,384]{2,1,0:T(8,128)(2,1)S(1)}, bf16[4,104,384]{2,1,0:T(8,128)(2,1)S(1)}, u32[]{:S(2)}, u32[]{:S(2)}) collective-permute-start(bf16[4,104,384]{2,1,0:T(8,128)(2,1)S(1)} %collective-permute-done.24.refs_0_), channel_id=1, source_target_pairs={{0,1},{1,0},{2,3},{3,2},{4,5},{5,4},{6,7},{7,6},{8,9},{9,8},{10,11... | collective-permute-start | bytes 958472 | tf_op jit(solution)/shard_map/ppermute | solution.py:481

commit v8 on v6

--- a/solution.py
+++ b/solution.py
@@ -20,7 +20,7 @@
 F32 = jnp.float32
 VMEM = pl.BlockSpec(memory_space=pltpu.VMEM)
 HBM = pl.BlockSpec(memory_space=pltpu.HBM)
-VMEM_LIMIT = 20 * 2**20
+VMEM_LIMIT = 16 * 2**20
 
 CROSS_AFF_SCALE, CROSS_AFF_SHIFT, CROSS_SCALE, CROSS_BIAS = 0, 1, 2, 3
 MIXER_AFF_SCALE, MIXER_AFF_SHIFT, MIXER_OUT_BIAS, MIXER_SCALE = 4, 5, 6, 7

time: 94.4 us -> 94.4 us (level)
  no operation moved by 1% of the time
where the time goes in v8:
time: 94.4 us; the launch traced here: 94.3 us
  Pallas kernels  35.8 us (38%)
  starting transfers between devices  33.5 us (35%)
  waiting for transfers between devices  22.5 us (24%)
  between operations  1.11 us (1%)
  other arithmetic  1.06 us (1%)
    pallas_call x8, Pallas kernels, call(): pl.pallas_call(kernel, out_shape=outs, in_specs=[VMEM] * len(args) if in_...  35.8 us
    ppermute x31, starting transfers between devices, exchange_bits(): return lax.ppermute(values, AXES, [(i, partner(i)) for i in places])  33.5 us
    ppermute x31, waiting for transfers between devices, exchange_bits(): return lax.ppermute(values, AXES, [(i, partner(i)) for i in places])  22.5 us
  transfers between devices with their start and end apart: 31, of which 14 were waited for; matrix products, arithmetic and copies ran while one was open for 1% of the time, Pallas kernels for 20%

profile of v8, /device:TPU:0, one launch (start us, length us, event | category | flops | bytes accessed | tf_op | source)
XLA Modules:
  0.0 94.3 jit_solution(7452257677406210152)
XLA Ops:
  0.7 15.3 %forward.1 = (f32[2,384]{1,0:T(2,128)S(1)}, f32[2,384]{1,0:T(2,128)S(1)}, f32[2,384]{1,0:T(2,128)S(1)}, f32[2,384]{1,0:T(2,128)S(1)}, f32[2,384]{1,0:T(2,128)S(1...) custom-call(bf16[4,196,4,384]{3,2,1,0:T(4,128)(2,1)} %bitcast.6, ...), custom_call_target="tpu_custom_call" | custom-call | flops 17999998976 | bytes 54000000 | tf_op jit(solution)/shard_map/forward/pallas_call | solution.py:682
  15.9 0.5 collective-permute-start
  16.4 2.6 %last_layer.1 = (f32[3,784,128]{2,1,0:T(8,128)S(1)}, f32[256,256]{1,0:T(8,128)S(1)}, f32[2,24,384]{2,1,0:T(8,128)S(1)}) custom-call(f32[3,784,128]{2,1,0:T(8,128)S(1)} %get-tuple-element.100.s2, f32[3,784,128]{2,1,0:T(8,128)S(1)} %get-tuple-element.101.s3, f32[3,784,128]{2,1,0:T(8,128)S(1)} %get-tuple-element.102.g_rows, ...), custom_call_target="tpu_custom_call" | custom-call | flops 4000000000 | bytes 12000000 | tf_op jit(solution)/shard_map/last_layer/pallas_call | solution.py:682
  19.0 0.1 add_convert_fusion.1
  19.2 2.8 %collective-permute-start.1 = (bf16[8,96,384]{2,1,0:T(8,128)(2,1)S(1)}, bf16[8,96,384]{2,1,0:T(8,128)(2,1)S(1)}, u32[]{:S(2)}, u32[]{:S(2)}) collective-permute-start(bf16[8,96,384]{2,1,0:T(8,128)(2,1)S(1)} %add_convert_fusion.1), channel_id=1, source_target_pairs={{0,2},{1,5},{2,0},{3,7},{4,6},{5,1},{6,4},{7,3},{8,10},{9,13},{10,... | collective-permute-start | bytes 1769480 | tf_op jit(solution)/shard_map/ppermute | solution.py:481
  22.0 7.7 %first_feed_forward.1 = (bf16[16,96,384]{2,1,0:T(8,128)(2,1)S(1)}, bf16[16,96,384]{2,1,0:T(8,128)(2,1)S(1)}, f32[3,784,128]{2,1,0:T(8,128)S(1)}, f32[2,24,384]{2,1,0:T(8,128)S(1)}, f32[3,784,128]{2,1,0:T(8,128)S(1)}) custom-call(f32[3,784,128]{2,1,0:T(8,128)S(1)} %get-tuple-element.99.s1, f32[3,784,128]{2,1,0:T(8,128)S(1)} %get-tuple-element.116.g2, ...), custom_call_target="tpu_custom_call" | custom-call | flops 8999999488 | bytes 27000000 | tf_op jit(solution)/shard_map/first_feed_forward/pallas_call | solution.py:682
  29.7 0.2 collective-permute-done.1
  29.9 0.0 collective-permute-start.2
  29.9 0.1 add_convert_fusion.3
  30.0 2.1 %collective-permute-start.6 = (bf16[4,96,384]{2,1,0:T(8,128)(2,1)S(1)}, bf16[4,96,384]{2,1,0:T(8,128)(2,1)S(1)}, u32[]{:S(2)}, u32[]{:S(2)}) collective-permute-start(bf16[4,96,384]{2,1,0:T(8,128)(2,1)S(1)} %add_convert_fusion.3), channel_id=1, source_target_pairs={{0,4},{1,3},{2,6},{3,1},{4,0},{5,7},{6,2},{7,5},{8,12},{9,11},{10,... | collective-permute-start | bytes 884744 | tf_op jit(solution)/shard_map/ppermute | solution.py:481
  32.1 3.0 %first_cross.1 = (bf16[1,196,4,384]{3,2,1,0:T(4,128)(2,1)}, bf16[1,196,4,384]{3,2,1,0:T(4,128)(2,1)}, bf16[16,8,384]{2,1,0:T(8,128)(2,1)S(1)}, bf16[16,8,384]{2,1,0:T(8,128)(2,1)S(1)}) custom-call(f32[3,784,128]{2,1,0:T(8,128)S(1)} %get-tuple-element.98.s0, f32[3,784,128]{2,1,0:T(8,128)S(1)} %get-tuple-element.127.g1, ...), custom_call_target="tpu_custom_call" | custom-call | flops 5000000000 | bytes 15000000 | tf_op jit(solution)/shard_map/first_cross/pallas_call | solution.py:682
  35.1 0.2 collective-permute-start.4
  35.3 0.1 add_convert_fusion
  35.4 1.4 %collective-permute-start.3 = (bf16[8,96,384]{2,1,0:T(8,128)(2,1)S(1)}, bf16[8,96,384]{2,1,0:T(8,128)(2,1)S(1)}, u32[]{:S(2)}, u32[]{:S(2)}) collective-permute-start(bf16[8,96,384]{2,1,0:T(8,128)(2,1)S(1)} %add_convert_fusion), channel_id=1, source_target_pairs={{0,2},{1,5},{2,0},{3,7},{4,6},{5,1},{6,4},{7,3},{8,10},{9,13},{10,... | collective-permute-start | bytes 1769480 | tf_op jit(solution)/shard_map/ppermute | solution.py:481
  36.8 0.0 collective-permute-done.6
  36.8 0.1 add_convert_fusion.10
  36.9 3.1 %collective-permute-start.7 = (bf16[1,96,384]{2,1,0:T(8,128)(2,1)S(1)}, bf16[1,96,384]{2,1,0:T(8,128)(2,1)S(1)}, u32[]{:S(2)}, u32[]{:S(2)}) collective-permute-start(bf16[1,96,384]{2,1,0:T(8,128)(2,1)S(1)} %get-tuple-element.187), channel_id=1, source_target_pairs={{0,16},{1,17},{2,18},{3,19},{4,20},{5,21},{6,22},{7,23},{8,24},{9,... | collective-permute-start | bytes 221192 | tf_op jit(solution)/shard_map/ppermute | solution.py:481
  40.1 1.6 %collective-permute-start.9 = (bf16[1,96,384]{2,1,0:T(8,128)(2,1)S(1)}, bf16[1,96,384]{2,1,0:T(8,128)(2,1)S(1)}, u32[]{:S(2)}, u32[]{:S(2)}) collective-permute-start(bf16[1,96,384]{2,1,0:T(8,128)(2,1)S(1)} %get-tuple-element.188), channel_id=1, source_target_pairs={{0,8},{1,9},{2,10},{3,11},{4,12},{5,13},{6,14},{7,15},{8,0},{9,1},... | collective-permute-start | bytes 221192 | tf_op jit(solution)/shard_map/ppermute | solution.py:481
  41.6 0.0 collective-permute-start.8
  41.6 0.0 collective-permute-done.4
  41.7 1.8 %collective-permute-start.5 = (bf16[8,8,384]{2,1,0:T(8,128)(2,1)S(1)}, bf16[8,8,384]{2,1,0:T(8,128)(2,1)S(1)}, u32[]{:S(2)}, u32[]{:S(2)}) collective-permute-start(bf16[8,8,384]{2,1,0:T(8,128)(2,1)S(1)} %add_convert_fusion.11), channel_id=1, source_target_pairs={{0,2},{1,5},{2,0},{3,7},{4,6},{5,1},{6,4},{7,3},{8,10},{9,13},{10,... | collective-permute-start | bytes 147464 | tf_op jit(solution)/shard_map/ppermute | solution.py:481
  43.4 0.0 collective-permute-done.7
  43.4 1.0 %collective-permute-done.9 = bf16[1,96,384]{2,1,0:T(8,128)(2,1)S(1)} collective-permute-done((bf16[1,96,384]{2,1,0:T(8,128)(2,1)S(1)}, bf16[1,96,384]{2,1,0:T(8,128)(2,1)S(1)}, u32[]{:S(2)}, u32[]{:S(2)}) %collective-permute-start.9) | collective-permute-done | bytes 73760 | tf_op jit(solution)/shard_map/ppermute | solution.py:481
  44.4 3.4 %collective-permute-done.8 = bf16[1,96,384]{2,1,0:T(8,128)(2,1)S(1)} collective-permute-done((bf16[1,96,384]{2,1,0:T(8,128)(2,1)S(1)}, bf16[1,96,384]{2,1,0:T(8,128)(2,1)S(1)}, u32[]{:S(2)}, u32[]{:S(2)}) %collective-permute-start.8) | collective-permute-done | bytes 73760 | tf_op jit(solution)/shard_map/ppermute | solution.py:481
  47.8 0.1 add_convert_fusion.7
  47.9 0.0 collective-permute-done.3
  47.9 0.1 add_convert_fusion.2
  48.1 1.6 %collective-permute-start.10 = (bf16[4,104,384]{2,1,0:T(8,128)(2,1)S(1)}, bf16[4,104,384]{2,1,0:T(8,128)(2,1)S(1)}, u32[]{:S(2)}, u32[]{:S(2)}) collective-permute-start(bf16[4,104,384]{2,1,0:T(8,128)(2,1)S(1)} %pad_maximum_fusion), channel_id=1, source_target_pairs={{0,4},{1,3},{2,6},{3,1},{4,0},{5,7},{6,2},{7,5},{8,12},{9,11},{10,... | collective-permute-start | bytes 958472 | tf_op jit(solution)/shard_map/ppermute | solution.py:481
  49.6 1.8 %collective-permute-start.19 = (bf16[1,96,384]{2,1,0:T(8,128)(2,1)S(1)}, bf16[1,96,384]{2,1,0:T(8,128)(2,1)S(1)}, u32[]{:S(2)}, u32[]{:S(2)}) collective-permute-start(bf16[1,96,384]{2,1,0:T(8,128)(2,1)S(1)} %add_convert_fusion.7), channel_id=1, source_target_pairs={{0,24},{1,25},{2,26},{3,27},{4,28},{5,29},{6,30},{7,31},{8,16},{9,... | collective-permute-start | bytes 221192 | tf_op jit(solution)/shard_map/ppermute | solution.py:481
  51.4 0.5 collective-permute-start.18
  51.9 2.1 %collective-permute-start.17 = (bf16[1,96,384]{2,1,0:T(8,128)(2,1)S(1)}, bf16[1,96,384]{2,1,0:T(8,128)(2,1)S(1)}, u32[]{:S(2)}, u32[]{:S(2)}) collective-permute-start(bf16[1,96,384]{2,1,0:T(8,128)(2,1)S(1)} %add_convert_fusion.7), channel_id=1, source_target_pairs={{0,16},{1,17},{2,18},{3,19},{4,20},{5,21},{6,22},{7,23},{8,24},{9,... | collective-permute-start | bytes 221192 | tf_op jit(solution)/shard_map/ppermute | solution.py:481
  54.1 1.1 %collective-permute-done.10 = bf16[4,104,384]{2,1,0:T(8,128)(2,1)S(1)} collective-permute-done((bf16[4,104,384]{2,1,0:T(8,128)(2,1)S(1)}, bf16[4,104,384]{2,1,0:T(8,128)(2,1)S(1)}, u32[]{:S(2)}, u32[]{:S(2)}) %collective-permute-start.10) | collective-permute-done | bytes 319520 | tf_op jit(solution)/shard_map/ppermute | solution.py:481
  55.1 0.1 convert_add_fusion
  55.3 1.8 %collective-permute-start.11 = (bf16[1,104,384]{2,1,0:T(8,128)(2,1)S(1)}, bf16[1,104,384]{2,1,0:T(8,128)(2,1)S(1)}, u32[]{:S(2)}, u32[]{:S(2)}) collective-permute-start(bf16[1,104,384]{2,1,0:T(8,128)(2,1)S(1)} %pad_maximum_fusion.2), channel_id=1, source_target_pairs={{0,16},{1,17},{2,18},{3,19},{4,20},{5,21},{6,22},{7,23},{8,24},{9,... | collective-permute-start | bytes 239624 | tf_op jit(solution)/shard_map/ppermute | solution.py:481
  57.1 0.5 collective-permute-start.12
  57.7 1.4 %collective-permute-start.13 = (bf16[1,104,384]{2,1,0:T(8,128)(2,1)S(1)}, bf16[1,104,384]{2,1,0:T(8,128)(2,1)S(1)}, u32[]{:S(2)}, u32[]{:S(2)}) collective-permute-start(bf16[1,104,384]{2,1,0:T(8,128)(2,1)S(1)} %pad_maximum_fusion.4), channel_id=1, source_target_pairs={{0,8},{1,9},{2,10},{3,11},{4,12},{5,13},{6,14},{7,15},{8,0},{9,1},... | collective-permute-start | bytes 239624 | tf_op jit(solution)/shard_map/ppermute | solution.py:481
  59.0 2.1 %collective-permute-done.17 = bf16[1,96,384]{2,1,0:T(8,128)(2,1)S(1)} collective-permute-done((bf16[1,96,384]{2,1,0:T(8,128)(2,1)S(1)}, bf16[1,96,384]{2,1,0:T(8,128)(2,1)S(1)}, u32[]{:S(2)}, u32[]{:S(2)}) %collective-permute-start.17) | collective-permute-done | bytes 73760 | tf_op jit(solution)/shard_map/ppermute | solution.py:481
  61.3 1.5 %collective-permute-start.21 = (bf16[4,96,384]{2,1,0:T(8,128)(2,1)S(1)}, bf16[4,96,384]{2,1,0:T(8,128)(2,1)S(1)}, u32[]{:S(2)}, u32[]{:S(2)}) collective-permute-start(bf16[4,96,384]{2,1,0:T(8,128)(2,1)S(1)} %get-tuple-element.195), channel_id=1, source_target_pairs={{0,2},{1,5},{2,0},{3,7},{4,6},{5,1},{6,4},{7,3},{8,10},{9,13},{10,... | collective-permute-start | bytes 884744 | tf_op jit(solution)/shard_map/ppermute | solution.py:481
  62.8 0.9 collective-permute-done.11
  63.7 0.2 collective-permute-done.13
  64.0 2.4 %collective-permute-start.16 = (bf16[1,104,384]{2,1,0:T(8,128)(2,1)S(1)}, bf16[1,104,384]{2,1,0:T(8,128)(2,1)S(1)}, u32[]{:S(2)}, u32[]{:S(2)}) collective-permute-start(bf16[1,104,384]{2,1,0:T(8,128)(2,1)S(1)} %get-tuple-element.182), channel_id=1, source_target_pairs={{0,24},{1,25},{2,26},{3,27},{4,28},{5,29},{6,30},{7,31},{8,16},{9,... | collective-permute-start | bytes 239624 | tf_op jit(solution)/shard_map/ppermute | solution.py:481
  66.5 0.5 collective-permute-start.15
  67.0 1.5 %collective-permute-start.14 = (bf16[1,104,384]{2,1,0:T(8,128)(2,1)S(1)}, bf16[1,104,384]{2,1,0:T(8,128)(2,1)S(1)}, u32[]{:S(2)}, u32[]{:S(2)}) collective-permute-start(bf16[1,104,384]{2,1,0:T(8,128)(2,1)S(1)} %get-tuple-element.182), channel_id=1, source_target_pairs={{0,16},{1,17},{2,18},{3,19},{4,20},{5,21},{6,22},{7,23},{8,24},{9,... | collective-permute-start | bytes 239624 | tf_op jit(solution)/shard_map/ppermute | solution.py:481
  68.5 1.0 %collective-permute-done.20 = bf16[4,96,384]{2,1,0:T(8,128)(2,1)S(1)} collective-permute-done((bf16[4,96,384]{2,1,0:T(8,128)(2,1)S(1)}, bf16[4,96,384]{2,1,0:T(8,128)(2,1)S(1)}, u32[]{:S(2)}, u32[]{:S(2)}) %collective-permute-start.20) | collective-permute-done | bytes 294944 | tf_op jit(solution)/shard_map/ppermute | solution.py:481
  69.5 0.5 collective-permute-start.25
  70.1 0.9 collective-permute-done.16
  71.0 1.6 %collective-permute-done.15 = bf16[1,104,384]{2,1,0:T(8,128)(2,1)S(1)} collective-permute-done((bf16[1,104,384]{2,1,0:T(8,128)(2,1)S(1)}, bf16[1,104,384]{2,1,0:T(8,128)(2,1)S(1)}, u32[]{:S(2)}, u32[]{:S(2)}) %collective-permute-start.15) | collective-permute-done | bytes 79904 | tf_op jit(solution)/shard_map/ppermute | solution.py:481
  72.6 1.1 %collective-permute-done.14 = bf16[1,104,384]{2,1,0:T(8,128)(2,1)S(1)} collective-permute-done((bf16[1,104,384]{2,1,0:T(8,128)(2,1)S(1)}, bf16[1,104,384]{2,1,0:T(8,128)(2,1)S(1)}, u32[]{:S(2)}, u32[]{:S(2)}) %collective-permute-start.14) | collective-permute-done | bytes 79904 | tf_op jit(solution)/shard_map/ppermute | solution.py:481
  73.7 0.1 pad_maximum_fusion.1
  73.8 1.5 %collective-permute-start.23 = (bf16[4,104,384]{2,1,0:T(8,128)(2,1)S(1)}, bf16[4,104,384]{2,1,0:T(8,128)(2,1)S(1)}, u32[]{:S(2)}, u32[]{:S(2)}) collective-permute-start(bf16[4,104,384]{2,1,0:T(8,128)(2,1)S(1)} %pad_maximum_fusion.1), channel_id=1, source_target_pairs={{0,2},{1,5},{2,0},{3,7},{4,6},{5,1},{6,4},{7,3},{8,10},{9,13},{10,... | collective-permute-start | bytes 958472 | tf_op jit(solution)/shard_map/ppermute | solution.py:481
  75.3 0.3 collective-permute-start.22
  75.6 0.1 collective-permute-start.29
  75.7 7.6 %collective-permute-done.23.refs_4_ = bf16[4,104,384]{2,1,0:T(8,128)(2,1)S(1)} collective-permute-done((bf16[4,104,384]{2,1,0:T(8,128)(2,1)S(1)}, bf16[4,104,384]{2,1,0:T(8,128)(2,1)S(1)}, u32[]{:S(2)}, u32[]{:S(2)}) %collective-permute-start.23) | collective-permute-done | bytes 319520 | tf_op jit(solution)/shard_map/ppermute | solution.py:481
  83.3 0.1 constant_dynamic-update-slice_fusion.6.refs_3_
  83.4 0.1 collective-permute-start.27
  83.6 0.6 collective-permute-start.26
  84.1 1.2 %collective-permute-start.24 = (bf16[4,104,384]{2,1,0:T(8,128)(2,1)S(1)}, bf16[4,104,384]{2,1,0:T(8,128)(2,1)S(1)}, u32[]{:S(2)}, u32[]{:S(2)}) collective-permute-start(bf16[4,104,384]{2,1,0:T(8,128)(2,1)S(1)} %collective-permute-done.22), channel_id=1, source_target_pairs={{0,2},{1,5},{2,0},{3,7},{4,6},{5,1},{6,4},{7,3},{8,10},{9,13},{10,... | collective-permute-start | bytes 958472 | tf_op jit(solution)/shard_map/ppermute | solution.py:481
  85.3 0.1 collective-permute-start.28
  85.5 3.0 %unpack_kept.1 = (f32[2,384,1536]{2,1,0:T(8,128)}, f32[2,1536,384]{2,1,0:T(8,128)}, f32[32,8,384]{2,1,0:T(8,128)S(1)}) custom-call(bf16[8,96,384]{2,1,0:T(8,128)(2,1)S(1)} %constant_dynamic-update-slice_fusion.11.refs_0_, bf16[8,96,384]{2,1,0:T(8,128)(2,1)S(1)} %collective-permute-done.29.refs_1_, ...), custom_call_target="tpu_custom_call" | custom-call | flops 4499999744 | bytes 13500000 | tf_op jit(solution)/shard_map/unpack_kept/pallas_call | solution.py:682
  88.5 2.0 %unpack_others.1 = (f32[2,384,1536]{2,1,0:T(8,128)}, f32[2,1536,384]{2,1,0:T(8,128)}, f32[32,8,384]{2,1,0:T(8,128)S(1)}) custom-call(bf16[8,96,384]{2,1,0:T(8,128)(2,1)S(1)} %collective-permute-done.26.refs_0_, bf16[8,104,384]{2,1,0:T(8,128)(2,1)S(1)} %collective-permute-done.27.refs_1_, ...), custom_call_target="tpu_custom_call", output_to_operand_aliasing={{0}: (3, {}), {1}: (4, {}), {2}: (5, {})} | custom-call | flops 2500000000 | bytes 7500000 | tf_op jit(solution)/shard_map/unpack_others/pallas_call | solution.py:682
  90.6 0.5 collective-permute-done.24.refs_0_
  91.1 0.9 unpack_latest.1
  92.0 0.7 collective-permute-done.30.other_late
  92.7 1.3 %unpack_rest.1 = (f32[2,384,1536]{2,1,0:T(8,128)}, f32[2,1536,384]{2,1,0:T(8,128)}, f32[32,8,384]{2,1,0:T(8,128)S(1)}, f32[196,2,196]{2,1,0:T(2,128)}, f32[2,384...) custom-call(bf16[4,104,384]{2,1,0:T(8,128)(2,1)S(1)} %collective-per, ...), custom_call_target="tpu_custom_call", output_to_operand_aliasing={{0}: (1, {}), {1}: (2, {}), {2}: (3, {})} | custom-call | flops 2000000000 | bytes 6000000 | tf_op jit(solution)/shard_map/unpack_rest/pallas_call | solution.py:682
  (33 shorter events, 0.5 us)
Async XLA Ops:
  15.9 3.1 %collective-permute-start = (bf16[16,96,384]{2,1,0:T(8,128)(2,1)S(1)}, bf16[16,96,384]{2,1,0:T(8,128)(2,1)S(1)}, u32[]{:S(2)}, u32[]{:S(2)}) collective-permute-start(bf16[16,96,384]{2,1,0:T(8,128)(2,1)S(1)} %get-tuple-element.115), channel_id=1, source_target_pairs={{0,1},{1,0},{2,3},{3,2},{4,5},{5,4},{6,7},{7,6},{8,9},{9,8},{10,11... | collective-permute-start | bytes 3538952 | tf_op jit(solution)/shard_map/ppermute | solution.py:481
  19.2 10.7 %collective-permute-start.1 = (bf16[8,96,384]{2,1,0:T(8,128)(2,1)S(1)}, bf16[8,96,384]{2,1,0:T(8,128)(2,1)S(1)}, u32[]{:S(2)}, u32[]{:S(2)}) collective-permute-start(bf16[8,96,384]{2,1,0:T(8,128)(2,1)S(1)} %add_convert_fusion.1), channel_id=1, source_target_pairs={{0,2},{1,5},{2,0},{3,7},{4,6},{5,1},{6,4},{7,3},{8,10},{9,13},{10,... | collective-permute-start | bytes 1769480 | tf_op jit(solution)/shard_map/ppermute | solution.py:481
  29.9 5.4 %collective-permute-start.2 = (bf16[16,96,384]{2,1,0:T(8,128)(2,1)S(1)}, bf16[16,96,384]{2,1,0:T(8,128)(2,1)S(1)}, u32[]{:S(2)}, u32[]{:S(2)}) collective-permute-start(bf16[16,96,384]{2,1,0:T(8,128)(2,1)S(1)} %get-tuple-element.138), channel_id=1, source_target_pairs={{0,1},{1,0},{2,3},{3,2},{4,5},{5,4},{6,7},{7,6},{8,9},{9,8},{10,11... | collective-permute-start | bytes 3538952 | tf_op jit(solution)/shard_map/ppermute | solution.py:481
  30.0 6.8 %collective-permute-start.6 = (bf16[4,96,384]{2,1,0:T(8,128)(2,1)S(1)}, bf16[4,96,384]{2,1,0:T(8,128)(2,1)S(1)}, u32[]{:S(2)}, u32[]{:S(2)}) collective-permute-start(bf16[4,96,384]{2,1,0:T(8,128)(2,1)S(1)} %add_convert_fusion.3), channel_id=1, source_target_pairs={{0,4},{1,3},{2,6},{3,1},{4,0},{5,7},{6,2},{7,5},{8,12},{9,11},{10,... | collective-permute-start | bytes 884744 | tf_op jit(solution)/shard_map/ppermute | solution.py:481
  35.1 6.5 %collective-permute-start.4 = (bf16[16,8,384]{2,1,0:T(8,128)(2,1)S(1)}, bf16[16,8,384]{2,1,0:T(8,128)(2,1)S(1)}, u32[]{:S(2)}, u32[]{:S(2)}) collective-permute-start(bf16[16,8,384]{2,1,0:T(8,128)(2,1)S(1)} %get-tuple-element.140), channel_id=1, source_target_pairs={{0,1},{1,0},{2,3},{3,2},{4,5},{5,4},{6,7},{7,6},{8,9},{9,8},{10,11... | collective-permute-start | bytes 294920 | tf_op jit(solution)/shard_map/ppermute | solution.py:481
  35.4 12.4 %collective-permute-start.3 = (bf16[8,96,384]{2,1,0:T(8,128)(2,1)S(1)}, bf16[8,96,384]{2,1,0:T(8,128)(2,1)S(1)}, u32[]{:S(2)}, u32[]{:S(2)}) collective-permute-start(bf16[8,96,384]{2,1,0:T(8,128)(2,1)S(1)} %add_convert_fusion), channel_id=1, source_target_pairs={{0,2},{1,5},{2,0},{3,7},{4,6},{5,1},{6,4},{7,3},{8,10},{9,13},{10,... | collective-permute-start | bytes 1769480 | tf_op jit(solution)/shard_map/ppermute | solution.py:481
  36.9 6.5 %collective-permute-start.7 = (bf16[1,96,384]{2,1,0:T(8,128)(2,1)S(1)}, bf16[1,96,384]{2,1,0:T(8,128)(2,1)S(1)}, u32[]{:S(2)}, u32[]{:S(2)}) collective-permute-start(bf16[1,96,384]{2,1,0:T(8,128)(2,1)S(1)} %get-tuple-element.187), channel_id=1, source_target_pairs={{0,16},{1,17},{2,18},{3,19},{4,20},{5,21},{6,22},{7,23},{8,24},{9,... | collective-permute-start | bytes 221192 | tf_op jit(solution)/shard_map/ppermute | solution.py:481
  40.1 4.4 %collective-permute-start.9 = (bf16[1,96,384]{2,1,0:T(8,128)(2,1)S(1)}, bf16[1,96,384]{2,1,0:T(8,128)(2,1)S(1)}, u32[]{:S(2)}, u32[]{:S(2)}) collective-permute-start(bf16[1,96,384]{2,1,0:T(8,128)(2,1)S(1)} %get-tuple-element.188), channel_id=1, source_target_pairs={{0,8},{1,9},{2,10},{3,11},{4,12},{5,13},{6,14},{7,15},{8,0},{9,1},... | collective-permute-start | bytes 221192 | tf_op jit(solution)/shard_map/ppermute | solution.py:481
  41.6 6.2 %collective-permute-start.8 = (bf16[1,96,384]{2,1,0:T(8,128)(2,1)S(1)}, bf16[1,96,384]{2,1,0:T(8,128)(2,1)S(1)}, u32[]{:S(2)}, u32[]{:S(2)}) collective-permute-start(bf16[1,96,384]{2,1,0:T(8,128)(2,1)S(1)} %get-tuple-element.189), channel_id=1, source_target_pairs={{0,24},{1,25},{2,26},{3,27},{4,28},{5,29},{6,30},{7,31},{8,16},{9,... | collective-permute-start | bytes 221192 | tf_op jit(solution)/shard_map/ppermute | solution.py:481
  41.7 6.2 %collective-permute-start.5 = (bf16[8,8,384]{2,1,0:T(8,128)(2,1)S(1)}, bf16[8,8,384]{2,1,0:T(8,128)(2,1)S(1)}, u32[]{:S(2)}, u32[]{:S(2)}) collective-permute-start(bf16[8,8,384]{2,1,0:T(8,128)(2,1)S(1)} %add_convert_fusion.11), channel_id=1, source_target_pairs={{0,2},{1,5},{2,0},{3,7},{4,6},{5,1},{6,4},{7,3},{8,10},{9,13},{10,... | collective-permute-start | bytes 147464 | tf_op jit(solution)/shard_map/ppermute | solution.py:481
  48.1 7.1 %collective-permute-start.10 = (bf16[4,104,384]{2,1,0:T(8,128)(2,1)S(1)}, bf16[4,104,384]{2,1,0:T(8,128)(2,1)S(1)}, u32[]{:S(2)}, u32[]{:S(2)}) collective-permute-start(bf16[4,104,384]{2,1,0:T(8,128)(2,1)S(1)} %pad_maximum_fusion), channel_id=1, source_target_pairs={{0,4},{1,3},{2,6},{3,1},{4,0},{5,7},{6,2},{7,5},{8,12},{9,11},{10,... | collective-permute-start | bytes 958472 | tf_op jit(solution)/shard_map/ppermute | solution.py:481
  49.6 8.0 %collective-permute-start.19 = (bf16[1,96,384]{2,1,0:T(8,128)(2,1)S(1)}, bf16[1,96,384]{2,1,0:T(8,128)(2,1)S(1)}, u32[]{:S(2)}, u32[]{:S(2)}) collective-permute-start(bf16[1,96,384]{2,1,0:T(8,128)(2,1)S(1)} %add_convert_fusion.7), channel_id=1, source_target_pairs={{0,24},{1,25},{2,26},{3,27},{4,28},{5,29},{6,30},{7,31},{8,16},{9,... | collective-permute-start | bytes 221192 | tf_op jit(solution)/shard_map/ppermute | solution.py:481
  51.4 7.6 %collective-permute-start.18 = (bf16[1,96,384]{2,1,0:T(8,128)(2,1)S(1)}, bf16[1,96,384]{2,1,0:T(8,128)(2,1)S(1)}, u32[]{:S(2)}, u32[]{:S(2)}) collective-permute-start(bf16[1,96,384]{2,1,0:T(8,128)(2,1)S(1)} %add_convert_fusion.7), channel_id=1, source_target_pairs={{0,8},{1,9},{2,10},{3,11},{4,12},{5,13},{6,14},{7,15},{8,0},{9,1},... | collective-permute-start | bytes 221192 | tf_op jit(solution)/shard_map/ppermute | solution.py:481
  51.9 9.2 %collective-permute-start.17 = (bf16[1,96,384]{2,1,0:T(8,128)(2,1)S(1)}, bf16[1,96,384]{2,1,0:T(8,128)(2,1)S(1)}, u32[]{:S(2)}, u32[]{:S(2)}) collective-permute-start(bf16[1,96,384]{2,1,0:T(8,128)(2,1)S(1)} %add_convert_fusion.7), channel_id=1, source_target_pairs={{0,16},{1,17},{2,18},{3,19},{4,20},{5,21},{6,22},{7,23},{8,24},{9,... | collective-permute-start | bytes 221192 | tf_op jit(solution)/shard_map/ppermute | solution.py:481
  55.3 8.4 %collective-permute-start.11 = (bf16[1,104,384]{2,1,0:T(8,128)(2,1)S(1)}, bf16[1,104,384]{2,1,0:T(8,128)(2,1)S(1)}, u32[]{:S(2)}, u32[]{:S(2)}) collective-permute-start(bf16[1,104,384]{2,1,0:T(8,128)(2,1)S(1)} %pad_maximum_fusion.2), channel_id=1, source_target_pairs={{0,16},{1,17},{2,18},{3,19},{4,20},{5,21},{6,22},{7,23},{8,24},{9,... | collective-permute-start | bytes 239624 | tf_op jit(solution)/shard_map/ppermute | solution.py:481
  57.1 6.6 %collective-permute-start.12 = (bf16[1,104,384]{2,1,0:T(8,128)(2,1)S(1)}, bf16[1,104,384]{2,1,0:T(8,128)(2,1)S(1)}, u32[]{:S(2)}, u32[]{:S(2)}) collective-permute-start(bf16[1,104,384]{2,1,0:T(8,128)(2,1)S(1)} %pad_maximum_fusion.3), channel_id=1, source_target_pairs={{0,24},{1,25},{2,26},{3,27},{4,28},{5,29},{6,30},{7,31},{8,16},{9,... | collective-permute-start | bytes 239624 | tf_op jit(solution)/shard_map/ppermute | solution.py:481
  57.7 6.3 %collective-permute-start.13 = (bf16[1,104,384]{2,1,0:T(8,128)(2,1)S(1)}, bf16[1,104,384]{2,1,0:T(8,128)(2,1)S(1)}, u32[]{:S(2)}, u32[]{:S(2)}) collective-permute-start(bf16[1,104,384]{2,1,0:T(8,128)(2,1)S(1)} %pad_maximum_fusion.4), channel_id=1, source_target_pairs={{0,8},{1,9},{2,10},{3,11},{4,12},{5,13},{6,14},{7,15},{8,0},{9,1},... | collective-permute-start | bytes 239624 | tf_op jit(solution)/shard_map/ppermute | solution.py:481
  61.3 12.5 %collective-permute-start.21 = (bf16[4,96,384]{2,1,0:T(8,128)(2,1)S(1)}, bf16[4,96,384]{2,1,0:T(8,128)(2,1)S(1)}, u32[]{:S(2)}, u32[]{:S(2)}) collective-permute-start(bf16[4,96,384]{2,1,0:T(8,128)(2,1)S(1)} %get-tuple-element.195), channel_id=1, source_target_pairs={{0,2},{1,5},{2,0},{3,7},{4,6},{5,1},{6,4},{7,3},{8,10},{9,13},{10,... | collective-permute-start | bytes 884744 | tf_op jit(solution)/shard_map/ppermute | solution.py:481
  62.8 6.7 %collective-permute-start.20 = (bf16[4,96,384]{2,1,0:T(8,128)(2,1)S(1)}, bf16[4,96,384]{2,1,0:T(8,128)(2,1)S(1)}, u32[]{:S(2)}, u32[]{:S(2)}) collective-permute-start(bf16[4,96,384]{2,1,0:T(8,128)(2,1)S(1)} %get-tuple-element.195), channel_id=1, source_target_pairs={{0,4},{1,3},{2,6},{3,1},{4,0},{5,7},{6,2},{7,5},{8,12},{9,11},{10,... | collective-permute-start | bytes 884744 | tf_op jit(solution)/shard_map/ppermute | solution.py:481
  64.0 7.0 %collective-permute-start.16 = (bf16[1,104,384]{2,1,0:T(8,128)(2,1)S(1)}, bf16[1,104,384]{2,1,0:T(8,128)(2,1)S(1)}, u32[]{:S(2)}, u32[]{:S(2)}) collective-permute-start(bf16[1,104,384]{2,1,0:T(8,128)(2,1)S(1)} %get-tuple-element.182), channel_id=1, source_target_pairs={{0,24},{1,25},{2,26},{3,27},{4,28},{5,29},{6,30},{7,31},{8,16},{9,... | collective-permute-start | bytes 239624 | tf_op jit(solution)/shard_map/ppermute | solution.py:481
  66.5 6.2 %collective-permute-start.15 = (bf16[1,104,384]{2,1,0:T(8,128)(2,1)S(1)}, bf16[1,104,384]{2,1,0:T(8,128)(2,1)S(1)}, u32[]{:S(2)}, u32[]{:S(2)}) collective-permute-start(bf16[1,104,384]{2,1,0:T(8,128)(2,1)S(1)} %get-tuple-element.182), channel_id=1, source_target_pairs={{0,8},{1,9},{2,10},{3,11},{4,12},{5,13},{6,14},{7,15},{8,0},{9,1},... | collective-permute-start | bytes 239624 | tf_op jit(solution)/shard_map/ppermute | solution.py:481
  67.0 6.7 %collective-permute-start.14 = (bf16[1,104,384]{2,1,0:T(8,128)(2,1)S(1)}, bf16[1,104,384]{2,1,0:T(8,128)(2,1)S(1)}, u32[]{:S(2)}, u32[]{:S(2)}) collective-permute-start(bf16[1,104,384]{2,1,0:T(8,128)(2,1)S(1)} %get-tuple-element.182), channel_id=1, source_target_pairs={{0,16},{1,17},{2,18},{3,19},{4,20},{5,21},{6,22},{7,23},{8,24},{9,... | collective-permute-start | bytes 239624 | tf_op jit(solution)/shard_map/ppermute | solution.py:481
  69.5 13.8 %collective-permute-start.25 = (bf16[4,96,384]{2,1,0:T(8,128)(2,1)S(1)}, bf16[4,96,384]{2,1,0:T(8,128)(2,1)S(1)}, u32[]{:S(2)}, u32[]{:S(2)}) collective-permute-start(bf16[4,96,384]{2,1,0:T(8,128)(2,1)S(1)} %collective-permute-done.20), channel_id=1, source_target_pairs={{0,2},{1,5},{2,0},{3,7},{4,6},{5,1},{6,4},{7,3},{8,10},{9,13},{10,... | collective-permute-start | bytes 884744 | tf_op jit(solution)/shard_map/ppermute | solution.py:481
  73.8 9.5 %collective-permute-start.23 = (bf16[4,104,384]{2,1,0:T(8,128)(2,1)S(1)}, bf16[4,104,384]{2,1,0:T(8,128)(2,1)S(1)}, u32[]{:S(2)}, u32[]{:S(2)}) collective-permute-start(bf16[4,104,384]{2,1,0:T(8,128)(2,1)S(1)} %pad_maximum_fusion.1), channel_id=1, source_target_pairs={{0,2},{1,5},{2,0},{3,7},{4,6},{5,1},{6,4},{7,3},{8,10},{9,13},{10,... | collective-permute-start | bytes 958472 | tf_op jit(solution)/shard_map/ppermute | solution.py:481
  75.3 8.1 %collective-permute-start.22 = (bf16[4,104,384]{2,1,0:T(8,128)(2,1)S(1)}, bf16[4,104,384]{2,1,0:T(8,128)(2,1)S(1)}, u32[]{:S(2)}, u32[]{:S(2)}) collective-permute-start(bf16[4,104,384]{2,1,0:T(8,128)(2,1)S(1)} %pad_maximum_fusion.1), channel_id=1, source_target_pairs={{0,4},{1,3},{2,6},{3,1},{4,0},{5,7},{6,2},{7,5},{8,12},{9,11},{10,... | collective-permute-start | bytes 958472 | tf_op jit(solution)/shard_map/ppermute | solution.py:481
  75.6 9.9 %collective-permute-start.29 = (bf16[8,96,384]{2,1,0:T(8,128)(2,1)S(1)}, bf16[8,96,384]{2,1,0:T(8,128)(2,1)S(1)}, u32[]{:S(2)}, u32[]{:S(2)}) collective-permute-start(bf16[8,96,384]{2,1,0:T(8,128)(2,1)S(1)} %constant_dynamic-update-slice_fusion.11.refs_0_), channel_id=1, source_target_pairs={{0,1},{1,0},{2,3},{3,2},{4,5},{5,4},{6,7},{7,6},{8,9},{9,8},{10,11... | collective-permute-start | bytes 1769480 | tf_op jit(solution)/shard_map/ppermute | solution.py:481
  83.4 5.1 %collective-permute-start.27 = (bf16[8,104,384]{2,1,0:T(8,128)(2,1)S(1)}, bf16[8,104,384]{2,1,0:T(8,128)(2,1)S(1)}, u32[]{:S(2)}, u32[]{:S(2)}) collective-permute-start(bf16[8,104,384]{2,1,0:T(8,128)(2,1)S(1)} %constant_dynamic-update-slice_fusion.6.refs_3_), channel_id=1, source_target_pairs={{0,1},{1,0},{2,3},{3,2},{4,5},{5,4},{6,7},{7,6},{8,9},{9,8},{10,11... | collective-permute-start | bytes 1916936 | tf_op jit(solution)/shard_map/ppermute | solution.py:481
  83.6 4.9 %collective-permute-start.26 = (bf16[8,96,384]{2,1,0:T(8,128)(2,1)S(1)}, bf16[8,96,384]{2,1,0:T(8,128)(2,1)S(1)}, u32[]{:S(2)}, u32[]{:S(2)}) collective-permute-start(bf16[8,96,384]{2,1,0:T(8,128)(2,1)S(1)} %constant_dynamic-update-slice_fusion.4.refs_2_), channel_id=1, source_target_pairs={{0,1},{1,0},{2,3},{3,2},{4,5},{5,4},{6,7},{7,6},{8,9},{9,8},{10,11... | collective-permute-start | bytes 1769480 | tf_op jit(solution)/shard_map/ppermute | solution.py:481
  84.1 7.0 %collective-permute-start.24 = (bf16[4,104,384]{2,1,0:T(8,128)(2,1)S(1)}, bf16[4,104,384]{2,1,0:T(8,128)(2,1)S(1)}, u32[]{:S(2)}, u32[]{:S(2)}) collective-permute-start(bf16[4,104,384]{2,1,0:T(8,128)(2,1)S(1)} %collective-permute-done.22), channel_id=1, source_target_pairs={{0,2},{1,5},{2,0},{3,7},{4,6},{5,1},{6,4},{7,3},{8,10},{9,13},{10,... | collective-permute-start | bytes 958472 | tf_op jit(solution)/shard_map/ppermute | solution.py:481
  85.3 3.2 %collective-permute-start.28 = (bf16[4,104,384]{2,1,0:T(8,128)(2,1)S(1)}, bf16[4,104,384]{2,1,0:T(8,128)(2,1)S(1)}, u32[]{:S(2)}, u32[]{:S(2)}) collective-permute-start(bf16[4,104,384]{2,1,0:T(8,128)(2,1)S(1)} %collective-permute-done.23.refs_4_), channel_id=1, source_target_pairs={{0,1},{1,0},{2,3},{3,2},{4,5},{5,4},{6,7},{7,6},{8,9},{9,8},{10,11... | collective-permute-start | bytes 958472 | tf_op jit(solution)/shard_map/ppermute | solution.py:481
  91.1 1.6 %collective-permute-start.30 = (bf16[4,104,384]{2,1,0:T(8,128)(2,1)S(1)}, bf16[4,104,384]{2,1,0:T(8,128)(2,1)S(1)}, u32[]{:S(2)}, u32[]{:S(2)}) collective-permute-start(bf16[4,104,384]{2,1,0:T(8,128)(2,1)S(1)} %collective-permute-done.24.refs_0_), channel_id=1, source_target_pairs={{0,1},{1,0},{2,3},{3,2},{4,5},{5,4},{6,7},{7,6},{8,9},{9,8},{10,11... | collective-permute-start | bytes 958472 | tf_op jit(solution)/shard_map/ppermute | solution.py:481
